TPU v7x, 32 devices: a whole 2x2x4 slice. The times are simulated.
32 devices in a mesh: dp: 4 (over y, x), tile: 8 (over z, core).
Axes of the slice: x: 2, y: 2, z: 4, core: 2. Of those that a mesh axis runs over, the one named last changes fastest.
Arguments:
- features: bfloat16 [4, 128, 64, 256], P('dp', 'tile'), may hold values from -6 to 6
- fpn_weight: bfloat16 [9, 256, 256], replicated, may hold values from -0.125 to 0.125
- mask_w1: bfloat16 [9, 256, 256], replicated, may hold values from -0.125 to 0.125
- mask_w2: bfloat16 [9, 256, 256], replicated, may hold values from -0.125 to 0.125
- owner: int32 [4, 32, 1], P('dp', 'tile'), may hold values from 0 to 7; in each aligned block of 4 rows (0 to 3, 4 to 7, ..., all dimensions but the last counted through in order) at most 2 rows name the same one
- row_off: int32 [4, 32], P('dp', 'tile'), may hold values from 0 to 2
- col_off: int32 [4, 32], P('dp', 'tile'), may hold values from 0 to 50
- cotangent: bfloat16 [4, 32, 14, 14, 256], P('dp', 'tile'), may hold values from -6 to 6
Outputs:
- grad_w1: float32 [2304, 256], P('dp')
- grad_w2: float32 [2304, 256], P('dp')
- grad_pyramid: bfloat16 [4, 128, 64, 256], P('dp', 'tile')
Inputs may be any that keep to these rules, and one draw needn't show every extreme that they name: `owner`: among the 4 regions of one device no tile is named more than 2 times.
All inputs are finite; a program needn't handle non-finite values.
Results may differ from a plain program's by a relative error of at most 0.017.
Values may be sent and summed in bfloat16 or wider, within the bound.
No kernel may reach another device: no remote copies, remote signals or barrier semaphores. Data moves between devices by JAX's collectives and lax.ppermute only.
A program may use at most 128 MiB of HBM per device.

v0:
```python
import jax
import jax.numpy as jnp
from jax import lax
from jax.sharding import PartitionSpec as P

CAP = 2


def extended(cells, sides, width):
    for axis, dim in sides:
        count = lax.axis_size(axis)
        ends = count - 1
        head = lax.slice_in_dim(cells, 0, width, axis=dim)
        tail = lax.slice_in_dim(cells, cells.shape[dim] - width, cells.shape[dim], axis=dim)
        cells = jnp.concatenate(
            [
                lax.ppermute(tail, axis, [(i, (i + 1) % count) for i in range(ends)]),
                cells,
                lax.ppermute(head, axis, [((i + 1) % count, i) for i in range(ends)]),
            ],
            axis=dim,
        )
    return cells


def smooth(values):
    return jax.nn.gelu(values, approximate=True)


def conv_padded(padded, kernel):
    batch, rows, cols, channels = padded.shape
    height, width = (rows - 2, cols - 2)
    running = jnp.zeros((batch * height * width, kernel.shape[2]), jnp.float32)
    for row_tap in range(3):
        for col_tap in range(3):
            window = padded[:, row_tap : row_tap + height, col_tap : col_tap + width, :]
            running = running + jnp.dot(
                window.reshape(-1, channels),
                kernel[3 * row_tap + col_tap],
                preferred_element_type=jnp.float32,
            )
    return running.reshape(batch, height, width, kernel.shape[2])


def conv_same(source, kernel):
    return conv_padded(jnp.pad(source, ((0, 0), (1, 1), (1, 1), (0, 0))), kernel)


def tap_grads(source, grads):
    batch, height, width, channels = source.shape
    padded = jnp.pad(source, ((0, 0), (1, 1), (1, 1), (0, 0)))
    flat_grads = grads.reshape(-1, grads.shape[3])
    pieces = []
    for row_tap in range(3):
        for col_tap in range(3):
            window = padded[:, row_tap : row_tap + height, col_tap : col_tap + width, :]
            pieces.append(
                jnp.dot(
                    window.reshape(-1, channels).T, flat_grads, preferred_element_type=jnp.float32
                )
            )
    return jnp.stack(pieces)


def conv_back(grads, kernel):
    batch, height, width, channels = grads.shape
    padded = jnp.pad(grads, ((0, 0), (1, 1), (1, 1), (0, 0)))
    running = jnp.zeros((batch * height * width, kernel.shape[1]), jnp.float32)
    for row_tap in range(3):
        for col_tap in range(3):
            window = padded[
                :, 2 - row_tap : 2 - row_tap + height, 2 - col_tap : 2 - col_tap + width, :
            ]
            running = running + jnp.dot(
                window.reshape(-1, channels),
                kernel[3 * row_tap + col_tap].T,
                preferred_element_type=jnp.float32,
            )
    return running.reshape(batch, height, width, kernel.shape[1])


def mask_head(crops, mask_w1, mask_w2, cotangent):
    pre1 = conv_same(crops, mask_w1)
    act1 = smooth(pre1).astype(jnp.bfloat16)
    pre2 = conv_same(act1, mask_w2)
    _, pull_two = jax.vjp(smooth, pre2)
    g2 = pull_two(cotangent.astype(jnp.float32))[0].astype(jnp.bfloat16)
    grad_two = tap_grads(act1, g2)
    gact1 = conv_back(g2, mask_w2)
    _, pull_one = jax.vjp(smooth, pre1)
    g1 = pull_one(gact1)[0].astype(jnp.bfloat16)
    grad_one = tap_grads(crops, g1)
    gcrop = conv_back(g1, mask_w1).astype(jnp.bfloat16)
    return (grad_one, grad_two, gcrop)


def owner_ranks(owner_grid):
    region_count = owner_grid.shape[1]
    same_owner = owner_grid[:, :, None] == owner_grid[:, None, :]
    earlier = jnp.arange(region_count)[None, :] < jnp.arange(region_count)[:, None]
    return jnp.sum((same_owner & earlier[None]).astype(jnp.int32), axis=2)


def body(features, fpn_weight, mask_w1, mask_w2, owner, row_off, col_off, cotangent):
    tile_count = lax.axis_size("tile")
    own_index = lax.axis_index("tile")
    height, width, channels = (features.shape[1], features.shape[2], features.shape[3])
    region_count = cotangent.shape[1]
    crop_size = cotangent.shape[2]
    slot_cap = CAP
    rimmed = extended(features, (("tile", 1),), 1)
    padded = jnp.pad(rimmed, ((0, 0), (0, 0), (1, 1), (0, 0)))
    pyramid = conv_padded(padded, fpn_weight)[0].astype(jnp.bfloat16)
    owners_all, rows_all, cols_all = (
        lax.all_gather(owner[0, :, 0], "tile", axis=0, tiled=True),
        lax.all_gather(row_off[0], "tile", axis=0, tiled=True),
        lax.all_gather(col_off[0], "tile", axis=0, tiled=True),
    )
    owner_grid = owners_all.reshape(tile_count, region_count)
    row_grid = rows_all.reshape(tile_count, region_count)
    col_grid = cols_all.reshape(tile_count, region_count)
    rank_grid = owner_ranks(owner_grid)
    slot_ids = jnp.arange(slot_cap)
    select = (
        (owner_grid == own_index)[:, None, :] & (rank_grid[:, None, :] == slot_ids[None, :, None])
    ).astype(jnp.int32)
    live = jnp.sum(select, axis=2)
    slot_rows = jnp.sum(select * row_grid[:, None, :], axis=2)
    slot_cols = jnp.sum(select * col_grid[:, None, :], axis=2)
    steps_crop = jnp.arange(crop_size)[None, None, :, None]
    row_take = (
        (jnp.arange(height)[None, None, None, :] == slot_rows[:, :, None, None] + steps_crop)
        & (live[:, :, None, None] > 0)
    ).astype(jnp.bfloat16)
    col_take = (
        jnp.arange(width)[None, None, None, :] == slot_cols[:, :, None, None] + steps_crop
    ).astype(jnp.bfloat16)
    flat_tile = pyramid.reshape(height, width * channels)

    def cut_owner(picks):
        row_pick, col_pick = picks
        row_band = jnp.dot(
            row_pick.reshape(slot_cap * crop_size, height),
            flat_tile,
            preferred_element_type=jnp.float32,
        )
        row_band = row_band.astype(jnp.bfloat16).reshape(slot_cap, crop_size, width, channels)
        return jnp.einsum(
            "sjw,siwc->sijc", col_pick, row_band, preferred_element_type=jnp.float32
        ).astype(jnp.bfloat16)

    outgoing = lax.map(cut_owner, (row_take, col_take))
    incoming = lax.all_to_all(outgoing, "tile", split_axis=0, concat_axis=0, tiled=True)
    own_owners = owner[0, :, 0]
    own_ranks = owner_ranks(own_owners[None])[0]
    slot_index = own_owners * slot_cap + own_ranks
    crops = jnp.take(
        incoming.reshape(tile_count * slot_cap, crop_size, crop_size, channels), slot_index, axis=0
    )
    grad_one, grad_two, gcrop = mask_head(crops, mask_w1, mask_w2, cotangent[0])
    outgoing_grads = (
        jnp.zeros((tile_count * slot_cap, crop_size, crop_size, channels), jnp.bfloat16)
        .at[slot_index]
        .set(gcrop)
    )
    outgoing_grads = outgoing_grads.reshape(tile_count, slot_cap, crop_size, crop_size, channels)
    returned = lax.all_to_all(outgoing_grads, "tile", split_axis=0, concat_axis=0, tiled=True)

    def spread_owner(inputs):
        col_pick, grad_piece = inputs
        spread = jnp.einsum(
            "sjw,sijc->siwc", col_pick, grad_piece, preferred_element_type=jnp.float32
        ).astype(jnp.bfloat16)
        return spread.reshape(slot_cap * crop_size, width * channels)

    spreads = lax.map(spread_owner, (col_take, returned))
    placed = jnp.dot(
        row_take.reshape(tile_count * slot_cap * crop_size, height).T,
        spreads.reshape(tile_count * slot_cap * crop_size, width * channels),
        preferred_element_type=jnp.float32,
    )
    grad_pyramid = placed.reshape(1, height, width, channels).astype(jnp.bfloat16)
    weight_terms = (grad_one.reshape(-1, channels), grad_two.reshape(-1, channels))
    summed = (
        lax.psum(weight_terms[0].astype(jnp.bfloat16), "tile").astype(jnp.float32),
        lax.psum(weight_terms[1].astype(jnp.bfloat16), "tile").astype(jnp.float32),
    )
    shares = (
        lax.psum_scatter(
            summed[0].astype(jnp.bfloat16), "dp", scatter_dimension=0, tiled=True
        ).astype(jnp.float32),
        lax.psum_scatter(
            summed[1].astype(jnp.bfloat16), "dp", scatter_dimension=0, tiled=True
        ).astype(jnp.float32),
    )
    return (shares[0], shares[1], grad_pyramid)


def solution(mesh):
    placed = (
        P("dp", "tile", None, None),
        P(),
        P(),
        P(),
        P("dp", "tile", None),
        P("dp", "tile"),
        P("dp", "tile"),
        P("dp", "tile", None, None, None),
    )
    return jax.shard_map(
        body,
        mesh=mesh,
        in_specs=placed,
        out_specs=(P("dp", None), P("dp", None), P("dp", "tile", None, None)),
        check_vma=False,
    )
```

profile of v0, /device:TPU:0, one launch (start us, length us, event | category | flops | bytes accessed | tf_op | source)
XLA Modules:
  0.0 345.1 jit_solution(12556986115128558904)
XLA Ops:
  7.9 2.3 collective-permute-start
  15.8 12.5 %all-reduce.8 = (s32[32]{0:T(128)S(1)}, s32[32]{0:T(128)S(1)}, s32[32]{0:T(128)S(1)}) all-reduce(s32[32]{0:T(128)S(1)} %bitcast_dynamic-update-slice_fusion.2, s32[32]{0:T(128)S(1)} %bitcast_dynamic-update-slice_fusion, s32[32]{0:T(128)S(1)} %bitcast_dynamic-update-slice_fusion.1), channel_id=2, replica_groups=mesh['dp'=4,'tile'=8] {'tile'}, use_global_device_ids=true, to_apply=%add.5 | all-reduce | flops 96 | bytes 768
  36.1 16.3 %while.20 = (s32[]{:T(128)}, bf16[8,2,14,14,256]{4,1,3,2,0:T(2,128)(2,1)}, bf16[8,2,14,16]{2,1,3,0:T(2,128)(2,1)S(1)}, bf16[16,16384]{1,0:T(8,128)(2,1)S(1)}, bf16[8,2,14,64]{3,2,1,0:T(8,128)(2,1)S(1)}, /*index=5*/s32[]{:T(128)}) while((s32[]{:T(128)}, bf16[8,2,14,14,256]{4,1,3,2,0:T(2,128)(2,1)}, bf16[8,2,14,16]{2,1,3,0:T(2,128)(2,1)S(1)}, ...), condition=%wide.region_6.7_spmd, body=%wide.region_5.6_spmd.sunk | while | flops 28084224 | bytes 6906329 | solution.py:152
  52.4 3.7 %all-to-all-start = ((bf16[8,2,14,14,256]{4,1,3,2,0:T(2,128)(2,1)}), bf16[8,2,14,14,256]{4,1,3,2,0:T(2,128)(2,1)S(1)}, u32[]{:S(2)}, u32[]{:S(2)}) async-start(bf16[8,2,14,14,256]{4,1,3,2,0:T(2,128)(2,1)} %get-tuple-element.52), calls=%async_computation | async-start | bytes 3211264 | tf_op jit(solution)/shard_map/all_to_all | solution.py:153
  57.7 36.9 %all-to-all-done = bf16[8,2,14,14,256]{4,1,3,2,0:T(2,128)(2,1)S(1)} async-done(((bf16[8,2,14,14,256]{4,1,3,2,0:T(2,128)(2,1)}), bf16[8,2,14,14,256]{4,1,3,2,0:T(2,128)(2,1)S(1)}, u32[]{:S(2)}, u32[]{:S(2)}) %all-to-all-start) | async-done | bytes 1605664 | tf_op jit(solution)/shard_map/all_to_all | solution.py:153
  97.8 1.9 reshape.489
  117.4 1.9 reshape.492
  122.9 2.0 reshape.496
  137.3 2.0 fusion.88
  140.3 2.1 pad_slice_fusion.8
  142.4 1.9 reshape.507
  144.3 1.9 reshape.501
  148.1 1.9 reshape.503
  150.0 1.9 reshape.504
  151.9 1.9 reshape.505
  176.2 1.9 reshape.517
  183.6 2.0 reshape.515
  196.4 3.6 %copy.51 = bf16[8,2,14,14,256]{4,1,3,2,0:T(2,128)(2,1)} copy(bf16[8,2,14,14,256]{4,3,2,1,0:T(8,128)(2,1)S(1)} %bitcast.551) | data formatting | bytes 3211264 | tf_op jit(solution)/shard_map/reshape | solution.py:166
  200.0 4.4 %all-to-all-start.1 = ((bf16[8,2,14,14,256]{4,1,3,2,0:T(2,128)(2,1)}), bf16[8,2,14,14,256]{4,1,3,2,0:T(2,128)(2,1)}, u32[]{:S(2)}, u32[]{:S(2)}) async-start(bf16[8,2,14,14,256]{4,1,3,2,0:T(2,128)(2,1)} %copy.51), calls=%async_computation.1 | async-start | bytes 3211264 | tf_op jit(solution)/shard_map/all_to_all | solution.py:167
  208.8 29.7 %reduce-scatter.3.cloned.1.call-done = bf16[576,256]{1,0:T(8,128)(2,1)} async-done(((bf16[2304,256]{1,0:T(8,128)(2,1)}), bf16[576,256]{1,0:T(8,128)(2,1)}) %reduce-scatter.3.cloned.1.call-update) | async-done | bytes 294928 | tf_op jit(solution)/shard_map/reduce_scatter | solution.py:189
  238.8 58.9 %all-reduce.12.cloned.1.call-done = (bf16[576,256]{1,0:T(8,128)(2,1)}, bf16[576,256]{1,0:T(8,128)(2,1)}) async-done(((bf16[576,256]{1,0:T(8,128)(2,1)}, bf16[576,256]{1,0:T(8,128)(2,1)}), (bf16[576,256]{1,0:T(8,128)(2,1)}, bf16[576,256]{1,0:T(8,128)(2,1)})) %all-reduce.12.cloned.1.call-update) | async-done | bytes 589840 | tf_op jit(solution)/shard_map/psum | solution.py:185
  301.3 24.9 %while.21 = (s32[]{:T(128)}, bf16[8,28,16384]{2,1,0:T(8,128)(2,1)}, bf16[8,2,14,14,256]{4,1,3,2,0:T(2,128)(2,1)}, bf16[8,2,14,64]{3,2,1,0:T(8,128)(2,1)S(1)}, s32[]{:T(128)}) while((s32[]{:T(128)}, bf16[8,28,16384]{2,1,0:T(8,128)(2,1)}, bf16[8,2,14,14,256]{4,1,3,2,0:T(2,128)(2,1)}, bf16[8,2,14,64]{3,2,1,0:T(8,128)(2,1)S(1)}, ...), condition=%wide.region_13.14_spmd, body=%wide.region_12.13_spmd.sunk | while | flops 13303810 | bytes 5328977 | solution.py:176
  326.2 7.2 %reshape.519 = bf16[224,16384]{1,0:T(8,128)(2,1)} reshape(bf16[8,28,16384]{2,1,0:T(8,128)(2,1)} %get-tuple-element.53) | data formatting | bytes 14680064 | tf_op jit(solution)/shard_map/reshape | solution.py:179
  333.4 4.1 %fusion.18 = bf16[1,16,64,256]{3,1,2,0:T(8,128)(2,1)S(1)} fusion(bf16[28,64,8,256]{3,2,1,0:T(8,128)(2,1)} %bitcast.550, s32[224]{0:T(256)S(1)} %add.322, pred[224]{0:T(512)(128)(4,1)S(1)} %and.61), kind=kOutput, calls=%fused_computation.73 | convolution fusion | flops 117709824 | bytes 7865440 | tf_op jit(solution)/shard_map/dot_general | solution.py:177
  (354 shorter events, 142.5 us)
Async XLA Ops:
  7.9 21.8 %collective-permute-start = (bf16[1,1,64,256]{3,2,1,0:T(8,128)(2,1)S(1)}, bf16[1,1,64,256]{3,2,1,0:T(8,128)(2,1)S(1)}, u32[]{:S(2)}, u32[]{:S(2)}) collective-permute-start(bf16[1,1,64,256]{3,2,1,0:T(8,128)(2,1)S(1)} %get-tuple-element.122), channel_id=1, source_target_pairs={{0,1},{1,2},{2,3},{3,4},{4,5},{5,6},{6,7},{8,9},{9,10},{10,11},{11... | collective-permute-start | bytes 98312 | tf_op jit(solution)/shard_map/ppermute | solution.py:17
  10.3 19.4 %collective-permute-start.1 = (bf16[1,1,64,256]{3,2,1,0:T(8,128)(2,1)S(1)}, bf16[1,1,64,256]{3,2,1,0:T(8,128)(2,1)S(1)}, u32[]{:S(2)}, u32[]{:S(2)}) collective-permute-start(bf16[1,1,64,256]{3,2,1,0:T(8,128)(2,1)S(1)} %get-tuple-element.123), channel_id=1, source_target_pairs={{1,0},{2,1},{3,2},{4,3},{5,4},{6,5},{7,6},{9,8},{10,9},{11,10},{12... | collective-permute-start | bytes 98312 | tf_op jit(solution)/shard_map/ppermute | solution.py:19
  31.0 1.3 copy-start.46
  52.4 4.0 %copy-start.12 = (bf16[1,4,14,14,256]{4,1,3,2,0:T(4,128)(2,1)S(1)}, bf16[1,4,14,14,256]{4,1,3,2,0:T(4,128)(2,1)}, u32[]{:S(2)}) copy-start(bf16[1,4,14,14,256]{4,1,3,2,0:T(4,128)(2,1)} %param.19) | copy-start | bytes 1204228
  52.4 42.2 %all-to-all-start = ((bf16[8,2,14,14,256]{4,1,3,2,0:T(2,128)(2,1)}), bf16[8,2,14,14,256]{4,1,3,2,0:T(2,128)(2,1)S(1)}, u32[]{:S(2)}, u32[]{:S(2)}) async-start(bf16[8,2,14,14,256]{4,1,3,2,0:T(2,128)(2,1)} %get-tuple-element.52), calls=%async_computation | async-start | bytes 3211264 | tf_op jit(solution)/shard_map/all_to_all | solution.py:153
  56.1 152.7 %reduce-scatter.5.cloned.1.call-start = ((), (), s32[]{:S(2)}) async-start(), calls=%async_computation.5 | async-start | bytes 1474560 | tf_op jit(solution)/shard_map/reduce_scatter | solution.py:192
  104.2 1.3 copy-start.2
  113.9 1.5 copy-start.7
  122.9 3.7 %copy-start.1 = (bf16[9,256,256]{2,1,0:T(8,128)(2,1)S(1)}, bf16[9,256,256]{2,1,0:T(8,128)(2,1)}, u32[]{:S(2)}) copy-start(bf16[9,256,256]{2,1,0:T(8,128)(2,1)} %param.15) | copy-start | bytes 3538948
  125.8 2.1 copy-start.38
  137.3 2.0 copy-start.8
  157.6 1.4 copy-start.39
  168.1 1.7 copy-start.5
  168.1 1.7 copy-start.9
  168.1 2.4 copy-start.44
  171.3 1.3 copy-start.47
  171.3 1.4 copy-start.51
  176.2 5.7 %copy-start.6 = (bf16[4,14,14,256]{3,2,1,0:T(8,128)(2,1)S(1)}, bf16[4,14,14,256]{3,2,1,0:T(8,128)(2,1)}, u32[]{:S(2)}) copy-start(bf16[4,14,14,256]{3,2,1,0:T(8,128)(2,1)} %get-tuple-element.127) | copy-start | bytes 1204228
  183.6 3.0 copy-start.3
  200.0 4.8 %copy-start.11 = (bf16[4,14,14,256]{3,2,1,0:T(8,128)(2,1)S(1)}, bf16[4,14,14,256]{3,2,1,0:T(8,128)(2,1)}, u32[]{:S(2)}) copy-start(bf16[4,14,14,256]{3,2,1,0:T(8,128)(2,1)} %copy-done.10) | copy-start | bytes 1204228
  200.0 4.8 %copy-start.42 = (bf16[9,256,256]{2,1,0:T(8,128)(2,1)S(1)}, bf16[9,256,256]{2,1,0:T(8,128)(2,1)}, u32[]{:S(2)}) copy-start(bf16[9,256,256]{2,1,0:T(8,128)(2,1)} %fusion.74) | copy-start | bytes 3538948
  200.0 101.3 %all-to-all-start.1 = ((bf16[8,2,14,14,256]{4,1,3,2,0:T(2,128)(2,1)}), bf16[8,2,14,14,256]{4,1,3,2,0:T(2,128)(2,1)}, u32[]{:S(2)}, u32[]{:S(2)}) async-start(bf16[8,2,14,14,256]{4,1,3,2,0:T(2,128)(2,1)} %copy.51), calls=%async_computation.1 | async-start | bytes 3211264 | tf_op jit(solution)/shard_map/all_to_all | solution.py:167
  204.4 34.1 %reduce-scatter.3.cloned.1.call-start = ((), (), s32[]{:S(2)}) async-start(), calls=%async_computation.4 | async-start | bytes 1474560 | tf_op jit(solution)/shard_map/reduce_scatter | solution.py:189
  208.7 89.0 %all-reduce.12.cloned.1.call-start = ((), (), s32[]{:S(2)}) async-start(), calls=%async_computation.6 | async-start | bytes 1179648 | tf_op jit(solution)/shard_map/psum | solution.py:185
  (37 other events, 37.9 us)
Sparse Core Ops, SparseCore 0:
  176.3 27.4 reduce-scatter.4
  208.9 29.6 reduce-scatter.2
  240.9 56.7 all-reduce.11
where the time goes:
time: 348 us; the launch traced here: 345 us
  local copies, waits for them, and re-layouts  133 us (38%)
  waiting for transfers between devices  126 us (36%)
  matrix products  37.5 us (11%)
  between operations  15.3 us (4%)
  blocking collectives  12.5 us (4%)
  starting transfers between devices  12.4 us (4%)
  other arithmetic  8.82 us (3%)
    psum x1, waiting for transfers between devices, body(): lax.psum(weight_terms[0].astype(jnp.bfloat16), 'tile').astype(jnp.float32)  58.9 us
    all_to_all x1, waiting for transfers between devices, body(): lax.all_to_all(outgoing, 'tile', split_axis=0, concat_axis=0, tiled=True)  36.9 us
    unnamed x116, local copies, waits for them, and re-layouts  30 us
    reduce_scatter x1, waiting for transfers between devices, body(): lax.psum_scatter(summed[0].astype(jnp.bfloat16), 'dp', scatter_dimension=...  29.7 us
    reshape x16, local copies, waits for them, and re-layouts, conv_back(): window.reshape(-1, channels)  25.6 us
    reshape x15, local copies, waits for them, and re-layouts, conv_padded(): window.reshape(-1, channels)  17.8 us
    unnamed x1, blocking collectives  12.5 us
    dot_general x27, matrix products, conv_padded(): jnp.dot(window.reshape(-1, channels), kernel[3 * row_tap + col_tap], pref...  8.54 us
  transfers between devices with their start and end apart: 7, of which 3 were waited for; matrix products, arithmetic and copies ran while one was open for 9% of the time, Pallas kernels for 0%

commit v1 on v0

v1 whole, which is shorter than its diff:
```python
import functools
import math

import jax
import jax.numpy as jnp
from jax import lax
from jax.experimental import pallas as pl
from jax.experimental.pallas import tpu as pltpu
from jax.sharding import PartitionSpec as P

BF = jnp.bfloat16
F32 = jnp.float32
VMEM_LIMIT = 56 * 1024 * 1024
PITCH = 16
SLOT = 208


def roundup(n, m):
    return (n + m - 1) // m * m


def call(kernel, outs, scratch=(), aliases=None):
    return pl.pallas_call(
        kernel,
        out_shape=outs,
        in_specs=None,
        scratch_shapes=list(scratch),
        input_output_aliases=aliases or {},
        compiler_params=pltpu.CompilerParams(vmem_limit_bytes=VMEM_LIMIT),
    )


def sds(shape, dtype):
    return jax.ShapeDtypeStruct(shape, dtype)


def pack_kernel(side, cot_ref, place_ref, out_ref, wide):
    regions = cot_ref.shape[0]
    lanes = lax.broadcasted_iota(jnp.int32, (16, 256), 1)
    rows = lax.broadcasted_iota(jnp.int32, (16, 256), 0)
    for r in range(regions):
        for i in range(side):
            wide[side * i : side * i + side, :] = cot_ref[r, i].astype(F32)
        tail = wide[192:208, :]
        spot = place_ref[r, 0].astype(F32)
        column = place_ref[r, 1].astype(F32)
        note = jnp.where(lanes == 0, spot, jnp.where(lanes == 1, column, 0.0))
        wide[192:208, :] = jnp.where(rows < 4, tail, note)
        out_ref[r] = wide[...].astype(BF)


def pack(cotangent, place):
    regions, side = cotangent.shape[0], cotangent.shape[1]
    return pl.pallas_call(
        functools.partial(pack_kernel, side),
        out_shape=sds((regions, SLOT, 256), BF),
        in_specs=[
            pl.BlockSpec(memory_space=pltpu.VMEM),
            pl.BlockSpec(memory_space=pltpu.SMEM),
        ],
        scratch_shapes=[pltpu.VMEM((SLOT, 256), F32)],
        compiler_params=pltpu.CompilerParams(vmem_limit_bytes=VMEM_LIMIT),
    )(cotangent, place)


def pyramid_part(height, width, own, other, rim_a, rim_b, wf, pyr, xp):
    core = lax.rem(lax.axis_index("tile"), 2)
    cells = height * width
    col = lax.broadcasted_iota(jnp.int32, (width, 256), 0)

    def fill(src, count, where):
        def step(t, carry):
            v = src[pl.ds(pl.multiple_of(t * width, width), width), :].astype(F32)
            to = pl.ds(pl.multiple_of(where + t * width, width), width)
            xp[to, 0:256] = jnp.where(col == 0, 0.0, pltpu.roll(v, 1, 0)).astype(BF)
            xp[to, 256:512] = v.astype(BF)
            xp[to, 512:768] = jnp.where(
                col == width - 1, 0.0, pltpu.roll(v, width - 1, 0)
            ).astype(BF)
            return carry

        lax.fori_loop(0, count, step, 0)

    bottom = width + 2 * cells
    fill(own, height, width + core * cells)
    fill(other, height, width + (1 - core) * cells)
    fill(rim_a, 1, core * bottom)
    fill(rim_b, 1, (1 - core) * bottom)

    def conv(t, carry):
        at = t * 256
        total = jnp.zeros((256, 256), F32)
        for a in range(3):
            piece = xp[pl.ds(pl.multiple_of(at + a * width, 64), 256), :]
            total += jnp.dot(piece, wf[a * 768 : a * 768 + 768, :], preferred_element_type=F32)
        pyr[pl.ds(pl.multiple_of(at, 256), 256), :] = total.astype(BF).astype(F32)
        return carry

    lax.fori_loop(0, 2 * cells // 256, conv, 0)
    pyr[2 * cells : 2 * cells + 16, :] = jnp.zeros((16, 256), F32)


def flip_part(w, wb):
    for k in range(9):
        block = w[(8 - k) * 256 : (9 - k) * 256, :].astype(F32)
        wb[k * 256 : k * 256 + 256, :] = block.T.astype(BF)


def gelu_pair(v):
    c = math.sqrt(2.0 / math.pi)
    sq = v * v
    t = jnp.tanh(c * (v + 0.044715 * (sq * v)))
    half = 0.5 * (1.0 + t)
    slope = half + 0.5 * v * (1.0 - t * t) * (c * (1.0 + 3 * 0.044715 * sq))
    return v * half, slope


def regions_part(side, height, width, blocks, pyr, w1, w2, wb1, wb2, acc1, acc2, gp, scratch):
    xs, hs, gs, wide, vs, slope1, todo = scratch
    cells = side * PITCH
    chip = lax.axis_index("tile") // 2
    lanes = lax.broadcasted_iota(jnp.int32, (16, 256), 1)
    rows16 = lax.broadcasted_iota(jnp.int32, (16, 256), 0)
    in_row = rows16 < side
    inside = lax.rem(lax.broadcasted_iota(jnp.int32, (cells, 256), 0), PITCH) < side
    per = blocks[0].shape[0]

    count = jnp.int32(0)
    for s, block in enumerate(blocks):
        for r in range(per):
            note = block[r, 192:208, :].astype(F32)
            note = jnp.where(rows16 == 15, note, 0.0)
            spot = jnp.sum(jnp.where(lanes == 0, note, 0.0)).astype(jnp.int32) - 1
            column = jnp.sum(jnp.where(lanes == 1, note, 0.0)).astype(jnp.int32)
            local = spot - chip * 2 * height
            here = (spot >= 0) & (local >= 0) & (local < 2 * height)
            todo[0, count] = jnp.int32(s * per + r)
            todo[1, count] = jnp.where(here, local * width + column // 8 * 8, 0)
            todo[2, count] = jnp.where(here, lax.rem(column, 8), 0)
            count = count + here.astype(jnp.int32)

    for buf in (xs, hs, gs):
        buf[0:16, :] = jnp.zeros((16, 768), BF)
        buf[cells + 16 : cells + 32, :] = jnp.zeros((16, 768), BF)

    def put(buf, v):
        buf[16 : 16 + cells, 0:256] = pltpu.roll(v, 1, 0).astype(BF)
        buf[16 : 16 + cells, 256:512] = v.astype(BF)
        buf[16 : 16 + cells, 512:768] = pltpu.roll(v, cells - 1, 0).astype(BF)

    def conv(buf, w):
        total = jnp.zeros((cells, 256), F32)
        for a in range(3):
            total += jnp.dot(
                buf[a * 16 : a * 16 + cells, :],
                w[a * 768 : a * 768 + 768, :],
                preferred_element_type=F32,
            )
        return total

    def taps(acc, buf, grad):
        turned = grad.T.astype(BF)
        for a in range(3):
            acc[:, a * 768 : a * 768 + 768] += jnp.dot(
                turned, buf[a * 16 : a * 16 + cells, :], preferred_element_type=F32
            )

    def region(n, carry):
        which = todo[0, n]
        base = pl.multiple_of(todo[1, n], 8)
        lead = todo[2, n]
        for s, block in enumerate(blocks):

            @pl.when(which // per == s)
            def _():
                wide[...] = block[lax.rem(which, per)].astype(F32)

        for i in range(side):
            got = pyr[pl.ds(pl.multiple_of(base + i * width, 8), 24), :]
            got = pltpu.roll(got, lax.rem(24 - lead, 24), 0)[0:16]
            vs[i * 16 : i * 16 + 16, :] = jnp.where(in_row, got, 0.0)
        put(xs, vs[...])
        pre1 = conv(xs, w1)
        act1, slope = gelu_pair(pre1)
        slope1[...] = slope
        put(hs, jnp.where(inside, act1, 0.0))
        pre2 = conv(hs, w2)
        _, slope = gelu_pair(pre2)
        for i in range(side):
            got = wide[i * side : i * side + 16, :]
            vs[i * 16 : i * 16 + 16, :] = jnp.where(in_row, got, 0.0)
        g2 = vs[...] * slope
        put(gs, g2)
        taps(acc2, hs, g2)
        gact1 = conv(gs, wb2)
        g1 = jnp.where(inside, gact1 * slope1[...], 0.0)
        put(gs, g1)
        taps(acc1, xs, g1)
        gcrop = jnp.where(inside, conv(gs, wb1), 0.0).astype(BF).astype(F32)
        vs[...] = gcrop
        for i in range(side):
            at = pl.ds(pl.multiple_of(base + i * width, 8), 24)
            piece = jnp.concatenate([vs[i * 16 : i * 16 + 16, :], jnp.zeros((8, 256), F32)])
            gp[at, :] = gp[at, :] + pltpu.roll(piece, lead, 0)
        return carry

    lax.fori_loop(0, count, region, 0)


def finish_part(height, width, acc1, acc2, gp, keep, send, gp_own, gp_other):
    core = lax.rem(lax.axis_index("tile"), 2)
    cells = height * width

    def write(acc, to):
        for k in range(9):
            to[k * 256 : k * 256 + 256, :] = acc[:, k * 256 : k * 256 + 256].T.astype(BF)

    @pl.when(core == 0)
    def _():
        write(acc1, keep)
        write(acc2, send)

    @pl.when(core == 1)
    def _():
        write(acc2, keep)
        write(acc1, send)

    gp_own[...] = gp[pl.ds(pl.multiple_of(core * cells, cells), cells), :]
    gp_other[...] = gp[pl.ds(pl.multiple_of((1 - core) * cells, cells), cells), :].astype(BF)


def main_call(side, height, width, first, last, state, weights, blocks):
    n = len(blocks)
    big = 2 * height * width + 16
    cells = side * PITCH
    kept = (
        sds((big, 256), F32),
        sds((2304, 256), BF),
        sds((2304, 256), BF),
    )
    sums = (sds((256, 2304), F32), sds((256, 2304), F32), sds((big, 256), F32))
    ends = (
        sds((2304, 256), BF),
        sds((2304, 256), BF),
        sds((height * width, 256), F32),
        sds((height * width, 256), BF),
    )
    outs = (kept if first and not last else ()) + (ends if last else sums)
    scratch = [
        pltpu.VMEM((cells + 32, 768), BF),
        pltpu.VMEM((cells + 32, 768), BF),
        pltpu.VMEM((cells + 32, 768), BF),
        pltpu.VMEM((SLOT, 256), F32),
        pltpu.VMEM((cells, 256), F32),
        pltpu.VMEM((cells, 256), F32),
        pltpu.SMEM((3, 128), jnp.int32),
    ]
    extra = []
    if first:
        extra.append(pltpu.VMEM(((2 * height + 2) * width, 768), BF))
    if first and last:
        extra += [pltpu.VMEM(s.shape, s.dtype) for s in kept]
    if last:
        extra += [pltpu.VMEM(s.shape, s.dtype) for s in sums]

    def kernel(*refs):
        refs = list(refs)

        def take(k):
            got = refs[:k]
            del refs[:k]
            return got

        state_refs = take(len(state))
        weight_refs = take(len(weights))
        block_refs = take(n)
        out_refs = take(len(outs))
        scratch_refs = take(len(scratch))
        if first:
            xp = take(1)[0]
            pyr, wb1, wb2 = take(3) if last else out_refs[:3]
            acc1, acc2, gp = take(3) if last else out_refs[3:]
            wf, w1, w2 = weight_refs
            pyramid_part(height, width, *state_refs, wf, pyr, xp)
            flip_part(w1, wb1)
            flip_part(w2, wb2)
            for total in (acc1, acc2, gp):
                total[...] = jnp.zeros(total.shape, F32)
        else:
            pyr, wb1, wb2 = state_refs[:3]
            acc1, acc2, gp = take(3) if last else out_refs
            w1, w2 = weight_refs
            for to, source in zip((acc1, acc2, gp), state_refs[3:]):
                to[...] = source[...]
        regions_part(
            side, height, width, block_refs, pyr, w1, w2, wb1, wb2, acc1, acc2, gp, scratch_refs
        )
        if last:
            finish_part(height, width, acc1, acc2, gp, *out_refs)

    aliases = {} if first or last else {3: 0, 4: 1, 5: 2}
    return pl.pallas_call(
        kernel,
        out_shape=outs,
        scratch_shapes=scratch + extra,
        input_output_aliases=aliases,
        compiler_params=pltpu.CompilerParams(vmem_limit_bytes=VMEM_LIMIT),
    )(*state, *weights, *blocks)


def local_kernel(fn, outs, *arrays):
    return pl.pallas_call(
        fn,
        out_shape=outs,
        compiler_params=pltpu.CompilerParams(vmem_limit_bytes=VMEM_LIMIT),
    )(*arrays)


def add(a, b):
    return (a.astype(F32) + b.astype(F32)).astype(BF)


def reduce_weights(keep, send, core_swap, dp, chips):
    rows = keep.shape[0] // dp
    bits = dp.bit_length() - 1
    low = roundup(rows // 2, 16)
    spans = ((0, low), (low, rows))
    orders = (list(range(bits)), list(reversed(range(bits))))
    got = lax.ppermute(send, "tile", core_swap)

    def split(members, order):
        bit = 1 << order[0]
        return [m for m in members if not m & bit], [m for m in members if m & bit]

    members = [list(range(dp)), list(range(dp))]
    shapes = []
    for half in range(2):
        size = spans[half][1] - spans[half][0]
        stay, go = split(members[half], orders[half])
        shapes += [sds((len(stay), size, 256), BF), sds((len(go), size, 256), BF)]

    def first(keep_ref, got_ref, *outs):
        me = lax.axis_index("dp")
        for half in range(2):
            lo, hi = spans[half]
            for out, group in zip(outs[2 * half : 2 * half + 2], split(members[half], orders[half])):
                for n, m in enumerate(group):
                    at = pl.ds(pl.multiple_of((me ^ m) * rows + lo, 16), hi - lo)
                    out[n] = add(keep_ref[at, :], got_ref[at, :])

    parts = local_kernel(first, tuple(shapes), keep, got)
    for stage in range(bits):
        received = []
        for half in range(2):
            bit = 1 << orders[half][stage]
            received.append(lax.ppermute(parts[2 * half + 1], "dp", [(i, i ^ bit) for i in range(dp)]))
        for half in range(2):
            members[half] = split(members[half], orders[half][stage:])[0]
        if stage == bits - 1:
            break
        shapes = []
        for half in range(2):
            size = spans[half][1] - spans[half][0]
            stay, go = split(members[half], orders[half][stage + 1 :])
            shapes += [sds((len(stay), size, 256), BF), sds((len(go), size, 256), BF)]

        def middle(p, pr, q, qr, *outs, stage=stage):
            for half, (mine, theirs) in enumerate(((p, pr), (q, qr))):
                groups = split(members[half], orders[half][stage + 1 :])
                for out, group in zip(outs[2 * half : 2 * half + 2], groups):
                    for n, m in enumerate(group):
                        k = members[half].index(m)
                        out[n] = add(mine[k], theirs[k])

        parts = local_kernel(middle, tuple(shapes), parts[0], received[0], parts[2], received[1])

    share = roundup(-(-rows // chips), 16)
    shifts = [
        [(2 * z + c, 2 * ((z + k) % chips) + c) for z in range(chips) for c in range(2)]
        for k in range(chips)
    ]

    def deal(p, pr, q, qr, *refs):
        outs, total = refs[:chips], refs[chips]
        chip = lax.axis_index("tile") // 2
        total[0:low, :] = add(p[0], pr[0])
        total[low:rows, :] = add(q[0], qr[0])
        if share * chips > rows:
            total[rows:, :] = jnp.zeros((share * chips - rows, 256), BF)
        for k in range(chips):
            to = lax.rem(chip + k, chips)
            outs[k][...] = total[pl.ds(pl.multiple_of(to * share, 16), share), :]

    dealt = pl.pallas_call(
        deal,
        out_shape=tuple(sds((share, 256), BF) for _ in range(chips)),
        scratch_shapes=[pltpu.VMEM((share * chips, 256), BF)],
        compiler_params=pltpu.CompilerParams(vmem_limit_bytes=VMEM_LIMIT),
    )(parts[0], received[0], parts[2], received[1])
    arrived = [lax.ppermute(dealt[k], "tile", shifts[k]) for k in range(1, chips)]

    def gather(*refs):
        total = refs[0][...].astype(F32)
        for ref in refs[1:-1]:
            total += ref[...].astype(F32)
        refs[-1][...] = total.astype(BF)

    mine = local_kernel(gather, sds((share, 256), BF), dealt[0], *arrived)
    pieces = [mine] + [lax.ppermute(mine, "tile", shifts[k]) for k in range(1, chips)]

    def lay(*refs):
        chip = lax.axis_index("tile") // 2
        for k in range(chips):
            source = lax.rem(chip - k + chips, chips)
            refs[-1][pl.ds(pl.multiple_of(source * share, 16), share), :] = refs[k][...]

    whole = local_kernel(lay, sds((share * chips, 256), BF), *pieces)
    theirs = lax.ppermute(whole, "tile", core_swap)

    def out(mine_ref, theirs_ref, one, two):
        core = lax.rem(lax.axis_index("tile"), 2)

        @pl.when(core == 0)
        def _():
            one[...] = mine_ref[0:rows, :].astype(F32)
            two[...] = theirs_ref[0:rows, :].astype(F32)

        @pl.when(core == 1)
        def _():
            one[...] = theirs_ref[0:rows, :].astype(F32)
            two[...] = mine_ref[0:rows, :].astype(F32)

    return local_kernel(out, (sds((rows, 256), F32), sds((rows, 256), F32)), whole, theirs)


def body(features, fpn_weight, mask_w1, mask_w2, owner, row_off, col_off, cotangent):
    tiles = lax.axis_size("tile")
    dp = lax.axis_size("dp")
    chips = tiles // 2
    core = lax.rem(lax.axis_index("tile"), 2)
    height, width, channels = features.shape[1:]
    side = cotangent.shape[2]
    swap = [(i, i ^ 1) for i in range(tiles)]

    place = jnp.stack([owner[0, :, 0] * height + row_off[0] + 1, col_off[0]], axis=1)
    packed = pack(cotangent[0], place)

    tile = features.reshape(height * width, channels)
    edge = jnp.where(core == 1, tile[(height - 1) * width :], tile[:width])
    rim_a = lax.ppermute(
        edge, "tile", [(i, i + 1 if i % 2 else i - 1) for i in range(1, tiles - 1)]
    )
    rim_b = lax.ppermute(
        edge,
        "tile",
        [(i, i + 2 if i % 2 else i - 2) for i in range(tiles) if 0 <= (i + 2 if i % 2 else i - 2) < tiles],
    )
    other = lax.ppermute(tile, "tile", swap)

    up = [(i, i + 2) for i in range(tiles - 2)]
    down = [(i + 2, i) for i in range(tiles - 2)]
    blocks = [packed]
    rising, falling = packed, packed
    for _ in range(chips - 1):
        rising = lax.ppermute(rising, "tile", up)
        falling = lax.ppermute(falling, "tile", down)
        blocks += [rising, falling]

    flat = lambda w: w.reshape(9 * channels, channels)
    weights = [flat(fpn_weight), flat(mask_w1), flat(mask_w2)]
    keep, send, gp_own, gp_other = main_call(
        side, height, width, True, True, [tile, other, rim_a, rim_b], weights, blocks
    )
    gp_got = lax.ppermute(gp_other, "tile", swap)
    grad_one, grad_two = reduce_weights(keep, send, swap, dp, chips)

    def join(a, b, out):
        out[...] = (a[...] + b[...].astype(F32)).astype(BF)

    grad_pyramid = local_kernel(join, sds((height * width, channels), BF), gp_own, gp_got)
    return grad_one, grad_two, grad_pyramid.reshape(1, height, width, channels)


def solution(mesh):
    placed = (
        P("dp", "tile", None, None),
        P(),
        P(),
        P(),
        P("dp", "tile", None),
        P("dp", "tile"),
        P("dp", "tile"),
        P("dp", "tile", None, None, None),
    )
    return jax.shard_map(
        body,
        mesh=mesh,
        in_specs=placed,
        out_specs=(P("dp", None), P("dp", None), P("dp", "tile", None, None)),
        check_vma=False,
    )
```

time: 348 us -> 145 us (0.42); the launches traced: 345 us -> 147 us
  local copies, waits for them, and re-layouts: 133 us -> 8.63 us
  waiting for transfers between devices: 126 us -> 45.3 us
  Pallas kernels: 0 us -> 50.2 us
  matrix products: 37.5 us -> 0 us
  starting transfers between devices: 12.4 us -> 40.4 us
  between operations: 15.3 us -> 0.86 us
  blocking collectives: 12.5 us -> 0 us
  other arithmetic: 8.82 us -> 1.38 us
    psum x1 -> x0, waiting for transfers between devices: 58.9 us -> none  [body(): lax.psum(weight_terms[0].astype(jnp.bfloat16), 'tile').astype(jnp.float32)]
    reshape x49 -> x0, local copies, waits for them, and re-layouts: 57.8 us -> none  [the longest x16 25.6 us: conv_back(): window.reshape(-1, channels)]
    pallas_call x0 -> x9, Pallas kernels: none -> 50.2 us  [the longest x1 33.7 us: main_call(): pl.pallas_call(kernel, out_shape=outs, scratch_shapes=scratch + extra, in...]
    ppermute x2 -> x22, waiting for transfers between devices: 0.01 us -> 45.3 us  [the longest x3 15 us: body(): falling = lax.ppermute(falling, 'tile', down)]
    dot_general x88 -> x0, matrix products: 37.5 us -> none  [the longest x27 8.54 us: conv_padded(): jnp.dot(window.reshape(-1, channels), kernel[3 * row_tap + col_tap], pref...]
    all_to_all x2 -> x0, waiting for transfers between devices: 36.9 us -> none  [the longest x1 36.9 us: body(): lax.all_to_all(outgoing, 'tile', split_axis=0, concat_axis=0, tiled=True)]
    ppermute x2 -> x22, starting transfers between devices: 3.64 us -> 40.4 us  [the longest x3 15.5 us: body(): rising = lax.ppermute(rising, 'tile', up)]
    reduce_scatter x2 -> x0, waiting for transfers between devices: 29.7 us -> none  [the longest x1 29.7 us: body(): lax.psum_scatter(summed[0].astype(jnp.bfloat16), 'dp', scatter_dimension=...]
  transfers between devices with their start and end apart: 7 -> 22, of which waited for: 3 -> 14; matrix products, arithmetic and copies ran while one was open for 9% -> 0% of each run, Pallas kernels for 0% -> 5%
where the time goes in v1:
time: 145 us; the launch traced here: 147 us
  Pallas kernels  50.2 us (35%)
  waiting for transfers between devices  45.3 us (31%)
  starting transfers between devices  40.4 us (28%)
  local copies, waits for them, and re-layouts  8.63 us (6%)
    pallas_call x1, Pallas kernels, main_call(): pl.pallas_call(kernel, out_shape=outs, scratch_shapes=scratch + extra, in...  33.7 us
    ppermute x3, starting transfers between devices, body(): rising = lax.ppermute(rising, 'tile', up)  15.5 us
    ppermute x3, waiting for transfers between devices, body(): falling = lax.ppermute(falling, 'tile', down)  15 us
    pallas_call x6, Pallas kernels, local_kernel(): pl.pallas_call(fn, out_shape=outs, compiler_params=pltpu.CompilerParams(v...  12.7 us
    ppermute x4, waiting for transfers between devices, reduce_weights(): lax.ppermute(parts[2 * half + 1], 'dp', [(i, i ^ bit) for i in range(dp)])  12.4 us
    ppermute x4, starting transfers between devices, reduce_weights(): lax.ppermute(parts[2 * half + 1], 'dp', [(i, i ^ bit) for i in range(dp)])  12 us
    unnamed x47, local copies, waits for them, and re-layouts  7.05 us
    ppermute x3, waiting for transfers between devices, reduce_weights(): lax.ppermute(mine, 'tile', shifts[k])  6.01 us
  transfers between devices with their start and end apart: 22, of which 14 were waited for; matrix products, arithmetic and copies ran while one was open for 0% of the time, Pallas kernels for 5%

profile of v1, /device:TPU:0, one launch (start us, length us, event | category | flops | bytes accessed | tf_op | source)
XLA Modules:
  0.0 146.8 jit_solution(15717969097648696958)
XLA Ops:
  2.9 1.8 %copy.16 = bf16[1,4,14,14,256]{4,3,2,1,0:T(8,128)(2,1)} copy(bf16[1,4,14,14,256]{4,1,3,2,0:T(4,128)(2,1)} %param.15) | data formatting | bytes 802816 | tf_op args[7]
  5.4 1.9 %shard_map.103.refs_7_ = bf16[4,208,256]{2,1,0:T(8,128)(2,1)} custom-call(bf16[4,14,14,256]{3,2,1,0:T(8,128)(2,1)} %bitcast.14, s32[4,2]{1,0:T(4,128)} %pad_add_fusion.place_ref), custom_call_target="tpu_custom_call" | custom-call | tf_op jit(solution)/shard_map/pallas_call | solution.py:54
  8.6 5.6 %collective-permute-start.3 = (bf16[4,208,256]{2,1,0:T(8,128)(2,1)}, bf16[4,208,256]{2,1,0:T(8,128)(2,1)S(1)}, u32[]{:S(2)}, u32[]{:S(2)}) collective-permute-start(bf16[4,208,256]{2,1,0:T(8,128)(2,1)} %shard_map.103.refs_7_), channel_id=1, source_target_pairs={{0,2},{1,3},{2,4},{3,5},{4,6},{5,7},{8,10},{9,11},{10,12},{11,13},... | collective-permute-start | bytes 1277960 | tf_op jit(solution)/shard_map/ppermute | solution.py:465
  14.2 8.1 %collective-permute-done.4.refs_9_ = bf16[4,208,256]{2,1,0:T(8,128)(2,1)S(1)} collective-permute-done((bf16[4,208,256]{2,1,0:T(8,128)(2,1)}, bf16[4,208,256]{2,1,0:T(8,128)(2,1)S(1)}, u32[]{:S(2)}, u32[]{:S(2)}) %collective-permute-start.4) | collective-permute-done | bytes 426016 | tf_op jit(solution)/shard_map/ppermute | solution.py:466
  23.5 4.6 %collective-permute-start.5 = (bf16[4,208,256]{2,1,0:T(8,128)(2,1)S(1)}, bf16[4,208,256]{2,1,0:T(8,128)(2,1)S(1)}, u32[]{:S(2)}, u32[]{:S(2)}) collective-permute-start(bf16[4,208,256]{2,1,0:T(8,128)(2,1)S(1)} %collective-permute-done.3.refs_8_), channel_id=1, source_target_pairs={{0,2},{1,3},{2,4},{3,5},{4,6},{5,7},{8,10},{9,11},{10,12},{11,13},... | collective-permute-start | bytes 1277960 | tf_op jit(solution)/shard_map/ppermute | solution.py:465
  28.2 6.9 %collective-permute-done.6.refs_11_ = bf16[4,208,256]{2,1,0:T(8,128)(2,1)S(1)} collective-permute-done((bf16[4,208,256]{2,1,0:T(8,128)(2,1)S(1)}, bf16[4,208,256]{2,1,0:T(8,128)(2,1)S(1)}, u32[]{:S(2)}, u32[]{:S(2)}) %collective-permute-start.6) | collective-permute-done | bytes 426016 | tf_op jit(solution)/shard_map/ppermute | solution.py:466
  36.4 5.3 %collective-permute-start.7 = (bf16[4,208,256]{2,1,0:T(8,128)(2,1)S(1)}, bf16[4,208,256]{2,1,0:T(8,128)(2,1)}, u32[]{:S(2)}, u32[]{:S(2)}) collective-permute-start(bf16[4,208,256]{2,1,0:T(8,128)(2,1)S(1)} %collective-permute-done.5.refs_10_), channel_id=1, source_target_pairs={{0,2},{1,3},{2,4},{3,5},{4,6},{5,7},{8,10},{9,11},{10,12},{11,13},... | collective-permute-start | bytes 1277960 | tf_op jit(solution)/shard_map/ppermute | solution.py:465
  43.7 3.8 %collective-permute-done.2.refs_3_ = bf16[64,256]{1,0:T(8,128)(2,1)S(1)} collective-permute-done((bf16[64,256]{1,0:T(8,128)(2,1)S(1)}, bf16[64,256]{1,0:T(8,128)(2,1)S(1)}, u32[]{:S(2)}, u32[]{:S(2)}) %collective-permute-start.2) | collective-permute-done | bytes 32800 | tf_op jit(solution)/shard_map/ppermute | solution.py:453
  49.0 33.7 %shard_map.104 = (bf16[2304,256]{1,0:T(8,128)(2,1)}, bf16[2304,256]{1,0:T(8,128)(2,1)}, f32[1024,256]{1,0:T(8,128)}, bf16[1024,256]{1,0:T(8,128)(2,1)}) custom-call(bf16[1024,256]{1,0:T(8,128)(2,1)} %bitcast.18, bf16[1024,256]{1,0:T(8,128)(2,1)} %copy-done.3, bf16[64,256]{1,0:T(8,128)(2,1)} %copy-done.21, bf16[64,256]{1,0:T(8,128)(2,1)} %copy-done.20, ...), custom_call_target="tpu_custom_call" | custom-call | tf_op jit(solution)/shard_map/pallas_call | solution.py:302
  82.7 3.1 %collective-permute-done.9.got_ref = bf16[2304,256]{1,0:T(8,128)(2,1)S(1)} collective-permute-done((bf16[2304,256]{1,0:T(8,128)(2,1)}, bf16[2304,256]{1,0:T(8,128)(2,1)S(1)}, u32[]{:S(2)}, u32[]{:S(2)}) %collective-permute-start.9) | collective-permute-done | bytes 1179680 | tf_op jit(solution)/shard_map/ppermute | solution.py:329
  86.8 2.8 %shard_map.105 = (bf16[2,288,256]{2,1,0:T(8,128)(2,1)}, bf16[2,288,256]{2,1,0:T(8,128)(2,1)}, bf16[2,288,256]{2,1,0:T(8,128)(2,1)}, bf16[2,288,256]{2,1,0:T(8,128)(2,1)}) custom-call(bf16[2304,256]{1,0:T(8,128)(2,1)} %get-tuple-element.21.keep_ref, bf16[2304,256]{1,0:T(8,128)(2,1)} %copy-done), custom_call_target="tpu_custom_call" | custom-call | tf_op jit(solution)/shard_map/pallas_call | solution.py:312
  89.7 2.2 %collective-permute-start.10 = (bf16[2,288,256]{2,1,0:T(8,128)(2,1)}, bf16[2,288,256]{2,1,0:T(8,128)(2,1)S(1)}, u32[]{:S(2)}, u32[]{:S(2)}) collective-permute-start(bf16[2,288,256]{2,1,0:T(8,128)(2,1)} %get-tuple-element.24), channel_id=1, source_target_pairs={{0,8},{8,0},{16,24},{24,16},{1,9},{9,1},{17,25},{25,17},{2,10},{10... | collective-permute-start | bytes 884744 | tf_op jit(solution)/shard_map/ppermute | solution.py:356
  91.9 7.7 %collective-permute-start.11 = (bf16[2,288,256]{2,1,0:T(8,128)(2,1)}, bf16[2,288,256]{2,1,0:T(8,128)(2,1)S(1)}, u32[]{:S(2)}, u32[]{:S(2)}) collective-permute-start(bf16[2,288,256]{2,1,0:T(8,128)(2,1)} %get-tuple-element.26), channel_id=1, source_target_pairs={{0,16},{8,24},{16,0},{24,8},{1,17},{9,25},{17,1},{25,9},{2,18},{10... | collective-permute-start | bytes 884744 | tf_op jit(solution)/shard_map/ppermute | solution.py:356
  99.6 7.4 %collective-permute-done.11.qr = bf16[2,288,256]{2,1,0:T(8,128)(2,1)S(1)} collective-permute-done((bf16[2,288,256]{2,1,0:T(8,128)(2,1)}, bf16[2,288,256]{2,1,0:T(8,128)(2,1)S(1)}, u32[]{:S(2)}, u32[]{:S(2)}) %collective-permute-start.11) | collective-permute-done | bytes 294944 | tf_op jit(solution)/shard_map/ppermute | solution.py:356
  107.7 2.1 %shard_map.106 = (bf16[1,288,256]{2,1,0:T(8,128)(2,1)}, bf16[1,288,256]{2,1,0:T(8,128)(2,1)}, bf16[1,288,256]{2,1,0:T(8,128)(2,1)}, bf16[1,288,256]{2,1,0:T(8,128)(2,1)}) custom-call(bf16[2,288,256]{2,1,0:T(8,128)(2,1)} %get-tuple-element.23.p, bf16[2,288,256]{2,1,0:T(8,128)(2,1)} %copy-done.10, bf16[2,288,256]{2,1,0:T(8,128)(2,1)} %get-tuple-element.25.q, ...), custom_call_target="tpu_custom_call" | custom-call | tf_op jit(solution)/shard_map/pallas_call | solution.py:312
  111.9 3.4 %collective-permute-done.12.pr = bf16[1,288,256]{2,1,0:T(8,128)(2,1)S(1)} collective-permute-done((bf16[1,288,256]{2,1,0:T(8,128)(2,1)}, bf16[1,288,256]{2,1,0:T(8,128)(2,1)S(1)}, u32[]{:S(2)}, u32[]{:S(2)}) %collective-permute-start.12) | collective-permute-done | bytes 147488 | tf_op jit(solution)/shard_map/ppermute | solution.py:356
  117.5 1.9 %shard_map.107 = (bf16[144,256]{1,0:T(8,128)(2,1)}, bf16[144,256]{1,0:T(8,128)(2,1)}, bf16[144,256]{1,0:T(8,128)(2,1)}, bf16[144,256]{1,0:T(8,128)(2,1)}) custom-call(bf16[1,288,256]{2,1,0:T(8,128)(2,1)} %get-tuple-element.27.p, bf16[1,288,256]{2,1,0:T(8,128)(2,1)} %copy-done.12, bf16[1,288,256]{2,1,0:T(8,128)(2,1)} %get-tuple-element.29.q, ...), custom_call_target="tpu_custom_call" | custom-call | tf_op jit(solution)/shard_map/pallas_call | solution.py:394
  119.5 3.8 %collective-permute-start.16 = (bf16[144,256]{1,0:T(8,128)(2,1)}, bf16[144,256]{1,0:T(8,128)(2,1)S(1)}, u32[]{:S(2)}, u32[]{:S(2)}) collective-permute-start(bf16[144,256]{1,0:T(8,128)(2,1)} %get-tuple-element.34), channel_id=1, source_target_pairs={{0,6},{1,7},{2,0},{3,1},{4,2},{5,3},{6,4},{7,5},{8,14},{9,15},{10,... | collective-permute-start | bytes 221192 | tf_op jit(solution)/shard_map/ppermute | solution.py:400
  123.3 2.7 %collective-permute-done.14.refs_1_ = bf16[144,256]{1,0:T(8,128)(2,1)S(1)} collective-permute-done((bf16[144,256]{1,0:T(8,128)(2,1)}, bf16[144,256]{1,0:T(8,128)(2,1)S(1)}, u32[]{:S(2)}, u32[]{:S(2)}) %collective-permute-start.14) | collective-permute-done | bytes 73760 | tf_op jit(solution)/shard_map/ppermute | solution.py:400
  129.2 2.7 %collective-permute-start.19 = (bf16[144,256]{1,0:T(8,128)(2,1)}, bf16[144,256]{1,0:T(8,128)(2,1)S(1)}, u32[]{:S(2)}, u32[]{:S(2)}) collective-permute-start(bf16[144,256]{1,0:T(8,128)(2,1)} %shard_map.108.refs_0_), channel_id=1, source_target_pairs={{0,6},{1,7},{2,0},{3,1},{4,2},{5,3},{6,4},{7,5},{8,14},{9,15},{10,... | collective-permute-start | bytes 221192 | tf_op jit(solution)/shard_map/ppermute | solution.py:409
  132.5 2.5 %collective-permute-done.19.refs_3_ = bf16[144,256]{1,0:T(8,128)(2,1)S(1)} collective-permute-done((bf16[144,256]{1,0:T(8,128)(2,1)}, bf16[144,256]{1,0:T(8,128)(2,1)S(1)}, u32[]{:S(2)}, u32[]{:S(2)}) %collective-permute-start.19) | collective-permute-done | bytes 73760 | tf_op jit(solution)/shard_map/ppermute | solution.py:409
  135.1 2.4 %collective-permute-done.18.refs_2_ = bf16[144,256]{1,0:T(8,128)(2,1)S(1)} collective-permute-done((bf16[144,256]{1,0:T(8,128)(2,1)}, bf16[144,256]{1,0:T(8,128)(2,1)S(1)}, u32[]{:S(2)}, u32[]{:S(2)}) %collective-permute-start.18) | collective-permute-done | bytes 73760 | tf_op jit(solution)/shard_map/ppermute | solution.py:409
  141.7 2.2 %shard_map.111 = bf16[1024,256]{1,0:T(8,128)(2,1)} custom-call(f32[1024,256]{1,0:T(8,128)} %get-tuple-element.37.a, bf16[1024,256]{1,0:T(8,128)(2,1)} %copy-done.2), custom_call_target="tpu_custom_call" | custom-call | tf_op jit(solution)/shard_map/pallas_call | solution.py:312
  144.7 2.1 %shard_map.110 = (f32[576,256]{1,0:T(8,128)}, f32[576,256]{1,0:T(8,128)}) custom-call(bf16[576,256]{1,0:T(8,128)(2,1)} %shard_map.109.mine_ref, bf16[576,256]{1,0:T(8,128)(2,1)} %copy-done.9), custom_call_target="tpu_custom_call" | custom-call | tf_op jit(solution)/shard_map/pallas_call | solution.py:312
  (83 shorter events, 25.3 us)
Async XLA Ops:
  0.6 27.5 %copy-start.1 = (bf16[1,16,64,256]{3,2,1,0:T(8,128)(2,1)S(1)}, bf16[1,16,64,256]{3,2,1,0:T(8,128)(2,1)}, u32[]{:S(2)}) copy-start(bf16[1,16,64,256]{3,2,1,0:T(8,128)(2,1)} %param.8) | copy-start | bytes 1572868
  7.3 14.9 %collective-permute-start.4 = (bf16[4,208,256]{2,1,0:T(8,128)(2,1)}, bf16[4,208,256]{2,1,0:T(8,128)(2,1)S(1)}, u32[]{:S(2)}, u32[]{:S(2)}) collective-permute-start(bf16[4,208,256]{2,1,0:T(8,128)(2,1)} %shard_map.103.refs_7_), channel_id=1, source_target_pairs={{2,0},{3,1},{4,2},{5,3},{6,4},{7,5},{10,8},{11,9},{12,10},{13,11},... | collective-permute-start | bytes 1277960 | tf_op jit(solution)/shard_map/ppermute | solution.py:466
  8.6 14.9 %collective-permute-start.3 = (bf16[4,208,256]{2,1,0:T(8,128)(2,1)}, bf16[4,208,256]{2,1,0:T(8,128)(2,1)S(1)}, u32[]{:S(2)}, u32[]{:S(2)}) collective-permute-start(bf16[4,208,256]{2,1,0:T(8,128)(2,1)} %shard_map.103.refs_7_), channel_id=1, source_target_pairs={{0,2},{1,3},{2,4},{3,5},{4,6},{5,7},{8,10},{9,11},{10,12},{11,13},... | collective-permute-start | bytes 1277960 | tf_op jit(solution)/shard_map/ppermute | solution.py:465
  22.2 26.8 %copy-start.4 = (bf16[4,208,256]{2,1,0:T(8,128)(2,1)}, bf16[4,208,256]{2,1,0:T(8,128)(2,1)S(1)}, u32[]{:S(2)}) copy-start(bf16[4,208,256]{2,1,0:T(8,128)(2,1)S(1)} %collective-permute-done.4.refs_9_) | copy-start | bytes 1277956
  22.2 12.9 %collective-permute-start.6 = (bf16[4,208,256]{2,1,0:T(8,128)(2,1)S(1)}, bf16[4,208,256]{2,1,0:T(8,128)(2,1)S(1)}, u32[]{:S(2)}, u32[]{:S(2)}) collective-permute-start(bf16[4,208,256]{2,1,0:T(8,128)(2,1)S(1)} %collective-permute-done.4.refs_9_), channel_id=1, source_target_pairs={{2,0},{3,1},{4,2},{5,3},{6,4},{7,5},{10,8},{11,9},{12,10},{13,11},... | collective-permute-start | bytes 1277960 | tf_op jit(solution)/shard_map/ppermute | solution.py:466
  23.5 12.9 %collective-permute-start.5 = (bf16[4,208,256]{2,1,0:T(8,128)(2,1)S(1)}, bf16[4,208,256]{2,1,0:T(8,128)(2,1)S(1)}, u32[]{:S(2)}, u32[]{:S(2)}) collective-permute-start(bf16[4,208,256]{2,1,0:T(8,128)(2,1)S(1)} %collective-permute-done.3.refs_8_), channel_id=1, source_target_pairs={{0,2},{1,3},{2,4},{3,5},{4,6},{5,7},{8,10},{9,11},{10,12},{11,13},... | collective-permute-start | bytes 1277960 | tf_op jit(solution)/shard_map/ppermute | solution.py:465
  28.1 19.4 %collective-permute-start = (bf16[1024,256]{1,0:T(8,128)(2,1)S(1)}, bf16[1024,256]{1,0:T(8,128)(2,1)S(1)}, u32[]{:S(2)}, u32[]{:S(2)}) collective-permute-start(bf16[1024,256]{1,0:T(8,128)(2,1)S(1)} %bitcast.19), channel_id=1, source_target_pairs={{0,1},{1,0},{2,3},{3,2},{4,5},{5,4},{6,7},{7,6},{8,9},{9,8},{10,11... | collective-permute-start | bytes 1572872 | tf_op jit(solution)/shard_map/ppermute | solution.py:458
  35.1 12.5 %collective-permute-start.8 = (bf16[4,208,256]{2,1,0:T(8,128)(2,1)S(1)}, bf16[4,208,256]{2,1,0:T(8,128)(2,1)S(1)}, u32[]{:S(2)}, u32[]{:S(2)}) collective-permute-start(bf16[4,208,256]{2,1,0:T(8,128)(2,1)S(1)} %collective-permute-done.6.refs_11_), channel_id=1, source_target_pairs={{2,0},{3,1},{4,2},{5,3},{6,4},{7,5},{10,8},{11,9},{12,10},{13,11},... | collective-permute-start | bytes 1277960 | tf_op jit(solution)/shard_map/ppermute | solution.py:466
  36.4 12.6 %collective-permute-start.7 = (bf16[4,208,256]{2,1,0:T(8,128)(2,1)S(1)}, bf16[4,208,256]{2,1,0:T(8,128)(2,1)}, u32[]{:S(2)}, u32[]{:S(2)}) collective-permute-start(bf16[4,208,256]{2,1,0:T(8,128)(2,1)S(1)} %collective-permute-done.5.refs_10_), channel_id=1, source_target_pairs={{0,2},{1,3},{2,4},{3,5},{4,6},{5,7},{8,10},{9,11},{10,12},{11,13},... | collective-permute-start | bytes 1277960 | tf_op jit(solution)/shard_map/ppermute | solution.py:465
  41.8 5.8 %collective-permute-start.2 = (bf16[64,256]{1,0:T(8,128)(2,1)S(1)}, bf16[64,256]{1,0:T(8,128)(2,1)S(1)}, u32[]{:S(2)}, u32[]{:S(2)}) collective-permute-start(bf16[64,256]{1,0:T(8,128)(2,1)S(1)} %select_bitcast_fusion), channel_id=1, source_target_pairs={{1,3},{2,0},{3,5},{4,2},{5,7},{6,4},{9,11},{10,8},{11,13},{12,10},... | collective-permute-start | bytes 98312 | tf_op jit(solution)/shard_map/ppermute | solution.py:453
  43.0 4.5 %collective-permute-start.1 = (bf16[64,256]{1,0:T(8,128)(2,1)S(1)}, bf16[64,256]{1,0:T(8,128)(2,1)S(1)}, u32[]{:S(2)}, u32[]{:S(2)}) collective-permute-start(bf16[64,256]{1,0:T(8,128)(2,1)S(1)} %select_bitcast_fusion), channel_id=1, source_target_pairs={{1,2},{2,1},{3,4},{4,3},{5,6},{6,5},{9,10},{10,9},{11,12},{12,11},... | collective-permute-start | bytes 98312 | tf_op jit(solution)/shard_map/ppermute | solution.py:450
  82.7 3.1 %collective-permute-start.9 = (bf16[2304,256]{1,0:T(8,128)(2,1)}, bf16[2304,256]{1,0:T(8,128)(2,1)S(1)}, u32[]{:S(2)}, u32[]{:S(2)}) collective-permute-start(bf16[2304,256]{1,0:T(8,128)(2,1)} %get-tuple-element.22), channel_id=1, source_target_pairs={{0,1},{1,0},{2,3},{3,2},{4,5},{5,4},{6,7},{7,6},{8,9},{9,8},{10,11... | collective-permute-start | bytes 3538952 | tf_op jit(solution)/shard_map/ppermute | solution.py:329
  89.7 9.9 %collective-permute-start.10 = (bf16[2,288,256]{2,1,0:T(8,128)(2,1)}, bf16[2,288,256]{2,1,0:T(8,128)(2,1)S(1)}, u32[]{:S(2)}, u32[]{:S(2)}) collective-permute-start(bf16[2,288,256]{2,1,0:T(8,128)(2,1)} %get-tuple-element.24), channel_id=1, source_target_pairs={{0,8},{8,0},{16,24},{24,16},{1,9},{9,1},{17,25},{25,17},{2,10},{10... | collective-permute-start | bytes 884744 | tf_op jit(solution)/shard_map/ppermute | solution.py:356
  91.9 15.1 %collective-permute-start.11 = (bf16[2,288,256]{2,1,0:T(8,128)(2,1)}, bf16[2,288,256]{2,1,0:T(8,128)(2,1)S(1)}, u32[]{:S(2)}, u32[]{:S(2)}) collective-permute-start(bf16[2,288,256]{2,1,0:T(8,128)(2,1)} %get-tuple-element.26), channel_id=1, source_target_pairs={{0,16},{8,24},{16,0},{24,8},{1,17},{9,25},{17,1},{25,9},{2,18},{10... | collective-permute-start | bytes 884744 | tf_op jit(solution)/shard_map/ppermute | solution.py:356
  109.8 5.5 %collective-permute-start.12 = (bf16[1,288,256]{2,1,0:T(8,128)(2,1)}, bf16[1,288,256]{2,1,0:T(8,128)(2,1)S(1)}, u32[]{:S(2)}, u32[]{:S(2)}) collective-permute-start(bf16[1,288,256]{2,1,0:T(8,128)(2,1)} %get-tuple-element.28), channel_id=1, source_target_pairs={{0,16},{8,24},{16,0},{24,8},{1,17},{9,25},{17,1},{25,9},{2,18},{10... | collective-permute-start | bytes 442376 | tf_op jit(solution)/shard_map/ppermute | solution.py:356
  111.5 5.4 %collective-permute-start.13 = (bf16[1,288,256]{2,1,0:T(8,128)(2,1)}, bf16[1,288,256]{2,1,0:T(8,128)(2,1)S(1)}, u32[]{:S(2)}, u32[]{:S(2)}) collective-permute-start(bf16[1,288,256]{2,1,0:T(8,128)(2,1)} %get-tuple-element.30), channel_id=1, source_target_pairs={{0,8},{8,0},{16,24},{24,16},{1,9},{9,1},{17,25},{25,17},{2,10},{10... | collective-permute-start | bytes 442376 | tf_op jit(solution)/shard_map/ppermute | solution.py:356
  111.9 29.0 %collective-permute-start.21 = (bf16[1024,256]{1,0:T(8,128)(2,1)S(1)}, bf16[1024,256]{1,0:T(8,128)(2,1)S(1)}, u32[]{:S(2)}, u32[]{:S(2)}) collective-permute-start(bf16[1024,256]{1,0:T(8,128)(2,1)S(1)} %copy-done.22), channel_id=1, source_target_pairs={{0,1},{1,0},{2,3},{3,2},{4,5},{5,4},{6,7},{7,6},{8,9},{9,8},{10,11... | collective-permute-start | bytes 1572872 | tf_op jit(solution)/shard_map/ppermute | solution.py:474
  119.5 6.5 %collective-permute-start.14 = (bf16[144,256]{1,0:T(8,128)(2,1)}, bf16[144,256]{1,0:T(8,128)(2,1)S(1)}, u32[]{:S(2)}, u32[]{:S(2)}) collective-permute-start(bf16[144,256]{1,0:T(8,128)(2,1)} %get-tuple-element.32), channel_id=1, source_target_pairs={{0,2},{1,3},{2,4},{3,5},{4,6},{5,7},{6,0},{7,1},{8,10},{9,11},{10,... | collective-permute-start | bytes 221192 | tf_op jit(solution)/shard_map/ppermute | solution.py:400
  119.5 7.4 %collective-permute-start.15 = (bf16[144,256]{1,0:T(8,128)(2,1)}, bf16[144,256]{1,0:T(8,128)(2,1)S(1)}, u32[]{:S(2)}, u32[]{:S(2)}) collective-permute-start(bf16[144,256]{1,0:T(8,128)(2,1)} %get-tuple-element.33), channel_id=1, source_target_pairs={{0,4},{1,5},{2,6},{3,7},{4,0},{5,1},{6,2},{7,3},{8,12},{9,13},{10,... | collective-permute-start | bytes 221192 | tf_op jit(solution)/shard_map/ppermute | solution.py:400
  119.5 7.4 %collective-permute-start.16 = (bf16[144,256]{1,0:T(8,128)(2,1)}, bf16[144,256]{1,0:T(8,128)(2,1)S(1)}, u32[]{:S(2)}, u32[]{:S(2)}) collective-permute-start(bf16[144,256]{1,0:T(8,128)(2,1)} %get-tuple-element.34), channel_id=1, source_target_pairs={{0,6},{1,7},{2,0},{3,1},{4,2},{5,3},{6,4},{7,5},{8,14},{9,15},{10,... | collective-permute-start | bytes 221192 | tf_op jit(solution)/shard_map/ppermute | solution.py:400
  129.2 5.8 %collective-permute-start.19 = (bf16[144,256]{1,0:T(8,128)(2,1)}, bf16[144,256]{1,0:T(8,128)(2,1)S(1)}, u32[]{:S(2)}, u32[]{:S(2)}) collective-permute-start(bf16[144,256]{1,0:T(8,128)(2,1)} %shard_map.108.refs_0_), channel_id=1, source_target_pairs={{0,6},{1,7},{2,0},{3,1},{4,2},{5,3},{6,4},{7,5},{8,14},{9,15},{10,... | collective-permute-start | bytes 221192 | tf_op jit(solution)/shard_map/ppermute | solution.py:409
  132.0 5.5 %collective-permute-start.18 = (bf16[144,256]{1,0:T(8,128)(2,1)}, bf16[144,256]{1,0:T(8,128)(2,1)S(1)}, u32[]{:S(2)}, u32[]{:S(2)}) collective-permute-start(bf16[144,256]{1,0:T(8,128)(2,1)} %shard_map.108.refs_0_), channel_id=1, source_target_pairs={{0,4},{1,5},{2,6},{3,7},{4,0},{5,1},{6,2},{7,3},{8,12},{9,13},{10,... | collective-permute-start | bytes 221192 | tf_op jit(solution)/shard_map/ppermute | solution.py:409
  132.2 6.4 %collective-permute-start.17 = (bf16[144,256]{1,0:T(8,128)(2,1)}, bf16[144,256]{1,0:T(8,128)(2,1)S(1)}, u32[]{:S(2)}, u32[]{:S(2)}) collective-permute-start(bf16[144,256]{1,0:T(8,128)(2,1)} %shard_map.108.refs_0_), channel_id=1, source_target_pairs={{0,2},{1,3},{2,4},{3,5},{4,6},{5,7},{6,0},{7,1},{8,10},{9,11},{10,... | collective-permute-start | bytes 221192 | tf_op jit(solution)/shard_map/ppermute | solution.py:409
  140.9 3.0 %collective-permute-start.20 = (bf16[576,256]{1,0:T(8,128)(2,1)}, bf16[576,256]{1,0:T(8,128)(2,1)S(1)}, u32[]{:S(2)}, u32[]{:S(2)}) collective-permute-start(bf16[576,256]{1,0:T(8,128)(2,1)} %shard_map.109.mine_ref), channel_id=1, source_target_pairs={{0,1},{1,0},{2,3},{3,2},{4,5},{5,4},{6,7},{7,6},{8,9},{9,8},{10,11... | collective-permute-start | bytes 884744 | tf_op jit(solution)/shard_map/ppermute | solution.py:418
  (21 other events, 100.4 us)

commit v2 on v1

--- a/solution.py
+++ b/solution.py
@@ -10,7 +10,7 @@
 
 BF = jnp.bfloat16
 F32 = jnp.float32
-VMEM_LIMIT = 56 * 1024 * 1024
+VMEM_LIMIT = 24 * 1024 * 1024
 PITCH = 16
 SLOT = 208
 
@@ -19,22 +19,32 @@
     return (n + m - 1) // m * m
 
 
-def call(kernel, outs, scratch=(), aliases=None):
+def run(kernel, outs, args, scratch=(), aliases=None, smem=(), hbm_out=()):
+    args = [
+        x if i in smem else pltpu.with_memory_space_constraint(x, pltpu.VMEM)
+        for i, x in enumerate(args)
+    ]
     return pl.pallas_call(
         kernel,
-        out_shape=outs,
-        in_specs=None,
+        out_shape=tuple(
+            s if i in hbm_out else pltpu.VMEM(s.shape, s.dtype) for i, s in enumerate(outs)
+        ),
+        in_specs=[
+            pl.BlockSpec(memory_space=pltpu.SMEM if i in smem else pltpu.VMEM)
+            for i in range(len(args))
+        ],
+        out_specs=tuple(pl.BlockSpec(memory_space=pltpu.VMEM) for _ in outs),
         scratch_shapes=list(scratch),
         input_output_aliases=aliases or {},
         compiler_params=pltpu.CompilerParams(vmem_limit_bytes=VMEM_LIMIT),
-    )
+    )(*args)
 
 
 def sds(shape, dtype):
     return jax.ShapeDtypeStruct(shape, dtype)
 
 
-def pack_kernel(side, cot_ref, place_ref, out_ref, wide):
+def pack_kernel(side, height, cot_ref, owner_ref, row_ref, col_ref, out_ref, wide):
     regions = cot_ref.shape[0]
     lanes = lax.broadcasted_iota(jnp.int32, (16, 256), 1)
     rows = lax.broadcasted_iota(jnp.int32, (16, 256), 0)
@@ -42,25 +52,22 @@
         for i in range(side):
             wide[side * i : side * i + side, :] = cot_ref[r, i].astype(F32)
         tail = wide[192:208, :]
-        spot = place_ref[r, 0].astype(F32)
-        column = place_ref[r, 1].astype(F32)
+        spot = (owner_ref[0, r, 0] * height + row_ref[0, r] + 1).astype(F32)
+        column = col_ref[0, r].astype(F32)
         note = jnp.where(lanes == 0, spot, jnp.where(lanes == 1, column, 0.0))
         wide[192:208, :] = jnp.where(rows < 4, tail, note)
         out_ref[r] = wide[...].astype(BF)
 
 
-def pack(cotangent, place):
+def pack(cotangent, height, place):
     regions, side = cotangent.shape[0], cotangent.shape[1]
-    return pl.pallas_call(
-        functools.partial(pack_kernel, side),
-        out_shape=sds((regions, SLOT, 256), BF),
-        in_specs=[
-            pl.BlockSpec(memory_space=pltpu.VMEM),
-            pl.BlockSpec(memory_space=pltpu.SMEM),
-        ],
-        scratch_shapes=[pltpu.VMEM((SLOT, 256), F32)],
-        compiler_params=pltpu.CompilerParams(vmem_limit_bytes=VMEM_LIMIT),
-    )(cotangent, place)
+    return run(
+        functools.partial(pack_kernel, side, height),
+        (sds((regions, SLOT, 256), BF),),
+        (cotangent, *place),
+        scratch=[pltpu.VMEM((SLOT, 256), F32)],
+        smem=(1, 2, 3),
+    )[0]
 
 
 def pyramid_part(height, width, own, other, rim_a, rim_b, wf, pyr, xp):
@@ -117,12 +124,10 @@
 
 def regions_part(side, height, width, blocks, pyr, w1, w2, wb1, wb2, acc1, acc2, gp, scratch):
     xs, hs, gs, wide, vs, slope1, todo = scratch
-    cells = side * PITCH
     chip = lax.axis_index("tile") // 2
     lanes = lax.broadcasted_iota(jnp.int32, (16, 256), 1)
     rows16 = lax.broadcasted_iota(jnp.int32, (16, 256), 0)
     in_row = rows16 < side
-    inside = lax.rem(lax.broadcasted_iota(jnp.int32, (cells, 256), 0), PITCH) < side
     per = blocks[0].shape[0]
 
     count = jnp.int32(0)
@@ -139,72 +144,91 @@
             todo[2, count] = jnp.where(here, lax.rem(column, 8), 0)
             count = count + here.astype(jnp.int32)
 
-    for buf in (xs, hs, gs):
-        buf[0:16, :] = jnp.zeros((16, 768), BF)
-        buf[cells + 16 : cells + 32, :] = jnp.zeros((16, 768), BF)
-
-    def put(buf, v):
-        buf[16 : 16 + cells, 0:256] = pltpu.roll(v, 1, 0).astype(BF)
-        buf[16 : 16 + cells, 256:512] = v.astype(BF)
-        buf[16 : 16 + cells, 512:768] = pltpu.roll(v, cells - 1, 0).astype(BF)
-
-    def conv(buf, w):
-        total = jnp.zeros((cells, 256), F32)
-        for a in range(3):
-            total += jnp.dot(
-                buf[a * 16 : a * 16 + cells, :],
-                w[a * 768 : a * 768 + 768, :],
-                preferred_element_type=F32,
-            )
-        return total
-
-    def taps(acc, buf, grad):
-        turned = grad.T.astype(BF)
-        for a in range(3):
-            acc[:, a * 768 : a * 768 + 768] += jnp.dot(
-                turned, buf[a * 16 : a * 16 + cells, :], preferred_element_type=F32
-            )
-
-    def region(n, carry):
-        which = todo[0, n]
-        base = pl.multiple_of(todo[1, n], 8)
-        lead = todo[2, n]
-        for s, block in enumerate(blocks):
-
-            @pl.when(which // per == s)
-            def _():
-                wide[...] = block[lax.rem(which, per)].astype(F32)
-
-        for i in range(side):
-            got = pyr[pl.ds(pl.multiple_of(base + i * width, 8), 24), :]
-            got = pltpu.roll(got, lax.rem(24 - lead, 24), 0)[0:16]
-            vs[i * 16 : i * 16 + 16, :] = jnp.where(in_row, got, 0.0)
-        put(xs, vs[...])
-        pre1 = conv(xs, w1)
-        act1, slope = gelu_pair(pre1)
-        slope1[...] = slope
+    def batch(size, start):
+        cells = (size * (side + 1) - 1) * PITCH
+        spot = lax.broadcasted_iota(jnp.int32, (cells, 256), 0)
+        inside = (lax.rem(spot, PITCH) < side) & (lax.rem(spot // PITCH, side + 1) < side)
+        used = pl.ds(16, cells)
+
+        def put(buf, v):
+            buf[used, 0:256] = pltpu.roll(v, 1, 0).astype(BF)
+            buf[used, 256:512] = v.astype(BF)
+            buf[used, 512:768] = pltpu.roll(v, cells - 1, 0).astype(BF)
+
+        def conv(buf, w):
+            total = jnp.zeros((cells, 256), F32)
+            for a in range(3):
+                total += jnp.dot(
+                    buf[a * 16 : a * 16 + cells, :],
+                    w[a * 768 : a * 768 + 768, :],
+                    preferred_element_type=F32,
+                )
+            return total
+
+        def taps(acc, buf, grad):
+            turned = grad.T.astype(BF)
+            for a in range(3):
+                acc[:, a * 768 : a * 768 + 768] += jnp.dot(
+                    turned, buf[a * 16 : a * 16 + cells, :], preferred_element_type=F32
+                )
+
+        for buf in (xs, hs, gs):
+            buf[0:16, :] = jnp.zeros((16, 768), BF)
+            buf[cells + 16 : cells + 32, :] = jnp.zeros((16, 768), BF)
+        for n in range(size - 1):
+            gap = ((n + 1) * (side + 1) - 1) * PITCH
+            vs[gap : gap + PITCH, :] = jnp.zeros((PITCH, 256), F32)
+        bases, leads = [], []
+        for n in range(size):
+            which = todo[0, start + n]
+            bases.append(pl.multiple_of(todo[1, start + n], 8))
+            leads.append(todo[2, start + n])
+            for s, block in enumerate(blocks):
+
+                @pl.when(which // per == s)
+                def _(block=block, n=n, which=which):
+                    wide[n] = block[lax.rem(which, per)].astype(F32)
+
+        for n in range(size):
+            for i in range(side):
+                got = pyr[pl.ds(pl.multiple_of(bases[n] + i * width, 8), 24), :]
+                got = pltpu.roll(got, lax.rem(24 - leads[n], 24), 0)[0:16]
+                at = (n * (side + 1) + i) * PITCH
+                vs[at : at + 16, :] = jnp.where(in_row, got, 0.0)
+        put(xs, vs[0:cells, :])
+        act1, slope = gelu_pair(conv(xs, w1))
+        slope1[0:cells, :] = slope
         put(hs, jnp.where(inside, act1, 0.0))
-        pre2 = conv(hs, w2)
-        _, slope = gelu_pair(pre2)
-        for i in range(side):
-            got = wide[i * side : i * side + 16, :]
-            vs[i * 16 : i * 16 + 16, :] = jnp.where(in_row, got, 0.0)
-        g2 = vs[...] * slope
+        _, slope = gelu_pair(conv(hs, w2))
+        for n in range(size):
+            for i in range(side):
+                got = wide[n, i * side : i * side + 16, :]
+                at = (n * (side + 1) + i) * PITCH
+                vs[at : at + 16, :] = jnp.where(in_row, got, 0.0)
+        g2 = vs[0:cells, :] * slope
         put(gs, g2)
         taps(acc2, hs, g2)
         gact1 = conv(gs, wb2)
-        g1 = jnp.where(inside, gact1 * slope1[...], 0.0)
+        g1 = jnp.where(inside, gact1 * slope1[0:cells, :], 0.0)
         put(gs, g1)
         taps(acc1, xs, g1)
-        gcrop = jnp.where(inside, conv(gs, wb1), 0.0).astype(BF).astype(F32)
-        vs[...] = gcrop
-        for i in range(side):
-            at = pl.ds(pl.multiple_of(base + i * width, 8), 24)
-            piece = jnp.concatenate([vs[i * 16 : i * 16 + 16, :], jnp.zeros((8, 256), F32)])
-            gp[at, :] = gp[at, :] + pltpu.roll(piece, lead, 0)
+        vs[0:cells, :] = jnp.where(inside, conv(gs, wb1), 0.0).astype(BF).astype(F32)
+        for n in range(size):
+            for i in range(side):
+                at = pl.ds(pl.multiple_of(bases[n] + i * width, 8), 24)
+                row = (n * (side + 1) + i) * PITCH
+                piece = jnp.concatenate([vs[row : row + 16, :], jnp.zeros((8, 256), F32)])
+                gp[at, :] = gp[at, :] + pltpu.roll(piece, leads[n], 0)
+
+    def pair(n, carry):
+        batch(2, 2 * n)
         return carry
 
-    lax.fori_loop(0, count, region, 0)
+    lax.fori_loop(0, count // 2, pair, 0)
+
+    @pl.when(lax.rem(count, 2) == 1)
+    def _():
+        batch(1, count - 1)
 
 
 def finish_part(height, width, acc1, acc2, gp, keep, send, gp_own, gp_other):
@@ -232,7 +256,7 @@
 def main_call(side, height, width, first, last, state, weights, blocks):
     n = len(blocks)
     big = 2 * height * width + 16
-    cells = side * PITCH
+    cells = (2 * side + 1) * PITCH
     kept = (
         sds((big, 256), F32),
         sds((2304, 256), BF),
@@ -245,23 +269,17 @@
         sds((height * width, 256), F32),
         sds((height * width, 256), BF),
     )
-    outs = (kept if first and not last else ()) + (ends if last else sums)
+    outs = (kept if first else ()) + sums + (ends if last else ())
     scratch = [
         pltpu.VMEM((cells + 32, 768), BF),
         pltpu.VMEM((cells + 32, 768), BF),
         pltpu.VMEM((cells + 32, 768), BF),
-        pltpu.VMEM((SLOT, 256), F32),
+        pltpu.VMEM((2, SLOT, 256), F32),
         pltpu.VMEM((cells, 256), F32),
         pltpu.VMEM((cells, 256), F32),
         pltpu.SMEM((3, 128), jnp.int32),
     ]
-    extra = []
-    if first:
-        extra.append(pltpu.VMEM(((2 * height + 2) * width, 768), BF))
-    if first and last:
-        extra += [pltpu.VMEM(s.shape, s.dtype) for s in kept]
-    if last:
-        extra += [pltpu.VMEM(s.shape, s.dtype) for s in sums]
+    extra = [pltpu.VMEM(((2 * height + 2) * width, 768), BF)] if first else []
 
     def kernel(*refs):
         refs = list(refs)
@@ -277,50 +295,40 @@
         out_refs = take(len(outs))
         scratch_refs = take(len(scratch))
         if first:
-            xp = take(1)[0]
-            pyr, wb1, wb2 = take(3) if last else out_refs[:3]
-            acc1, acc2, gp = take(3) if last else out_refs[3:]
+            pyr, wb1, wb2 = out_refs[:3]
+            acc1, acc2, gp = out_refs[3:6]
             wf, w1, w2 = weight_refs
-            pyramid_part(height, width, *state_refs, wf, pyr, xp)
+            pyramid_part(height, width, *state_refs, wf, pyr, refs[0])
             flip_part(w1, wb1)
             flip_part(w2, wb2)
             for total in (acc1, acc2, gp):
                 total[...] = jnp.zeros(total.shape, F32)
         else:
             pyr, wb1, wb2 = state_refs[:3]
-            acc1, acc2, gp = take(3) if last else out_refs
+            acc1, acc2, gp = out_refs[:3]
             w1, w2 = weight_refs
-            for to, source in zip((acc1, acc2, gp), state_refs[3:]):
-                to[...] = source[...]
-        regions_part(
-            side, height, width, block_refs, pyr, w1, w2, wb1, wb2, acc1, acc2, gp, scratch_refs
-        )
+        if n:
+            regions_part(
+                side, height, width, block_refs, pyr, w1, w2, wb1, wb2, acc1, acc2, gp, scratch_refs
+            )
         if last:
-            finish_part(height, width, acc1, acc2, gp, *out_refs)
-
-    aliases = {} if first or last else {3: 0, 4: 1, 5: 2}
-    return pl.pallas_call(
-        kernel,
-        out_shape=outs,
-        scratch_shapes=scratch + extra,
-        input_output_aliases=aliases,
-        compiler_params=pltpu.CompilerParams(vmem_limit_bytes=VMEM_LIMIT),
-    )(*state, *weights, *blocks)
-
-
-def local_kernel(fn, outs, *arrays):
-    return pl.pallas_call(
-        fn,
-        out_shape=outs,
-        compiler_params=pltpu.CompilerParams(vmem_limit_bytes=VMEM_LIMIT),
-    )(*arrays)
+            finish_part(height, width, acc1, acc2, gp, *out_refs[-4:])
+
+    aliases = {} if first else {3: 0, 4: 1, 5: 2}
+    return run(kernel, outs, [*state, *weights, *blocks], scratch=scratch + extra, aliases=aliases)
+
+
+def local_kernel(fn, outs, *arrays, **more):
+    if isinstance(outs, tuple):
+        return run(fn, outs, arrays, **more)
+    return run(fn, (outs,), arrays, **more)[0]
 
 
 def add(a, b):
     return (a.astype(F32) + b.astype(F32)).astype(BF)
 
 
-def reduce_weights(keep, send, core_swap, dp, chips):
+def reduce_weights(keep, send, core_swap, dp, chips, beside):
     rows = keep.shape[0] // dp
     bits = dp.bit_length() - 1
     low = roundup(rows // 2, 16)
@@ -354,6 +362,8 @@
         for half in range(2):
             bit = 1 << orders[half][stage]
             received.append(lax.ppermute(parts[2 * half + 1], "dp", [(i, i ^ bit) for i in range(dp)]))
+        if stage == 0:
+            received[0], beside = lax.optimization_barrier((received[0], beside))
         for half in range(2):
             members[half] = split(members[half], orders[half][stage:])[0]
         if stage == bits - 1:
@@ -391,12 +401,12 @@
             to = lax.rem(chip + k, chips)
             outs[k][...] = total[pl.ds(pl.multiple_of(to * share, 16), share), :]
 
-    dealt = pl.pallas_call(
+    dealt = local_kernel(
         deal,
-        out_shape=tuple(sds((share, 256), BF) for _ in range(chips)),
-        scratch_shapes=[pltpu.VMEM((share * chips, 256), BF)],
-        compiler_params=pltpu.CompilerParams(vmem_limit_bytes=VMEM_LIMIT),
-    )(parts[0], received[0], parts[2], received[1])
+        tuple(sds((share, 256), BF) for _ in range(chips)),
+        *(parts[0], received[0], parts[2], received[1]),
+        scratch=[pltpu.VMEM((share * chips, 256), BF)],
+    )
     arrived = [lax.ppermute(dealt[k], "tile", shifts[k]) for k in range(1, chips)]
 
     def gather(*refs):
@@ -430,7 +440,10 @@
             one[...] = theirs_ref[0:rows, :].astype(F32)
             two[...] = mine_ref[0:rows, :].astype(F32)
 
-    return local_kernel(out, (sds((rows, 256), F32), sds((rows, 256), F32)), whole, theirs)
+    one, two = local_kernel(
+        out, (sds((rows, 256), F32), sds((rows, 256), F32)), whole, theirs, hbm_out=(0, 1)
+    )
+    return one, two, beside
 
 
 def body(features, fpn_weight, mask_w1, mask_w2, owner, row_off, col_off, cotangent):
@@ -442,8 +455,7 @@
     side = cotangent.shape[2]
     swap = [(i, i ^ 1) for i in range(tiles)]
 
-    place = jnp.stack([owner[0, :, 0] * height + row_off[0] + 1, col_off[0]], axis=1)
-    packed = pack(cotangent[0], place)
+    packed = pack(cotangent[0], height, (owner, row_off, col_off))
 
     tile = features.reshape(height * width, channels)
     edge = jnp.where(core == 1, tile[(height - 1) * width :], tile[:width])
@@ -459,25 +471,42 @@
 
     up = [(i, i + 2) for i in range(tiles - 2)]
     down = [(i + 2, i) for i in range(tiles - 2)]
-    blocks = [packed]
-    rising, falling = packed, packed
-    for _ in range(chips - 1):
-        rising = lax.ppermute(rising, "tile", up)
-        falling = lax.ppermute(falling, "tile", down)
-        blocks += [rising, falling]
-
     flat = lambda w: w.reshape(9 * channels, channels)
-    weights = [flat(fpn_weight), flat(mask_w1), flat(mask_w2)]
-    keep, send, gp_own, gp_other = main_call(
-        side, height, width, True, True, [tile, other, rim_a, rim_b], weights, blocks
-    )
+    wf, w1, w2 = flat(fpn_weight), flat(mask_w1), flat(mask_w2)
+    blocks = [lax.ppermute(packed, "tile", up), lax.ppermute(packed, "tile", down)]
+    start = main_call(
+        side, height, width, True, False, [tile, other, rim_a, rim_b], [wf, w1, w2], []
+    )
+    kept, sums = list(start[:3]), list(start[3:])
+    for step in range(1, chips):
+        last = step == chips - 1
+        held = blocks
+        if not last:
+            held[0], held[1], kept[0] = lax.optimization_barrier((held[0], held[1], kept[0]))
+            blocks = [lax.ppermute(held[0], "tile", up), lax.ppermute(held[1], "tile", down)]
+        got = main_call(
+            side,
+            height,
+            width,
+            False,
+            last,
+            [*kept, *sums],
+            [w1, w2],
+            ([packed] if step == 1 else []) + held,
+        )
+        sums, ends = list(got[:3]), got[3:]
+        if not last:
+            kept[0], sums[0] = lax.optimization_barrier((kept[0], sums[0]))
+    keep, send, gp_own, gp_other = ends
     gp_got = lax.ppermute(gp_other, "tile", swap)
-    grad_one, grad_two = reduce_weights(keep, send, swap, dp, chips)
 
     def join(a, b, out):
         out[...] = (a[...] + b[...].astype(F32)).astype(BF)
 
-    grad_pyramid = local_kernel(join, sds((height * width, channels), BF), gp_own, gp_got)
+    joined = local_kernel(
+        join, sds((height * width, channels), BF), gp_own, gp_got, hbm_out=(0,)
+    )
+    grad_one, grad_two, grad_pyramid = reduce_weights(keep, send, swap, dp, chips, joined)
     return grad_one, grad_two, grad_pyramid.reshape(1, height, width, channels)
 
 

time: 145 us -> 115 us (0.79); the launches traced: 147 us -> 114 us
  Pallas kernels: 50.2 us -> 24 us
  local copies, waits for them, and re-layouts: 8.63 us -> 5.65 us
  waiting for transfers between devices: 45.3 us -> 43.6 us
    pallas_call x9 -> x12, Pallas kernels: 50.2 us -> 24 us  [run(): pl.pallas_call(kernel, out_shape=tuple((s if i in hbm_out else pltpu.VMEM...]
    ppermute x4, starting transfers between devices: 12 us -> 6.63 us  [reduce_weights(): lax.ppermute(parts[2 * half + 1], 'dp', [(i, i ^ bit) for i in range(dp)])]
    ppermute x1, starting transfers between devices: 0.01 us -> 4.68 us  [reduce_weights(): got = lax.ppermute(send, 'tile', core_swap)]
    ppermute x6, waiting for transfers between devices: 16.4 us -> 12.8 us  [the longest x2 10 us: body(): lax.ppermute(held[1], 'tile', down)]
    ppermute x1, waiting for transfers between devices: 3.84 us -> 5.98 us  [body(): lax.ppermute(edge, 'tile', [(i, i + 2 if i % 2 else i - 2) for i in range...]
    ppermute x1, waiting for transfers between devices: 0.01 us -> 1.57 us  [reduce_weights(): theirs = lax.ppermute(whole, 'tile', core_swap)]
    unnamed x47 -> x14, local copies, waits for them, and re-layouts: 7.05 us -> 5.65 us
  transfers between devices with their start and end apart: 22 -> 22, of which waited for: 14 -> 16; matrix products, arithmetic and copies ran while one was open for 0% -> 2% of each run, Pallas kernels for 5% -> 16%
where the time goes in v2:
time: 115 us; the launch traced here: 114 us
  waiting for transfers between devices  43.6 us (38%)
  starting transfers between devices  39.4 us (34%)
  Pallas kernels  24 us (21%)
  local copies, waits for them, and re-layouts  5.65 us (5%)
    pallas_call x12, Pallas kernels, run(): pl.pallas_call(kernel, out_shape=tuple((s if i in hbm_out else pltpu.VMEM...  24 us
    ppermute x4, waiting for transfers between devices, reduce_weights(): lax.ppermute(parts[2 * half + 1], 'dp', [(i, i ^ bit) for i in range(dp)])  11 us
    ppermute x2, waiting for transfers between devices, body(): lax.ppermute(held[1], 'tile', down)  10 us
    ppermute x2, starting transfers between devices, body(): lax.ppermute(held[0], 'tile', up)  9.24 us
    ppermute x4, starting transfers between devices, reduce_weights(): lax.ppermute(parts[2 * half + 1], 'dp', [(i, i ^ bit) for i in range(dp)])  6.63 us
    ppermute x3, waiting for transfers between devices, reduce_weights(): lax.ppermute(mine, 'tile', shifts[k])  6.15 us
    ppermute x1, waiting for transfers between devices, body(): lax.ppermute(edge, 'tile', [(i, i + 2 if i % 2 else i - 2) for i in range...  5.98 us
    unnamed x14, local copies, waits for them, and re-layouts  5.65 us
  transfers between devices with their start and end apart: 22, of which 16 were waited for; matrix products, arithmetic and copies ran while one was open for 2% of the time, Pallas kernels for 16%

profile of v2, /device:TPU:0, one launch (start us, length us, event | category | flops | bytes accessed | tf_op | source)
XLA Modules:
  0.0 114.4 jit_solution(17793322168552559628)
XLA Ops:
  6.3 5.3 %collective-permute-start = (bf16[4,208,256]{2,1,0:T(8,128)(2,1)S(1)}, bf16[4,208,256]{2,1,0:T(8,128)(2,1)S(1)}, u32[]{:S(2)}, u32[]{:S(2)}) collective-permute-start(bf16[4,208,256]{2,1,0:T(8,128)(2,1)S(1)} %shard_map.103.refs_8_), channel_id=1, source_target_pairs={{0,2},{1,3},{2,4},{3,5},{4,6},{5,7},{8,10},{9,11},{10,12},{11,13},... | collective-permute-start | bytes 1277960 | tf_op jit(solution)/shard_map/ppermute | solution.py:476
  14.3 6.0 %collective-permute-done.4.refs_3_ = bf16[64,256]{1,0:T(8,128)(2,1)S(1)} collective-permute-done((bf16[64,256]{1,0:T(8,128)(2,1)S(1)}, bf16[64,256]{1,0:T(8,128)(2,1)S(1)}, u32[]{:S(2)}, u32[]{:S(2)}) %collective-permute-start.4) | collective-permute-done | bytes 32800 | tf_op jit(solution)/shard_map/ppermute | solution.py:465
  22.8 5.5 %shard_map.104 = (f32[2064,256]{1,0:T(8,128)S(1)}, bf16[2304,256]{1,0:T(8,128)(2,1)S(1)}, bf16[2304,256]{1,0:T(8,128)(2,1)S(1)}, f32[256,2304]{1,0:T(8,128)S(1)}...) custom-call(bf16[1024,256]{1,0:T(8,128)(2,1)S(1)} %bitcast.21, bf16[1024,256]{1,0:T(8,128)(2,1)S(1)} %collective-permute-done.2.refs_1_, ...), custom_call_target="tpu_custom_call" | custom-call | tf_op jit(solution)/shard_map/pallas_call | solution.py:27
  28.3 5.9 %collective-permute-start.5 = (bf16[4,208,256]{2,1,0:T(8,128)(2,1)S(1)}, bf16[4,208,256]{2,1,0:T(8,128)(2,1)S(1)}, u32[]{:S(2)}, u32[]{:S(2)}) collective-permute-start(bf16[4,208,256]{2,1,0:T(8,128)(2,1)S(1)} %collective-permute-done.refs_9_), channel_id=1, source_target_pairs={{0,2},{1,3},{2,4},{3,5},{4,6},{5,7},{8,10},{9,11},{10,12},{11,13},... | collective-permute-start | bytes 1277960 | tf_op jit(solution)/shard_map/ppermute | solution.py:486
  35.6 7.2 %shard_map.105 = (f32[256,2304]{1,0:T(8,128)S(1)}, f32[256,2304]{1,0:T(8,128)S(1)}, f32[2064,256]{1,0:T(8,128)S(1)}) custom-call(f32[2064,256]{1,0:T(8,128)S(1)} %get-tuple-element.63.refs_0_, bf16[2304,256]{1,0:T(8,128)(2,1)S(1)} %get-tuple-element.49.refs_1_, ...), custom_call_target="tpu_custom_call", output_to_operand_aliasing={{0}: (3, {}), {1}: (4, {}), {2}: (5, {})} | custom-call | tf_op jit(solution)/shard_map/pallas_call | solution.py:27
  43.1 4.1 %collective-permute-done.6.refs_9_ = bf16[4,208,256]{2,1,0:T(8,128)(2,1)S(1)} collective-permute-done((bf16[4,208,256]{2,1,0:T(8,128)(2,1)S(1)}, bf16[4,208,256]{2,1,0:T(8,128)(2,1)S(1)}, u32[]{:S(2)}, u32[]{:S(2)}) %collective-permute-start.6) | collective-permute-done | bytes 426016 | tf_op jit(solution)/shard_map/ppermute | solution.py:486
  47.2 3.3 %collective-permute-start.7 = (bf16[4,208,256]{2,1,0:T(8,128)(2,1)S(1)}, bf16[4,208,256]{2,1,0:T(8,128)(2,1)S(1)}, u32[]{:S(2)}, u32[]{:S(2)}) collective-permute-start(bf16[4,208,256]{2,1,0:T(8,128)(2,1)S(1)} %collective-permute-done.5.refs_8_), channel_id=1, source_target_pairs={{0,2},{1,3},{2,4},{3,5},{4,6},{5,7},{8,10},{9,11},{10,12},{11,13},... | collective-permute-start | bytes 1277960 | tf_op jit(solution)/shard_map/ppermute | solution.py:486
  51.8 3.6 %shard_map.106 = (f32[256,2304]{1,0:T(8,128)S(1)}, f32[256,2304]{1,0:T(8,128)S(1)}, f32[2064,256]{1,0:T(8,128)S(1)}) custom-call(f32[2064,256]{1,0:T(8,128)S(1)} %get-tuple-element.63.refs_0_, bf16[2304,256]{1,0:T(8,128)(2,1)S(1)} %get-tuple-element.49.refs_1_, ...), custom_call_target="tpu_custom_call", output_to_operand_aliasing={{0}: (3, {}), {1}: (4, {}), {2}: (5, {})} | custom-call | tf_op jit(solution)/shard_map/pallas_call | solution.py:27
  55.5 2.5 %collective-permute-done.7.refs_8_ = bf16[4,208,256]{2,1,0:T(8,128)(2,1)S(1)} collective-permute-done((bf16[4,208,256]{2,1,0:T(8,128)(2,1)S(1)}, bf16[4,208,256]{2,1,0:T(8,128)(2,1)S(1)}, u32[]{:S(2)}, u32[]{:S(2)}) %collective-permute-start.7) | collective-permute-done | bytes 426016 | tf_op jit(solution)/shard_map/ppermute | solution.py:486
  57.9 5.9 %collective-permute-done.8.refs_9_ = bf16[4,208,256]{2,1,0:T(8,128)(2,1)S(1)} collective-permute-done((bf16[4,208,256]{2,1,0:T(8,128)(2,1)S(1)}, bf16[4,208,256]{2,1,0:T(8,128)(2,1)S(1)}, u32[]{:S(2)}, u32[]{:S(2)}) %collective-permute-start.8) | collective-permute-done | bytes 426016 | tf_op jit(solution)/shard_map/ppermute | solution.py:486
  63.8 4.5 %shard_map.107 = (f32[256,2304]{1,0:T(8,128)S(1)}, f32[256,2304]{1,0:T(8,128)S(1)}, f32[2064,256]{1,0:T(8,128)S(1)}, bf16[2304,256]{1,0:T(8,128)(2,1)S(1)}, bf16...) custom-call(f32[2064,256]{1,0:T(8,128)S(1)} %get-tuple-element.63.re, ...), custom_call_target="tpu_custom_call", output_to_operand_aliasing={{0}: (3, {}), {1}: (4, {}), {2}: (5, {})} | custom-call | tf_op jit(solution)/shard_map/pallas_call | solution.py:27
  68.3 4.7 %collective-permute-start.9 = (bf16[2304,256]{1,0:T(8,128)(2,1)S(1)}, bf16[2304,256]{1,0:T(8,128)(2,1)S(1)}, u32[]{:S(2)}, u32[]{:S(2)}) collective-permute-start(bf16[2304,256]{1,0:T(8,128)(2,1)S(1)} %get-tuple-element.68), channel_id=1, source_target_pairs={{0,1},{1,0},{2,3},{3,2},{4,5},{5,4},{6,7},{7,6},{8,9},{9,8},{10,11... | collective-permute-start | bytes 3538952 | tf_op jit(solution)/shard_map/ppermute | solution.py:337
  73.1 2.4 %collective-permute-done.9.got_ref = bf16[2304,256]{1,0:T(8,128)(2,1)S(1)} collective-permute-done((bf16[2304,256]{1,0:T(8,128)(2,1)S(1)}, bf16[2304,256]{1,0:T(8,128)(2,1)S(1)}, u32[]{:S(2)}, u32[]{:S(2)}) %collective-permute-start.9) | collective-permute-done | bytes 1179680 | tf_op jit(solution)/shard_map/ppermute | solution.py:337
  75.7 3.0 %collective-permute-start.10 = (bf16[2,288,256]{2,1,0:T(8,128)(2,1)S(1)}, bf16[2,288,256]{2,1,0:T(8,128)(2,1)S(1)}, u32[]{:S(2)}, u32[]{:S(2)}) collective-permute-start(bf16[2,288,256]{2,1,0:T(8,128)(2,1)S(1)} %get-tuple-element.70), channel_id=1, source_target_pairs={{0,8},{8,0},{16,24},{24,16},{1,9},{9,1},{17,25},{25,17},{2,10},{10... | collective-permute-start | bytes 884744 | tf_op jit(solution)/shard_map/ppermute | solution.py:364
  81.1 4.9 %collective-permute-done.10.pr = bf16[2,288,256]{2,1,0:T(8,128)(2,1)S(1)} collective-permute-done((bf16[2,288,256]{2,1,0:T(8,128)(2,1)S(1)}, bf16[2,288,256]{2,1,0:T(8,128)(2,1)S(1)}, u32[]{:S(2)}, u32[]{:S(2)}) %collective-permute-start.10) | collective-permute-done | bytes 294944 | tf_op jit(solution)/shard_map/ppermute | solution.py:364
  87.6 1.6 %collective-permute-start.13 = (bf16[1,288,256]{2,1,0:T(8,128)(2,1)S(1)}, bf16[1,288,256]{2,1,0:T(8,128)(2,1)S(1)}, u32[]{:S(2)}, u32[]{:S(2)}) collective-permute-start(bf16[1,288,256]{2,1,0:T(8,128)(2,1)S(1)} %get-tuple-element.77), channel_id=1, source_target_pairs={{0,16},{8,24},{16,0},{24,8},{1,17},{9,25},{17,1},{25,9},{2,18},{10... | collective-permute-start | bytes 442376 | tf_op jit(solution)/shard_map/ppermute | solution.py:364
  89.7 3.1 %collective-permute-done.13.pr = bf16[1,288,256]{2,1,0:T(8,128)(2,1)S(1)} collective-permute-done((bf16[1,288,256]{2,1,0:T(8,128)(2,1)S(1)}, bf16[1,288,256]{2,1,0:T(8,128)(2,1)S(1)}, u32[]{:S(2)}, u32[]{:S(2)}) %collective-permute-start.13) | collective-permute-done | bytes 147488 | tf_op jit(solution)/shard_map/ppermute | solution.py:364
  95.5 2.8 %collective-permute-start.17 = (bf16[144,256]{1,0:T(8,128)(2,1)S(1)}, bf16[144,256]{1,0:T(8,128)(2,1)S(1)}, u32[]{:S(2)}, u32[]{:S(2)}) collective-permute-start(bf16[144,256]{1,0:T(8,128)(2,1)S(1)} %get-tuple-element.83), channel_id=1, source_target_pairs={{0,6},{1,7},{2,0},{3,1},{4,2},{5,3},{6,4},{7,5},{8,14},{9,15},{10,... | collective-permute-start | bytes 221192 | tf_op jit(solution)/shard_map/ppermute | solution.py:410
  98.4 2.4 %collective-permute-done.15.refs_1_ = bf16[144,256]{1,0:T(8,128)(2,1)S(1)} collective-permute-done((bf16[144,256]{1,0:T(8,128)(2,1)S(1)}, bf16[144,256]{1,0:T(8,128)(2,1)S(1)}, u32[]{:S(2)}, u32[]{:S(2)}) %collective-permute-start.15) | collective-permute-done | bytes 73760 | tf_op jit(solution)/shard_map/ppermute | solution.py:410
  102.2 2.4 %collective-permute-start.20 = (bf16[144,256]{1,0:T(8,128)(2,1)S(1)}, bf16[144,256]{1,0:T(8,128)(2,1)S(1)}, u32[]{:S(2)}, u32[]{:S(2)}) collective-permute-start(bf16[144,256]{1,0:T(8,128)(2,1)S(1)} %shard_map.112.refs_0_), channel_id=1, source_target_pairs={{0,6},{1,7},{2,0},{3,1},{4,2},{5,3},{6,4},{7,5},{8,14},{9,15},{10,... | collective-permute-start | bytes 221192 | tf_op jit(solution)/shard_map/ppermute | solution.py:419
  105.5 1.9 %collective-permute-done.20.refs_3_ = bf16[144,256]{1,0:T(8,128)(2,1)S(1)} collective-permute-done((bf16[144,256]{1,0:T(8,128)(2,1)S(1)}, bf16[144,256]{1,0:T(8,128)(2,1)S(1)}, u32[]{:S(2)}, u32[]{:S(2)}) %collective-permute-start.20) | collective-permute-done | bytes 73760 | tf_op jit(solution)/shard_map/ppermute | solution.py:419
  107.4 2.5 %collective-permute-done.19.refs_2_ = bf16[144,256]{1,0:T(8,128)(2,1)S(1)} collective-permute-done((bf16[144,256]{1,0:T(8,128)(2,1)S(1)}, bf16[144,256]{1,0:T(8,128)(2,1)S(1)}, u32[]{:S(2)}, u32[]{:S(2)}) %collective-permute-start.19) | collective-permute-done | bytes 73760 | tf_op jit(solution)/shard_map/ppermute | solution.py:419
  109.9 1.7 %collective-permute-done.18.refs_1_ = bf16[144,256]{1,0:T(8,128)(2,1)S(1)} collective-permute-done((bf16[144,256]{1,0:T(8,128)(2,1)S(1)}, bf16[144,256]{1,0:T(8,128)(2,1)S(1)}, u32[]{:S(2)}, u32[]{:S(2)}) %collective-permute-start.18) | collective-permute-done | bytes 73760 | tf_op jit(solution)/shard_map/ppermute | solution.py:419
  111.7 1.6 %collective-permute-done.21.theirs_ref = bf16[576,256]{1,0:T(8,128)(2,1)S(1)} collective-permute-done((bf16[576,256]{1,0:T(8,128)(2,1)S(1)}, bf16[576,256]{1,0:T(8,128)(2,1)S(1)}, u32[]{:S(2)}, u32[]{:S(2)}) %collective-permute-start.21) | collective-permute-done | bytes 294944 | tf_op jit(solution)/shard_map/ppermute | solution.py:428
  (47 shorter events, 24.8 us)
Async XLA Ops:
  0.6 19.6 %copy-start.3 = (bf16[1,16,64,256]{3,2,1,0:T(8,128)(2,1)S(1)}, bf16[1,16,64,256]{3,2,1,0:T(8,128)(2,1)}, u32[]{:S(2)}) copy-start(bf16[1,16,64,256]{3,2,1,0:T(8,128)(2,1)} %param.8) | copy-start | bytes 1572868
  0.6 19.6 %copy-start = (bf16[9,256,256]{2,1,0:T(8,128)(2,1)S(1)}, bf16[9,256,256]{2,1,0:T(8,128)(2,1)}, u32[]{:S(2)}) copy-start(bf16[9,256,256]{2,1,0:T(8,128)(2,1)} %param.10) | copy-start | bytes 3538948
  0.7 19.6 %collective-permute-start.2 = (bf16[1024,256]{1,0:T(8,128)(2,1)}, bf16[1024,256]{1,0:T(8,128)(2,1)S(1)}, u32[]{:S(2)}, u32[]{:S(2)}) collective-permute-start(bf16[1024,256]{1,0:T(8,128)(2,1)} %bitcast.20), channel_id=1, source_target_pairs={{0,1},{1,0},{2,3},{3,2},{4,5},{5,4},{6,7},{7,6},{8,9},{9,8},{10,11... | collective-permute-start | bytes 1572872 | tf_op jit(solution)/shard_map/ppermute | solution.py:470
  5.0 23.4 %collective-permute-start.1 = (bf16[4,208,256]{2,1,0:T(8,128)(2,1)S(1)}, bf16[4,208,256]{2,1,0:T(8,128)(2,1)S(1)}, u32[]{:S(2)}, u32[]{:S(2)}) collective-permute-start(bf16[4,208,256]{2,1,0:T(8,128)(2,1)S(1)} %shard_map.103.refs_8_), channel_id=1, source_target_pairs={{2,0},{3,1},{4,2},{5,3},{6,4},{7,5},{10,8},{11,9},{12,10},{13,11},... | collective-permute-start | bytes 1277960 | tf_op jit(solution)/shard_map/ppermute | solution.py:476
  6.3 22.1 %collective-permute-start = (bf16[4,208,256]{2,1,0:T(8,128)(2,1)S(1)}, bf16[4,208,256]{2,1,0:T(8,128)(2,1)S(1)}, u32[]{:S(2)}, u32[]{:S(2)}) collective-permute-start(bf16[4,208,256]{2,1,0:T(8,128)(2,1)S(1)} %shard_map.103.refs_8_), channel_id=1, source_target_pairs={{0,2},{1,3},{2,4},{3,5},{4,6},{5,7},{8,10},{9,11},{10,12},{11,13},... | collective-permute-start | bytes 1277960 | tf_op jit(solution)/shard_map/ppermute | solution.py:476
  12.3 7.9 %collective-permute-start.4 = (bf16[64,256]{1,0:T(8,128)(2,1)S(1)}, bf16[64,256]{1,0:T(8,128)(2,1)S(1)}, u32[]{:S(2)}, u32[]{:S(2)}) collective-permute-start(bf16[64,256]{1,0:T(8,128)(2,1)S(1)} %select_bitcast_fusion), channel_id=1, source_target_pairs={{1,3},{2,0},{3,5},{4,2},{5,7},{6,4},{9,11},{10,8},{11,13},{12,10},... | collective-permute-start | bytes 98312 | tf_op jit(solution)/shard_map/ppermute | solution.py:465
  13.6 6.7 %collective-permute-start.3 = (bf16[64,256]{1,0:T(8,128)(2,1)S(1)}, bf16[64,256]{1,0:T(8,128)(2,1)S(1)}, u32[]{:S(2)}, u32[]{:S(2)}) collective-permute-start(bf16[64,256]{1,0:T(8,128)(2,1)S(1)} %select_bitcast_fusion), channel_id=1, source_target_pairs={{1,2},{2,1},{3,4},{4,3},{5,6},{6,5},{9,10},{10,9},{11,12},{12,11},... | collective-permute-start | bytes 98312 | tf_op jit(solution)/shard_map/ppermute | solution.py:462
  28.3 14.7 %collective-permute-start.5 = (bf16[4,208,256]{2,1,0:T(8,128)(2,1)S(1)}, bf16[4,208,256]{2,1,0:T(8,128)(2,1)S(1)}, u32[]{:S(2)}, u32[]{:S(2)}) collective-permute-start(bf16[4,208,256]{2,1,0:T(8,128)(2,1)S(1)} %collective-permute-done.refs_9_), channel_id=1, source_target_pairs={{0,2},{1,3},{2,4},{3,5},{4,6},{5,7},{8,10},{9,11},{10,12},{11,13},... | collective-permute-start | bytes 1277960 | tf_op jit(solution)/shard_map/ppermute | solution.py:486
  34.3 12.9 %collective-permute-start.6 = (bf16[4,208,256]{2,1,0:T(8,128)(2,1)S(1)}, bf16[4,208,256]{2,1,0:T(8,128)(2,1)S(1)}, u32[]{:S(2)}, u32[]{:S(2)}) collective-permute-start(bf16[4,208,256]{2,1,0:T(8,128)(2,1)S(1)} %collective-permute-done.1.refs_10_), channel_id=1, source_target_pairs={{2,0},{3,1},{4,2},{5,3},{6,4},{7,5},{10,8},{11,9},{12,10},{13,11},... | collective-permute-start | bytes 1277960 | tf_op jit(solution)/shard_map/ppermute | solution.py:486
  47.2 10.7 %collective-permute-start.7 = (bf16[4,208,256]{2,1,0:T(8,128)(2,1)S(1)}, bf16[4,208,256]{2,1,0:T(8,128)(2,1)S(1)}, u32[]{:S(2)}, u32[]{:S(2)}) collective-permute-start(bf16[4,208,256]{2,1,0:T(8,128)(2,1)S(1)} %collective-permute-done.5.refs_8_), channel_id=1, source_target_pairs={{0,2},{1,3},{2,4},{3,5},{4,6},{5,7},{8,10},{9,11},{10,12},{11,13},... | collective-permute-start | bytes 1277960 | tf_op jit(solution)/shard_map/ppermute | solution.py:486
  50.5 13.3 %collective-permute-start.8 = (bf16[4,208,256]{2,1,0:T(8,128)(2,1)S(1)}, bf16[4,208,256]{2,1,0:T(8,128)(2,1)S(1)}, u32[]{:S(2)}, u32[]{:S(2)}) collective-permute-start(bf16[4,208,256]{2,1,0:T(8,128)(2,1)S(1)} %collective-permute-done.6.refs_9_), channel_id=1, source_target_pairs={{2,0},{3,1},{4,2},{5,3},{6,4},{7,5},{10,8},{11,9},{12,10},{13,11},... | collective-permute-start | bytes 1277960 | tf_op jit(solution)/shard_map/ppermute | solution.py:486
  68.3 7.2 %collective-permute-start.9 = (bf16[2304,256]{1,0:T(8,128)(2,1)S(1)}, bf16[2304,256]{1,0:T(8,128)(2,1)S(1)}, u32[]{:S(2)}, u32[]{:S(2)}) collective-permute-start(bf16[2304,256]{1,0:T(8,128)(2,1)S(1)} %get-tuple-element.68), channel_id=1, source_target_pairs={{0,1},{1,0},{2,3},{3,2},{4,5},{5,4},{6,7},{7,6},{8,9},{9,8},{10,11... | collective-permute-start | bytes 3538952 | tf_op jit(solution)/shard_map/ppermute | solution.py:337
  73.0 7.3 %collective-permute-start.11 = (bf16[1024,256]{1,0:T(8,128)(2,1)S(1)}, bf16[1024,256]{1,0:T(8,128)(2,1)S(1)}, u32[]{:S(2)}, u32[]{:S(2)}) collective-permute-start(bf16[1024,256]{1,0:T(8,128)(2,1)S(1)} %get-tuple-element.72), channel_id=1, source_target_pairs={{0,1},{1,0},{2,3},{3,2},{4,5},{5,4},{6,7},{7,6},{8,9},{9,8},{10,11... | collective-permute-start | bytes 1572872 | tf_op jit(solution)/shard_map/ppermute | solution.py:501
  75.7 10.3 %collective-permute-start.10 = (bf16[2,288,256]{2,1,0:T(8,128)(2,1)S(1)}, bf16[2,288,256]{2,1,0:T(8,128)(2,1)S(1)}, u32[]{:S(2)}, u32[]{:S(2)}) collective-permute-start(bf16[2,288,256]{2,1,0:T(8,128)(2,1)S(1)} %get-tuple-element.70), channel_id=1, source_target_pairs={{0,8},{8,0},{16,24},{24,16},{1,9},{9,1},{17,25},{25,17},{2,10},{10... | collective-permute-start | bytes 884744 | tf_op jit(solution)/shard_map/ppermute | solution.py:364
  78.7 8.8 %collective-permute-start.12 = (bf16[2,288,256]{2,1,0:T(8,128)(2,1)S(1)}, bf16[2,288,256]{2,1,0:T(8,128)(2,1)S(1)}, u32[]{:S(2)}, u32[]{:S(2)}) collective-permute-start(bf16[2,288,256]{2,1,0:T(8,128)(2,1)S(1)} %get-tuple-element.75), channel_id=1, source_target_pairs={{0,16},{8,24},{16,0},{24,8},{1,17},{9,25},{17,1},{25,9},{2,18},{10... | collective-permute-start | bytes 884744 | tf_op jit(solution)/shard_map/ppermute | solution.py:364
  87.6 5.2 %collective-permute-start.13 = (bf16[1,288,256]{2,1,0:T(8,128)(2,1)S(1)}, bf16[1,288,256]{2,1,0:T(8,128)(2,1)S(1)}, u32[]{:S(2)}, u32[]{:S(2)}) collective-permute-start(bf16[1,288,256]{2,1,0:T(8,128)(2,1)S(1)} %get-tuple-element.77), channel_id=1, source_target_pairs={{0,16},{8,24},{16,0},{24,8},{1,17},{9,25},{17,1},{25,9},{2,18},{10... | collective-permute-start | bytes 442376 | tf_op jit(solution)/shard_map/ppermute | solution.py:364
  89.2 5.1 %collective-permute-start.14 = (bf16[1,288,256]{2,1,0:T(8,128)(2,1)S(1)}, bf16[1,288,256]{2,1,0:T(8,128)(2,1)S(1)}, u32[]{:S(2)}, u32[]{:S(2)}) collective-permute-start(bf16[1,288,256]{2,1,0:T(8,128)(2,1)S(1)} %get-tuple-element.79), channel_id=1, source_target_pairs={{0,8},{8,0},{16,24},{24,16},{1,9},{9,1},{17,25},{25,17},{2,10},{10... | collective-permute-start | bytes 442376 | tf_op jit(solution)/shard_map/ppermute | solution.py:364
  94.5 6.3 %collective-permute-start.15 = (bf16[144,256]{1,0:T(8,128)(2,1)S(1)}, bf16[144,256]{1,0:T(8,128)(2,1)S(1)}, u32[]{:S(2)}, u32[]{:S(2)}) collective-permute-start(bf16[144,256]{1,0:T(8,128)(2,1)S(1)} %get-tuple-element.81), channel_id=1, source_target_pairs={{0,2},{1,3},{2,4},{3,5},{4,6},{5,7},{6,0},{7,1},{8,10},{9,11},{10,... | collective-permute-start | bytes 221192 | tf_op jit(solution)/shard_map/ppermute | solution.py:410
  94.5 6.2 %collective-permute-start.16 = (bf16[144,256]{1,0:T(8,128)(2,1)S(1)}, bf16[144,256]{1,0:T(8,128)(2,1)S(1)}, u32[]{:S(2)}, u32[]{:S(2)}) collective-permute-start(bf16[144,256]{1,0:T(8,128)(2,1)S(1)} %get-tuple-element.82), channel_id=1, source_target_pairs={{0,4},{1,5},{2,6},{3,7},{4,0},{5,1},{6,2},{7,3},{8,12},{9,13},{10,... | collective-permute-start | bytes 221192 | tf_op jit(solution)/shard_map/ppermute | solution.py:410
  95.5 6.6 %collective-permute-start.17 = (bf16[144,256]{1,0:T(8,128)(2,1)S(1)}, bf16[144,256]{1,0:T(8,128)(2,1)S(1)}, u32[]{:S(2)}, u32[]{:S(2)}) collective-permute-start(bf16[144,256]{1,0:T(8,128)(2,1)S(1)} %get-tuple-element.83), channel_id=1, source_target_pairs={{0,6},{1,7},{2,0},{3,1},{4,2},{5,3},{6,4},{7,5},{8,14},{9,15},{10,... | collective-permute-start | bytes 221192 | tf_op jit(solution)/shard_map/ppermute | solution.py:410
  102.2 5.2 %collective-permute-start.20 = (bf16[144,256]{1,0:T(8,128)(2,1)S(1)}, bf16[144,256]{1,0:T(8,128)(2,1)S(1)}, u32[]{:S(2)}, u32[]{:S(2)}) collective-permute-start(bf16[144,256]{1,0:T(8,128)(2,1)S(1)} %shard_map.112.refs_0_), channel_id=1, source_target_pairs={{0,6},{1,7},{2,0},{3,1},{4,2},{5,3},{6,4},{7,5},{8,14},{9,15},{10,... | collective-permute-start | bytes 221192 | tf_op jit(solution)/shard_map/ppermute | solution.py:419
  104.6 5.3 %collective-permute-start.19 = (bf16[144,256]{1,0:T(8,128)(2,1)S(1)}, bf16[144,256]{1,0:T(8,128)(2,1)S(1)}, u32[]{:S(2)}, u32[]{:S(2)}) collective-permute-start(bf16[144,256]{1,0:T(8,128)(2,1)S(1)} %shard_map.112.refs_0_), channel_id=1, source_target_pairs={{0,4},{1,5},{2,6},{3,7},{4,0},{5,1},{6,2},{7,3},{8,12},{9,13},{10,... | collective-permute-start | bytes 221192 | tf_op jit(solution)/shard_map/ppermute | solution.py:419
  105.5 6.2 %collective-permute-start.18 = (bf16[144,256]{1,0:T(8,128)(2,1)S(1)}, bf16[144,256]{1,0:T(8,128)(2,1)S(1)}, u32[]{:S(2)}, u32[]{:S(2)}) collective-permute-start(bf16[144,256]{1,0:T(8,128)(2,1)S(1)} %shard_map.112.refs_0_), channel_id=1, source_target_pairs={{0,2},{1,3},{2,4},{3,5},{4,6},{5,7},{6,0},{7,1},{8,10},{9,11},{10,... | collective-permute-start | bytes 221192 | tf_op jit(solution)/shard_map/ppermute | solution.py:419
  111.6 1.6 %collective-permute-start.21 = (bf16[576,256]{1,0:T(8,128)(2,1)S(1)}, bf16[576,256]{1,0:T(8,128)(2,1)S(1)}, u32[]{:S(2)}, u32[]{:S(2)}) collective-permute-start(bf16[576,256]{1,0:T(8,128)(2,1)S(1)} %shard_map.113.mine_ref), channel_id=1, source_target_pairs={{0,1},{1,0},{2,3},{3,2},{4,5},{5,4},{6,7},{7,6},{8,9},{9,8},{10,11... | collective-permute-start | bytes 884744 | tf_op jit(solution)/shard_map/ppermute | solution.py:428
  (4 other events, 3.9 us)

commit v3 on v2

--- a/solution.py
+++ b/solution.py
@@ -19,9 +19,9 @@
     return (n + m - 1) // m * m
 
 
-def run(kernel, outs, args, scratch=(), aliases=None, smem=(), hbm_out=()):
+def run(kernel, outs, args, scratch=(), aliases=None, hbm=(), hbm_out=()):
     args = [
-        x if i in smem else pltpu.with_memory_space_constraint(x, pltpu.VMEM)
+        pltpu.with_memory_space_constraint(x, pltpu.HBM if i in hbm else pltpu.VMEM)
         for i, x in enumerate(args)
     ]
     return pl.pallas_call(
@@ -30,7 +30,7 @@
             s if i in hbm_out else pltpu.VMEM(s.shape, s.dtype) for i, s in enumerate(outs)
         ),
         in_specs=[
-            pl.BlockSpec(memory_space=pltpu.SMEM if i in smem else pltpu.VMEM)
+            pl.BlockSpec(memory_space=pltpu.HBM if i in hbm else pltpu.VMEM)
             for i in range(len(args))
         ],
         out_specs=tuple(pl.BlockSpec(memory_space=pltpu.VMEM) for _ in outs),
@@ -44,33 +44,67 @@
     return jax.ShapeDtypeStruct(shape, dtype)
 
 
-def pack_kernel(side, height, cot_ref, owner_ref, row_ref, col_ref, out_ref, wide):
-    regions = cot_ref.shape[0]
+def edge_of(tile, height, width):
+    def kernel(tile, edge, sem):
+        core = lax.rem(lax.axis_index("tile"), 2)
+        line = pl.ds(pl.multiple_of(core * (height - 1) * width, width), width)
+        copy = pltpu.make_async_copy(tile.at[line, :], edge, sem)
+        copy.start()
+        copy.wait()
+
+    return local_kernel(
+        kernel, sds((width, 256), BF), tile, scratch=[pltpu.SemaphoreType.DMA], hbm=(0,)
+    )
+
+
+def pack_kernel(side, height, cot, owner, row, col, packed, low, high, wide, places, sems):
+    regions = cot.shape[2]
+    copies = [
+        pltpu.make_async_copy(source, places.at[n], sems.at[n])
+        for n, source in enumerate((owner, row, col))
+    ]
+    for copy in copies:
+        copy.start()
+    for i in range(side):
+        for j in range(side):
+            at = (i * side + j) * regions
+            cell = cot[i, j].astype(F32)
+            low[at : at + regions, :] = cell[:, 0:128]
+            high[at : at + regions, :] = cell[:, 128:256]
+    for copy in copies:
+        copy.wait()
     lanes = lax.broadcasted_iota(jnp.int32, (16, 256), 1)
     rows = lax.broadcasted_iota(jnp.int32, (16, 256), 0)
+    cells = side * side
     for r in range(regions):
-        for i in range(side):
-            wide[side * i : side * i + side, :] = cot_ref[r, i].astype(F32)
-        tail = wide[192:208, :]
-        spot = (owner_ref[0, r, 0] * height + row_ref[0, r] + 1).astype(F32)
-        column = col_ref[0, r].astype(F32)
+        wide[0:cells, 0:128] = low[pl.ds(r, cells, stride=regions), :]
+        wide[0:cells, 128:256] = high[pl.ds(r, cells, stride=regions), :]
+        spot = (places[0, 0, r] * height + places[1, 0, r] + 1).astype(F32)
+        column = places[2, 0, r].astype(F32)
         note = jnp.where(lanes == 0, spot, jnp.where(lanes == 1, column, 0.0))
-        wide[192:208, :] = jnp.where(rows < 4, tail, note)
-        out_ref[r] = wide[...].astype(BF)
+        wide[192:208, :] = jnp.where(rows < cells - 192, wide[192:208, :], note)
+        packed[r] = wide[...].astype(BF)
 
 
 def pack(cotangent, height, place):
-    regions, side = cotangent.shape[0], cotangent.shape[1]
-    return run(
+    side, regions = cotangent.shape[0], cotangent.shape[2]
+    return local_kernel(
         functools.partial(pack_kernel, side, height),
-        (sds((regions, SLOT, 256), BF),),
-        (cotangent, *place),
-        scratch=[pltpu.VMEM((SLOT, 256), F32)],
-        smem=(1, 2, 3),
-    )[0]
-
-
-def pyramid_part(height, width, own, other, rim_a, rim_b, wf, pyr, xp):
+        sds((regions, SLOT, 256), BF),
+        cotangent,
+        *place,
+        scratch=[
+            pltpu.VMEM((side * side * regions, 128), F32),
+            pltpu.VMEM((side * side * regions, 128), F32),
+            pltpu.VMEM((SLOT, 256), F32),
+            pltpu.SMEM((3, 1, regions), jnp.int32),
+            pltpu.SemaphoreType.DMA((3,)),
+        ],
+        hbm=(1, 2, 3),
+    )
+
+
+def pyramid_part(height, width, own, other, rim_a, rim_b, wf, pyr, xp, fetched):
     core = lax.rem(lax.axis_index("tile"), 2)
     cells = height * width
     col = lax.broadcasted_iota(jnp.int32, (width, 256), 0)
@@ -93,6 +127,8 @@
     fill(other, height, width + (1 - core) * cells)
     fill(rim_a, 1, core * bottom)
     fill(rim_b, 1, (1 - core) * bottom)
+
+    fetched.wait()
 
     def conv(t, carry):
         at = t * 256
@@ -257,11 +293,7 @@
     n = len(blocks)
     big = 2 * height * width + 16
     cells = (2 * side + 1) * PITCH
-    kept = (
-        sds((big, 256), F32),
-        sds((2304, 256), BF),
-        sds((2304, 256), BF),
-    )
+    kept = (sds((big, 256), F32),) + (sds((2304, 256), BF),) * 4
     sums = (sds((256, 2304), F32), sds((256, 2304), F32), sds((big, 256), F32))
     ends = (
         sds((2304, 256), BF),
@@ -279,7 +311,14 @@
         pltpu.VMEM((cells, 256), F32),
         pltpu.SMEM((3, 128), jnp.int32),
     ]
-    extra = [pltpu.VMEM(((2 * height + 2) * width, 768), BF)] if first else []
+    extra = []
+    if first:
+        extra = [
+            pltpu.VMEM(((2 * height + 2) * width, 768), BF),
+            pltpu.VMEM((2304, 256), BF),
+            pltpu.VMEM((height * width, 256), BF),
+            pltpu.SemaphoreType.DMA((4,)),
+        ]
 
     def kernel(*refs):
         refs = list(refs)
@@ -295,27 +334,41 @@
         out_refs = take(len(outs))
         scratch_refs = take(len(scratch))
         if first:
-            pyr, wb1, wb2 = out_refs[:3]
-            acc1, acc2, gp = out_refs[3:6]
-            wf, w1, w2 = weight_refs
-            pyramid_part(height, width, *state_refs, wf, pyr, refs[0])
-            flip_part(w1, wb1)
-            flip_part(w2, wb2)
+            pyr, wb1, wb2, w1, w2 = out_refs[:5]
+            acc1, acc2, gp = out_refs[5:8]
+            xp, wf, own, sems = refs
+            copies = [
+                pltpu.make_async_copy(source, to, sems.at[k])
+                for k, (source, to) in enumerate(zip((state_refs[0], *weight_refs), (own, wf, w1, w2)))
+            ]
+            for copy in copies:
+                copy.start()
             for total in (acc1, acc2, gp):
                 total[...] = jnp.zeros(total.shape, F32)
+            copies[0].wait()
+            pyramid_part(height, width, own, *state_refs[1:], wf, pyr, xp, copies[1])
+            copies[2].wait()
+            flip_part(w1, wb1)
+            copies[3].wait()
+            flip_part(w2, wb2)
         else:
-            pyr, wb1, wb2 = state_refs[:3]
+            pyr, wb1, wb2, w1, w2 = state_refs[:5]
             acc1, acc2, gp = out_refs[:3]
-            w1, w2 = weight_refs
-        if n:
-            regions_part(
-                side, height, width, block_refs, pyr, w1, w2, wb1, wb2, acc1, acc2, gp, scratch_refs
-            )
+        regions_part(
+            side, height, width, block_refs, pyr, w1, w2, wb1, wb2, acc1, acc2, gp, scratch_refs
+        )
         if last:
             finish_part(height, width, acc1, acc2, gp, *out_refs[-4:])
 
-    aliases = {} if first else {3: 0, 4: 1, 5: 2}
-    return run(kernel, outs, [*state, *weights, *blocks], scratch=scratch + extra, aliases=aliases)
+    aliases = {} if first else {5: 0, 6: 1, 7: 2}
+    return run(
+        kernel,
+        outs,
+        [*state, *weights, *blocks],
+        scratch=scratch + extra,
+        aliases=aliases,
+        hbm=(0, *range(len(state), len(state) + len(weights))) if first else (),
+    )
 
 
 def local_kernel(fn, outs, *arrays, **more):
@@ -450,24 +503,22 @@
     tiles = lax.axis_size("tile")
     dp = lax.axis_size("dp")
     chips = tiles // 2
-    core = lax.rem(lax.axis_index("tile"), 2)
     height, width, channels = features.shape[1:]
     side = cotangent.shape[2]
     swap = [(i, i ^ 1) for i in range(tiles)]
 
-    packed = pack(cotangent[0], height, (owner, row_off, col_off))
-
     tile = features.reshape(height * width, channels)
-    edge = jnp.where(core == 1, tile[(height - 1) * width :], tile[:width])
+    regions = cotangent.shape[1]
+    place = [x.reshape(1, regions) for x in (owner, row_off, col_off)]
+    edge = edge_of(tile, height, width)
     rim_a = lax.ppermute(
         edge, "tile", [(i, i + 1 if i % 2 else i - 1) for i in range(1, tiles - 1)]
     )
-    rim_b = lax.ppermute(
-        edge,
-        "tile",
-        [(i, i + 2 if i % 2 else i - 2) for i in range(tiles) if 0 <= (i + 2 if i % 2 else i - 2) < tiles],
-    )
+    across = [(i, i + 2 if i % 2 else i - 2) for i in range(tiles)]
+    rim_b = lax.ppermute(edge, "tile", [(i, j) for i, j in across if 0 <= j < tiles])
     other = lax.ppermute(tile, "tile", swap)
+    packed = pack(cotangent[0].transpose(1, 2, 0, 3), height, place)
+    packed, rim_a, rim_b = lax.optimization_barrier((packed, rim_a, rim_b))
 
     up = [(i, i + 2) for i in range(tiles - 2)]
     down = [(i + 2, i) for i in range(tiles - 2)]
@@ -475,9 +526,9 @@
     wf, w1, w2 = flat(fpn_weight), flat(mask_w1), flat(mask_w2)
     blocks = [lax.ppermute(packed, "tile", up), lax.ppermute(packed, "tile", down)]
     start = main_call(
-        side, height, width, True, False, [tile, other, rim_a, rim_b], [wf, w1, w2], []
-    )
-    kept, sums = list(start[:3]), list(start[3:])
+        side, height, width, True, False, [tile, other, rim_a, rim_b], [wf, w1, w2], [packed]
+    )
+    kept, sums = list(start[:5]), list(start[5:])
     for step in range(1, chips):
         last = step == chips - 1
         held = blocks
@@ -491,8 +542,8 @@
             False,
             last,
             [*kept, *sums],
-            [w1, w2],
-            ([packed] if step == 1 else []) + held,
+            [],
+            held,
         )
         sums, ends = list(got[:3]), got[3:]
         if not last:

time: 115 us -> 109 us (0.948)
  Pallas kernels: 24 us -> 18.8 us
  waiting for transfers between devices: 43.6 us -> 48.7 us
  local copies, waits for them, and re-layouts: 5.65 us -> 0.99 us
    ppermute x2, waiting for transfers between devices: 2.74 us -> 12.2 us  [body(): lax.ppermute(held[0], 'tile', up)]
    pallas_call x12 -> x13, Pallas kernels: 24 us -> 18.8 us  [run(): pl.pallas_call(kernel, out_shape=tuple((s if i in hbm_out else pltpu.VMEM...]
    unnamed x14 -> x2, local copies, waits for them, and re-layouts: 5.65 us -> 0.99 us
    ppermute x1, waiting for transfers between devices: 5.98 us -> 2.63 us  [body(): lax.ppermute(edge, 'tile', [(i, j) for i, j in across if 0 <= j < tiles])]
    ppermute x1, starting transfers between devices: 4.68 us -> 2.16 us  [reduce_weights(): got = lax.ppermute(send, 'tile', core_swap)]
    ppermute x3, starting transfers between devices: 3.87 us -> 5.49 us  [reduce_weights(): lax.ppermute(dealt[k], 'tile', shifts[k])]
    ppermute x2, waiting for transfers between devices: 10 us -> 8.6 us  [body(): lax.ppermute(held[1], 'tile', down)]
  transfers between devices with their start and end apart: 22 -> 22, of which waited for: 16 -> 18; matrix products, arithmetic and copies ran while one was open for 2% -> 0% of each run, Pallas kernels for 16% -> 15%
where the time goes in v3:
time: 109 us; the launch traced here: 108 us
  waiting for transfers between devices  48.7 us (45%)
  starting transfers between devices  39.1 us (36%)
  Pallas kernels  18.8 us (17%)
    pallas_call x13, Pallas kernels, run(): pl.pallas_call(kernel, out_shape=tuple((s if i in hbm_out else pltpu.VMEM...  18.8 us
    ppermute x2, waiting for transfers between devices, body(): lax.ppermute(held[0], 'tile', up)  12.2 us
    ppermute x4, waiting for transfers between devices, reduce_weights(): lax.ppermute(parts[2 * half + 1], 'dp', [(i, i ^ bit) for i in range(dp)])  10.9 us
    ppermute x2, starting transfers between devices, body(): lax.ppermute(held[0], 'tile', up)  9.13 us
    ppermute x2, waiting for transfers between devices, body(): lax.ppermute(held[1], 'tile', down)  8.6 us
    ppermute x4, starting transfers between devices, reduce_weights(): lax.ppermute(parts[2 * half + 1], 'dp', [(i, i ^ bit) for i in range(dp)])  6.77 us
    ppermute x1, starting transfers between devices, body(): lax.ppermute(packed, 'tile', up)  6.24 us
    ppermute x3, waiting for transfers between devices, reduce_weights(): lax.ppermute(mine, 'tile', shifts[k])  5.62 us
  transfers between devices with their start and end apart: 22, of which 18 were waited for; matrix products, arithmetic and copies ran while one was open for 0% of the time, Pallas kernels for 15%

profile of v3, /device:TPU:0, one launch (start us, length us, event | category | flops | bytes accessed | tf_op | source)
XLA Modules:
  0.0 108.5 jit_solution(11138431131716650180)
XLA Ops:
  5.7 2.6 %collective-permute-done.1.refs_3_ = bf16[64,256]{1,0:T(8,128)(2,1)S(1)} collective-permute-done((bf16[64,256]{1,0:T(8,128)(2,1)S(1)}, bf16[64,256]{1,0:T(8,128)(2,1)S(1)}, u32[]{:S(2)}, u32[]{:S(2)}) %collective-permute-start.1) | collective-permute-done | bytes 32800 | tf_op jit(solution)/shard_map/ppermute | solution.py:518
  9.6 6.2 %collective-permute-start.2 = (bf16[4,208,256]{2,1,0:T(8,128)(2,1)S(1)}, bf16[4,208,256]{2,1,0:T(8,128)(2,1)S(1)}, u32[]{:S(2)}, u32[]{:S(2)}) collective-permute-start(bf16[4,208,256]{2,1,0:T(8,128)(2,1)S(1)} %shard_map.103.refs_7_), channel_id=1, source_target_pairs={{0,2},{1,3},{2,4},{3,5},{4,6},{5,7},{8,10},{9,11},{10,12},{11,13},... | collective-permute-start | bytes 1277960 | tf_op jit(solution)/shard_map/ppermute | solution.py:527
  15.9 9.5 %shard_map.105 = (f32[2064,256]{1,0:T(8,128)S(1)}, bf16[2304,256]{1,0:T(8,128)(2,1)S(1)}, bf16[2304,256]{1,0:T(8,128)(2,1)S(1)}, bf16[2304,256]{1,0:T(8,128)(2,1...) custom-call(bf16[1024,256]{1,0:T(8,128)(2,1)} %bitcast.12, ...), custom_call_target="tpu_custom_call" | custom-call | tf_op jit(solution)/shard_map/pallas_call | solution.py:27
  25.4 4.4 %collective-permute-start.5 = (bf16[4,208,256]{2,1,0:T(8,128)(2,1)S(1)}, bf16[4,208,256]{2,1,0:T(8,128)(2,1)S(1)}, u32[]{:S(2)}, u32[]{:S(2)}) collective-permute-start(bf16[4,208,256]{2,1,0:T(8,128)(2,1)S(1)} %collective-permute-done.2.refs_8_), channel_id=1, source_target_pairs={{0,2},{1,3},{2,4},{3,5},{4,6},{5,7},{8,10},{9,11},{10,12},{11,13},... | collective-permute-start | bytes 1277960 | tf_op jit(solution)/shard_map/ppermute | solution.py:537
  31.6 7.9 %collective-permute-done.5.refs_8_ = bf16[4,208,256]{2,1,0:T(8,128)(2,1)S(1)} collective-permute-done((bf16[4,208,256]{2,1,0:T(8,128)(2,1)S(1)}, bf16[4,208,256]{2,1,0:T(8,128)(2,1)S(1)}, u32[]{:S(2)}, u32[]{:S(2)}) %collective-permute-start.5) | collective-permute-done | bytes 426016 | tf_op jit(solution)/shard_map/ppermute | solution.py:537
  39.5 4.5 %collective-permute-done.6.refs_9_ = bf16[4,208,256]{2,1,0:T(8,128)(2,1)S(1)} collective-permute-done((bf16[4,208,256]{2,1,0:T(8,128)(2,1)S(1)}, bf16[4,208,256]{2,1,0:T(8,128)(2,1)S(1)}, u32[]{:S(2)}, u32[]{:S(2)}) %collective-permute-start.6) | collective-permute-done | bytes 426016 | tf_op jit(solution)/shard_map/ppermute | solution.py:537
  43.9 4.7 %collective-permute-start.7 = (bf16[4,208,256]{2,1,0:T(8,128)(2,1)S(1)}, bf16[4,208,256]{2,1,0:T(8,128)(2,1)S(1)}, u32[]{:S(2)}, u32[]{:S(2)}) collective-permute-start(bf16[4,208,256]{2,1,0:T(8,128)(2,1)S(1)} %collective-permute-done.5.refs_8_), channel_id=1, source_target_pairs={{0,2},{1,3},{2,4},{3,5},{4,6},{5,7},{8,10},{9,11},{10,12},{11,13},... | collective-permute-start | bytes 1277960 | tf_op jit(solution)/shard_map/ppermute | solution.py:537
  50.0 3.7 %shard_map.107 = (f32[256,2304]{1,0:T(8,128)S(1)}, f32[256,2304]{1,0:T(8,128)S(1)}, f32[2064,256]{1,0:T(8,128)S(1)}) custom-call(f32[2064,256]{1,0:T(8,128)S(1)} %get-tuple-element.73.refs_0_, bf16[2304,256]{1,0:T(8,128)(2,1)S(1)} %get-tuple-element.57.refs_1_, ...), custom_call_target="tpu_custom_call", output_to_operand_aliasing={{0}: (5, {}), {1}: (6, {}), {2}: (7, {})} | custom-call | tf_op jit(solution)/shard_map/pallas_call | solution.py:27
  53.7 4.3 %collective-permute-done.7.refs_8_ = bf16[4,208,256]{2,1,0:T(8,128)(2,1)S(1)} collective-permute-done((bf16[4,208,256]{2,1,0:T(8,128)(2,1)S(1)}, bf16[4,208,256]{2,1,0:T(8,128)(2,1)S(1)}, u32[]{:S(2)}, u32[]{:S(2)}) %collective-permute-start.7) | collective-permute-done | bytes 426016 | tf_op jit(solution)/shard_map/ppermute | solution.py:537
  57.9 4.1 %collective-permute-done.8.refs_9_ = bf16[4,208,256]{2,1,0:T(8,128)(2,1)S(1)} collective-permute-done((bf16[4,208,256]{2,1,0:T(8,128)(2,1)S(1)}, bf16[4,208,256]{2,1,0:T(8,128)(2,1)S(1)}, u32[]{:S(2)}, u32[]{:S(2)}) %collective-permute-start.8) | collective-permute-done | bytes 426016 | tf_op jit(solution)/shard_map/ppermute | solution.py:537
  63.1 2.2 %collective-permute-start.9 = (bf16[2304,256]{1,0:T(8,128)(2,1)S(1)}, bf16[2304,256]{1,0:T(8,128)(2,1)S(1)}, u32[]{:S(2)}, u32[]{:S(2)}) collective-permute-start(bf16[2304,256]{1,0:T(8,128)(2,1)S(1)} %get-tuple-element.78), channel_id=1, source_target_pairs={{0,1},{1,0},{2,3},{3,2},{4,5},{5,4},{6,7},{7,6},{8,9},{9,8},{10,11... | collective-permute-start | bytes 3538952 | tf_op jit(solution)/shard_map/ppermute | solution.py:390
  65.4 2.4 %collective-permute-done.9.got_ref = bf16[2304,256]{1,0:T(8,128)(2,1)S(1)} collective-permute-done((bf16[2304,256]{1,0:T(8,128)(2,1)S(1)}, bf16[2304,256]{1,0:T(8,128)(2,1)S(1)}, u32[]{:S(2)}, u32[]{:S(2)}) %collective-permute-start.9) | collective-permute-done | bytes 1179680 | tf_op jit(solution)/shard_map/ppermute | solution.py:390
  68.1 4.5 %collective-permute-start.12 = (bf16[2,288,256]{2,1,0:T(8,128)(2,1)S(1)}, bf16[2,288,256]{2,1,0:T(8,128)(2,1)S(1)}, u32[]{:S(2)}, u32[]{:S(2)}) collective-permute-start(bf16[2,288,256]{2,1,0:T(8,128)(2,1)S(1)} %get-tuple-element.85), channel_id=1, source_target_pairs={{0,16},{8,24},{16,0},{24,8},{1,17},{9,25},{17,1},{25,9},{2,18},{10... | collective-permute-start | bytes 884744 | tf_op jit(solution)/shard_map/ppermute | solution.py:417
  73.5 3.9 %collective-permute-done.10.pr = bf16[2,288,256]{2,1,0:T(8,128)(2,1)S(1)} collective-permute-done((bf16[2,288,256]{2,1,0:T(8,128)(2,1)S(1)}, bf16[2,288,256]{2,1,0:T(8,128)(2,1)S(1)}, u32[]{:S(2)}, u32[]{:S(2)}) %collective-permute-start.10) | collective-permute-done | bytes 294944 | tf_op jit(solution)/shard_map/ppermute | solution.py:417
  77.4 2.3 %collective-permute-done.12.qr = bf16[2,288,256]{2,1,0:T(8,128)(2,1)S(1)} collective-permute-done((bf16[2,288,256]{2,1,0:T(8,128)(2,1)S(1)}, bf16[2,288,256]{2,1,0:T(8,128)(2,1)S(1)}, u32[]{:S(2)}, u32[]{:S(2)}) %collective-permute-start.12) | collective-permute-done | bytes 294944 | tf_op jit(solution)/shard_map/ppermute | solution.py:417
  79.8 1.8 %collective-permute-start.13 = (bf16[1,288,256]{2,1,0:T(8,128)(2,1)S(1)}, bf16[1,288,256]{2,1,0:T(8,128)(2,1)S(1)}, u32[]{:S(2)}, u32[]{:S(2)}) collective-permute-start(bf16[1,288,256]{2,1,0:T(8,128)(2,1)S(1)} %get-tuple-element.87), channel_id=1, source_target_pairs={{0,16},{8,24},{16,0},{24,8},{1,17},{9,25},{17,1},{25,9},{2,18},{10... | collective-permute-start | bytes 442376 | tf_op jit(solution)/shard_map/ppermute | solution.py:417
  82.0 3.0 %collective-permute-done.13.pr = bf16[1,288,256]{2,1,0:T(8,128)(2,1)S(1)} collective-permute-done((bf16[1,288,256]{2,1,0:T(8,128)(2,1)S(1)}, bf16[1,288,256]{2,1,0:T(8,128)(2,1)S(1)}, u32[]{:S(2)}, u32[]{:S(2)}) %collective-permute-start.13) | collective-permute-done | bytes 147488 | tf_op jit(solution)/shard_map/ppermute | solution.py:417
  85.0 1.7 %collective-permute-done.14.qr = bf16[1,288,256]{2,1,0:T(8,128)(2,1)S(1)} collective-permute-done((bf16[1,288,256]{2,1,0:T(8,128)(2,1)S(1)}, bf16[1,288,256]{2,1,0:T(8,128)(2,1)S(1)}, u32[]{:S(2)}, u32[]{:S(2)}) %collective-permute-start.14) | collective-permute-done | bytes 147488 | tf_op jit(solution)/shard_map/ppermute | solution.py:417
  87.0 5.4 %collective-permute-start.16 = (bf16[144,256]{1,0:T(8,128)(2,1)S(1)}, bf16[144,256]{1,0:T(8,128)(2,1)S(1)}, u32[]{:S(2)}, u32[]{:S(2)}) collective-permute-start(bf16[144,256]{1,0:T(8,128)(2,1)S(1)} %get-tuple-element.92), channel_id=1, source_target_pairs={{0,4},{1,5},{2,6},{3,7},{4,0},{5,1},{6,2},{7,3},{8,12},{9,13},{10,... | collective-permute-start | bytes 221192 | tf_op jit(solution)/shard_map/ppermute | solution.py:463
  92.4 2.0 %collective-permute-done.15.refs_1_ = bf16[144,256]{1,0:T(8,128)(2,1)S(1)} collective-permute-done((bf16[144,256]{1,0:T(8,128)(2,1)S(1)}, bf16[144,256]{1,0:T(8,128)(2,1)S(1)}, u32[]{:S(2)}, u32[]{:S(2)}) %collective-permute-start.15) | collective-permute-done | bytes 73760 | tf_op jit(solution)/shard_map/ppermute | solution.py:463
  94.4 2.3 %collective-permute-done.16.refs_2_ = bf16[144,256]{1,0:T(8,128)(2,1)S(1)} collective-permute-done((bf16[144,256]{1,0:T(8,128)(2,1)S(1)}, bf16[144,256]{1,0:T(8,128)(2,1)S(1)}, u32[]{:S(2)}, u32[]{:S(2)}) %collective-permute-start.16) | collective-permute-done | bytes 73760 | tf_op jit(solution)/shard_map/ppermute | solution.py:463
  97.2 2.2 %collective-permute-start.20 = (bf16[144,256]{1,0:T(8,128)(2,1)S(1)}, bf16[144,256]{1,0:T(8,128)(2,1)S(1)}, u32[]{:S(2)}, u32[]{:S(2)}) collective-permute-start(bf16[144,256]{1,0:T(8,128)(2,1)S(1)} %shard_map.113.refs_0_), channel_id=1, source_target_pairs={{0,6},{1,7},{2,0},{3,1},{4,2},{5,3},{6,4},{7,5},{8,14},{9,15},{10,... | collective-permute-start | bytes 221192 | tf_op jit(solution)/shard_map/ppermute | solution.py:472
  100.1 2.0 %collective-permute-done.20.refs_3_ = bf16[144,256]{1,0:T(8,128)(2,1)S(1)} collective-permute-done((bf16[144,256]{1,0:T(8,128)(2,1)S(1)}, bf16[144,256]{1,0:T(8,128)(2,1)S(1)}, u32[]{:S(2)}, u32[]{:S(2)}) %collective-permute-start.20) | collective-permute-done | bytes 73760 | tf_op jit(solution)/shard_map/ppermute | solution.py:472
  102.1 2.7 %collective-permute-done.19.refs_2_ = bf16[144,256]{1,0:T(8,128)(2,1)S(1)} collective-permute-done((bf16[144,256]{1,0:T(8,128)(2,1)S(1)}, bf16[144,256]{1,0:T(8,128)(2,1)S(1)}, u32[]{:S(2)}, u32[]{:S(2)}) %collective-permute-start.19) | collective-permute-done | bytes 73760 | tf_op jit(solution)/shard_map/ppermute | solution.py:472
  (35 shorter events, 17.2 us)
Async XLA Ops:
  0.6 15.2 %collective-permute-start.4 = (bf16[1024,256]{1,0:T(8,128)(2,1)}, bf16[1024,256]{1,0:T(8,128)(2,1)S(1)}, u32[]{:S(2)}, u32[]{:S(2)}) collective-permute-start(bf16[1024,256]{1,0:T(8,128)(2,1)} %bitcast.10), channel_id=1, source_target_pairs={{0,1},{1,0},{2,3},{3,2},{4,5},{5,4},{6,7},{7,6},{8,9},{9,8},{10,11... | collective-permute-start | bytes 1572872 | tf_op jit(solution)/shard_map/ppermute | solution.py:519
  1.9 6.4 %collective-permute-start.1 = (bf16[64,256]{1,0:T(8,128)(2,1)S(1)}, bf16[64,256]{1,0:T(8,128)(2,1)S(1)}, u32[]{:S(2)}, u32[]{:S(2)}) collective-permute-start(bf16[64,256]{1,0:T(8,128)(2,1)S(1)} %shard_map.104), channel_id=1, source_target_pairs={{1,3},{2,0},{3,5},{4,2},{5,7},{6,4},{9,11},{10,8},{11,13},{12,10},... | collective-permute-start | bytes 98312 | tf_op jit(solution)/shard_map/ppermute | solution.py:518
  3.2 5.1 %collective-permute-start = (bf16[64,256]{1,0:T(8,128)(2,1)S(1)}, bf16[64,256]{1,0:T(8,128)(2,1)S(1)}, u32[]{:S(2)}, u32[]{:S(2)}) collective-permute-start(bf16[64,256]{1,0:T(8,128)(2,1)S(1)} %shard_map.104), channel_id=1, source_target_pairs={{1,2},{2,1},{3,4},{4,3},{5,6},{6,5},{9,10},{10,9},{11,12},{12,11},... | collective-permute-start | bytes 98312 | tf_op jit(solution)/shard_map/ppermute | solution.py:514
  3.9 1.0 copy-start
  8.3 17.1 %collective-permute-start.3 = (bf16[4,208,256]{2,1,0:T(8,128)(2,1)S(1)}, bf16[4,208,256]{2,1,0:T(8,128)(2,1)S(1)}, u32[]{:S(2)}, u32[]{:S(2)}) collective-permute-start(bf16[4,208,256]{2,1,0:T(8,128)(2,1)S(1)} %shard_map.103.refs_7_), channel_id=1, source_target_pairs={{2,0},{3,1},{4,2},{5,3},{6,4},{7,5},{10,8},{11,9},{12,10},{13,11},... | collective-permute-start | bytes 1277960 | tf_op jit(solution)/shard_map/ppermute | solution.py:527
  9.6 15.8 %collective-permute-start.2 = (bf16[4,208,256]{2,1,0:T(8,128)(2,1)S(1)}, bf16[4,208,256]{2,1,0:T(8,128)(2,1)S(1)}, u32[]{:S(2)}, u32[]{:S(2)}) collective-permute-start(bf16[4,208,256]{2,1,0:T(8,128)(2,1)S(1)} %shard_map.103.refs_7_), channel_id=1, source_target_pairs={{0,2},{1,3},{2,4},{3,5},{4,6},{5,7},{8,10},{9,11},{10,12},{11,13},... | collective-permute-start | bytes 1277960 | tf_op jit(solution)/shard_map/ppermute | solution.py:527
  25.4 14.0 %collective-permute-start.5 = (bf16[4,208,256]{2,1,0:T(8,128)(2,1)S(1)}, bf16[4,208,256]{2,1,0:T(8,128)(2,1)S(1)}, u32[]{:S(2)}, u32[]{:S(2)}) collective-permute-start(bf16[4,208,256]{2,1,0:T(8,128)(2,1)S(1)} %collective-permute-done.2.refs_8_), channel_id=1, source_target_pairs={{0,2},{1,3},{2,4},{3,5},{4,6},{5,7},{8,10},{9,11},{10,12},{11,13},... | collective-permute-start | bytes 1277960 | tf_op jit(solution)/shard_map/ppermute | solution.py:537
  29.9 14.1 %collective-permute-start.6 = (bf16[4,208,256]{2,1,0:T(8,128)(2,1)S(1)}, bf16[4,208,256]{2,1,0:T(8,128)(2,1)S(1)}, u32[]{:S(2)}, u32[]{:S(2)}) collective-permute-start(bf16[4,208,256]{2,1,0:T(8,128)(2,1)S(1)} %collective-permute-done.3.refs_9_), channel_id=1, source_target_pairs={{2,0},{3,1},{4,2},{5,3},{6,4},{7,5},{10,8},{11,9},{12,10},{13,11},... | collective-permute-start | bytes 1277960 | tf_op jit(solution)/shard_map/ppermute | solution.py:537
  43.9 14.0 %collective-permute-start.7 = (bf16[4,208,256]{2,1,0:T(8,128)(2,1)S(1)}, bf16[4,208,256]{2,1,0:T(8,128)(2,1)S(1)}, u32[]{:S(2)}, u32[]{:S(2)}) collective-permute-start(bf16[4,208,256]{2,1,0:T(8,128)(2,1)S(1)} %collective-permute-done.5.refs_8_), channel_id=1, source_target_pairs={{0,2},{1,3},{2,4},{3,5},{4,6},{5,7},{8,10},{9,11},{10,12},{11,13},... | collective-permute-start | bytes 1277960 | tf_op jit(solution)/shard_map/ppermute | solution.py:537
  48.7 13.4 %collective-permute-start.8 = (bf16[4,208,256]{2,1,0:T(8,128)(2,1)S(1)}, bf16[4,208,256]{2,1,0:T(8,128)(2,1)S(1)}, u32[]{:S(2)}, u32[]{:S(2)}) collective-permute-start(bf16[4,208,256]{2,1,0:T(8,128)(2,1)S(1)} %collective-permute-done.6.refs_9_), channel_id=1, source_target_pairs={{2,0},{3,1},{4,2},{5,3},{6,4},{7,5},{10,8},{11,9},{12,10},{13,11},... | collective-permute-start | bytes 1277960 | tf_op jit(solution)/shard_map/ppermute | solution.py:537
  63.1 4.6 %collective-permute-start.9 = (bf16[2304,256]{1,0:T(8,128)(2,1)S(1)}, bf16[2304,256]{1,0:T(8,128)(2,1)S(1)}, u32[]{:S(2)}, u32[]{:S(2)}) collective-permute-start(bf16[2304,256]{1,0:T(8,128)(2,1)S(1)} %get-tuple-element.78), channel_id=1, source_target_pairs={{0,1},{1,0},{2,3},{3,2},{4,5},{5,4},{6,7},{7,6},{8,9},{9,8},{10,11... | collective-permute-start | bytes 3538952 | tf_op jit(solution)/shard_map/ppermute | solution.py:390
  65.3 7.4 %collective-permute-start.11 = (bf16[1024,256]{1,0:T(8,128)(2,1)S(1)}, bf16[1024,256]{1,0:T(8,128)(2,1)S(1)}, u32[]{:S(2)}, u32[]{:S(2)}) collective-permute-start(bf16[1024,256]{1,0:T(8,128)(2,1)S(1)} %get-tuple-element.82), channel_id=1, source_target_pairs={{0,1},{1,0},{2,3},{3,2},{4,5},{5,4},{6,7},{7,6},{8,9},{9,8},{10,11... | collective-permute-start | bytes 1572872 | tf_op jit(solution)/shard_map/ppermute | solution.py:552
  68.0 9.4 %collective-permute-start.10 = (bf16[2,288,256]{2,1,0:T(8,128)(2,1)S(1)}, bf16[2,288,256]{2,1,0:T(8,128)(2,1)S(1)}, u32[]{:S(2)}, u32[]{:S(2)}) collective-permute-start(bf16[2,288,256]{2,1,0:T(8,128)(2,1)S(1)} %get-tuple-element.80), channel_id=1, source_target_pairs={{0,8},{8,0},{16,24},{24,16},{1,9},{9,1},{17,25},{25,17},{2,10},{10... | collective-permute-start | bytes 884744 | tf_op jit(solution)/shard_map/ppermute | solution.py:417
  68.1 11.6 %collective-permute-start.12 = (bf16[2,288,256]{2,1,0:T(8,128)(2,1)S(1)}, bf16[2,288,256]{2,1,0:T(8,128)(2,1)S(1)}, u32[]{:S(2)}, u32[]{:S(2)}) collective-permute-start(bf16[2,288,256]{2,1,0:T(8,128)(2,1)S(1)} %get-tuple-element.85), channel_id=1, source_target_pairs={{0,16},{8,24},{16,0},{24,8},{1,17},{9,25},{17,1},{25,9},{2,18},{10... | collective-permute-start | bytes 884744 | tf_op jit(solution)/shard_map/ppermute | solution.py:417
  79.8 5.2 %collective-permute-start.13 = (bf16[1,288,256]{2,1,0:T(8,128)(2,1)S(1)}, bf16[1,288,256]{2,1,0:T(8,128)(2,1)S(1)}, u32[]{:S(2)}, u32[]{:S(2)}) collective-permute-start(bf16[1,288,256]{2,1,0:T(8,128)(2,1)S(1)} %get-tuple-element.87), channel_id=1, source_target_pairs={{0,16},{8,24},{16,0},{24,8},{1,17},{9,25},{17,1},{25,9},{2,18},{10... | collective-permute-start | bytes 442376 | tf_op jit(solution)/shard_map/ppermute | solution.py:417
  81.6 5.1 %collective-permute-start.14 = (bf16[1,288,256]{2,1,0:T(8,128)(2,1)S(1)}, bf16[1,288,256]{2,1,0:T(8,128)(2,1)S(1)}, u32[]{:S(2)}, u32[]{:S(2)}) collective-permute-start(bf16[1,288,256]{2,1,0:T(8,128)(2,1)S(1)} %get-tuple-element.89), channel_id=1, source_target_pairs={{0,8},{8,0},{16,24},{24,16},{1,9},{9,1},{17,25},{25,17},{2,10},{10... | collective-permute-start | bytes 442376 | tf_op jit(solution)/shard_map/ppermute | solution.py:417
  86.9 7.5 %collective-permute-start.15 = (bf16[144,256]{1,0:T(8,128)(2,1)S(1)}, bf16[144,256]{1,0:T(8,128)(2,1)S(1)}, u32[]{:S(2)}, u32[]{:S(2)}) collective-permute-start(bf16[144,256]{1,0:T(8,128)(2,1)S(1)} %get-tuple-element.91), channel_id=1, source_target_pairs={{0,2},{1,3},{2,4},{3,5},{4,6},{5,7},{6,0},{7,1},{8,10},{9,11},{10,... | collective-permute-start | bytes 221192 | tf_op jit(solution)/shard_map/ppermute | solution.py:463
  87.0 9.8 %collective-permute-start.16 = (bf16[144,256]{1,0:T(8,128)(2,1)S(1)}, bf16[144,256]{1,0:T(8,128)(2,1)S(1)}, u32[]{:S(2)}, u32[]{:S(2)}) collective-permute-start(bf16[144,256]{1,0:T(8,128)(2,1)S(1)} %get-tuple-element.92), channel_id=1, source_target_pairs={{0,4},{1,5},{2,6},{3,7},{4,0},{5,1},{6,2},{7,3},{8,12},{9,13},{10,... | collective-permute-start | bytes 221192 | tf_op jit(solution)/shard_map/ppermute | solution.py:463
  92.4 4.8 %collective-permute-start.17 = (bf16[144,256]{1,0:T(8,128)(2,1)S(1)}, bf16[144,256]{1,0:T(8,128)(2,1)S(1)}, u32[]{:S(2)}, u32[]{:S(2)}) collective-permute-start(bf16[144,256]{1,0:T(8,128)(2,1)S(1)} %get-tuple-element.93), channel_id=1, source_target_pairs={{0,6},{1,7},{2,0},{3,1},{4,2},{5,3},{6,4},{7,5},{8,14},{9,15},{10,... | collective-permute-start | bytes 221192 | tf_op jit(solution)/shard_map/ppermute | solution.py:463
  97.2 4.9 %collective-permute-start.20 = (bf16[144,256]{1,0:T(8,128)(2,1)S(1)}, bf16[144,256]{1,0:T(8,128)(2,1)S(1)}, u32[]{:S(2)}, u32[]{:S(2)}) collective-permute-start(bf16[144,256]{1,0:T(8,128)(2,1)S(1)} %shard_map.113.refs_0_), channel_id=1, source_target_pairs={{0,6},{1,7},{2,0},{3,1},{4,2},{5,3},{6,4},{7,5},{8,14},{9,15},{10,... | collective-permute-start | bytes 221192 | tf_op jit(solution)/shard_map/ppermute | solution.py:472
  99.4 5.3 %collective-permute-start.19 = (bf16[144,256]{1,0:T(8,128)(2,1)S(1)}, bf16[144,256]{1,0:T(8,128)(2,1)S(1)}, u32[]{:S(2)}, u32[]{:S(2)}) collective-permute-start(bf16[144,256]{1,0:T(8,128)(2,1)S(1)} %shard_map.113.refs_0_), channel_id=1, source_target_pairs={{0,4},{1,5},{2,6},{3,7},{4,0},{5,1},{6,2},{7,3},{8,12},{9,13},{10,... | collective-permute-start | bytes 221192 | tf_op jit(solution)/shard_map/ppermute | solution.py:472
  99.6 6.2 %collective-permute-start.18 = (bf16[144,256]{1,0:T(8,128)(2,1)S(1)}, bf16[144,256]{1,0:T(8,128)(2,1)S(1)}, u32[]{:S(2)}, u32[]{:S(2)}) collective-permute-start(bf16[144,256]{1,0:T(8,128)(2,1)S(1)} %shard_map.113.refs_0_), channel_id=1, source_target_pairs={{0,2},{1,3},{2,4},{3,5},{4,6},{5,7},{6,0},{7,1},{8,10},{9,11},{10,... | collective-permute-start | bytes 221192 | tf_op jit(solution)/shard_map/ppermute | solution.py:472
  105.7 1.6 %collective-permute-start.21 = (bf16[576,256]{1,0:T(8,128)(2,1)S(1)}, bf16[576,256]{1,0:T(8,128)(2,1)S(1)}, u32[]{:S(2)}, u32[]{:S(2)}) collective-permute-start(bf16[576,256]{1,0:T(8,128)(2,1)S(1)} %shard_map.114.mine_ref), channel_id=1, source_target_pairs={{0,1},{1,0},{2,3},{3,2},{4,5},{5,4},{6,7},{7,6},{8,9},{9,8},{10,11... | collective-permute-start | bytes 884744 | tf_op jit(solution)/shard_map/ppermute | solution.py:481

commit v4 on v3

--- a/solution.py
+++ b/solution.py
@@ -183,7 +183,8 @@
     def batch(size, start):
         cells = (size * (side + 1) - 1) * PITCH
         spot = lax.broadcasted_iota(jnp.int32, (cells, 256), 0)
-        inside = (lax.rem(spot, PITCH) < side) & (lax.rem(spot // PITCH, side + 1) < side)
+        gap = side * PITCH
+        inside = ((spot & (PITCH - 1)) < side) & ((spot < gap) | (spot >= gap + PITCH))
         used = pl.ds(16, cells)
 
         def put(buf, v):
@@ -212,7 +213,6 @@
             buf[0:16, :] = jnp.zeros((16, 768), BF)
             buf[cells + 16 : cells + 32, :] = jnp.zeros((16, 768), BF)
         for n in range(size - 1):
-            gap = ((n + 1) * (side + 1) - 1) * PITCH
             vs[gap : gap + PITCH, :] = jnp.zeros((PITCH, 256), F32)
         bases, leads = [], []
         for n in range(size):
@@ -520,21 +520,21 @@
     packed = pack(cotangent[0].transpose(1, 2, 0, 3), height, place)
     packed, rim_a, rim_b = lax.optimization_barrier((packed, rim_a, rim_b))
 
-    up = [(i, i + 2) for i in range(tiles - 2)]
-    down = [(i + 2, i) for i in range(tiles - 2)]
+    ring = [(i, (i + 2) % tiles) for i in range(tiles)]
+
     flat = lambda w: w.reshape(9 * channels, channels)
     wf, w1, w2 = flat(fpn_weight), flat(mask_w1), flat(mask_w2)
-    blocks = [lax.ppermute(packed, "tile", up), lax.ppermute(packed, "tile", down)]
+    block = lax.ppermute(packed, "tile", ring)
     start = main_call(
         side, height, width, True, False, [tile, other, rim_a, rim_b], [wf, w1, w2], [packed]
     )
     kept, sums = list(start[:5]), list(start[5:])
     for step in range(1, chips):
         last = step == chips - 1
-        held = blocks
+        held = block
         if not last:
-            held[0], held[1], kept[0] = lax.optimization_barrier((held[0], held[1], kept[0]))
-            blocks = [lax.ppermute(held[0], "tile", up), lax.ppermute(held[1], "tile", down)]
+            held, kept[0] = lax.optimization_barrier((held, kept[0]))
+            block = lax.ppermute(held, "tile", ring)
         got = main_call(
             side,
             height,
@@ -543,7 +543,7 @@
             last,
             [*kept, *sums],
             [],
-            held,
+            [held],
         )
         sums, ends = list(got[:3]), got[3:]
         if not last:

time: 109 us -> 96.2 us (0.88)
  starting transfers between devices: 39.1 us -> 22 us
  waiting for transfers between devices: 48.7 us -> 53.4 us
    ppermute x6 -> x3, starting transfers between devices: 19.2 us -> 4.69 us  [the longest x1 3.73 us: body(): block = lax.ppermute(packed, 'tile', ring)]
    ppermute x4, starting transfers between devices: 6.77 us -> 2.16 us  [reduce_weights(): lax.ppermute(parts[2 * half + 1], 'dp', [(i, i ^ bit) for i in range(dp)])]
    ppermute x6 -> x3, waiting for transfers between devices: 20.8 us -> 25 us  [the longest x2 19.1 us: body(): block = lax.ppermute(held, 'tile', ring)]
    ppermute x1, starting transfers between devices: 2.16 us -> 5.43 us  [reduce_weights(): got = lax.ppermute(send, 'tile', core_swap)]
    ppermute x3, starting transfers between devices: 5.49 us -> 3.88 us  [reduce_weights(): lax.ppermute(dealt[k], 'tile', shifts[k])]
  transfers between devices with their start and end apart: 22 -> 19, of which waited for: 18 -> 16; matrix products, arithmetic and copies ran while one was open for 0% -> 0% of each run, Pallas kernels for 15% -> 14%
where the time goes in v4:
time: 96.2 us; the launch traced here: 95.6 us
  waiting for transfers between devices  53.4 us (56%)
  starting transfers between devices  22 us (23%)
  Pallas kernels  18.5 us (19%)
  local copies, waits for them, and re-layouts  0.99 us (1%)
    ppermute x2, waiting for transfers between devices, body(): block = lax.ppermute(held, 'tile', ring)  19.1 us
    pallas_call x13, Pallas kernels, run(): pl.pallas_call(kernel, out_shape=tuple((s if i in hbm_out else pltpu.VMEM...  18.5 us
    ppermute x4, waiting for transfers between devices, reduce_weights(): lax.ppermute(parts[2 * half + 1], 'dp', [(i, i ^ bit) for i in range(dp)])  11.7 us
    ppermute x1, waiting for transfers between devices, body(): block = lax.ppermute(packed, 'tile', ring)  5.93 us
    ppermute x3, waiting for transfers between devices, reduce_weights(): lax.ppermute(mine, 'tile', shifts[k])  5.83 us
    ppermute x1, starting transfers between devices, reduce_weights(): got = lax.ppermute(send, 'tile', core_swap)  5.43 us
    ppermute x3, waiting for transfers between devices, reduce_weights(): lax.ppermute(dealt[k], 'tile', shifts[k])  3.91 us
    ppermute x3, starting transfers between devices, reduce_weights(): lax.ppermute(dealt[k], 'tile', shifts[k])  3.88 us
  transfers between devices with their start and end apart: 19, of which 16 were waited for; matrix products, arithmetic and copies ran while one was open for 0% of the time, Pallas kernels for 14%

profile of v4, /device:TPU:0, one launch (start us, length us, event | category | flops | bytes accessed | tf_op | source)
XLA Modules:
  0.0 95.6 jit_solution(9631069780288414513)
XLA Ops:
  1.9 1.3 %collective-permute-start.1 = (bf16[64,256]{1,0:T(8,128)(2,1)S(1)}, bf16[64,256]{1,0:T(8,128)(2,1)S(1)}, u32[]{:S(2)}, u32[]{:S(2)}) collective-permute-start(bf16[64,256]{1,0:T(8,128)(2,1)S(1)} %shard_map.104), channel_id=1, source_target_pairs={{1,3},{2,0},{3,5},{4,2},{5,7},{6,4},{9,11},{10,8},{11,13},{12,10},... | collective-permute-start | bytes 98312 | tf_op jit(solution)/shard_map/ppermute | solution.py:518
  5.7 2.6 %collective-permute-done.1.refs_3_ = bf16[64,256]{1,0:T(8,128)(2,1)S(1)} collective-permute-done((bf16[64,256]{1,0:T(8,128)(2,1)S(1)}, bf16[64,256]{1,0:T(8,128)(2,1)S(1)}, u32[]{:S(2)}, u32[]{:S(2)}) %collective-permute-start.1) | collective-permute-done | bytes 32800 | tf_op jit(solution)/shard_map/ppermute | solution.py:518
  8.3 3.7 %collective-permute-start.2 = (bf16[4,208,256]{2,1,0:T(8,128)(2,1)S(1)}, bf16[4,208,256]{2,1,0:T(8,128)(2,1)S(1)}, u32[]{:S(2)}, u32[]{:S(2)}) collective-permute-start(bf16[4,208,256]{2,1,0:T(8,128)(2,1)S(1)} %shard_map.103.refs_7_), channel_id=1, source_target_pairs={{0,2},{1,3},{2,4},{3,5},{4,6},{5,7},{6,0},{7,1},{8,10},{9,11},{10,... | collective-permute-start | bytes 1277960 | tf_op jit(solution)/shard_map/ppermute | solution.py:527
  12.0 6.3 %shard_map.105 = (f32[2064,256]{1,0:T(8,128)S(1)}, bf16[2304,256]{1,0:T(8,128)(2,1)S(1)}, bf16[2304,256]{1,0:T(8,128)(2,1)S(1)}, bf16[2304,256]{1,0:T(8,128)(2,1...) custom-call(bf16[1024,256]{1,0:T(8,128)(2,1)} %bitcast.12, ...), custom_call_target="tpu_custom_call" | custom-call | tf_op jit(solution)/shard_map/pallas_call | solution.py:27
  18.4 5.9 %collective-permute-done.2.refs_8_ = bf16[4,208,256]{2,1,0:T(8,128)(2,1)S(1)} collective-permute-done((bf16[4,208,256]{2,1,0:T(8,128)(2,1)S(1)}, bf16[4,208,256]{2,1,0:T(8,128)(2,1)S(1)}, u32[]{:S(2)}, u32[]{:S(2)}) %collective-permute-start.2) | collective-permute-done | bytes 426016 | tf_op jit(solution)/shard_map/ppermute | solution.py:527
  24.4 3.5 %shard_map.106 = (f32[256,2304]{1,0:T(8,128)S(1)}, f32[256,2304]{1,0:T(8,128)S(1)}, f32[2064,256]{1,0:T(8,128)S(1)}) custom-call(f32[2064,256]{1,0:T(8,128)S(1)} %get-tuple-element.69.refs_0_, bf16[2304,256]{1,0:T(8,128)(2,1)S(1)} %get-tuple-element.54.refs_1_, ...), custom_call_target="tpu_custom_call", output_to_operand_aliasing={{0}: (5, {}), {1}: (6, {}), {2}: (7, {})} | custom-call | tf_op jit(solution)/shard_map/pallas_call | solution.py:27
  27.9 7.9 %collective-permute-done.4.refs_8_ = bf16[4,208,256]{2,1,0:T(8,128)(2,1)S(1)} collective-permute-done((bf16[4,208,256]{2,1,0:T(8,128)(2,1)S(1)}, bf16[4,208,256]{2,1,0:T(8,128)(2,1)S(1)}, u32[]{:S(2)}, u32[]{:S(2)}) %collective-permute-start.4) | collective-permute-done | bytes 426016 | tf_op jit(solution)/shard_map/ppermute | solution.py:537
  37.1 11.2 %collective-permute-done.5.refs_8_ = bf16[4,208,256]{2,1,0:T(8,128)(2,1)S(1)} collective-permute-done((bf16[4,208,256]{2,1,0:T(8,128)(2,1)S(1)}, bf16[4,208,256]{2,1,0:T(8,128)(2,1)S(1)}, u32[]{:S(2)}, u32[]{:S(2)}) %collective-permute-start.5) | collective-permute-done | bytes 426016 | tf_op jit(solution)/shard_map/ppermute | solution.py:537
  48.3 4.2 %shard_map.108 = (f32[256,2304]{1,0:T(8,128)S(1)}, f32[256,2304]{1,0:T(8,128)S(1)}, f32[2064,256]{1,0:T(8,128)S(1)}, bf16[2304,256]{1,0:T(8,128)(2,1)S(1)}, bf16...) custom-call(f32[2064,256]{1,0:T(8,128)S(1)} %get-tuple-element.69.re, ...), custom_call_target="tpu_custom_call", output_to_operand_aliasing={{0}: (5, {}), {1}: (6, {}), {2}: (7, {})} | custom-call | tf_op jit(solution)/shard_map/pallas_call | solution.py:27
  52.5 5.4 %collective-permute-start.6 = (bf16[2304,256]{1,0:T(8,128)(2,1)S(1)}, bf16[2304,256]{1,0:T(8,128)(2,1)S(1)}, u32[]{:S(2)}, u32[]{:S(2)}) collective-permute-start(bf16[2304,256]{1,0:T(8,128)(2,1)S(1)} %get-tuple-element.74), channel_id=1, source_target_pairs={{0,1},{1,0},{2,3},{3,2},{4,5},{5,4},{6,7},{7,6},{8,9},{9,8},{10,11... | collective-permute-start | bytes 3538952 | tf_op jit(solution)/shard_map/ppermute | solution.py:390
  58.0 2.4 %collective-permute-done.6.got_ref = bf16[2304,256]{1,0:T(8,128)(2,1)S(1)} collective-permute-done((bf16[2304,256]{1,0:T(8,128)(2,1)S(1)}, bf16[2304,256]{1,0:T(8,128)(2,1)S(1)}, u32[]{:S(2)}, u32[]{:S(2)}) %collective-permute-start.6) | collective-permute-done | bytes 1179680 | tf_op jit(solution)/shard_map/ppermute | solution.py:390
  62.0 8.0 %collective-permute-done.7.pr = bf16[2,288,256]{2,1,0:T(8,128)(2,1)S(1)} collective-permute-done((bf16[2,288,256]{2,1,0:T(8,128)(2,1)S(1)}, bf16[2,288,256]{2,1,0:T(8,128)(2,1)S(1)}, u32[]{:S(2)}, u32[]{:S(2)}) %collective-permute-start.7) | collective-permute-done | bytes 294944 | tf_op jit(solution)/shard_map/ppermute | solution.py:417
  70.6 1.7 %collective-permute-start.11 = (bf16[1,288,256]{2,1,0:T(8,128)(2,1)S(1)}, bf16[1,288,256]{2,1,0:T(8,128)(2,1)S(1)}, u32[]{:S(2)}, u32[]{:S(2)}) collective-permute-start(bf16[1,288,256]{2,1,0:T(8,128)(2,1)S(1)} %get-tuple-element.85), channel_id=1, source_target_pairs={{0,8},{8,0},{16,24},{24,16},{1,9},{9,1},{17,25},{25,17},{2,10},{10... | collective-permute-start | bytes 442376 | tf_op jit(solution)/shard_map/ppermute | solution.py:417
  72.2 3.4 %collective-permute-done.10.pr = bf16[1,288,256]{2,1,0:T(8,128)(2,1)S(1)} collective-permute-done((bf16[1,288,256]{2,1,0:T(8,128)(2,1)S(1)}, bf16[1,288,256]{2,1,0:T(8,128)(2,1)S(1)}, u32[]{:S(2)}, u32[]{:S(2)}) %collective-permute-start.10) | collective-permute-done | bytes 147488 | tf_op jit(solution)/shard_map/ppermute | solution.py:417
  76.8 1.7 %collective-permute-start.13 = (bf16[144,256]{1,0:T(8,128)(2,1)S(1)}, bf16[144,256]{1,0:T(8,128)(2,1)S(1)}, u32[]{:S(2)}, u32[]{:S(2)}) collective-permute-start(bf16[144,256]{1,0:T(8,128)(2,1)S(1)} %get-tuple-element.88), channel_id=1, source_target_pairs={{0,4},{1,5},{2,6},{3,7},{4,0},{5,1},{6,2},{7,3},{8,12},{9,13},{10,... | collective-permute-start | bytes 221192 | tf_op jit(solution)/shard_map/ppermute | solution.py:463
  78.5 1.3 %collective-permute-start.14 = (bf16[144,256]{1,0:T(8,128)(2,1)S(1)}, bf16[144,256]{1,0:T(8,128)(2,1)S(1)}, u32[]{:S(2)}, u32[]{:S(2)}) collective-permute-start(bf16[144,256]{1,0:T(8,128)(2,1)S(1)} %get-tuple-element.89), channel_id=1, source_target_pairs={{0,6},{1,7},{2,0},{3,1},{4,2},{5,3},{6,4},{7,5},{8,14},{9,15},{10,... | collective-permute-start | bytes 221192 | tf_op jit(solution)/shard_map/ppermute | solution.py:463
  79.9 2.4 %collective-permute-done.12.refs_1_ = bf16[144,256]{1,0:T(8,128)(2,1)S(1)} collective-permute-done((bf16[144,256]{1,0:T(8,128)(2,1)S(1)}, bf16[144,256]{1,0:T(8,128)(2,1)S(1)}, u32[]{:S(2)}, u32[]{:S(2)}) %collective-permute-start.12) | collective-permute-done | bytes 73760 | tf_op jit(solution)/shard_map/ppermute | solution.py:463
  82.3 1.5 %collective-permute-done.13.refs_2_ = bf16[144,256]{1,0:T(8,128)(2,1)S(1)} collective-permute-done((bf16[144,256]{1,0:T(8,128)(2,1)S(1)}, bf16[144,256]{1,0:T(8,128)(2,1)S(1)}, u32[]{:S(2)}, u32[]{:S(2)}) %collective-permute-start.13) | collective-permute-done | bytes 73760 | tf_op jit(solution)/shard_map/ppermute | solution.py:463
  83.8 2.5 %collective-permute-start.17 = (bf16[144,256]{1,0:T(8,128)(2,1)S(1)}, bf16[144,256]{1,0:T(8,128)(2,1)S(1)}, u32[]{:S(2)}, u32[]{:S(2)}) collective-permute-start(bf16[144,256]{1,0:T(8,128)(2,1)S(1)} %shard_map.113.refs_0_), channel_id=1, source_target_pairs={{0,6},{1,7},{2,0},{3,1},{4,2},{5,3},{6,4},{7,5},{8,14},{9,15},{10,... | collective-permute-start | bytes 221192 | tf_op jit(solution)/shard_map/ppermute | solution.py:472
  87.0 2.0 %collective-permute-done.17.refs_3_ = bf16[144,256]{1,0:T(8,128)(2,1)S(1)} collective-permute-done((bf16[144,256]{1,0:T(8,128)(2,1)S(1)}, bf16[144,256]{1,0:T(8,128)(2,1)S(1)}, u32[]{:S(2)}, u32[]{:S(2)}) %collective-permute-start.17) | collective-permute-done | bytes 73760 | tf_op jit(solution)/shard_map/ppermute | solution.py:472
  89.0 2.6 %collective-permute-done.16.refs_2_ = bf16[144,256]{1,0:T(8,128)(2,1)S(1)} collective-permute-done((bf16[144,256]{1,0:T(8,128)(2,1)S(1)}, bf16[144,256]{1,0:T(8,128)(2,1)S(1)}, u32[]{:S(2)}, u32[]{:S(2)}) %collective-permute-start.16) | collective-permute-done | bytes 73760 | tf_op jit(solution)/shard_map/ppermute | solution.py:472
  91.6 1.2 %collective-permute-done.15.refs_1_ = bf16[144,256]{1,0:T(8,128)(2,1)S(1)} collective-permute-done((bf16[144,256]{1,0:T(8,128)(2,1)S(1)}, bf16[144,256]{1,0:T(8,128)(2,1)S(1)}, u32[]{:S(2)}, u32[]{:S(2)}) %collective-permute-start.15) | collective-permute-done | bytes 73760 | tf_op jit(solution)/shard_map/ppermute | solution.py:472
  93.0 1.6 %collective-permute-done.18.theirs_ref = bf16[576,256]{1,0:T(8,128)(2,1)S(1)} collective-permute-done((bf16[576,256]{1,0:T(8,128)(2,1)S(1)}, bf16[576,256]{1,0:T(8,128)(2,1)S(1)}, u32[]{:S(2)}, u32[]{:S(2)}) %collective-permute-start.18) | collective-permute-done | bytes 294944 | tf_op jit(solution)/shard_map/ppermute | solution.py:481
  94.5 1.1 %shard_map.115 = (f32[576,256]{1,0:T(8,128)}, f32[576,256]{1,0:T(8,128)}) custom-call(bf16[576,256]{1,0:T(8,128)(2,1)S(1)} %shard_map.114.mine_ref, bf16[576,256]{1,0:T(8,128)(2,1)S(1)} %collective-permute-done.18.theirs_ref), custom_call_target="tpu_custom_call" | custom-call | tf_op jit(solution)/shard_map/pallas_call | solution.py:27
  (29 shorter events, 9.3 us)
Async XLA Ops:
  0.6 11.4 %collective-permute-start.3 = (bf16[1024,256]{1,0:T(8,128)(2,1)}, bf16[1024,256]{1,0:T(8,128)(2,1)S(1)}, u32[]{:S(2)}, u32[]{:S(2)}) collective-permute-start(bf16[1024,256]{1,0:T(8,128)(2,1)} %bitcast.10), channel_id=1, source_target_pairs={{0,1},{1,0},{2,3},{3,2},{4,5},{5,4},{6,7},{7,6},{8,9},{9,8},{10,11... | collective-permute-start | bytes 1572872 | tf_op jit(solution)/shard_map/ppermute | solution.py:519
  1.9 6.4 %collective-permute-start.1 = (bf16[64,256]{1,0:T(8,128)(2,1)S(1)}, bf16[64,256]{1,0:T(8,128)(2,1)S(1)}, u32[]{:S(2)}, u32[]{:S(2)}) collective-permute-start(bf16[64,256]{1,0:T(8,128)(2,1)S(1)} %shard_map.104), channel_id=1, source_target_pairs={{1,3},{2,0},{3,5},{4,2},{5,7},{6,4},{9,11},{10,8},{11,13},{12,10},... | collective-permute-start | bytes 98312 | tf_op jit(solution)/shard_map/ppermute | solution.py:518
  3.2 5.1 %collective-permute-start = (bf16[64,256]{1,0:T(8,128)(2,1)S(1)}, bf16[64,256]{1,0:T(8,128)(2,1)S(1)}, u32[]{:S(2)}, u32[]{:S(2)}) collective-permute-start(bf16[64,256]{1,0:T(8,128)(2,1)S(1)} %shard_map.104), channel_id=1, source_target_pairs={{1,2},{2,1},{3,4},{4,3},{5,6},{6,5},{9,10},{10,9},{11,12},{12,11},... | collective-permute-start | bytes 98312 | tf_op jit(solution)/shard_map/ppermute | solution.py:514
  3.9 1.0 %copy-start = (bf16[1,4,14,14,256]{4,1,3,2,0:T(4,128)(2,1)S(1)}, bf16[1,4,14,14,256]{4,1,3,2,0:T(4,128)(2,1)}, u32[]{:S(2)}) copy-start(bf16[1,4,14,14,256]{4,1,3,2,0:T(4,128)(2,1)} %param.15) | copy-start | bytes 1204228
  8.3 16.0 %collective-permute-start.2 = (bf16[4,208,256]{2,1,0:T(8,128)(2,1)S(1)}, bf16[4,208,256]{2,1,0:T(8,128)(2,1)S(1)}, u32[]{:S(2)}, u32[]{:S(2)}) collective-permute-start(bf16[4,208,256]{2,1,0:T(8,128)(2,1)S(1)} %shard_map.103.refs_7_), channel_id=1, source_target_pairs={{0,2},{1,3},{2,4},{3,5},{4,6},{5,7},{6,0},{7,1},{8,10},{9,11},{10,... | collective-permute-start | bytes 1277960 | tf_op jit(solution)/shard_map/ppermute | solution.py:527
  24.3 11.5 %collective-permute-start.4 = (bf16[4,208,256]{2,1,0:T(8,128)(2,1)S(1)}, bf16[4,208,256]{2,1,0:T(8,128)(2,1)S(1)}, u32[]{:S(2)}, u32[]{:S(2)}) collective-permute-start(bf16[4,208,256]{2,1,0:T(8,128)(2,1)S(1)} %collective-permute-done.2.refs_8_), channel_id=1, source_target_pairs={{0,2},{1,3},{2,4},{3,5},{4,6},{5,7},{6,0},{7,1},{8,10},{9,11},{10,... | collective-permute-start | bytes 1277960 | tf_op jit(solution)/shard_map/ppermute | solution.py:537
  35.8 12.5 %collective-permute-start.5 = (bf16[4,208,256]{2,1,0:T(8,128)(2,1)S(1)}, bf16[4,208,256]{2,1,0:T(8,128)(2,1)S(1)}, u32[]{:S(2)}, u32[]{:S(2)}) collective-permute-start(bf16[4,208,256]{2,1,0:T(8,128)(2,1)S(1)} %collective-permute-done.4.refs_8_), channel_id=1, source_target_pairs={{0,2},{1,3},{2,4},{3,5},{4,6},{5,7},{6,0},{7,1},{8,10},{9,11},{10,... | collective-permute-start | bytes 1277960 | tf_op jit(solution)/shard_map/ppermute | solution.py:537
  52.5 7.9 %collective-permute-start.6 = (bf16[2304,256]{1,0:T(8,128)(2,1)S(1)}, bf16[2304,256]{1,0:T(8,128)(2,1)S(1)}, u32[]{:S(2)}, u32[]{:S(2)}) collective-permute-start(bf16[2304,256]{1,0:T(8,128)(2,1)S(1)} %get-tuple-element.74), channel_id=1, source_target_pairs={{0,1},{1,0},{2,3},{3,2},{4,5},{5,4},{6,7},{7,6},{8,9},{9,8},{10,11... | collective-permute-start | bytes 3538952 | tf_op jit(solution)/shard_map/ppermute | solution.py:390
  57.9 3.2 %collective-permute-start.8 = (bf16[1024,256]{1,0:T(8,128)(2,1)S(1)}, bf16[1024,256]{1,0:T(8,128)(2,1)S(1)}, u32[]{:S(2)}, u32[]{:S(2)}) collective-permute-start(bf16[1024,256]{1,0:T(8,128)(2,1)S(1)} %get-tuple-element.78), channel_id=1, source_target_pairs={{0,1},{1,0},{2,3},{3,2},{4,5},{5,4},{6,7},{7,6},{8,9},{9,8},{10,11... | collective-permute-start | bytes 1572872 | tf_op jit(solution)/shard_map/ppermute | solution.py:552
  60.7 9.4 %collective-permute-start.7 = (bf16[2,288,256]{2,1,0:T(8,128)(2,1)S(1)}, bf16[2,288,256]{2,1,0:T(8,128)(2,1)S(1)}, u32[]{:S(2)}, u32[]{:S(2)}) collective-permute-start(bf16[2,288,256]{2,1,0:T(8,128)(2,1)S(1)} %get-tuple-element.76), channel_id=1, source_target_pairs={{0,8},{8,0},{16,24},{24,16},{1,9},{9,1},{17,25},{25,17},{2,10},{10... | collective-permute-start | bytes 884744 | tf_op jit(solution)/shard_map/ppermute | solution.py:417
  60.7 9.4 %collective-permute-start.9 = (bf16[2,288,256]{2,1,0:T(8,128)(2,1)S(1)}, bf16[2,288,256]{2,1,0:T(8,128)(2,1)S(1)}, u32[]{:S(2)}, u32[]{:S(2)}) collective-permute-start(bf16[2,288,256]{2,1,0:T(8,128)(2,1)S(1)} %get-tuple-element.81), channel_id=1, source_target_pairs={{0,16},{8,24},{16,0},{24,8},{1,17},{9,25},{17,1},{25,9},{2,18},{10... | collective-permute-start | bytes 884744 | tf_op jit(solution)/shard_map/ppermute | solution.py:417
  70.2 5.4 %collective-permute-start.10 = (bf16[1,288,256]{2,1,0:T(8,128)(2,1)S(1)}, bf16[1,288,256]{2,1,0:T(8,128)(2,1)S(1)}, u32[]{:S(2)}, u32[]{:S(2)}) collective-permute-start(bf16[1,288,256]{2,1,0:T(8,128)(2,1)S(1)} %get-tuple-element.83), channel_id=1, source_target_pairs={{0,16},{8,24},{16,0},{24,8},{1,17},{9,25},{17,1},{25,9},{2,18},{10... | collective-permute-start | bytes 442376 | tf_op jit(solution)/shard_map/ppermute | solution.py:417
  70.6 5.3 %collective-permute-start.11 = (bf16[1,288,256]{2,1,0:T(8,128)(2,1)S(1)}, bf16[1,288,256]{2,1,0:T(8,128)(2,1)S(1)}, u32[]{:S(2)}, u32[]{:S(2)}) collective-permute-start(bf16[1,288,256]{2,1,0:T(8,128)(2,1)S(1)} %get-tuple-element.85), channel_id=1, source_target_pairs={{0,8},{8,0},{16,24},{24,16},{1,9},{9,1},{17,25},{25,17},{2,10},{10... | collective-permute-start | bytes 442376 | tf_op jit(solution)/shard_map/ppermute | solution.py:417
  76.0 6.3 %collective-permute-start.12 = (bf16[144,256]{1,0:T(8,128)(2,1)S(1)}, bf16[144,256]{1,0:T(8,128)(2,1)S(1)}, u32[]{:S(2)}, u32[]{:S(2)}) collective-permute-start(bf16[144,256]{1,0:T(8,128)(2,1)S(1)} %get-tuple-element.87), channel_id=1, source_target_pairs={{0,2},{1,3},{2,4},{3,5},{4,6},{5,7},{6,0},{7,1},{8,10},{9,11},{10,... | collective-permute-start | bytes 221192 | tf_op jit(solution)/shard_map/ppermute | solution.py:463
  76.8 7.0 %collective-permute-start.13 = (bf16[144,256]{1,0:T(8,128)(2,1)S(1)}, bf16[144,256]{1,0:T(8,128)(2,1)S(1)}, u32[]{:S(2)}, u32[]{:S(2)}) collective-permute-start(bf16[144,256]{1,0:T(8,128)(2,1)S(1)} %get-tuple-element.88), channel_id=1, source_target_pairs={{0,4},{1,5},{2,6},{3,7},{4,0},{5,1},{6,2},{7,3},{8,12},{9,13},{10,... | collective-permute-start | bytes 221192 | tf_op jit(solution)/shard_map/ppermute | solution.py:463
  78.5 5.2 %collective-permute-start.14 = (bf16[144,256]{1,0:T(8,128)(2,1)S(1)}, bf16[144,256]{1,0:T(8,128)(2,1)S(1)}, u32[]{:S(2)}, u32[]{:S(2)}) collective-permute-start(bf16[144,256]{1,0:T(8,128)(2,1)S(1)} %get-tuple-element.89), channel_id=1, source_target_pairs={{0,6},{1,7},{2,0},{3,1},{4,2},{5,3},{6,4},{7,5},{8,14},{9,15},{10,... | collective-permute-start | bytes 221192 | tf_op jit(solution)/shard_map/ppermute | solution.py:463
  83.8 5.1 %collective-permute-start.17 = (bf16[144,256]{1,0:T(8,128)(2,1)S(1)}, bf16[144,256]{1,0:T(8,128)(2,1)S(1)}, u32[]{:S(2)}, u32[]{:S(2)}) collective-permute-start(bf16[144,256]{1,0:T(8,128)(2,1)S(1)} %shard_map.113.refs_0_), channel_id=1, source_target_pairs={{0,6},{1,7},{2,0},{3,1},{4,2},{5,3},{6,4},{7,5},{8,14},{9,15},{10,... | collective-permute-start | bytes 221192 | tf_op jit(solution)/shard_map/ppermute | solution.py:472
  86.4 5.3 %collective-permute-start.16 = (bf16[144,256]{1,0:T(8,128)(2,1)S(1)}, bf16[144,256]{1,0:T(8,128)(2,1)S(1)}, u32[]{:S(2)}, u32[]{:S(2)}) collective-permute-start(bf16[144,256]{1,0:T(8,128)(2,1)S(1)} %shard_map.113.refs_0_), channel_id=1, source_target_pairs={{0,4},{1,5},{2,6},{3,7},{4,0},{5,1},{6,2},{7,3},{8,12},{9,13},{10,... | collective-permute-start | bytes 221192 | tf_op jit(solution)/shard_map/ppermute | solution.py:472
  86.7 6.2 %collective-permute-start.15 = (bf16[144,256]{1,0:T(8,128)(2,1)S(1)}, bf16[144,256]{1,0:T(8,128)(2,1)S(1)}, u32[]{:S(2)}, u32[]{:S(2)}) collective-permute-start(bf16[144,256]{1,0:T(8,128)(2,1)S(1)} %shard_map.113.refs_0_), channel_id=1, source_target_pairs={{0,2},{1,3},{2,4},{3,5},{4,6},{5,7},{6,0},{7,1},{8,10},{9,11},{10,... | collective-permute-start | bytes 221192 | tf_op jit(solution)/shard_map/ppermute | solution.py:472
  92.9 1.6 %collective-permute-start.18 = (bf16[576,256]{1,0:T(8,128)(2,1)S(1)}, bf16[576,256]{1,0:T(8,128)(2,1)S(1)}, u32[]{:S(2)}, u32[]{:S(2)}) collective-permute-start(bf16[576,256]{1,0:T(8,128)(2,1)S(1)} %shard_map.114.mine_ref), channel_id=1, source_target_pairs={{0,1},{1,0},{2,3},{3,2},{4,5},{5,4},{6,7},{7,6},{8,9},{9,8},{10,11... | collective-permute-start | bytes 884744 | tf_op jit(solution)/shard_map/ppermute | solution.py:481

commit v5 on v4

--- a/solution.py
+++ b/solution.py
@@ -256,48 +256,63 @@
                 piece = jnp.concatenate([vs[row : row + 16, :], jnp.zeros((8, 256), F32)])
                 gp[at, :] = gp[at, :] + pltpu.roll(piece, leads[n], 0)
 
-    def pair(n, carry):
-        batch(2, 2 * n)
+    def one(n, carry):
+        batch(1, n)
         return carry
 
-    lax.fori_loop(0, count // 2, pair, 0)
-
-    @pl.when(lax.rem(count, 2) == 1)
-    def _():
-        batch(1, count - 1)
-
-
-def finish_part(height, width, acc1, acc2, gp, keep, send, gp_own, gp_other):
+    lax.fori_loop(0, count, one, 0)
+
+
+def chunks_of(rows, chips):
+    unit = 16 * chips if rows >= 32 * chips else 16
+    cut = roundup(rows // 2, unit)
+    return ((0, cut), (cut, rows))
+
+
+def finish_part(height, width, dp, chips, acc1, acc2, gp, keep, sends, gp_own, gp_other):
     core = lax.rem(lax.axis_index("tile"), 2)
     cells = height * width
-
-    def write(acc, to):
+    rows = 2304 // dp
+    parts = chunks_of(rows, chips)
+
+    def write_keep(acc):
         for k in range(9):
-            to[k * 256 : k * 256 + 256, :] = acc[:, k * 256 : k * 256 + 256].T.astype(BF)
+            keep[k * 256 : k * 256 + 256, :] = acc[:, k * 256 : k * 256 + 256].T.astype(BF)
+
+    def write_sends(acc):
+        for k in range(9):
+            value = acc[:, k * 256 : k * 256 + 256].T.astype(BF)
+            for d in range(dp):
+                for to, (lo, hi) in zip(sends, parts):
+                    first = max(d * rows + lo, k * 256)
+                    end = min(d * rows + hi, k * 256 + 256)
+                    if first < end:
+                        at = d * (hi - lo) + first - d * rows - lo
+                        to[at : at + end - first, :] = value[first - k * 256 : end - k * 256, :]
 
     @pl.when(core == 0)
     def _():
-        write(acc1, keep)
-        write(acc2, send)
+        write_sends(acc2)
+        write_keep(acc1)
 
     @pl.when(core == 1)
     def _():
-        write(acc2, keep)
-        write(acc1, send)
+        write_sends(acc1)
+        write_keep(acc2)
 
     gp_own[...] = gp[pl.ds(pl.multiple_of(core * cells, cells), cells), :]
     gp_other[...] = gp[pl.ds(pl.multiple_of((1 - core) * cells, cells), cells), :].astype(BF)
 
 
-def main_call(side, height, width, first, last, state, weights, blocks):
+def main_call(side, height, width, dp, chips, first, last, state, weights, blocks):
     n = len(blocks)
     big = 2 * height * width + 16
-    cells = (2 * side + 1) * PITCH
+    cells = side * PITCH
     kept = (sds((big, 256), F32),) + (sds((2304, 256), BF),) * 4
     sums = (sds((256, 2304), F32), sds((256, 2304), F32), sds((big, 256), F32))
     ends = (
         sds((2304, 256), BF),
-        sds((2304, 256), BF),
+        *(sds((dp * (hi - lo), 256), BF) for lo, hi in chunks_of(2304 // dp, chips)),
         sds((height * width, 256), F32),
         sds((height * width, 256), BF),
     )
@@ -306,7 +321,7 @@
         pltpu.VMEM((cells + 32, 768), BF),
         pltpu.VMEM((cells + 32, 768), BF),
         pltpu.VMEM((cells + 32, 768), BF),
-        pltpu.VMEM((2, SLOT, 256), F32),
+        pltpu.VMEM((1, SLOT, 256), F32),
         pltpu.VMEM((cells, 256), F32),
         pltpu.VMEM((cells, 256), F32),
         pltpu.SMEM((3, 128), jnp.int32),
@@ -358,7 +373,8 @@
             side, height, width, block_refs, pyr, w1, w2, wb1, wb2, acc1, acc2, gp, scratch_refs
         )
         if last:
-            finish_part(height, width, acc1, acc2, gp, *out_refs[-4:])
+            keep, *sends, gp_own, gp_other = out_refs[3:]
+            finish_part(height, width, dp, chips, acc1, acc2, gp, keep, sends, gp_own, gp_other)
 
     aliases = {} if first else {5: 0, 6: 1, 7: 2}
     return run(
@@ -381,120 +397,154 @@
     return (a.astype(F32) + b.astype(F32)).astype(BF)
 
 
-def reduce_weights(keep, send, core_swap, dp, chips, beside):
+def reduce_weights(keep, sends, core_swap, dp, chips, beside):
     rows = keep.shape[0] // dp
     bits = dp.bit_length() - 1
-    low = roundup(rows // 2, 16)
-    spans = ((0, low), (low, rows))
     orders = (list(range(bits)), list(reversed(range(bits))))
-    got = lax.ppermute(send, "tile", core_swap)
-
-    def split(members, order):
-        bit = 1 << order[0]
+    shifts = [
+        [(2 * z + c, 2 * ((z + k) % chips) + c) for z in range(chips) for c in range(2)]
+        for k in range(chips)
+    ]
+    arrived = [lax.ppermute(send, "tile", core_swap) for send in sends]
+
+    def split(members, bit):
         return [m for m in members if not m & bit], [m for m in members if m & bit]
 
-    members = [list(range(dp)), list(range(dp))]
-    shapes = []
-    for half in range(2):
-        size = spans[half][1] - spans[half][0]
-        stay, go = split(members[half], orders[half])
-        shapes += [sds((len(stay), size, 256), BF), sds((len(go), size, 256), BF)]
-
-    def first(keep_ref, got_ref, *outs):
-        me = lax.axis_index("dp")
+    class Chunk:
+        pass
+
+    def begin(lo, hi, got):
+        c = Chunk()
+        c.rows = hi - lo
+        low = roundup(c.rows // 2, 16)
+        c.spans = ((0, low), (low, c.rows))
+        c.members = [list(range(dp)), list(range(dp))]
+
+        def first(keep_ref, got_ref, *outs):
+            me = lax.axis_index("dp")
+            for half in range(2):
+                start, size = c.spans[half][0], c.spans[half][1] - c.spans[half][0]
+                groups = split(c.members[half], 1 << orders[half][0])
+                for out, group in zip(outs[2 * half : 2 * half + 2], groups):
+                    for n, m in enumerate(group):
+                        a = pl.ds(pl.multiple_of((me ^ m) * rows + lo + start, 16), size)
+                        b = pl.ds(pl.multiple_of((me ^ m) * c.rows + start, 16), size)
+                        out[n] = add(keep_ref[a, :], got_ref[b, :])
+
+        shapes = []
         for half in range(2):
-            lo, hi = spans[half]
-            for out, group in zip(outs[2 * half : 2 * half + 2], split(members[half], orders[half])):
-                for n, m in enumerate(group):
-                    at = pl.ds(pl.multiple_of((me ^ m) * rows + lo, 16), hi - lo)
-                    out[n] = add(keep_ref[at, :], got_ref[at, :])
-
-    parts = local_kernel(first, tuple(shapes), keep, got)
-    for stage in range(bits):
-        received = []
+            shapes += [sds((dp // 2, c.spans[half][1] - c.spans[half][0], 256), BF)] * 2
+        c.parts = local_kernel(first, tuple(shapes), keep, got)
+        return c
+
+    def exchange(c, stage):
+        c.received = []
         for half in range(2):
             bit = 1 << orders[half][stage]
-            received.append(lax.ppermute(parts[2 * half + 1], "dp", [(i, i ^ bit) for i in range(dp)]))
-        if stage == 0:
-            received[0], beside = lax.optimization_barrier((received[0], beside))
-        for half in range(2):
-            members[half] = split(members[half], orders[half][stage:])[0]
-        if stage == bits - 1:
-            break
+            pairs = [(i, i ^ bit) for i in range(dp)]
+            c.received.append(lax.ppermute(c.parts[2 * half + 1], "dp", pairs))
+            c.members[half] = split(c.members[half], bit)[0]
+
+    def halve(c, stage):
         shapes = []
         for half in range(2):
-            size = spans[half][1] - spans[half][0]
-            stay, go = split(members[half], orders[half][stage + 1 :])
-            shapes += [sds((len(stay), size, 256), BF), sds((len(go), size, 256), BF)]
-
-        def middle(p, pr, q, qr, *outs, stage=stage):
+            size = c.spans[half][1] - c.spans[half][0]
+            shapes += [sds((len(c.members[half]) // 2, size, 256), BF)] * 2
+        members = [list(m) for m in c.members]
+
+        def kernel(p, pr, q, qr, *outs):
             for half, (mine, theirs) in enumerate(((p, pr), (q, qr))):
-                groups = split(members[half], orders[half][stage + 1 :])
+                groups = split(members[half], 1 << orders[half][stage])
                 for out, group in zip(outs[2 * half : 2 * half + 2], groups):
                     for n, m in enumerate(group):
                         k = members[half].index(m)
                         out[n] = add(mine[k], theirs[k])
 
-        parts = local_kernel(middle, tuple(shapes), parts[0], received[0], parts[2], received[1])
-
-    share = roundup(-(-rows // chips), 16)
-    shifts = [
-        [(2 * z + c, 2 * ((z + k) % chips) + c) for z in range(chips) for c in range(2)]
-        for k in range(chips)
-    ]
-
-    def deal(p, pr, q, qr, *refs):
-        outs, total = refs[:chips], refs[chips]
-        chip = lax.axis_index("tile") // 2
-        total[0:low, :] = add(p[0], pr[0])
-        total[low:rows, :] = add(q[0], qr[0])
-        if share * chips > rows:
-            total[rows:, :] = jnp.zeros((share * chips - rows, 256), BF)
-        for k in range(chips):
-            to = lax.rem(chip + k, chips)
-            outs[k][...] = total[pl.ds(pl.multiple_of(to * share, 16), share), :]
-
-    dealt = local_kernel(
-        deal,
-        tuple(sds((share, 256), BF) for _ in range(chips)),
-        *(parts[0], received[0], parts[2], received[1]),
-        scratch=[pltpu.VMEM((share * chips, 256), BF)],
-    )
-    arrived = [lax.ppermute(dealt[k], "tile", shifts[k]) for k in range(1, chips)]
-
-    def gather(*refs):
-        total = refs[0][...].astype(F32)
-        for ref in refs[1:-1]:
-            total += ref[...].astype(F32)
-        refs[-1][...] = total.astype(BF)
-
-    mine = local_kernel(gather, sds((share, 256), BF), dealt[0], *arrived)
-    pieces = [mine] + [lax.ppermute(mine, "tile", shifts[k]) for k in range(1, chips)]
-
-    def lay(*refs):
-        chip = lax.axis_index("tile") // 2
-        for k in range(chips):
-            source = lax.rem(chip - k + chips, chips)
-            refs[-1][pl.ds(pl.multiple_of(source * share, 16), share), :] = refs[k][...]
-
-    whole = local_kernel(lay, sds((share * chips, 256), BF), *pieces)
-    theirs = lax.ppermute(whole, "tile", core_swap)
-
-    def out(mine_ref, theirs_ref, one, two):
+        c.parts = local_kernel(
+            kernel, tuple(shapes), c.parts[0], c.received[0], c.parts[2], c.received[1]
+        )
+
+    def deal(c):
+        c.share = roundup(-(-c.rows // chips), 16)
+        low = c.spans[0][1]
+
+        def kernel(p, pr, q, qr, *refs):
+            outs, total = refs[:chips], refs[chips]
+            chip = lax.axis_index("tile") // 2
+            total[0:low, :] = add(p[0], pr[0])
+            total[low : c.rows, :] = add(q[0], qr[0])
+            if c.share * chips > c.rows:
+                total[c.rows :, :] = jnp.zeros((c.share * chips - c.rows, 256), BF)
+            for k in range(chips):
+                to = lax.rem(chip + k, chips)
+                outs[k][...] = total[pl.ds(pl.multiple_of(to * c.share, 16), c.share), :]
+
+        dealt = local_kernel(
+            kernel,
+            tuple(sds((c.share, 256), BF) for _ in range(chips)),
+            *(c.parts[0], c.received[0], c.parts[2], c.received[1]),
+            scratch=[pltpu.VMEM((c.share * chips, 256), BF)],
+        )
+        c.mine = dealt[0]
+        c.others = [lax.ppermute(dealt[k], "tile", shifts[k]) for k in range(1, chips)]
+
+    def gather(c):
+        def kernel(*refs):
+            total = refs[0][...].astype(F32)
+            for ref in refs[1:-1]:
+                total += ref[...].astype(F32)
+            refs[-1][...] = total.astype(BF)
+
+        c.mine = local_kernel(kernel, sds((c.share, 256), BF), c.mine, *c.others)
+        c.others = [lax.ppermute(c.mine, "tile", shifts[k]) for k in range(1, chips)]
+
+    def lay(c):
+        def kernel(*refs):
+            chip = lax.axis_index("tile") // 2
+            for k in range(chips):
+                source = lax.rem(chip - k + chips, chips)
+                refs[-1][pl.ds(pl.multiple_of(source * c.share, 16), c.share), :] = refs[k][...]
+
+        c.whole = local_kernel(kernel, sds((c.share * chips, 256), BF), c.mine, *c.others)
+        c.theirs = lax.ppermute(c.whole, "tile", core_swap)
+
+    spans = chunks_of(rows, chips)
+    chunks = [begin(lo, hi, got) for (lo, hi), got in zip(spans, arrived)]
+    for c in chunks:
+        exchange(c, 0)
+    chunks[0].received[0], beside = lax.optimization_barrier((chunks[0].received[0], beside))
+    for stage in range(1, bits):
+        for c in chunks:
+            halve(c, stage)
+            exchange(c, stage)
+    for step in (deal, gather, lay):
+        for c in chunks:
+            step(c)
+
+    def out(*refs):
         core = lax.rem(lax.axis_index("tile"), 2)
+        one, two = refs[-2:]
+
+        def write(to, sources):
+            for (lo, hi), source in zip(spans, sources):
+                to[lo:hi, :] = source[0 : hi - lo, :].astype(F32)
 
         @pl.when(core == 0)
         def _():
-            one[...] = mine_ref[0:rows, :].astype(F32)
-            two[...] = theirs_ref[0:rows, :].astype(F32)
+            write(one, refs[0:2])
+            write(two, refs[2:4])
 
         @pl.when(core == 1)
         def _():
-            one[...] = theirs_ref[0:rows, :].astype(F32)
-            two[...] = mine_ref[0:rows, :].astype(F32)
+            write(one, refs[2:4])
+            write(two, refs[0:2])
 
     one, two = local_kernel(
-        out, (sds((rows, 256), F32), sds((rows, 256), F32)), whole, theirs, hbm_out=(0, 1)
+        out,
+        (sds((rows, 256), F32), sds((rows, 256), F32)),
+        *(c.whole for c in chunks),
+        *(c.theirs for c in chunks),
+        hbm_out=(0, 1),
     )
     return one, two, beside
 
@@ -514,19 +564,21 @@
     rim_a = lax.ppermute(
         edge, "tile", [(i, i + 1 if i % 2 else i - 1) for i in range(1, tiles - 1)]
     )
-    across = [(i, i + 2 if i % 2 else i - 2) for i in range(tiles)]
-    rim_b = lax.ppermute(edge, "tile", [(i, j) for i, j in across if 0 <= j < tiles])
     other = lax.ppermute(tile, "tile", swap)
     packed = pack(cotangent[0].transpose(1, 2, 0, 3), height, place)
-    packed, rim_a, rim_b = lax.optimization_barrier((packed, rim_a, rim_b))
-
-    ring = [(i, (i + 2) % tiles) for i in range(tiles)]
+    packed, rim_a = lax.optimization_barrier((packed, rim_a))
+    rim_b = lax.ppermute(rim_a, "tile", swap)
+
+    order = [0] + list(range(1, chips, 2)) + list(range(2, chips, 2))[::-1]
+    ring = [
+        (2 * z + c, 2 * order[(k + 1) % chips] + c) for k, z in enumerate(order) for c in range(2)
+    ]
 
     flat = lambda w: w.reshape(9 * channels, channels)
     wf, w1, w2 = flat(fpn_weight), flat(mask_w1), flat(mask_w2)
     block = lax.ppermute(packed, "tile", ring)
     start = main_call(
-        side, height, width, True, False, [tile, other, rim_a, rim_b], [wf, w1, w2], [packed]
+        side, height, width, dp, chips, True, False, [tile, other, rim_a, rim_b], [wf, w1, w2], [packed]
     )
     kept, sums = list(start[:5]), list(start[5:])
     for step in range(1, chips):
@@ -536,11 +588,7 @@
             held, kept[0] = lax.optimization_barrier((held, kept[0]))
             block = lax.ppermute(held, "tile", ring)
         got = main_call(
-            side,
-            height,
-            width,
-            False,
-            last,
+            *(side, height, width, dp, chips, False, last),
             [*kept, *sums],
             [],
             [held],
@@ -548,7 +596,7 @@
         sums, ends = list(got[:3]), got[3:]
         if not last:
             kept[0], sums[0] = lax.optimization_barrier((kept[0], sums[0]))
-    keep, send, gp_own, gp_other = ends
+    keep, *sends, gp_own, gp_other = ends
     gp_got = lax.ppermute(gp_other, "tile", swap)
 
     def join(a, b, out):
@@ -557,7 +605,7 @@
     joined = local_kernel(
         join, sds((height * width, channels), BF), gp_own, gp_got, hbm_out=(0,)
     )
-    grad_one, grad_two, grad_pyramid = reduce_weights(keep, send, swap, dp, chips, joined)
+    grad_one, grad_two, grad_pyramid = reduce_weights(keep, sends, swap, dp, chips, joined)
     return grad_one, grad_two, grad_pyramid.reshape(1, height, width, channels)
 
 

time: 96.2 us -> 102 us (1.060)
  waiting for transfers between devices: 53.4 us -> 32.2 us
  Pallas kernels: 18.5 us -> 33.7 us
  starting transfers between devices: 22 us -> 33.7 us
    pallas_call x13 -> x18, Pallas kernels: 18.5 us -> 33.7 us  [run(): pl.pallas_call(kernel, out_shape=tuple((s if i in hbm_out else pltpu.VMEM...]
    ppermute x13 -> x25, starting transfers between devices: 16 us -> 25.9 us  [the longest x6 9.7 us: deal(): lax.ppermute(dealt[k], 'tile', shifts[k])]
    ppermute x13 -> x25, waiting for transfers between devices: 28 us -> 20.1 us  [the longest x8 7.25 us: exchange(): c.received.append(lax.ppermute(c.parts[2 * half + 1], 'dp', pairs))]
    ppermute x2, waiting for transfers between devices: 19.1 us -> 11.3 us  [body(): block = lax.ppermute(held, 'tile', ring)]
    ppermute x1, waiting for transfers between devices: 5.93 us -> 0.82 us  [body(): block = lax.ppermute(packed, 'tile', ring)]
    ppermute x1, starting transfers between devices: 3.73 us -> 5.36 us  [body(): block = lax.ppermute(packed, 'tile', ring)]
  transfers between devices with their start and end apart: 19 -> 31, of which waited for: 16 -> 17; matrix products, arithmetic and copies ran while one was open for 0% -> 0% of each run, Pallas kernels for 14% -> 25%
where the time goes in v5:
time: 102 us; the launch traced here: 101 us
  starting transfers between devices  33.7 us (33%)
  Pallas kernels  33.7 us (33%)
  waiting for transfers between devices  32.2 us (32%)
    pallas_call x18, Pallas kernels, run(): pl.pallas_call(kernel, out_shape=tuple((s if i in hbm_out else pltpu.VMEM...  33.7 us
    ppermute x2, waiting for transfers between devices, body(): block = lax.ppermute(held, 'tile', ring)  11.3 us
    ppermute x6, starting transfers between devices, deal(): lax.ppermute(dealt[k], 'tile', shifts[k])  9.7 us
    ppermute x6, starting transfers between devices, gather(): lax.ppermute(c.mine, 'tile', shifts[k])  8.43 us
    ppermute x8, waiting for transfers between devices, exchange(): c.received.append(lax.ppermute(c.parts[2 * half + 1], 'dp', pairs))  7.25 us
    ppermute x8, starting transfers between devices, exchange(): c.received.append(lax.ppermute(c.parts[2 * half + 1], 'dp', pairs))  6.88 us
    ppermute x1, starting transfers between devices, body(): block = lax.ppermute(packed, 'tile', ring)  5.36 us
    ppermute x6, waiting for transfers between devices, gather(): lax.ppermute(c.mine, 'tile', shifts[k])  4.96 us
  transfers between devices with their start and end apart: 31, of which 17 were waited for; matrix products, arithmetic and copies ran while one was open for 0% of the time, Pallas kernels for 25%

profile of v5, /device:TPU:0, one launch (start us, length us, event | category | flops | bytes accessed | tf_op | source)
XLA Modules:
  0.0 101.5 jit_solution(9793905092416090569)
XLA Ops:
  4.4 5.4 %collective-permute-start.1 = (bf16[4,208,256]{2,1,0:T(8,128)(2,1)S(1)}, bf16[4,208,256]{2,1,0:T(8,128)(2,1)S(1)}, u32[]{:S(2)}, u32[]{:S(2)}) collective-permute-start(bf16[4,208,256]{2,1,0:T(8,128)(2,1)S(1)} %shard_map.103.refs_7_), channel_id=1, source_target_pairs={{0,2},{1,3},{2,6},{3,7},{6,4},{7,5},{4,0},{5,1},{8,10},{9,11},{10,... | collective-permute-start | bytes 1277960 | tf_op jit(solution)/shard_map/ppermute | solution.py:579
  11.0 9.4 %shard_map.105 = (f32[2064,256]{1,0:T(8,128)S(1)}, bf16[2304,256]{1,0:T(8,128)(2,1)S(1)}, bf16[2304,256]{1,0:T(8,128)(2,1)S(1)}, bf16[2304,256]{1,0:T(8,128)(2,1...) custom-call(bf16[1024,256]{1,0:T(8,128)(2,1)} %bitcast.12, ...), custom_call_target="tpu_custom_call" | custom-call | tf_op jit(solution)/shard_map/pallas_call | solution.py:27
  22.0 6.4 %shard_map.106 = (f32[256,2304]{1,0:T(8,128)S(1)}, f32[256,2304]{1,0:T(8,128)S(1)}, f32[2064,256]{1,0:T(8,128)S(1)}) custom-call(f32[2064,256]{1,0:T(8,128)S(1)} %get-tuple-element.80.refs_0_, bf16[2304,256]{1,0:T(8,128)(2,1)S(1)} %get-tuple-element.65.refs_1_, ...), custom_call_target="tpu_custom_call", output_to_operand_aliasing={{0}: (5, {}), {1}: (6, {}), {2}: (7, {})} | custom-call | tf_op jit(solution)/shard_map/pallas_call | solution.py:27
  28.4 4.8 %collective-permute-done.4.refs_8_ = bf16[4,208,256]{2,1,0:T(8,128)(2,1)S(1)} collective-permute-done((bf16[4,208,256]{2,1,0:T(8,128)(2,1)S(1)}, bf16[4,208,256]{2,1,0:T(8,128)(2,1)S(1)}, u32[]{:S(2)}, u32[]{:S(2)}) %collective-permute-start.4) | collective-permute-done | bytes 426016 | tf_op jit(solution)/shard_map/ppermute | solution.py:589
  33.5 6.4 %shard_map.107 = (f32[256,2304]{1,0:T(8,128)S(1)}, f32[256,2304]{1,0:T(8,128)S(1)}, f32[2064,256]{1,0:T(8,128)S(1)}) custom-call(f32[2064,256]{1,0:T(8,128)S(1)} %get-tuple-element.80.refs_0_, bf16[2304,256]{1,0:T(8,128)(2,1)S(1)} %get-tuple-element.65.refs_1_, ...), custom_call_target="tpu_custom_call", output_to_operand_aliasing={{0}: (5, {}), {1}: (6, {}), {2}: (7, {})} | custom-call | tf_op jit(solution)/shard_map/pallas_call | solution.py:27
  39.9 6.5 %collective-permute-done.5.refs_8_ = bf16[4,208,256]{2,1,0:T(8,128)(2,1)S(1)} collective-permute-done((bf16[4,208,256]{2,1,0:T(8,128)(2,1)S(1)}, bf16[4,208,256]{2,1,0:T(8,128)(2,1)S(1)}, u32[]{:S(2)}, u32[]{:S(2)}) %collective-permute-start.5) | collective-permute-done | bytes 426016 | tf_op jit(solution)/shard_map/ppermute | solution.py:589
  46.4 7.4 %shard_map.108 = (f32[256,2304]{1,0:T(8,128)S(1)}, f32[256,2304]{1,0:T(8,128)S(1)}, f32[2064,256]{1,0:T(8,128)S(1)}, bf16[2304,256]{1,0:T(8,128)(2,1)S(1)}, bf16...) custom-call(f32[2064,256]{1,0:T(8,128)S(1)} %get-tuple-element.80.re, ...), custom_call_target="tpu_custom_call", output_to_operand_aliasing={{0}: (5, {}), {1}: (6, {}), {2}: (7, {})} | custom-call | tf_op jit(solution)/shard_map/pallas_call | solution.py:27
  54.6 1.4 %collective-permute-done.6.got_ref = bf16[1280,256]{1,0:T(8,128)(2,1)S(1)} collective-permute-done((bf16[1280,256]{1,0:T(8,128)(2,1)S(1)}, bf16[1280,256]{1,0:T(8,128)(2,1)S(1)}, u32[]{:S(2)}, u32[]{:S(2)}) %collective-permute-start.6) | collective-permute-done | bytes 655392 | tf_op jit(solution)/shard_map/ppermute | solution.py:408
  56.1 3.0 %collective-permute-start.7 = (bf16[2,160,256]{2,1,0:T(8,128)(2,1)S(1)}, bf16[2,160,256]{2,1,0:T(8,128)(2,1)S(1)}, u32[]{:S(2)}, u32[]{:S(2)}) collective-permute-start(bf16[2,160,256]{2,1,0:T(8,128)(2,1)S(1)} %get-tuple-element.87), channel_id=1, source_target_pairs={{0,8},{8,0},{16,24},{24,16},{1,9},{9,1},{17,25},{25,17},{2,10},{10... | collective-permute-start | bytes 491528 | tf_op jit(solution)/shard_map/ppermute | solution.py:445
  59.8 1.6 %collective-permute-start.20 = (bf16[2,128,256]{2,1,0:T(8,128)(2,1)S(1)}, bf16[2,128,256]{2,1,0:T(8,128)(2,1)S(1)}, u32[]{:S(2)}, u32[]{:S(2)}) collective-permute-start(bf16[2,128,256]{2,1,0:T(8,128)(2,1)S(1)} %get-tuple-element.105), channel_id=1, source_target_pairs={{0,16},{8,24},{16,0},{24,8},{1,17},{9,25},{17,1},{25,9},{2,18},{10... | collective-permute-start | bytes 393224 | tf_op jit(solution)/shard_map/ppermute | solution.py:445
  62.2 1.9 %collective-permute-done.7.pr = bf16[2,160,256]{2,1,0:T(8,128)(2,1)S(1)} collective-permute-done((bf16[2,160,256]{2,1,0:T(8,128)(2,1)S(1)}, bf16[2,160,256]{2,1,0:T(8,128)(2,1)S(1)}, u32[]{:S(2)}, u32[]{:S(2)}) %collective-permute-start.7) | collective-permute-done | bytes 163872 | tf_op jit(solution)/shard_map/ppermute | solution.py:445
  64.1 2.0 %collective-permute-done.9.qr = bf16[2,160,256]{2,1,0:T(8,128)(2,1)S(1)} collective-permute-done((bf16[2,160,256]{2,1,0:T(8,128)(2,1)S(1)}, bf16[2,160,256]{2,1,0:T(8,128)(2,1)S(1)}, u32[]{:S(2)}, u32[]{:S(2)}) %collective-permute-start.9) | collective-permute-done | bytes 163872 | tf_op jit(solution)/shard_map/ppermute | solution.py:445
  66.6 2.2 %collective-permute-done.20.qr = bf16[2,128,256]{2,1,0:T(8,128)(2,1)S(1)} collective-permute-done((bf16[2,128,256]{2,1,0:T(8,128)(2,1)S(1)}, bf16[2,128,256]{2,1,0:T(8,128)(2,1)S(1)}, u32[]{:S(2)}, u32[]{:S(2)}) %collective-permute-start.20) | collective-permute-done | bytes 131104 | tf_op jit(solution)/shard_map/ppermute | solution.py:445
  68.9 1.5 %collective-permute-start.22 = (bf16[1,128,256]{2,1,0:T(8,128)(2,1)S(1)}, bf16[1,128,256]{2,1,0:T(8,128)(2,1)S(1)}, u32[]{:S(2)}, u32[]{:S(2)}) collective-permute-start(bf16[1,128,256]{2,1,0:T(8,128)(2,1)S(1)} %get-tuple-element.109), channel_id=1, source_target_pairs={{0,8},{8,0},{16,24},{24,16},{1,9},{9,1},{17,25},{25,17},{2,10},{10... | collective-permute-start | bytes 196616 | tf_op jit(solution)/shard_map/ppermute | solution.py:445
  71.6 3.7 %collective-permute-start.14 = (bf16[80,256]{1,0:T(8,128)(2,1)S(1)}, bf16[80,256]{1,0:T(8,128)(2,1)S(1)}, u32[]{:S(2)}, u32[]{:S(2)}) collective-permute-start(bf16[80,256]{1,0:T(8,128)(2,1)S(1)} %get-tuple-element.100), channel_id=1, source_target_pairs={{0,6},{1,7},{2,0},{3,1},{4,2},{5,3},{6,4},{7,5},{8,14},{9,15},{10,... | collective-permute-start | bytes 122888 | tf_op jit(solution)/shard_map/ppermute | solution.py:489
  76.0 1.7 %collective-permute-done.12.refs_1_ = bf16[80,256]{1,0:T(8,128)(2,1)S(1)} collective-permute-done((bf16[80,256]{1,0:T(8,128)(2,1)S(1)}, bf16[80,256]{1,0:T(8,128)(2,1)S(1)}, u32[]{:S(2)}, u32[]{:S(2)}) %collective-permute-start.12) | collective-permute-done | bytes 40992 | tf_op jit(solution)/shard_map/ppermute | solution.py:489
  78.5 2.8 %collective-permute-start.17 = (bf16[80,256]{1,0:T(8,128)(2,1)S(1)}, bf16[80,256]{1,0:T(8,128)(2,1)S(1)}, u32[]{:S(2)}, u32[]{:S(2)}) collective-permute-start(bf16[80,256]{1,0:T(8,128)(2,1)S(1)} %shard_map.113.refs_0_), channel_id=1, source_target_pairs={{0,6},{1,7},{2,0},{3,1},{4,2},{5,3},{6,4},{7,5},{8,14},{9,15},{10,... | collective-permute-start | bytes 122888 | tf_op jit(solution)/shard_map/ppermute | solution.py:499
  81.9 2.3 %collective-permute-start.24 = (bf16[64,256]{1,0:T(8,128)(2,1)S(1)}, bf16[64,256]{1,0:T(8,128)(2,1)S(1)}, u32[]{:S(2)}, u32[]{:S(2)}) collective-permute-start(bf16[64,256]{1,0:T(8,128)(2,1)S(1)} %get-tuple-element.112), channel_id=1, source_target_pairs={{0,4},{1,5},{2,6},{3,7},{4,0},{5,1},{6,2},{7,3},{8,12},{9,13},{10,... | collective-permute-start | bytes 98312 | tf_op jit(solution)/shard_map/ppermute | solution.py:489
  84.2 2.9 %collective-permute-start.25 = (bf16[64,256]{1,0:T(8,128)(2,1)S(1)}, bf16[64,256]{1,0:T(8,128)(2,1)S(1)}, u32[]{:S(2)}, u32[]{:S(2)}) collective-permute-start(bf16[64,256]{1,0:T(8,128)(2,1)S(1)} %get-tuple-element.113), channel_id=1, source_target_pairs={{0,6},{1,7},{2,0},{3,1},{4,2},{5,3},{6,4},{7,5},{8,14},{9,15},{10,... | collective-permute-start | bytes 98312 | tf_op jit(solution)/shard_map/ppermute | solution.py:489
  87.2 1.7 %collective-permute-done.25.refs_3_ = bf16[64,256]{1,0:T(8,128)(2,1)S(1)} collective-permute-done((bf16[64,256]{1,0:T(8,128)(2,1)S(1)}, bf16[64,256]{1,0:T(8,128)(2,1)S(1)}, u32[]{:S(2)}, u32[]{:S(2)}) %collective-permute-start.25) | collective-permute-done | bytes 32800 | tf_op jit(solution)/shard_map/ppermute | solution.py:489
  88.9 4.3 %collective-permute-start.28 = (bf16[64,256]{1,0:T(8,128)(2,1)S(1)}, bf16[64,256]{1,0:T(8,128)(2,1)S(1)}, u32[]{:S(2)}, u32[]{:S(2)}) collective-permute-start(bf16[64,256]{1,0:T(8,128)(2,1)S(1)} %shard_map.118.refs_0_), channel_id=1, source_target_pairs={{0,6},{1,7},{2,0},{3,1},{4,2},{5,3},{6,4},{7,5},{8,14},{9,15},{10,... | collective-permute-start | bytes 98312 | tf_op jit(solution)/shard_map/ppermute | solution.py:499
  94.8 3.2 %collective-permute-done.27.refs_2_ = bf16[64,256]{1,0:T(8,128)(2,1)S(1)} collective-permute-done((bf16[64,256]{1,0:T(8,128)(2,1)S(1)}, bf16[64,256]{1,0:T(8,128)(2,1)S(1)}, u32[]{:S(2)}, u32[]{:S(2)}) %collective-permute-start.27) | collective-permute-done | bytes 32800 | tf_op jit(solution)/shard_map/ppermute | solution.py:499
  99.1 1.3 %collective-permute-done.30.refs_3_ = bf16[256,256]{1,0:T(8,128)(2,1)S(1)} collective-permute-done((bf16[256,256]{1,0:T(8,128)(2,1)S(1)}, bf16[256,256]{1,0:T(8,128)(2,1)S(1)}, u32[]{:S(2)}, u32[]{:S(2)}) %collective-permute-start.30) | collective-permute-done | bytes 131104 | tf_op jit(solution)/shard_map/ppermute | solution.py:509
  100.4 1.1 %shard_map.120 = (f32[576,256]{1,0:T(8,128)}, f32[576,256]{1,0:T(8,128)}) custom-call(bf16[320,256]{1,0:T(8,128)(2,1)S(1)} %shard_map.114.refs_0_, bf16[256,256]{1,0:T(8,128)(2,1)S(1)} %shard_map.119.refs_1_, bf16[320,256]{1,0:T(8,128)(2,1)S(1)} %collective-permute-done.29.refs_2_, bf16[256,256]{1,0:T(8,128)(2,1)S(1)} %collective-permute-done.30.refs_3_), custom_call_target="tpu_custom_call" | custom-call | tf_op jit(solution)/shard_map/pallas_call | solution.py:27
  (58 shorter events, 15.8 us)
Async XLA Ops:
  0.6 10.3 %collective-permute-start.2 = (bf16[1024,256]{1,0:T(8,128)(2,1)}, bf16[1024,256]{1,0:T(8,128)(2,1)S(1)}, u32[]{:S(2)}, u32[]{:S(2)}) collective-permute-start(bf16[1024,256]{1,0:T(8,128)(2,1)} %bitcast.10), channel_id=1, source_target_pairs={{0,1},{1,0},{2,3},{3,2},{4,5},{5,4},{6,7},{7,6},{8,9},{9,8},{10,11... | collective-permute-start | bytes 1572872 | tf_op jit(solution)/shard_map/ppermute | solution.py:567
  4.4 16.8 %collective-permute-start.1 = (bf16[4,208,256]{2,1,0:T(8,128)(2,1)S(1)}, bf16[4,208,256]{2,1,0:T(8,128)(2,1)S(1)}, u32[]{:S(2)}, u32[]{:S(2)}) collective-permute-start(bf16[4,208,256]{2,1,0:T(8,128)(2,1)S(1)} %shard_map.103.refs_7_), channel_id=1, source_target_pairs={{0,2},{1,3},{2,6},{3,7},{6,4},{7,5},{4,0},{5,1},{8,10},{9,11},{10,... | collective-permute-start | bytes 1277960 | tf_op jit(solution)/shard_map/ppermute | solution.py:579
  21.2 12.0 %collective-permute-start.4 = (bf16[4,208,256]{2,1,0:T(8,128)(2,1)S(1)}, bf16[4,208,256]{2,1,0:T(8,128)(2,1)S(1)}, u32[]{:S(2)}, u32[]{:S(2)}) collective-permute-start(bf16[4,208,256]{2,1,0:T(8,128)(2,1)S(1)} %collective-permute-done.1.refs_8_), channel_id=1, source_target_pairs={{0,2},{1,3},{2,6},{3,7},{6,4},{7,5},{4,0},{5,1},{8,10},{9,11},{10,... | collective-permute-start | bytes 1277960 | tf_op jit(solution)/shard_map/ppermute | solution.py:589
  33.2 13.2 %collective-permute-start.5 = (bf16[4,208,256]{2,1,0:T(8,128)(2,1)S(1)}, bf16[4,208,256]{2,1,0:T(8,128)(2,1)S(1)}, u32[]{:S(2)}, u32[]{:S(2)}) collective-permute-start(bf16[4,208,256]{2,1,0:T(8,128)(2,1)S(1)} %collective-permute-done.4.refs_8_), channel_id=1, source_target_pairs={{0,2},{1,3},{2,6},{3,7},{6,4},{7,5},{4,0},{5,1},{8,10},{9,11},{10,... | collective-permute-start | bytes 1277960 | tf_op jit(solution)/shard_map/ppermute | solution.py:589
  54.3 7.0 %collective-permute-start.8 = (bf16[1024,256]{1,0:T(8,128)(2,1)S(1)}, bf16[1024,256]{1,0:T(8,128)(2,1)S(1)}, u32[]{:S(2)}, u32[]{:S(2)}) collective-permute-start(bf16[1024,256]{1,0:T(8,128)(2,1)S(1)} %get-tuple-element.89), channel_id=1, source_target_pairs={{0,1},{1,0},{2,3},{3,2},{4,5},{5,4},{6,7},{7,6},{8,9},{9,8},{10,11... | collective-permute-start | bytes 1572872 | tf_op jit(solution)/shard_map/ppermute | solution.py:600
  56.1 8.0 %collective-permute-start.7 = (bf16[2,160,256]{2,1,0:T(8,128)(2,1)S(1)}, bf16[2,160,256]{2,1,0:T(8,128)(2,1)S(1)}, u32[]{:S(2)}, u32[]{:S(2)}) collective-permute-start(bf16[2,160,256]{2,1,0:T(8,128)(2,1)S(1)} %get-tuple-element.87), channel_id=1, source_target_pairs={{0,8},{8,0},{16,24},{24,16},{1,9},{9,1},{17,25},{25,17},{2,10},{10... | collective-permute-start | bytes 491528 | tf_op jit(solution)/shard_map/ppermute | solution.py:445
  59.0 7.1 %collective-permute-start.9 = (bf16[2,160,256]{2,1,0:T(8,128)(2,1)S(1)}, bf16[2,160,256]{2,1,0:T(8,128)(2,1)S(1)}, u32[]{:S(2)}, u32[]{:S(2)}) collective-permute-start(bf16[2,160,256]{2,1,0:T(8,128)(2,1)S(1)} %get-tuple-element.92), channel_id=1, source_target_pairs={{0,16},{8,24},{16,0},{24,8},{1,17},{9,25},{17,1},{25,9},{2,18},{10... | collective-permute-start | bytes 491528 | tf_op jit(solution)/shard_map/ppermute | solution.py:445
  59.2 7.4 %collective-permute-start.19 = (bf16[2,128,256]{2,1,0:T(8,128)(2,1)S(1)}, bf16[2,128,256]{2,1,0:T(8,128)(2,1)S(1)}, u32[]{:S(2)}, u32[]{:S(2)}) collective-permute-start(bf16[2,128,256]{2,1,0:T(8,128)(2,1)S(1)} %get-tuple-element.103), channel_id=1, source_target_pairs={{0,8},{8,0},{16,24},{24,16},{1,9},{9,1},{17,25},{25,17},{2,10},{10... | collective-permute-start | bytes 393224 | tf_op jit(solution)/shard_map/ppermute | solution.py:445
  59.8 9.0 %collective-permute-start.20 = (bf16[2,128,256]{2,1,0:T(8,128)(2,1)S(1)}, bf16[2,128,256]{2,1,0:T(8,128)(2,1)S(1)}, u32[]{:S(2)}, u32[]{:S(2)}) collective-permute-start(bf16[2,128,256]{2,1,0:T(8,128)(2,1)S(1)} %get-tuple-element.105), channel_id=1, source_target_pairs={{0,16},{8,24},{16,0},{24,8},{1,17},{9,25},{17,1},{25,9},{2,18},{10... | collective-permute-start | bytes 393224 | tf_op jit(solution)/shard_map/ppermute | solution.py:445
  66.2 5.2 %collective-permute-start.10 = (bf16[1,160,256]{2,1,0:T(8,128)(2,1)S(1)}, bf16[1,160,256]{2,1,0:T(8,128)(2,1)S(1)}, u32[]{:S(2)}, u32[]{:S(2)}) collective-permute-start(bf16[1,160,256]{2,1,0:T(8,128)(2,1)S(1)} %get-tuple-element.94), channel_id=1, source_target_pairs={{0,16},{8,24},{16,0},{24,8},{1,17},{9,25},{17,1},{25,9},{2,18},{10... | collective-permute-start | bytes 245768 | tf_op jit(solution)/shard_map/ppermute | solution.py:445
  66.3 5.1 %collective-permute-start.11 = (bf16[1,160,256]{2,1,0:T(8,128)(2,1)S(1)}, bf16[1,160,256]{2,1,0:T(8,128)(2,1)S(1)}, u32[]{:S(2)}, u32[]{:S(2)}) collective-permute-start(bf16[1,160,256]{2,1,0:T(8,128)(2,1)S(1)} %get-tuple-element.96), channel_id=1, source_target_pairs={{0,8},{8,0},{16,24},{24,16},{1,9},{9,1},{17,25},{25,17},{2,10},{10... | collective-permute-start | bytes 245768 | tf_op jit(solution)/shard_map/ppermute | solution.py:445
  68.9 6.5 %collective-permute-start.21 = (bf16[1,128,256]{2,1,0:T(8,128)(2,1)S(1)}, bf16[1,128,256]{2,1,0:T(8,128)(2,1)S(1)}, u32[]{:S(2)}, u32[]{:S(2)}) collective-permute-start(bf16[1,128,256]{2,1,0:T(8,128)(2,1)S(1)} %get-tuple-element.107), channel_id=1, source_target_pairs={{0,16},{8,24},{16,0},{24,8},{1,17},{9,25},{17,1},{25,9},{2,18},{10... | collective-permute-start | bytes 196616 | tf_op jit(solution)/shard_map/ppermute | solution.py:445
  68.9 6.4 %collective-permute-start.22 = (bf16[1,128,256]{2,1,0:T(8,128)(2,1)S(1)}, bf16[1,128,256]{2,1,0:T(8,128)(2,1)S(1)}, u32[]{:S(2)}, u32[]{:S(2)}) collective-permute-start(bf16[1,128,256]{2,1,0:T(8,128)(2,1)S(1)} %get-tuple-element.109), channel_id=1, source_target_pairs={{0,8},{8,0},{16,24},{24,16},{1,9},{9,1},{17,25},{25,17},{2,10},{10... | collective-permute-start | bytes 196616 | tf_op jit(solution)/shard_map/ppermute | solution.py:445
  71.4 6.2 %collective-permute-start.12 = (bf16[80,256]{1,0:T(8,128)(2,1)S(1)}, bf16[80,256]{1,0:T(8,128)(2,1)S(1)}, u32[]{:S(2)}, u32[]{:S(2)}) collective-permute-start(bf16[80,256]{1,0:T(8,128)(2,1)S(1)} %get-tuple-element.98), channel_id=1, source_target_pairs={{0,2},{1,3},{2,4},{3,5},{4,6},{5,7},{6,0},{7,1},{8,10},{9,11},{10,... | collective-permute-start | bytes 122888 | tf_op jit(solution)/shard_map/ppermute | solution.py:489
  71.5 6.2 %collective-permute-start.13 = (bf16[80,256]{1,0:T(8,128)(2,1)S(1)}, bf16[80,256]{1,0:T(8,128)(2,1)S(1)}, u32[]{:S(2)}, u32[]{:S(2)}) collective-permute-start(bf16[80,256]{1,0:T(8,128)(2,1)S(1)} %get-tuple-element.99), channel_id=1, source_target_pairs={{0,4},{1,5},{2,6},{3,7},{4,0},{5,1},{6,2},{7,3},{8,12},{9,13},{10,... | collective-permute-start | bytes 122888 | tf_op jit(solution)/shard_map/ppermute | solution.py:489
  71.6 6.9 %collective-permute-start.14 = (bf16[80,256]{1,0:T(8,128)(2,1)S(1)}, bf16[80,256]{1,0:T(8,128)(2,1)S(1)}, u32[]{:S(2)}, u32[]{:S(2)}) collective-permute-start(bf16[80,256]{1,0:T(8,128)(2,1)S(1)} %get-tuple-element.100), channel_id=1, source_target_pairs={{0,6},{1,7},{2,0},{3,1},{4,2},{5,3},{6,4},{7,5},{8,14},{9,15},{10,... | collective-permute-start | bytes 122888 | tf_op jit(solution)/shard_map/ppermute | solution.py:489
  75.4 8.9 %collective-permute-start.23 = (bf16[64,256]{1,0:T(8,128)(2,1)S(1)}, bf16[64,256]{1,0:T(8,128)(2,1)S(1)}, u32[]{:S(2)}, u32[]{:S(2)}) collective-permute-start(bf16[64,256]{1,0:T(8,128)(2,1)S(1)} %get-tuple-element.111), channel_id=1, source_target_pairs={{0,2},{1,3},{2,4},{3,5},{4,6},{5,7},{6,0},{7,1},{8,10},{9,11},{10,... | collective-permute-start | bytes 98312 | tf_op jit(solution)/shard_map/ppermute | solution.py:489
  78.5 14.8 %collective-permute-start.17 = (bf16[80,256]{1,0:T(8,128)(2,1)S(1)}, bf16[80,256]{1,0:T(8,128)(2,1)S(1)}, u32[]{:S(2)}, u32[]{:S(2)}) collective-permute-start(bf16[80,256]{1,0:T(8,128)(2,1)S(1)} %shard_map.113.refs_0_), channel_id=1, source_target_pairs={{0,6},{1,7},{2,0},{3,1},{4,2},{5,3},{6,4},{7,5},{8,14},{9,15},{10,... | collective-permute-start | bytes 122888 | tf_op jit(solution)/shard_map/ppermute | solution.py:499
  81.3 12.6 %collective-permute-start.16 = (bf16[80,256]{1,0:T(8,128)(2,1)S(1)}, bf16[80,256]{1,0:T(8,128)(2,1)S(1)}, u32[]{:S(2)}, u32[]{:S(2)}) collective-permute-start(bf16[80,256]{1,0:T(8,128)(2,1)S(1)} %shard_map.113.refs_0_), channel_id=1, source_target_pairs={{0,4},{1,5},{2,6},{3,7},{4,0},{5,1},{6,2},{7,3},{8,12},{9,13},{10,... | collective-permute-start | bytes 122888 | tf_op jit(solution)/shard_map/ppermute | solution.py:499
  81.9 12.0 %collective-permute-start.15 = (bf16[80,256]{1,0:T(8,128)(2,1)S(1)}, bf16[80,256]{1,0:T(8,128)(2,1)S(1)}, u32[]{:S(2)}, u32[]{:S(2)}) collective-permute-start(bf16[80,256]{1,0:T(8,128)(2,1)S(1)} %shard_map.113.refs_0_), channel_id=1, source_target_pairs={{0,2},{1,3},{2,4},{3,5},{4,6},{5,7},{6,0},{7,1},{8,10},{9,11},{10,... | collective-permute-start | bytes 122888 | tf_op jit(solution)/shard_map/ppermute | solution.py:499
  81.9 5.2 %collective-permute-start.24 = (bf16[64,256]{1,0:T(8,128)(2,1)S(1)}, bf16[64,256]{1,0:T(8,128)(2,1)S(1)}, u32[]{:S(2)}, u32[]{:S(2)}) collective-permute-start(bf16[64,256]{1,0:T(8,128)(2,1)S(1)} %get-tuple-element.112), channel_id=1, source_target_pairs={{0,4},{1,5},{2,6},{3,7},{4,0},{5,1},{6,2},{7,3},{8,12},{9,13},{10,... | collective-permute-start | bytes 98312 | tf_op jit(solution)/shard_map/ppermute | solution.py:489
  88.9 5.9 %collective-permute-start.28 = (bf16[64,256]{1,0:T(8,128)(2,1)S(1)}, bf16[64,256]{1,0:T(8,128)(2,1)S(1)}, u32[]{:S(2)}, u32[]{:S(2)}) collective-permute-start(bf16[64,256]{1,0:T(8,128)(2,1)S(1)} %shard_map.118.refs_0_), channel_id=1, source_target_pairs={{0,6},{1,7},{2,0},{3,1},{4,2},{5,3},{6,4},{7,5},{8,14},{9,15},{10,... | collective-permute-start | bytes 98312 | tf_op jit(solution)/shard_map/ppermute | solution.py:499
  93.2 5.7 %collective-permute-start.26 = (bf16[64,256]{1,0:T(8,128)(2,1)S(1)}, bf16[64,256]{1,0:T(8,128)(2,1)S(1)}, u32[]{:S(2)}, u32[]{:S(2)}) collective-permute-start(bf16[64,256]{1,0:T(8,128)(2,1)S(1)} %shard_map.118.refs_0_), channel_id=1, source_target_pairs={{0,2},{1,3},{2,4},{3,5},{4,6},{5,7},{6,0},{7,1},{8,10},{9,11},{10,... | collective-permute-start | bytes 98312 | tf_op jit(solution)/shard_map/ppermute | solution.py:499
  93.9 6.5 %collective-permute-start.29 = (bf16[320,256]{1,0:T(8,128)(2,1)S(1)}, bf16[320,256]{1,0:T(8,128)(2,1)S(1)}, u32[]{:S(2)}, u32[]{:S(2)}) collective-permute-start(bf16[320,256]{1,0:T(8,128)(2,1)S(1)} %shard_map.114.refs_0_), channel_id=1, source_target_pairs={{0,1},{1,0},{2,3},{3,2},{4,5},{5,4},{6,7},{7,6},{8,9},{9,8},{10,11... | collective-permute-start | bytes 491528 | tf_op jit(solution)/shard_map/ppermute | solution.py:509
  (8 other events, 22.7 us)

commit v6 on v5

--- a/solution.py
+++ b/solution.py
@@ -263,17 +263,15 @@
     lax.fori_loop(0, count, one, 0)
 
 
-def chunks_of(rows, chips):
-    unit = 16 * chips if rows >= 32 * chips else 16
-    cut = roundup(rows // 2, unit)
-    return ((0, cut), (cut, rows))
+def chunks_of(rows):
+    return ((0, rows),)
 
 
 def finish_part(height, width, dp, chips, acc1, acc2, gp, keep, sends, gp_own, gp_other):
     core = lax.rem(lax.axis_index("tile"), 2)
     cells = height * width
     rows = 2304 // dp
-    parts = chunks_of(rows, chips)
+    parts = chunks_of(rows)
 
     def write_keep(acc):
         for k in range(9):
@@ -312,7 +310,7 @@
     sums = (sds((256, 2304), F32), sds((256, 2304), F32), sds((big, 256), F32))
     ends = (
         sds((2304, 256), BF),
-        *(sds((dp * (hi - lo), 256), BF) for lo, hi in chunks_of(2304 // dp, chips)),
+        *(sds((dp * (hi - lo), 256), BF) for lo, hi in chunks_of(2304 // dp)),
         sds((height * width, 256), F32),
         sds((height * width, 256), BF),
     )
@@ -508,7 +506,7 @@
         c.whole = local_kernel(kernel, sds((c.share * chips, 256), BF), c.mine, *c.others)
         c.theirs = lax.ppermute(c.whole, "tile", core_swap)
 
-    spans = chunks_of(rows, chips)
+    spans = chunks_of(rows)
     chunks = [begin(lo, hi, got) for (lo, hi), got in zip(spans, arrived)]
     for c in chunks:
         exchange(c, 0)
@@ -531,13 +529,13 @@
 
         @pl.when(core == 0)
         def _():
-            write(one, refs[0:2])
-            write(two, refs[2:4])
+            write(one, refs[0 : len(spans)])
+            write(two, refs[len(spans) : -2])
 
         @pl.when(core == 1)
         def _():
-            write(one, refs[2:4])
-            write(two, refs[0:2])
+            write(one, refs[len(spans) : -2])
+            write(two, refs[0 : len(spans)])
 
     one, two = local_kernel(
         out,

time: 102 us -> 95.8 us (0.939)
  starting transfers between devices: 33.7 us -> 23.6 us
  waiting for transfers between devices: 32.2 us -> 37.1 us
    ppermute x6 -> x3, starting transfers between devices: 9.7 us -> 3.86 us  [deal(): lax.ppermute(dealt[k], 'tile', shifts[k])]
    ppermute x8 -> x4, waiting for transfers between devices: 7.25 us -> 12.7 us  [exchange(): c.received.append(lax.ppermute(c.parts[2 * half + 1], 'dp', pairs))]
    ppermute x6 -> x3, starting transfers between devices: 8.43 us -> 3.28 us  [gather(): lax.ppermute(c.mine, 'tile', shifts[k])]
    ppermute x2, waiting for transfers between devices: 11.3 us -> 9.49 us  [body(): block = lax.ppermute(held, 'tile', ring)]
    ppermute x2, starting transfers between devices: 1.05 us -> 2.63 us  [body(): block = lax.ppermute(held, 'tile', ring)]
    ppermute x8 -> x4, starting transfers between devices: 6.88 us -> 5.37 us  [exchange(): c.received.append(lax.ppermute(c.parts[2 * half + 1], 'dp', pairs))]
    ppermute x6 -> x3, waiting for transfers between devices: 4.96 us -> 6.15 us  [gather(): lax.ppermute(c.mine, 'tile', shifts[k])]
    ppermute x2 -> x1, waiting for transfers between devices: 1.36 us -> 2.4 us  [reduce_weights(): arrived = [lax.ppermute(send, 'tile', core_swap) for send in sends]]
  transfers between devices with their start and end apart: 31 -> 19, of which waited for: 17 -> 14; matrix products, arithmetic and copies ran while one was open for 0% -> 0% of each run, Pallas kernels for 25% -> 29%
where the time goes in v6:
time: 95.8 us; the launch traced here: 96.2 us
  waiting for transfers between devices  37.1 us (39%)
  Pallas kernels  33.7 us (35%)
  starting transfers between devices  23.6 us (25%)
  local copies, waits for them, and re-layouts  0.99 us (1%)
    pallas_call x13, Pallas kernels, run(): pl.pallas_call(kernel, out_shape=tuple((s if i in hbm_out else pltpu.VMEM...  33.7 us
    ppermute x4, waiting for transfers between devices, exchange(): c.received.append(lax.ppermute(c.parts[2 * half + 1], 'dp', pairs))  12.7 us
    ppermute x2, waiting for transfers between devices, body(): block = lax.ppermute(held, 'tile', ring)  9.49 us
    ppermute x3, waiting for transfers between devices, gather(): lax.ppermute(c.mine, 'tile', shifts[k])  6.15 us
    ppermute x4, starting transfers between devices, exchange(): c.received.append(lax.ppermute(c.parts[2 * half + 1], 'dp', pairs))  5.37 us
    ppermute x1, starting transfers between devices, body(): block = lax.ppermute(packed, 'tile', ring)  5.36 us
    ppermute x3, starting transfers between devices, deal(): lax.ppermute(dealt[k], 'tile', shifts[k])  3.86 us
    ppermute x3, waiting for transfers between devices, deal(): lax.ppermute(dealt[k], 'tile', shifts[k])  3.83 us
  transfers between devices with their start and end apart: 19, of which 14 were waited for; matrix products, arithmetic and copies ran while one was open for 0% of the time, Pallas kernels for 29%

profile of v6, /device:TPU:0, one launch (start us, length us, event | category | flops | bytes accessed | tf_op | source)
XLA Modules:
  0.0 96.2 jit_solution(3675326892577036710)
XLA Ops:
  4.4 5.4 %collective-permute-start.1 = (bf16[4,208,256]{2,1,0:T(8,128)(2,1)S(1)}, bf16[4,208,256]{2,1,0:T(8,128)(2,1)S(1)}, u32[]{:S(2)}, u32[]{:S(2)}) collective-permute-start(bf16[4,208,256]{2,1,0:T(8,128)(2,1)S(1)} %shard_map.103.refs_7_), channel_id=1, source_target_pairs={{0,2},{1,3},{2,6},{3,7},{6,4},{7,5},{4,0},{5,1},{8,10},{9,11},{10,... | collective-permute-start | bytes 1277960 | tf_op jit(solution)/shard_map/ppermute | solution.py:577
  10.0 1.0 %collective-permute-done.3.refs_3_ = bf16[64,256]{1,0:T(8,128)(2,1)S(1)} collective-permute-done((bf16[64,256]{1,0:T(8,128)(2,1)S(1)}, bf16[64,256]{1,0:T(8,128)(2,1)S(1)}, u32[]{:S(2)}, u32[]{:S(2)}) %collective-permute-start.3) | collective-permute-done | bytes 32800 | tf_op jit(solution)/shard_map/ppermute | solution.py:568
  11.0 12.5 %shard_map.105 = (f32[2064,256]{1,0:T(8,128)S(1)}, bf16[2304,256]{1,0:T(8,128)(2,1)S(1)}, bf16[2304,256]{1,0:T(8,128)(2,1)S(1)}, bf16[2304,256]{1,0:T(8,128)(2,1...) custom-call(bf16[1024,256]{1,0:T(8,128)(2,1)} %bitcast.12, ...), custom_call_target="tpu_custom_call" | custom-call | tf_op jit(solution)/shard_map/pallas_call | solution.py:27
  23.5 2.6 %collective-permute-start.4 = (bf16[4,208,256]{2,1,0:T(8,128)(2,1)S(1)}, bf16[4,208,256]{2,1,0:T(8,128)(2,1)S(1)}, u32[]{:S(2)}, u32[]{:S(2)}) collective-permute-start(bf16[4,208,256]{2,1,0:T(8,128)(2,1)S(1)} %collective-permute-done.1.refs_8_), channel_id=1, source_target_pairs={{0,2},{1,3},{2,6},{3,7},{6,4},{7,5},{4,0},{5,1},{8,10},{9,11},{10,... | collective-permute-start | bytes 1277960 | tf_op jit(solution)/shard_map/ppermute | solution.py:587
  26.1 6.4 %shard_map.106 = (f32[256,2304]{1,0:T(8,128)S(1)}, f32[256,2304]{1,0:T(8,128)S(1)}, f32[2064,256]{1,0:T(8,128)S(1)}) custom-call(f32[2064,256]{1,0:T(8,128)S(1)} %get-tuple-element.67.refs_0_, bf16[2304,256]{1,0:T(8,128)(2,1)S(1)} %get-tuple-element.52.refs_1_, ...), custom_call_target="tpu_custom_call", output_to_operand_aliasing={{0}: (5, {}), {1}: (6, {}), {2}: (7, {})} | custom-call | tf_op jit(solution)/shard_map/pallas_call | solution.py:27
  32.5 3.9 %collective-permute-done.4.refs_8_ = bf16[4,208,256]{2,1,0:T(8,128)(2,1)S(1)} collective-permute-done((bf16[4,208,256]{2,1,0:T(8,128)(2,1)S(1)}, bf16[4,208,256]{2,1,0:T(8,128)(2,1)S(1)}, u32[]{:S(2)}, u32[]{:S(2)}) %collective-permute-start.4) | collective-permute-done | bytes 426016 | tf_op jit(solution)/shard_map/ppermute | solution.py:587
  36.4 6.4 %shard_map.107 = (f32[256,2304]{1,0:T(8,128)S(1)}, f32[256,2304]{1,0:T(8,128)S(1)}, f32[2064,256]{1,0:T(8,128)S(1)}) custom-call(f32[2064,256]{1,0:T(8,128)S(1)} %get-tuple-element.67.refs_0_, bf16[2304,256]{1,0:T(8,128)(2,1)S(1)} %get-tuple-element.52.refs_1_, ...), custom_call_target="tpu_custom_call", output_to_operand_aliasing={{0}: (5, {}), {1}: (6, {}), {2}: (7, {})} | custom-call | tf_op jit(solution)/shard_map/pallas_call | solution.py:27
  42.8 5.6 %collective-permute-done.5.refs_8_ = bf16[4,208,256]{2,1,0:T(8,128)(2,1)S(1)} collective-permute-done((bf16[4,208,256]{2,1,0:T(8,128)(2,1)S(1)}, bf16[4,208,256]{2,1,0:T(8,128)(2,1)S(1)}, u32[]{:S(2)}, u32[]{:S(2)}) %collective-permute-start.5) | collective-permute-done | bytes 426016 | tf_op jit(solution)/shard_map/ppermute | solution.py:587
  48.4 4.3 %shard_map.108 = (f32[256,2304]{1,0:T(8,128)S(1)}, f32[256,2304]{1,0:T(8,128)S(1)}, f32[2064,256]{1,0:T(8,128)S(1)}, bf16[2304,256]{1,0:T(8,128)(2,1)S(1)}, bf16...) custom-call(f32[2064,256]{1,0:T(8,128)S(1)} %get-tuple-element.67.re, ...), custom_call_target="tpu_custom_call", output_to_operand_aliasing={{0}: (5, {}), {1}: (6, {}), {2}: (7, {})} | custom-call | tf_op jit(solution)/shard_map/pallas_call | solution.py:27
  52.7 1.6 %collective-permute-start.6 = (bf16[2304,256]{1,0:T(8,128)(2,1)S(1)}, bf16[2304,256]{1,0:T(8,128)(2,1)S(1)}, u32[]{:S(2)}, u32[]{:S(2)}) collective-permute-start(bf16[2304,256]{1,0:T(8,128)(2,1)S(1)} %get-tuple-element.72), channel_id=1, source_target_pairs={{0,1},{1,0},{2,3},{3,2},{4,5},{5,4},{6,7},{7,6},{8,9},{9,8},{10,11... | collective-permute-start | bytes 3538952 | tf_op jit(solution)/shard_map/ppermute | solution.py:406
  54.4 2.4 %collective-permute-done.6.got_ref = bf16[2304,256]{1,0:T(8,128)(2,1)S(1)} collective-permute-done((bf16[2304,256]{1,0:T(8,128)(2,1)S(1)}, bf16[2304,256]{1,0:T(8,128)(2,1)S(1)}, u32[]{:S(2)}, u32[]{:S(2)}) %collective-permute-start.6) | collective-permute-done | bytes 1179680 | tf_op jit(solution)/shard_map/ppermute | solution.py:406
  57.0 4.7 %collective-permute-start.7 = (bf16[2,288,256]{2,1,0:T(8,128)(2,1)S(1)}, bf16[2,288,256]{2,1,0:T(8,128)(2,1)S(1)}, u32[]{:S(2)}, u32[]{:S(2)}) collective-permute-start(bf16[2,288,256]{2,1,0:T(8,128)(2,1)S(1)} %get-tuple-element.74), channel_id=1, source_target_pairs={{0,8},{8,0},{16,24},{24,16},{1,9},{9,1},{17,25},{25,17},{2,10},{10... | collective-permute-start | bytes 884744 | tf_op jit(solution)/shard_map/ppermute | solution.py:443
  62.6 6.4 %collective-permute-done.7.pr = bf16[2,288,256]{2,1,0:T(8,128)(2,1)S(1)} collective-permute-done((bf16[2,288,256]{2,1,0:T(8,128)(2,1)S(1)}, bf16[2,288,256]{2,1,0:T(8,128)(2,1)S(1)}, u32[]{:S(2)}, u32[]{:S(2)}) %collective-permute-start.7) | collective-permute-done | bytes 294944 | tf_op jit(solution)/shard_map/ppermute | solution.py:443
  69.0 1.5 %collective-permute-done.9.qr = bf16[2,288,256]{2,1,0:T(8,128)(2,1)S(1)} collective-permute-done((bf16[2,288,256]{2,1,0:T(8,128)(2,1)S(1)}, bf16[2,288,256]{2,1,0:T(8,128)(2,1)S(1)}, u32[]{:S(2)}, u32[]{:S(2)}) %collective-permute-start.9) | collective-permute-done | bytes 294944 | tf_op jit(solution)/shard_map/ppermute | solution.py:443
  71.3 4.5 %collective-permute-done.10.pr = bf16[1,288,256]{2,1,0:T(8,128)(2,1)S(1)} collective-permute-done((bf16[1,288,256]{2,1,0:T(8,128)(2,1)S(1)}, bf16[1,288,256]{2,1,0:T(8,128)(2,1)S(1)}, u32[]{:S(2)}, u32[]{:S(2)}) %collective-permute-start.10) | collective-permute-done | bytes 147488 | tf_op jit(solution)/shard_map/ppermute | solution.py:443
  76.3 3.7 %collective-permute-start.14 = (bf16[144,256]{1,0:T(8,128)(2,1)S(1)}, bf16[144,256]{1,0:T(8,128)(2,1)S(1)}, u32[]{:S(2)}, u32[]{:S(2)}) collective-permute-start(bf16[144,256]{1,0:T(8,128)(2,1)S(1)} %get-tuple-element.87), channel_id=1, source_target_pairs={{0,6},{1,7},{2,0},{3,1},{4,2},{5,3},{6,4},{7,5},{8,14},{9,15},{10,... | collective-permute-start | bytes 221192 | tf_op jit(solution)/shard_map/ppermute | solution.py:487
  80.1 2.4 %collective-permute-done.12.refs_1_ = bf16[144,256]{1,0:T(8,128)(2,1)S(1)} collective-permute-done((bf16[144,256]{1,0:T(8,128)(2,1)S(1)}, bf16[144,256]{1,0:T(8,128)(2,1)S(1)}, u32[]{:S(2)}, u32[]{:S(2)}) %collective-permute-start.12) | collective-permute-done | bytes 73760 | tf_op jit(solution)/shard_map/ppermute | solution.py:487
  82.5 1.4 %collective-permute-done.14.refs_3_ = bf16[144,256]{1,0:T(8,128)(2,1)S(1)} collective-permute-done((bf16[144,256]{1,0:T(8,128)(2,1)S(1)}, bf16[144,256]{1,0:T(8,128)(2,1)S(1)}, u32[]{:S(2)}, u32[]{:S(2)}) %collective-permute-start.14) | collective-permute-done | bytes 73760 | tf_op jit(solution)/shard_map/ppermute | solution.py:487
  84.0 2.4 %collective-permute-start.17 = (bf16[144,256]{1,0:T(8,128)(2,1)S(1)}, bf16[144,256]{1,0:T(8,128)(2,1)S(1)}, u32[]{:S(2)}, u32[]{:S(2)}) collective-permute-start(bf16[144,256]{1,0:T(8,128)(2,1)S(1)} %shard_map.113.refs_0_), channel_id=1, source_target_pairs={{0,6},{1,7},{2,0},{3,1},{4,2},{5,3},{6,4},{7,5},{8,14},{9,15},{10,... | collective-permute-start | bytes 221192 | tf_op jit(solution)/shard_map/ppermute | solution.py:497
  87.2 1.9 %collective-permute-done.17.refs_3_ = bf16[144,256]{1,0:T(8,128)(2,1)S(1)} collective-permute-done((bf16[144,256]{1,0:T(8,128)(2,1)S(1)}, bf16[144,256]{1,0:T(8,128)(2,1)S(1)}, u32[]{:S(2)}, u32[]{:S(2)}) %collective-permute-start.17) | collective-permute-done | bytes 73760 | tf_op jit(solution)/shard_map/ppermute | solution.py:497
  89.2 2.4 %collective-permute-done.16.refs_2_ = bf16[144,256]{1,0:T(8,128)(2,1)S(1)} collective-permute-done((bf16[144,256]{1,0:T(8,128)(2,1)S(1)}, bf16[144,256]{1,0:T(8,128)(2,1)S(1)}, u32[]{:S(2)}, u32[]{:S(2)}) %collective-permute-start.16) | collective-permute-done | bytes 73760 | tf_op jit(solution)/shard_map/ppermute | solution.py:497
  91.6 1.8 %collective-permute-done.15.refs_1_ = bf16[144,256]{1,0:T(8,128)(2,1)S(1)} collective-permute-done((bf16[144,256]{1,0:T(8,128)(2,1)S(1)}, bf16[144,256]{1,0:T(8,128)(2,1)S(1)}, u32[]{:S(2)}, u32[]{:S(2)}) %collective-permute-start.15) | collective-permute-done | bytes 73760 | tf_op jit(solution)/shard_map/ppermute | solution.py:497
  93.5 1.6 %collective-permute-done.18.refs_1_ = bf16[576,256]{1,0:T(8,128)(2,1)S(1)} collective-permute-done((bf16[576,256]{1,0:T(8,128)(2,1)S(1)}, bf16[576,256]{1,0:T(8,128)(2,1)S(1)}, u32[]{:S(2)}, u32[]{:S(2)}) %collective-permute-start.18) | collective-permute-done | bytes 294944 | tf_op jit(solution)/shard_map/ppermute | solution.py:507
  95.1 1.1 %shard_map.115 = (f32[576,256]{1,0:T(8,128)}, f32[576,256]{1,0:T(8,128)}) custom-call(bf16[576,256]{1,0:T(8,128)(2,1)S(1)} %shard_map.114.refs_0_, bf16[576,256]{1,0:T(8,128)(2,1)S(1)} %collective-permute-done.18.refs_1_), custom_call_target="tpu_custom_call" | custom-call | tf_op jit(solution)/shard_map/pallas_call | solution.py:27
  (29 shorter events, 7.6 us)
Async XLA Ops:
  0.6 10.3 %collective-permute-start.2 = (bf16[1024,256]{1,0:T(8,128)(2,1)}, bf16[1024,256]{1,0:T(8,128)(2,1)S(1)}, u32[]{:S(2)}, u32[]{:S(2)}) collective-permute-start(bf16[1024,256]{1,0:T(8,128)(2,1)} %bitcast.10), channel_id=1, source_target_pairs={{0,1},{1,0},{2,3},{3,2},{4,5},{5,4},{6,7},{7,6},{8,9},{9,8},{10,11... | collective-permute-start | bytes 1572872 | tf_op jit(solution)/shard_map/ppermute | solution.py:565
  1.9 2.5 %collective-permute-start = (bf16[64,256]{1,0:T(8,128)(2,1)S(1)}, bf16[64,256]{1,0:T(8,128)(2,1)S(1)}, u32[]{:S(2)}, u32[]{:S(2)}) collective-permute-start(bf16[64,256]{1,0:T(8,128)(2,1)S(1)} %shard_map.104), channel_id=1, source_target_pairs={{1,2},{2,1},{3,4},{4,3},{5,6},{6,5},{9,10},{10,9},{11,12},{12,11},... | collective-permute-start | bytes 98312 | tf_op jit(solution)/shard_map/ppermute | solution.py:562
  2.6 1.0 %copy-start = (bf16[1,4,14,14,256]{4,1,3,2,0:T(4,128)(2,1)S(1)}, bf16[1,4,14,14,256]{4,1,3,2,0:T(4,128)(2,1)}, u32[]{:S(2)}) copy-start(bf16[1,4,14,14,256]{4,1,3,2,0:T(4,128)(2,1)} %param.15) | copy-start | bytes 1204228
  4.4 19.1 %collective-permute-start.1 = (bf16[4,208,256]{2,1,0:T(8,128)(2,1)S(1)}, bf16[4,208,256]{2,1,0:T(8,128)(2,1)S(1)}, u32[]{:S(2)}, u32[]{:S(2)}) collective-permute-start(bf16[4,208,256]{2,1,0:T(8,128)(2,1)S(1)} %shard_map.103.refs_7_), channel_id=1, source_target_pairs={{0,2},{1,3},{2,6},{3,7},{6,4},{7,5},{4,0},{5,1},{8,10},{9,11},{10,... | collective-permute-start | bytes 1277960 | tf_op jit(solution)/shard_map/ppermute | solution.py:577
  9.8 1.2 %collective-permute-start.3 = (bf16[64,256]{1,0:T(8,128)(2,1)S(1)}, bf16[64,256]{1,0:T(8,128)(2,1)S(1)}, u32[]{:S(2)}, u32[]{:S(2)}) collective-permute-start(bf16[64,256]{1,0:T(8,128)(2,1)S(1)} %collective-permute-done.refs_2_), channel_id=1, source_target_pairs={{0,1},{1,0},{2,3},{3,2},{4,5},{5,4},{6,7},{7,6},{8,9},{9,8},{10,11... | collective-permute-start | bytes 98312 | tf_op jit(solution)/shard_map/ppermute | solution.py:568
  23.5 12.9 %collective-permute-start.4 = (bf16[4,208,256]{2,1,0:T(8,128)(2,1)S(1)}, bf16[4,208,256]{2,1,0:T(8,128)(2,1)S(1)}, u32[]{:S(2)}, u32[]{:S(2)}) collective-permute-start(bf16[4,208,256]{2,1,0:T(8,128)(2,1)S(1)} %collective-permute-done.1.refs_8_), channel_id=1, source_target_pairs={{0,2},{1,3},{2,6},{3,7},{6,4},{7,5},{4,0},{5,1},{8,10},{9,11},{10,... | collective-permute-start | bytes 1277960 | tf_op jit(solution)/shard_map/ppermute | solution.py:587
  36.4 12.0 %collective-permute-start.5 = (bf16[4,208,256]{2,1,0:T(8,128)(2,1)S(1)}, bf16[4,208,256]{2,1,0:T(8,128)(2,1)S(1)}, u32[]{:S(2)}, u32[]{:S(2)}) collective-permute-start(bf16[4,208,256]{2,1,0:T(8,128)(2,1)S(1)} %collective-permute-done.4.refs_8_), channel_id=1, source_target_pairs={{0,2},{1,3},{2,6},{3,7},{6,4},{7,5},{4,0},{5,1},{8,10},{9,11},{10,... | collective-permute-start | bytes 1277960 | tf_op jit(solution)/shard_map/ppermute | solution.py:587
  52.7 4.1 %collective-permute-start.6 = (bf16[2304,256]{1,0:T(8,128)(2,1)S(1)}, bf16[2304,256]{1,0:T(8,128)(2,1)S(1)}, u32[]{:S(2)}, u32[]{:S(2)}) collective-permute-start(bf16[2304,256]{1,0:T(8,128)(2,1)S(1)} %get-tuple-element.72), channel_id=1, source_target_pairs={{0,1},{1,0},{2,3},{3,2},{4,5},{5,4},{6,7},{7,6},{8,9},{9,8},{10,11... | collective-permute-start | bytes 3538952 | tf_op jit(solution)/shard_map/ppermute | solution.py:406
  54.3 7.4 %collective-permute-start.8 = (bf16[1024,256]{1,0:T(8,128)(2,1)S(1)}, bf16[1024,256]{1,0:T(8,128)(2,1)S(1)}, u32[]{:S(2)}, u32[]{:S(2)}) collective-permute-start(bf16[1024,256]{1,0:T(8,128)(2,1)S(1)} %get-tuple-element.76), channel_id=1, source_target_pairs={{0,1},{1,0},{2,3},{3,2},{4,5},{5,4},{6,7},{7,6},{8,9},{9,8},{10,11... | collective-permute-start | bytes 1572872 | tf_op jit(solution)/shard_map/ppermute | solution.py:598
  57.0 12.0 %collective-permute-start.7 = (bf16[2,288,256]{2,1,0:T(8,128)(2,1)S(1)}, bf16[2,288,256]{2,1,0:T(8,128)(2,1)S(1)}, u32[]{:S(2)}, u32[]{:S(2)}) collective-permute-start(bf16[2,288,256]{2,1,0:T(8,128)(2,1)S(1)} %get-tuple-element.74), channel_id=1, source_target_pairs={{0,8},{8,0},{16,24},{24,16},{1,9},{9,1},{17,25},{25,17},{2,10},{10... | collective-permute-start | bytes 884744 | tf_op jit(solution)/shard_map/ppermute | solution.py:443
  61.7 8.8 %collective-permute-start.9 = (bf16[2,288,256]{2,1,0:T(8,128)(2,1)S(1)}, bf16[2,288,256]{2,1,0:T(8,128)(2,1)S(1)}, u32[]{:S(2)}, u32[]{:S(2)}) collective-permute-start(bf16[2,288,256]{2,1,0:T(8,128)(2,1)S(1)} %get-tuple-element.79), channel_id=1, source_target_pairs={{0,16},{8,24},{16,0},{24,8},{1,17},{9,25},{17,1},{25,9},{2,18},{10... | collective-permute-start | bytes 884744 | tf_op jit(solution)/shard_map/ppermute | solution.py:443
  70.6 5.2 %collective-permute-start.10 = (bf16[1,288,256]{2,1,0:T(8,128)(2,1)S(1)}, bf16[1,288,256]{2,1,0:T(8,128)(2,1)S(1)}, u32[]{:S(2)}, u32[]{:S(2)}) collective-permute-start(bf16[1,288,256]{2,1,0:T(8,128)(2,1)S(1)} %get-tuple-element.81), channel_id=1, source_target_pairs={{0,16},{8,24},{16,0},{24,8},{1,17},{9,25},{17,1},{25,9},{2,18},{10... | collective-permute-start | bytes 442376 | tf_op jit(solution)/shard_map/ppermute | solution.py:443
  70.9 5.1 %collective-permute-start.11 = (bf16[1,288,256]{2,1,0:T(8,128)(2,1)S(1)}, bf16[1,288,256]{2,1,0:T(8,128)(2,1)S(1)}, u32[]{:S(2)}, u32[]{:S(2)}) collective-permute-start(bf16[1,288,256]{2,1,0:T(8,128)(2,1)S(1)} %get-tuple-element.83), channel_id=1, source_target_pairs={{0,8},{8,0},{16,24},{24,16},{1,9},{9,1},{17,25},{25,17},{2,10},{10... | collective-permute-start | bytes 442376 | tf_op jit(solution)/shard_map/ppermute | solution.py:443
  76.2 6.3 %collective-permute-start.12 = (bf16[144,256]{1,0:T(8,128)(2,1)S(1)}, bf16[144,256]{1,0:T(8,128)(2,1)S(1)}, u32[]{:S(2)}, u32[]{:S(2)}) collective-permute-start(bf16[144,256]{1,0:T(8,128)(2,1)S(1)} %get-tuple-element.85), channel_id=1, source_target_pairs={{0,2},{1,3},{2,4},{3,5},{4,6},{5,7},{6,0},{7,1},{8,10},{9,11},{10,... | collective-permute-start | bytes 221192 | tf_op jit(solution)/shard_map/ppermute | solution.py:487
  76.3 6.2 %collective-permute-start.13 = (bf16[144,256]{1,0:T(8,128)(2,1)S(1)}, bf16[144,256]{1,0:T(8,128)(2,1)S(1)}, u32[]{:S(2)}, u32[]{:S(2)}) collective-permute-start(bf16[144,256]{1,0:T(8,128)(2,1)S(1)} %get-tuple-element.86), channel_id=1, source_target_pairs={{0,4},{1,5},{2,6},{3,7},{4,0},{5,1},{6,2},{7,3},{8,12},{9,13},{10,... | collective-permute-start | bytes 221192 | tf_op jit(solution)/shard_map/ppermute | solution.py:487
  76.3 7.6 %collective-permute-start.14 = (bf16[144,256]{1,0:T(8,128)(2,1)S(1)}, bf16[144,256]{1,0:T(8,128)(2,1)S(1)}, u32[]{:S(2)}, u32[]{:S(2)}) collective-permute-start(bf16[144,256]{1,0:T(8,128)(2,1)S(1)} %get-tuple-element.87), channel_id=1, source_target_pairs={{0,6},{1,7},{2,0},{3,1},{4,2},{5,3},{6,4},{7,5},{8,14},{9,15},{10,... | collective-permute-start | bytes 221192 | tf_op jit(solution)/shard_map/ppermute | solution.py:487
  84.0 5.2 %collective-permute-start.17 = (bf16[144,256]{1,0:T(8,128)(2,1)S(1)}, bf16[144,256]{1,0:T(8,128)(2,1)S(1)}, u32[]{:S(2)}, u32[]{:S(2)}) collective-permute-start(bf16[144,256]{1,0:T(8,128)(2,1)S(1)} %shard_map.113.refs_0_), channel_id=1, source_target_pairs={{0,6},{1,7},{2,0},{3,1},{4,2},{5,3},{6,4},{7,5},{8,14},{9,15},{10,... | collective-permute-start | bytes 221192 | tf_op jit(solution)/shard_map/ppermute | solution.py:497
  86.3 5.3 %collective-permute-start.16 = (bf16[144,256]{1,0:T(8,128)(2,1)S(1)}, bf16[144,256]{1,0:T(8,128)(2,1)S(1)}, u32[]{:S(2)}, u32[]{:S(2)}) collective-permute-start(bf16[144,256]{1,0:T(8,128)(2,1)S(1)} %shard_map.113.refs_0_), channel_id=1, source_target_pairs={{0,4},{1,5},{2,6},{3,7},{4,0},{5,1},{6,2},{7,3},{8,12},{9,13},{10,... | collective-permute-start | bytes 221192 | tf_op jit(solution)/shard_map/ppermute | solution.py:497
  87.2 6.2 %collective-permute-start.15 = (bf16[144,256]{1,0:T(8,128)(2,1)S(1)}, bf16[144,256]{1,0:T(8,128)(2,1)S(1)}, u32[]{:S(2)}, u32[]{:S(2)}) collective-permute-start(bf16[144,256]{1,0:T(8,128)(2,1)S(1)} %shard_map.113.refs_0_), channel_id=1, source_target_pairs={{0,2},{1,3},{2,4},{3,5},{4,6},{5,7},{6,0},{7,1},{8,10},{9,11},{10,... | collective-permute-start | bytes 221192 | tf_op jit(solution)/shard_map/ppermute | solution.py:497
  93.4 1.6 %collective-permute-start.18 = (bf16[576,256]{1,0:T(8,128)(2,1)S(1)}, bf16[576,256]{1,0:T(8,128)(2,1)S(1)}, u32[]{:S(2)}, u32[]{:S(2)}) collective-permute-start(bf16[576,256]{1,0:T(8,128)(2,1)S(1)} %shard_map.114.refs_0_), channel_id=1, source_target_pairs={{0,1},{1,0},{2,3},{3,2},{4,5},{5,4},{6,7},{7,6},{8,9},{9,8},{10,11... | collective-permute-start | bytes 884744 | tf_op jit(solution)/shard_map/ppermute | solution.py:507

commit v7 on v6

--- a/solution.py
+++ b/solution.py
@@ -57,7 +57,7 @@
     )
 
 
-def pack_kernel(side, height, cot, owner, row, col, packed, low, high, wide, places, sems):
+def pack_kernel(side, height, cot, owner, row, col, packed, notes, low, high, wide, places, sems):
     regions = cot.shape[2]
     copies = [
         pltpu.make_async_copy(source, places.at[n], sems.at[n])
@@ -84,13 +84,14 @@
         note = jnp.where(lanes == 0, spot, jnp.where(lanes == 1, column, 0.0))
         wide[192:208, :] = jnp.where(rows < cells - 192, wide[192:208, :], note)
         packed[r] = wide[...].astype(BF)
+        notes[r] = note.astype(BF)
 
 
 def pack(cotangent, height, place):
     side, regions = cotangent.shape[0], cotangent.shape[2]
     return local_kernel(
         functools.partial(pack_kernel, side, height),
-        sds((regions, SLOT, 256), BF),
+        (sds((regions, SLOT, 256), BF), sds((regions, 16, 256), BF)),
         cotangent,
         *place,
         scratch=[
@@ -158,109 +159,139 @@
     return v * half, slope
 
 
-def regions_part(side, height, width, blocks, pyr, w1, w2, wb1, wb2, acc1, acc2, gp, scratch):
+def regions_part(side, height, width, plan, blocks, early, stash, tables, sums, scratch):
+    pyr, wb1, wb2, w1, w2 = tables
+    acc1, acc2, gp = sums
     xs, hs, gs, wide, vs, slope1, todo = scratch
     chip = lax.axis_index("tile") // 2
     lanes = lax.broadcasted_iota(jnp.int32, (16, 256), 1)
     rows16 = lax.broadcasted_iota(jnp.int32, (16, 256), 0)
     in_row = rows16 < side
-    per = blocks[0].shape[0]
+    cells = side * PITCH
+    inside = (lax.broadcasted_iota(jnp.int32, (cells, 256), 0) & (PITCH - 1)) < side
+    used = pl.ds(16, cells)
+    per = (blocks or early)[0].shape[0]
+    tail = pl.ds(192, 16)
 
     count = jnp.int32(0)
+    start, end = jnp.int32(0), jnp.int32(0)
+
+    def enlist(s, r, note):
+        note = jnp.where(rows16 == 15, note.astype(F32), 0.0)
+        spot = jnp.sum(jnp.where(lanes == 0, note, 0.0)).astype(jnp.int32) - 1
+        column = jnp.sum(jnp.where(lanes == 1, note, 0.0)).astype(jnp.int32)
+        local = spot - chip * 2 * height
+        here = (spot >= 0) & (local >= 0) & (local < 2 * height)
+        todo[0, count] = jnp.int32(s * per + r)
+        todo[1, count] = jnp.where(here, local * width + column // 8 * 8, 0)
+        todo[2, count] = jnp.where(here, lax.rem(column, 8), 0)
+        return count + here.astype(jnp.int32)
+
     for s, block in enumerate(blocks):
         for r in range(per):
-            note = block[r, 192:208, :].astype(F32)
-            note = jnp.where(rows16 == 15, note, 0.0)
-            spot = jnp.sum(jnp.where(lanes == 0, note, 0.0)).astype(jnp.int32) - 1
-            column = jnp.sum(jnp.where(lanes == 1, note, 0.0)).astype(jnp.int32)
-            local = spot - chip * 2 * height
-            here = (spot >= 0) & (local >= 0) & (local < 2 * height)
-            todo[0, count] = jnp.int32(s * per + r)
-            todo[1, count] = jnp.where(here, local * width + column // 8 * 8, 0)
-            todo[2, count] = jnp.where(here, lax.rem(column, 8), 0)
-            count = count + here.astype(jnp.int32)
-
-    def batch(size, start):
-        cells = (size * (side + 1) - 1) * PITCH
-        spot = lax.broadcasted_iota(jnp.int32, (cells, 256), 0)
-        gap = side * PITCH
-        inside = ((spot & (PITCH - 1)) < side) & ((spot < gap) | (spot >= gap + PITCH))
-        used = pl.ds(16, cells)
-
-        def put(buf, v):
-            buf[used, 0:256] = pltpu.roll(v, 1, 0).astype(BF)
-            buf[used, 256:512] = v.astype(BF)
-            buf[used, 512:768] = pltpu.roll(v, cells - 1, 0).astype(BF)
-
-        def conv(buf, w):
-            total = jnp.zeros((cells, 256), F32)
-            for a in range(3):
-                total += jnp.dot(
-                    buf[a * 16 : a * 16 + cells, :],
-                    w[a * 768 : a * 768 + 768, :],
-                    preferred_element_type=F32,
-                )
-            return total
-
-        def taps(acc, buf, grad):
-            turned = grad.T.astype(BF)
-            for a in range(3):
-                acc[:, a * 768 : a * 768 + 768] += jnp.dot(
-                    turned, buf[a * 16 : a * 16 + cells, :], preferred_element_type=F32
-                )
-
-        for buf in (xs, hs, gs):
-            buf[0:16, :] = jnp.zeros((16, 768), BF)
-            buf[cells + 16 : cells + 32, :] = jnp.zeros((16, 768), BF)
-        for n in range(size - 1):
-            vs[gap : gap + PITCH, :] = jnp.zeros((PITCH, 256), F32)
-        bases, leads = [], []
-        for n in range(size):
-            which = todo[0, start + n]
-            bases.append(pl.multiple_of(todo[1, start + n], 8))
-            leads.append(todo[2, start + n])
-            for s, block in enumerate(blocks):
-
-                @pl.when(which // per == s)
-                def _(block=block, n=n, which=which):
-                    wide[n] = block[lax.rem(which, per)].astype(F32)
-
-        for n in range(size):
-            for i in range(side):
-                got = pyr[pl.ds(pl.multiple_of(bases[n] + i * width, 8), 24), :]
-                got = pltpu.roll(got, lax.rem(24 - leads[n], 24), 0)[0:16]
-                at = (n * (side + 1) + i) * PITCH
-                vs[at : at + 16, :] = jnp.where(in_row, got, 0.0)
-        put(xs, vs[0:cells, :])
+            count = enlist(s, r, block[r, tail, :])
+        most = plan[s]
+        start, end = end, count if most is None else jnp.minimum(count, end + most)
+    total = count
+    for block in early:
+        for r in range(per):
+            count = enlist(len(blocks), r, block[r])
+
+    for buf in (xs, hs, gs):
+        buf[0:16, :] = jnp.zeros((16, 768), BF)
+        buf[cells + 16 : cells + 32, :] = jnp.zeros((16, 768), BF)
+
+    def put(buf, v):
+        buf[used, 0:256] = pltpu.roll(v, 1, 0).astype(BF)
+        buf[used, 256:512] = v.astype(BF)
+        buf[used, 512:768] = pltpu.roll(v, cells - 1, 0).astype(BF)
+
+    def conv(buf, w):
+        total = jnp.zeros((cells, 256), F32)
+        for a in range(3):
+            total += jnp.dot(
+                buf[a * 16 : a * 16 + cells, :],
+                w[a * 768 : a * 768 + 768, :],
+                preferred_element_type=F32,
+            )
+        return total
+
+    def taps(acc, buf, grad):
+        turned = grad.T.astype(BF)
+        for a in range(3):
+            acc[:, a * 768 : a * 768 + 768] += jnp.dot(
+                turned, buf[a * 16 : a * 16 + cells, :], preferred_element_type=F32
+            )
+
+    def crop(n):
+        base, lead = todo[1, n], todo[2, n]
+        for i in range(side):
+            got = pyr[pl.ds(pl.multiple_of(base + i * width, 8), 24), :]
+            got = pltpu.roll(got, lax.rem(24 - lead, 24), 0)[0:16]
+            vs[i * 16 : i * 16 + 16, :] = jnp.where(in_row, got, 0.0)
+        put(xs, vs[...])
+
+    def forward(n):
+        crop(n)
         act1, slope = gelu_pair(conv(xs, w1))
-        slope1[0:cells, :] = slope
-        put(hs, jnp.where(inside, act1, 0.0))
+        slope1[...] = slope
+        act1 = jnp.where(inside, act1, 0.0)
+        put(hs, act1)
         _, slope = gelu_pair(conv(hs, w2))
-        for n in range(size):
-            for i in range(side):
-                got = wide[n, i * side : i * side + 16, :]
-                at = (n * (side + 1) + i) * PITCH
-                vs[at : at + 16, :] = jnp.where(in_row, got, 0.0)
-        g2 = vs[0:cells, :] * slope
+        return act1, slope
+
+    def backward(n, slope2):
+        which = todo[0, n]
+        base, lead = todo[1, n], todo[2, n]
+        for s, block in enumerate(blocks):
+
+            @pl.when(which // per == s)
+            def _(block=block):
+                wide[...] = block[lax.rem(which, per)].astype(F32)
+
+        for i in range(side):
+            got = wide[i * side : i * side + 16, :]
+            vs[i * 16 : i * 16 + 16, :] = jnp.where(in_row, got, 0.0)
+        g2 = vs[...] * slope2
         put(gs, g2)
         taps(acc2, hs, g2)
-        gact1 = conv(gs, wb2)
-        g1 = jnp.where(inside, gact1 * slope1[0:cells, :], 0.0)
+        g1 = jnp.where(inside, conv(gs, wb2) * slope1[...], 0.0)
         put(gs, g1)
         taps(acc1, xs, g1)
-        vs[0:cells, :] = jnp.where(inside, conv(gs, wb1), 0.0).astype(BF).astype(F32)
-        for n in range(size):
-            for i in range(side):
-                at = pl.ds(pl.multiple_of(bases[n] + i * width, 8), 24)
-                row = (n * (side + 1) + i) * PITCH
-                piece = jnp.concatenate([vs[row : row + 16, :], jnp.zeros((8, 256), F32)])
-                gp[at, :] = gp[at, :] + pltpu.roll(piece, leads[n], 0)
-
-    def one(n, carry):
-        batch(1, n)
+        vs[...] = jnp.where(inside, conv(gs, wb1), 0.0).astype(BF).astype(F32)
+        for i in range(side):
+            at = pl.ds(pl.multiple_of(base + i * width, 8), 24)
+            piece = jnp.concatenate([vs[i * 16 : i * 16 + 16, :], jnp.zeros((8, 256), F32)])
+            gp[at, :] = gp[at, :] + pltpu.roll(piece, lead, 0)
+
+    def whole(n, carry):
+        _, slope2 = forward(n)
+        backward(n, slope2)
         return carry
 
-    lax.fori_loop(0, count, one, 0)
+    def ahead(n, carry):
+        r = lax.rem(todo[0, n], per)
+        act1, slope2 = forward(n)
+        stash[0][r] = act1.astype(BF)
+        stash[1][r] = slope1[...]
+        stash[2][r] = slope2
+        return carry
+
+    def behind(n, carry):
+        r = lax.rem(todo[0, n], per)
+        crop(n)
+        put(hs, stash[0][r].astype(F32))
+        slope1[...] = stash[1][r]
+        backward(n, stash[2][r])
+        return carry
+
+    if early:
+        lax.fori_loop(start, end, whole, 0)
+        lax.fori_loop(total, count, ahead, 0)
+    elif stash:
+        lax.fori_loop(0, total, behind, 0)
+    else:
+        lax.fori_loop(start, end, whole, 0)
 
 
 def chunks_of(rows):
@@ -302,7 +333,7 @@
     gp_other[...] = gp[pl.ds(pl.multiple_of((1 - core) * cells, cells), cells), :].astype(BF)
 
 
-def main_call(side, height, width, dp, chips, first, last, state, weights, blocks):
+def main_call(side, height, width, dp, chips, first, last, plan, state, weights, blocks, early, stash):
     n = len(blocks)
     big = 2 * height * width + 16
     cells = side * PITCH
@@ -314,15 +345,21 @@
         sds((height * width, 256), F32),
         sds((height * width, 256), BF),
     )
-    outs = (kept if first else ()) + sums + (ends if last else ())
+    per = blocks[0].shape[0]
+    stashed = (
+        sds((per, cells, 256), BF),
+        sds((per, cells, 256), F32),
+        sds((per, cells, 256), F32),
+    )
+    outs = (kept if first else ()) + sums + (ends if last else ()) + (stashed if early else ())
     scratch = [
         pltpu.VMEM((cells + 32, 768), BF),
         pltpu.VMEM((cells + 32, 768), BF),
         pltpu.VMEM((cells + 32, 768), BF),
-        pltpu.VMEM((1, SLOT, 256), F32),
+        pltpu.VMEM((SLOT, 256), F32),
         pltpu.VMEM((cells, 256), F32),
         pltpu.VMEM((cells, 256), F32),
-        pltpu.SMEM((3, 128), jnp.int32),
+        pltpu.SMEM((3, 256), jnp.int32),
     ]
     extra = []
     if first:
@@ -344,7 +381,11 @@
         state_refs = take(len(state))
         weight_refs = take(len(weights))
         block_refs = take(n)
+        early_refs = take(len(early))
+        stash_refs = take(len(stash))
         out_refs = take(len(outs))
+        if early:
+            stash_refs = out_refs[-3:]
         scratch_refs = take(len(scratch))
         if first:
             pyr, wb1, wb2, w1, w2 = out_refs[:5]
@@ -368,7 +409,8 @@
             pyr, wb1, wb2, w1, w2 = state_refs[:5]
             acc1, acc2, gp = out_refs[:3]
         regions_part(
-            side, height, width, block_refs, pyr, w1, w2, wb1, wb2, acc1, acc2, gp, scratch_refs
+            *(side, height, width, plan, block_refs, early_refs, stash_refs),
+            *((pyr, wb1, wb2, w1, w2), (acc1, acc2, gp), scratch_refs),
         )
         if last:
             keep, *sends, gp_own, gp_other = out_refs[3:]
@@ -378,7 +420,7 @@
     return run(
         kernel,
         outs,
-        [*state, *weights, *blocks],
+        [*state, *weights, *blocks, *early, *stash],
         scratch=scratch + extra,
         aliases=aliases,
         hbm=(0, *range(len(state), len(state) + len(weights))) if first else (),
@@ -563,7 +605,7 @@
         edge, "tile", [(i, i + 1 if i % 2 else i - 1) for i in range(1, tiles - 1)]
     )
     other = lax.ppermute(tile, "tile", swap)
-    packed = pack(cotangent[0].transpose(1, 2, 0, 3), height, place)
+    packed, notes = pack(cotangent[0].transpose(1, 2, 0, 3), height, place)
     packed, rim_a = lax.optimization_barrier((packed, rim_a))
     rim_b = lax.ppermute(rim_a, "tile", swap)
 
@@ -575,25 +617,30 @@
     flat = lambda w: w.reshape(9 * channels, channels)
     wf, w1, w2 = flat(fpn_weight), flat(mask_w1), flat(mask_w2)
     block = lax.ppermute(packed, "tile", ring)
-    start = main_call(
-        side, height, width, dp, chips, True, False, [tile, other, rim_a, rim_b], [wf, w1, w2], [packed]
-    )
-    kept, sums = list(start[:5]), list(start[5:])
-    for step in range(1, chips):
-        last = step == chips - 1
-        held = block
-        if not last:
-            held, kept[0] = lax.optimization_barrier((held, kept[0]))
-            block = lax.ppermute(held, "tile", ring)
-        got = main_call(
-            *(side, height, width, dp, chips, False, last),
-            [*kept, *sums],
-            [],
-            [held],
-        )
-        sums, ends = list(got[:3]), got[3:]
-        if not last:
-            kept[0], sums[0] = lax.optimization_barrier((kept[0], sums[0]))
+    notes = lax.ppermute(notes, "tile", [(j, i) for i, j in ring])
+    sizes = (side, height, width, dp, chips)
+    held, plan = [packed], [1] + [4] * (chips - 2) if chips > 2 else [None]
+    if chips > 2:
+        plan[-1] = None
+    state, weights, stash = [tile, other, rim_a, rim_b], [wf, w1, w2], []
+    for step in range(chips):
+        first, last = step == 0, step == chips - 1
+        early = [notes] if step == chips - 2 else []
+        if last:
+            got = main_call(*sizes, first, last, [None], state, [], [block], [], stash)
+            ends = got[3:]
+            break
+        got = list(main_call(*sizes, first, last, plan, state, weights, held, early, []))
+        if first:
+            kept, got = got[:5], got[5:]
+        sums, stash, weights = got[:3], got[3:], []
+        if step < chips - 2:
+            block, kept[0], sums[0], notes = lax.optimization_barrier(
+                (block, kept[0], sums[0], notes)
+            )
+            held = held + [block]
+            block = lax.ppermute(block, "tile", ring)
+        state = kept + sums
     keep, *sends, gp_own, gp_other = ends
     gp_got = lax.ppermute(gp_other, "tile", swap)
 

time: 95.8 us -> 90.9 us (0.949)
  Pallas kernels: 33.7 us -> 21.6 us
  waiting for transfers between devices: 37.1 us -> 41.1 us
  starting transfers between devices: 23.6 us -> 26.2 us
    pallas_call x13, Pallas kernels: 33.7 us -> 21.6 us  [run(): pl.pallas_call(kernel, out_shape=tuple((s if i in hbm_out else pltpu.VMEM...]
    ppermute x2 -> x3, waiting for transfers between devices: 9.49 us -> 16.8 us  [the longest x2 15.6 us: body(): block = lax.ppermute(block, 'tile', ring)]
    ppermute x4, waiting for transfers between devices: 12.7 us -> 9.9 us  [exchange(): c.received.append(lax.ppermute(c.parts[2 * half + 1], 'dp', pairs))]
    ppermute x4, starting transfers between devices: 5.37 us -> 7.08 us  [exchange(): c.received.append(lax.ppermute(c.parts[2 * half + 1], 'dp', pairs))]
    ppermute x3, starting transfers between devices: 3.86 us -> 5.5 us  [deal(): lax.ppermute(dealt[k], 'tile', shifts[k])]
    ppermute x1, starting transfers between devices: 1.6 us -> 0.3 us  [reduce_weights(): arrived = [lax.ppermute(send, 'tile', core_swap) for send in sends]]
    ppermute x1, waiting for transfers between devices: 1.01 us -> 0.01 us  [body(): rim_b = lax.ppermute(rim_a, 'tile', swap)]
    ppermute x2 -> x3, starting transfers between devices: 2.63 us -> 3.38 us  [the longest x2 2.09 us: body(): block = lax.ppermute(block, 'tile', ring)]
  transfers between devices with their start and end apart: 19 -> 20, of which waited for: 14 -> 15; matrix products, arithmetic and copies ran while one was open for 0% -> 0% of each run, Pallas kernels for 29% -> 21%
where the time goes in v7:
time: 90.9 us; the launch traced here: 90.6 us
  waiting for transfers between devices  41.1 us (45%)
  starting transfers between devices  26.2 us (29%)
  Pallas kernels  21.6 us (24%)
  local copies, waits for them, and re-layouts  0.99 us (1%)
    pallas_call x13, Pallas kernels, run(): pl.pallas_call(kernel, out_shape=tuple((s if i in hbm_out else pltpu.VMEM...  21.6 us
    ppermute x2, waiting for transfers between devices, body(): block = lax.ppermute(block, 'tile', ring)  15.6 us
    ppermute x4, waiting for transfers between devices, exchange(): c.received.append(lax.ppermute(c.parts[2 * half + 1], 'dp', pairs))  9.9 us
    ppermute x4, starting transfers between devices, exchange(): c.received.append(lax.ppermute(c.parts[2 * half + 1], 'dp', pairs))  7.08 us
    ppermute x3, waiting for transfers between devices, gather(): lax.ppermute(c.mine, 'tile', shifts[k])  5.62 us
    ppermute x3, starting transfers between devices, deal(): lax.ppermute(dealt[k], 'tile', shifts[k])  5.5 us
    ppermute x1, starting transfers between devices, body(): block = lax.ppermute(packed, 'tile', ring)  5.36 us
    ppermute x3, waiting for transfers between devices, deal(): lax.ppermute(dealt[k], 'tile', shifts[k])  4.77 us
  transfers between devices with their start and end apart: 20, of which 15 were waited for; matrix products, arithmetic and copies ran while one was open for 0% of the time, Pallas kernels for 21%

profile of v7, /device:TPU:0, one launch (start us, length us, event | category | flops | bytes accessed | tf_op | source)
XLA Modules:
  0.0 90.6 jit_solution(2924123797583430765)
XLA Ops:
  4.4 5.4 %collective-permute-start.1 = (bf16[4,208,256]{2,1,0:T(8,128)(2,1)S(1)}, bf16[4,208,256]{2,1,0:T(8,128)(2,1)S(1)}, u32[]{:S(2)}, u32[]{:S(2)}) collective-permute-start(bf16[4,208,256]{2,1,0:T(8,128)(2,1)S(1)} %get-tuple-element.53.refs_7_.refs_8_), channel_id=1, source_target_pairs={{0,2},{1,3},{2,6},{3,7},{6,4},{7,5},{4,0},{5,1},{8,10},{9,11},{10,... | collective-permute-start | bytes 1277960 | tf_op jit(solution)/shard_map/ppermute | solution.py:619
  10.0 1.3 %collective-permute-start.4 = (bf16[4,16,256]{2,1,0:T(8,128)(2,1)S(1)}, bf16[4,16,256]{2,1,0:T(8,128)(2,1)S(1)}, u32[]{:S(2)}, u32[]{:S(2)}) collective-permute-start(bf16[4,16,256]{2,1,0:T(8,128)(2,1)S(1)} %get-tuple-element.57), channel_id=1, source_target_pairs={{2,0},{3,1},{6,2},{7,3},{4,6},{5,7},{0,4},{1,5},{10,8},{11,9},{14,... | collective-permute-start | bytes 98312 | tf_op jit(solution)/shard_map/ppermute | solution.py:620
  11.3 9.5 %shard_map.105 = (f32[2064,256]{1,0:T(8,128)S(1)}, bf16[2304,256]{1,0:T(8,128)(2,1)S(1)}, bf16[2304,256]{1,0:T(8,128)(2,1)S(1)}, bf16[2304,256]{1,0:T(8,128)(2,1...) custom-call(bf16[1024,256]{1,0:T(8,128)(2,1)} %bitcast.12, ...), custom_call_target="tpu_custom_call" | custom-call | tf_op jit(solution)/shard_map/pallas_call | solution.py:27
  21.9 1.7 %collective-permute-start.5 = (bf16[4,208,256]{2,1,0:T(8,128)(2,1)S(1)}, bf16[4,208,256]{2,1,0:T(8,128)(2,1)S(1)}, u32[]{:S(2)}, u32[]{:S(2)}) collective-permute-start(bf16[4,208,256]{2,1,0:T(8,128)(2,1)S(1)} %collective-permute-done.1.refs_9_), channel_id=1, source_target_pairs={{0,2},{1,3},{2,6},{3,7},{6,4},{7,5},{4,0},{5,1},{8,10},{9,11},{10,... | collective-permute-start | bytes 1277960 | tf_op jit(solution)/shard_map/ppermute | solution.py:642
  23.7 6.5 %shard_map.106 = (f32[256,2304]{1,0:T(8,128)S(1)}, f32[256,2304]{1,0:T(8,128)S(1)}, f32[2064,256]{1,0:T(8,128)S(1)}) custom-call(f32[2064,256]{1,0:T(8,128)S(1)} %get-tuple-element.69.refs_0_, bf16[2304,256]{1,0:T(8,128)(2,1)S(1)} %get-tuple-element.60.refs_1_, ...), custom_call_target="tpu_custom_call", output_to_operand_aliasing={{0}: (5, {}), {1}: (6, {}), {2}: (7, {})} | custom-call | tf_op jit(solution)/shard_map/pallas_call | solution.py:27
  30.2 4.5 %collective-permute-done.5.refs_10_ = bf16[4,208,256]{2,1,0:T(8,128)(2,1)S(1)} collective-permute-done((bf16[4,208,256]{2,1,0:T(8,128)(2,1)S(1)}, bf16[4,208,256]{2,1,0:T(8,128)(2,1)S(1)}, u32[]{:S(2)}, u32[]{:S(2)}) %collective-permute-start.5) | collective-permute-done | bytes 426016 | tf_op jit(solution)/shard_map/ppermute | solution.py:642
  35.4 11.2 %collective-permute-done.6.refs_8_ = bf16[4,208,256]{2,1,0:T(8,128)(2,1)S(1)} collective-permute-done((bf16[4,208,256]{2,1,0:T(8,128)(2,1)S(1)}, bf16[4,208,256]{2,1,0:T(8,128)(2,1)S(1)}, u32[]{:S(2)}, u32[]{:S(2)}) %collective-permute-start.6) | collective-permute-done | bytes 426016 | tf_op jit(solution)/shard_map/ppermute | solution.py:642
  48.3 2.3 %collective-permute-done.7.got_ref = bf16[2304,256]{1,0:T(8,128)(2,1)S(1)} collective-permute-done((bf16[2304,256]{1,0:T(8,128)(2,1)S(1)}, bf16[2304,256]{1,0:T(8,128)(2,1)S(1)}, u32[]{:S(2)}, u32[]{:S(2)}) %collective-permute-start.7) | collective-permute-done | bytes 1179680 | tf_op jit(solution)/shard_map/ppermute | solution.py:448
  50.9 1.6 %collective-permute-start.8 = (bf16[2,288,256]{2,1,0:T(8,128)(2,1)S(1)}, bf16[2,288,256]{2,1,0:T(8,128)(2,1)S(1)}, u32[]{:S(2)}, u32[]{:S(2)}) collective-permute-start(bf16[2,288,256]{2,1,0:T(8,128)(2,1)S(1)} %get-tuple-element.84), channel_id=1, source_target_pairs={{0,8},{8,0},{16,24},{24,16},{1,9},{9,1},{17,25},{25,17},{2,10},{10... | collective-permute-start | bytes 884744 | tf_op jit(solution)/shard_map/ppermute | solution.py:485
  52.5 2.0 %collective-permute-start.10 = (bf16[2,288,256]{2,1,0:T(8,128)(2,1)S(1)}, bf16[2,288,256]{2,1,0:T(8,128)(2,1)S(1)}, u32[]{:S(2)}, u32[]{:S(2)}) collective-permute-start(bf16[2,288,256]{2,1,0:T(8,128)(2,1)S(1)} %get-tuple-element.89), channel_id=1, source_target_pairs={{0,16},{8,24},{16,0},{24,8},{1,17},{9,25},{17,1},{25,9},{2,18},{10... | collective-permute-start | bytes 884744 | tf_op jit(solution)/shard_map/ppermute | solution.py:485
  55.4 4.7 %collective-permute-done.8.pr = bf16[2,288,256]{2,1,0:T(8,128)(2,1)S(1)} collective-permute-done((bf16[2,288,256]{2,1,0:T(8,128)(2,1)S(1)}, bf16[2,288,256]{2,1,0:T(8,128)(2,1)S(1)}, u32[]{:S(2)}, u32[]{:S(2)}) %collective-permute-start.8) | collective-permute-done | bytes 294944 | tf_op jit(solution)/shard_map/ppermute | solution.py:485
  60.1 1.7 %collective-permute-done.10.qr = bf16[2,288,256]{2,1,0:T(8,128)(2,1)S(1)} collective-permute-done((bf16[2,288,256]{2,1,0:T(8,128)(2,1)S(1)}, bf16[2,288,256]{2,1,0:T(8,128)(2,1)S(1)}, u32[]{:S(2)}, u32[]{:S(2)}) %collective-permute-start.10) | collective-permute-done | bytes 294944 | tf_op jit(solution)/shard_map/ppermute | solution.py:485
  62.0 1.8 %collective-permute-start.11 = (bf16[1,288,256]{2,1,0:T(8,128)(2,1)S(1)}, bf16[1,288,256]{2,1,0:T(8,128)(2,1)S(1)}, u32[]{:S(2)}, u32[]{:S(2)}) collective-permute-start(bf16[1,288,256]{2,1,0:T(8,128)(2,1)S(1)} %get-tuple-element.91), channel_id=1, source_target_pairs={{0,16},{8,24},{16,0},{24,8},{1,17},{9,25},{17,1},{25,9},{2,18},{10... | collective-permute-start | bytes 442376 | tf_op jit(solution)/shard_map/ppermute | solution.py:485
  63.8 1.7 %collective-permute-start.12 = (bf16[1,288,256]{2,1,0:T(8,128)(2,1)S(1)}, bf16[1,288,256]{2,1,0:T(8,128)(2,1)S(1)}, u32[]{:S(2)}, u32[]{:S(2)}) collective-permute-start(bf16[1,288,256]{2,1,0:T(8,128)(2,1)S(1)} %get-tuple-element.93), channel_id=1, source_target_pairs={{0,8},{8,0},{16,24},{24,16},{1,9},{9,1},{17,25},{25,17},{2,10},{10... | collective-permute-start | bytes 442376 | tf_op jit(solution)/shard_map/ppermute | solution.py:485
  65.4 1.9 %collective-permute-done.11.pr = bf16[1,288,256]{2,1,0:T(8,128)(2,1)S(1)} collective-permute-done((bf16[1,288,256]{2,1,0:T(8,128)(2,1)S(1)}, bf16[1,288,256]{2,1,0:T(8,128)(2,1)S(1)}, u32[]{:S(2)}, u32[]{:S(2)}) %collective-permute-start.11) | collective-permute-done | bytes 147488 | tf_op jit(solution)/shard_map/ppermute | solution.py:485
  67.4 1.5 %collective-permute-done.12.qr = bf16[1,288,256]{2,1,0:T(8,128)(2,1)S(1)} collective-permute-done((bf16[1,288,256]{2,1,0:T(8,128)(2,1)S(1)}, bf16[1,288,256]{2,1,0:T(8,128)(2,1)S(1)}, u32[]{:S(2)}, u32[]{:S(2)}) %collective-permute-start.12) | collective-permute-done | bytes 147488 | tf_op jit(solution)/shard_map/ppermute | solution.py:485
  69.0 1.7 %collective-permute-start.13 = (bf16[144,256]{1,0:T(8,128)(2,1)S(1)}, bf16[144,256]{1,0:T(8,128)(2,1)S(1)}, u32[]{:S(2)}, u32[]{:S(2)}) collective-permute-start(bf16[144,256]{1,0:T(8,128)(2,1)S(1)} %get-tuple-element.95), channel_id=1, source_target_pairs={{0,2},{1,3},{2,4},{3,5},{4,6},{5,7},{6,0},{7,1},{8,10},{9,11},{10,... | collective-permute-start | bytes 221192 | tf_op jit(solution)/shard_map/ppermute | solution.py:529
  70.7 3.8 %collective-permute-start.14 = (bf16[144,256]{1,0:T(8,128)(2,1)S(1)}, bf16[144,256]{1,0:T(8,128)(2,1)S(1)}, u32[]{:S(2)}, u32[]{:S(2)}) collective-permute-start(bf16[144,256]{1,0:T(8,128)(2,1)S(1)} %get-tuple-element.96), channel_id=1, source_target_pairs={{0,4},{1,5},{2,6},{3,7},{4,0},{5,1},{6,2},{7,3},{8,12},{9,13},{10,... | collective-permute-start | bytes 221192 | tf_op jit(solution)/shard_map/ppermute | solution.py:529
  74.5 2.0 %collective-permute-done.13.refs_1_ = bf16[144,256]{1,0:T(8,128)(2,1)S(1)} collective-permute-done((bf16[144,256]{1,0:T(8,128)(2,1)S(1)}, bf16[144,256]{1,0:T(8,128)(2,1)S(1)}, u32[]{:S(2)}, u32[]{:S(2)}) %collective-permute-start.13) | collective-permute-done | bytes 73760 | tf_op jit(solution)/shard_map/ppermute | solution.py:529
  76.6 2.3 %collective-permute-done.14.refs_2_ = bf16[144,256]{1,0:T(8,128)(2,1)S(1)} collective-permute-done((bf16[144,256]{1,0:T(8,128)(2,1)S(1)}, bf16[144,256]{1,0:T(8,128)(2,1)S(1)}, u32[]{:S(2)}, u32[]{:S(2)}) %collective-permute-start.14) | collective-permute-done | bytes 73760 | tf_op jit(solution)/shard_map/ppermute | solution.py:529
  79.3 2.2 %collective-permute-start.18 = (bf16[144,256]{1,0:T(8,128)(2,1)S(1)}, bf16[144,256]{1,0:T(8,128)(2,1)S(1)}, u32[]{:S(2)}, u32[]{:S(2)}) collective-permute-start(bf16[144,256]{1,0:T(8,128)(2,1)S(1)} %shard_map.113.refs_0_), channel_id=1, source_target_pairs={{0,6},{1,7},{2,0},{3,1},{4,2},{5,3},{6,4},{7,5},{8,14},{9,15},{10,... | collective-permute-start | bytes 221192 | tf_op jit(solution)/shard_map/ppermute | solution.py:539
  82.2 2.0 %collective-permute-done.18.refs_3_ = bf16[144,256]{1,0:T(8,128)(2,1)S(1)} collective-permute-done((bf16[144,256]{1,0:T(8,128)(2,1)S(1)}, bf16[144,256]{1,0:T(8,128)(2,1)S(1)}, u32[]{:S(2)}, u32[]{:S(2)}) %collective-permute-start.18) | collective-permute-done | bytes 73760 | tf_op jit(solution)/shard_map/ppermute | solution.py:539
  84.2 2.7 %collective-permute-done.17.refs_2_ = bf16[144,256]{1,0:T(8,128)(2,1)S(1)} collective-permute-done((bf16[144,256]{1,0:T(8,128)(2,1)S(1)}, bf16[144,256]{1,0:T(8,128)(2,1)S(1)}, u32[]{:S(2)}, u32[]{:S(2)}) %collective-permute-start.17) | collective-permute-done | bytes 73760 | tf_op jit(solution)/shard_map/ppermute | solution.py:539
  88.0 1.6 %collective-permute-done.19.refs_1_ = bf16[576,256]{1,0:T(8,128)(2,1)S(1)} collective-permute-done((bf16[576,256]{1,0:T(8,128)(2,1)S(1)}, bf16[576,256]{1,0:T(8,128)(2,1)S(1)}, u32[]{:S(2)}, u32[]{:S(2)}) %collective-permute-start.19) | collective-permute-done | bytes 294944 | tf_op jit(solution)/shard_map/ppermute | solution.py:549
  (31 shorter events, 12.2 us)
Async XLA Ops:
  0.6 10.6 %collective-permute-start.2 = (bf16[1024,256]{1,0:T(8,128)(2,1)}, bf16[1024,256]{1,0:T(8,128)(2,1)S(1)}, u32[]{:S(2)}, u32[]{:S(2)}) collective-permute-start(bf16[1024,256]{1,0:T(8,128)(2,1)} %bitcast.10), channel_id=1, source_target_pairs={{0,1},{1,0},{2,3},{3,2},{4,5},{5,4},{6,7},{7,6},{8,9},{9,8},{10,11... | collective-permute-start | bytes 1572872 | tf_op jit(solution)/shard_map/ppermute | solution.py:607
  1.9 2.5 %collective-permute-start = (bf16[64,256]{1,0:T(8,128)(2,1)S(1)}, bf16[64,256]{1,0:T(8,128)(2,1)S(1)}, u32[]{:S(2)}, u32[]{:S(2)}) collective-permute-start(bf16[64,256]{1,0:T(8,128)(2,1)S(1)} %shard_map.104), channel_id=1, source_target_pairs={{1,2},{2,1},{3,4},{4,3},{5,6},{6,5},{9,10},{10,9},{11,12},{12,11},... | collective-permute-start | bytes 98312 | tf_op jit(solution)/shard_map/ppermute | solution.py:604
  2.6 1.0 %copy-start = (bf16[1,4,14,14,256]{4,1,3,2,0:T(4,128)(2,1)S(1)}, bf16[1,4,14,14,256]{4,1,3,2,0:T(4,128)(2,1)}, u32[]{:S(2)}) copy-start(bf16[1,4,14,14,256]{4,1,3,2,0:T(4,128)(2,1)} %param.15) | copy-start | bytes 1204228
  4.4 17.5 %collective-permute-start.1 = (bf16[4,208,256]{2,1,0:T(8,128)(2,1)S(1)}, bf16[4,208,256]{2,1,0:T(8,128)(2,1)S(1)}, u32[]{:S(2)}, u32[]{:S(2)}) collective-permute-start(bf16[4,208,256]{2,1,0:T(8,128)(2,1)S(1)} %get-tuple-element.53.refs_7_.refs_8_), channel_id=1, source_target_pairs={{0,2},{1,3},{2,6},{3,7},{6,4},{7,5},{4,0},{5,1},{8,10},{9,11},{10,... | collective-permute-start | bytes 1277960 | tf_op jit(solution)/shard_map/ppermute | solution.py:619
  9.8 1.5 %collective-permute-start.3 = (bf16[64,256]{1,0:T(8,128)(2,1)S(1)}, bf16[64,256]{1,0:T(8,128)(2,1)S(1)}, u32[]{:S(2)}, u32[]{:S(2)}) collective-permute-start(bf16[64,256]{1,0:T(8,128)(2,1)S(1)} %collective-permute-done.refs_2_), channel_id=1, source_target_pairs={{0,1},{1,0},{2,3},{3,2},{4,5},{5,4},{6,7},{7,6},{8,9},{9,8},{10,11... | collective-permute-start | bytes 98312 | tf_op jit(solution)/shard_map/ppermute | solution.py:610
  10.0 12.0 %collective-permute-start.4 = (bf16[4,16,256]{2,1,0:T(8,128)(2,1)S(1)}, bf16[4,16,256]{2,1,0:T(8,128)(2,1)S(1)}, u32[]{:S(2)}, u32[]{:S(2)}) collective-permute-start(bf16[4,16,256]{2,1,0:T(8,128)(2,1)S(1)} %get-tuple-element.57), channel_id=1, source_target_pairs={{2,0},{3,1},{6,2},{7,3},{4,6},{5,7},{0,4},{1,5},{10,8},{11,9},{14,... | collective-permute-start | bytes 98312 | tf_op jit(solution)/shard_map/ppermute | solution.py:620
  21.9 12.7 %collective-permute-start.5 = (bf16[4,208,256]{2,1,0:T(8,128)(2,1)S(1)}, bf16[4,208,256]{2,1,0:T(8,128)(2,1)S(1)}, u32[]{:S(2)}, u32[]{:S(2)}) collective-permute-start(bf16[4,208,256]{2,1,0:T(8,128)(2,1)S(1)} %collective-permute-done.1.refs_9_), channel_id=1, source_target_pairs={{0,2},{1,3},{2,6},{3,7},{6,4},{7,5},{4,0},{5,1},{8,10},{9,11},{10,... | collective-permute-start | bytes 1277960 | tf_op jit(solution)/shard_map/ppermute | solution.py:642
  34.7 11.9 %collective-permute-start.6 = (bf16[4,208,256]{2,1,0:T(8,128)(2,1)S(1)}, bf16[4,208,256]{2,1,0:T(8,128)(2,1)S(1)}, u32[]{:S(2)}, u32[]{:S(2)}) collective-permute-start(bf16[4,208,256]{2,1,0:T(8,128)(2,1)S(1)} %collective-permute-done.5.refs_10_), channel_id=1, source_target_pairs={{0,2},{1,3},{2,6},{3,7},{6,4},{7,5},{4,0},{5,1},{8,10},{9,11},{10,... | collective-permute-start | bytes 1277960 | tf_op jit(solution)/shard_map/ppermute | solution.py:642
  47.7 2.9 %collective-permute-start.7 = (bf16[2304,256]{1,0:T(8,128)(2,1)S(1)}, bf16[2304,256]{1,0:T(8,128)(2,1)S(1)}, u32[]{:S(2)}, u32[]{:S(2)}) collective-permute-start(bf16[2304,256]{1,0:T(8,128)(2,1)S(1)} %get-tuple-element.82), channel_id=1, source_target_pairs={{0,1},{1,0},{2,3},{3,2},{4,5},{5,4},{6,7},{7,6},{8,9},{9,8},{10,11... | collective-permute-start | bytes 3538952 | tf_op jit(solution)/shard_map/ppermute | solution.py:448
  48.0 6.5 %collective-permute-start.9 = (bf16[1024,256]{1,0:T(8,128)(2,1)S(1)}, bf16[1024,256]{1,0:T(8,128)(2,1)S(1)}, u32[]{:S(2)}, u32[]{:S(2)}) collective-permute-start(bf16[1024,256]{1,0:T(8,128)(2,1)S(1)} %get-tuple-element.86), channel_id=1, source_target_pairs={{0,1},{1,0},{2,3},{3,2},{4,5},{5,4},{6,7},{7,6},{8,9},{9,8},{10,11... | collective-permute-start | bytes 1572872 | tf_op jit(solution)/shard_map/ppermute | solution.py:645
  50.9 9.2 %collective-permute-start.8 = (bf16[2,288,256]{2,1,0:T(8,128)(2,1)S(1)}, bf16[2,288,256]{2,1,0:T(8,128)(2,1)S(1)}, u32[]{:S(2)}, u32[]{:S(2)}) collective-permute-start(bf16[2,288,256]{2,1,0:T(8,128)(2,1)S(1)} %get-tuple-element.84), channel_id=1, source_target_pairs={{0,8},{8,0},{16,24},{24,16},{1,9},{9,1},{17,25},{25,17},{2,10},{10... | collective-permute-start | bytes 884744 | tf_op jit(solution)/shard_map/ppermute | solution.py:485
  52.5 9.3 %collective-permute-start.10 = (bf16[2,288,256]{2,1,0:T(8,128)(2,1)S(1)}, bf16[2,288,256]{2,1,0:T(8,128)(2,1)S(1)}, u32[]{:S(2)}, u32[]{:S(2)}) collective-permute-start(bf16[2,288,256]{2,1,0:T(8,128)(2,1)S(1)} %get-tuple-element.89), channel_id=1, source_target_pairs={{0,16},{8,24},{16,0},{24,8},{1,17},{9,25},{17,1},{25,9},{2,18},{10... | collective-permute-start | bytes 884744 | tf_op jit(solution)/shard_map/ppermute | solution.py:485
  62.0 5.4 %collective-permute-start.11 = (bf16[1,288,256]{2,1,0:T(8,128)(2,1)S(1)}, bf16[1,288,256]{2,1,0:T(8,128)(2,1)S(1)}, u32[]{:S(2)}, u32[]{:S(2)}) collective-permute-start(bf16[1,288,256]{2,1,0:T(8,128)(2,1)S(1)} %get-tuple-element.91), channel_id=1, source_target_pairs={{0,16},{8,24},{16,0},{24,8},{1,17},{9,25},{17,1},{25,9},{2,18},{10... | collective-permute-start | bytes 442376 | tf_op jit(solution)/shard_map/ppermute | solution.py:485
  63.8 5.1 %collective-permute-start.12 = (bf16[1,288,256]{2,1,0:T(8,128)(2,1)S(1)}, bf16[1,288,256]{2,1,0:T(8,128)(2,1)S(1)}, u32[]{:S(2)}, u32[]{:S(2)}) collective-permute-start(bf16[1,288,256]{2,1,0:T(8,128)(2,1)S(1)} %get-tuple-element.93), channel_id=1, source_target_pairs={{0,8},{8,0},{16,24},{24,16},{1,9},{9,1},{17,25},{25,17},{2,10},{10... | collective-permute-start | bytes 442376 | tf_op jit(solution)/shard_map/ppermute | solution.py:485
  69.0 7.5 %collective-permute-start.13 = (bf16[144,256]{1,0:T(8,128)(2,1)S(1)}, bf16[144,256]{1,0:T(8,128)(2,1)S(1)}, u32[]{:S(2)}, u32[]{:S(2)}) collective-permute-start(bf16[144,256]{1,0:T(8,128)(2,1)S(1)} %get-tuple-element.95), channel_id=1, source_target_pairs={{0,2},{1,3},{2,4},{3,5},{4,6},{5,7},{6,0},{7,1},{8,10},{9,11},{10,... | collective-permute-start | bytes 221192 | tf_op jit(solution)/shard_map/ppermute | solution.py:529
  70.7 8.2 %collective-permute-start.14 = (bf16[144,256]{1,0:T(8,128)(2,1)S(1)}, bf16[144,256]{1,0:T(8,128)(2,1)S(1)}, u32[]{:S(2)}, u32[]{:S(2)}) collective-permute-start(bf16[144,256]{1,0:T(8,128)(2,1)S(1)} %get-tuple-element.96), channel_id=1, source_target_pairs={{0,4},{1,5},{2,6},{3,7},{4,0},{5,1},{6,2},{7,3},{8,12},{9,13},{10,... | collective-permute-start | bytes 221192 | tf_op jit(solution)/shard_map/ppermute | solution.py:529
  74.5 4.8 %collective-permute-start.15 = (bf16[144,256]{1,0:T(8,128)(2,1)S(1)}, bf16[144,256]{1,0:T(8,128)(2,1)S(1)}, u32[]{:S(2)}, u32[]{:S(2)}) collective-permute-start(bf16[144,256]{1,0:T(8,128)(2,1)S(1)} %get-tuple-element.97), channel_id=1, source_target_pairs={{0,6},{1,7},{2,0},{3,1},{4,2},{5,3},{6,4},{7,5},{8,14},{9,15},{10,... | collective-permute-start | bytes 221192 | tf_op jit(solution)/shard_map/ppermute | solution.py:529
  79.3 4.9 %collective-permute-start.18 = (bf16[144,256]{1,0:T(8,128)(2,1)S(1)}, bf16[144,256]{1,0:T(8,128)(2,1)S(1)}, u32[]{:S(2)}, u32[]{:S(2)}) collective-permute-start(bf16[144,256]{1,0:T(8,128)(2,1)S(1)} %shard_map.113.refs_0_), channel_id=1, source_target_pairs={{0,6},{1,7},{2,0},{3,1},{4,2},{5,3},{6,4},{7,5},{8,14},{9,15},{10,... | collective-permute-start | bytes 221192 | tf_op jit(solution)/shard_map/ppermute | solution.py:539
  81.6 5.3 %collective-permute-start.17 = (bf16[144,256]{1,0:T(8,128)(2,1)S(1)}, bf16[144,256]{1,0:T(8,128)(2,1)S(1)}, u32[]{:S(2)}, u32[]{:S(2)}) collective-permute-start(bf16[144,256]{1,0:T(8,128)(2,1)S(1)} %shard_map.113.refs_0_), channel_id=1, source_target_pairs={{0,4},{1,5},{2,6},{3,7},{4,0},{5,1},{6,2},{7,3},{8,12},{9,13},{10,... | collective-permute-start | bytes 221192 | tf_op jit(solution)/shard_map/ppermute | solution.py:539
  81.7 6.2 %collective-permute-start.16 = (bf16[144,256]{1,0:T(8,128)(2,1)S(1)}, bf16[144,256]{1,0:T(8,128)(2,1)S(1)}, u32[]{:S(2)}, u32[]{:S(2)}) collective-permute-start(bf16[144,256]{1,0:T(8,128)(2,1)S(1)} %shard_map.113.refs_0_), channel_id=1, source_target_pairs={{0,2},{1,3},{2,4},{3,5},{4,6},{5,7},{6,0},{7,1},{8,10},{9,11},{10,... | collective-permute-start | bytes 221192 | tf_op jit(solution)/shard_map/ppermute | solution.py:539
  87.9 1.6 %collective-permute-start.19 = (bf16[576,256]{1,0:T(8,128)(2,1)S(1)}, bf16[576,256]{1,0:T(8,128)(2,1)S(1)}, u32[]{:S(2)}, u32[]{:S(2)}) collective-permute-start(bf16[576,256]{1,0:T(8,128)(2,1)S(1)} %shard_map.114.refs_0_), channel_id=1, source_target_pairs={{0,1},{1,0},{2,3},{3,2},{4,5},{5,4},{6,7},{7,6},{8,9},{9,8},{10,11... | collective-permute-start | bytes 884744 | tf_op jit(solution)/shard_map/ppermute | solution.py:549

commit v8 on v7

--- a/solution.py
+++ b/solution.py
@@ -44,22 +44,14 @@
     return jax.ShapeDtypeStruct(shape, dtype)
 
 
-def edge_of(tile, height, width):
-    def kernel(tile, edge, sem):
-        core = lax.rem(lax.axis_index("tile"), 2)
-        line = pl.ds(pl.multiple_of(core * (height - 1) * width, width), width)
-        copy = pltpu.make_async_copy(tile.at[line, :], edge, sem)
-        copy.start()
-        copy.wait()
-
-    return local_kernel(
-        kernel, sds((width, 256), BF), tile, scratch=[pltpu.SemaphoreType.DMA], hbm=(0,)
-    )
-
-
-def pack_kernel(side, height, cot, owner, row, col, packed, notes, low, high, wide, places, sems):
+def pack_kernel(
+    side, height, width, cot, owner, row, col, tile, packed, notes, edge, low, high, wide, places, sems
+):
     regions = cot.shape[2]
-    copies = [
+    core = lax.rem(lax.axis_index("tile"), 2)
+    line = pl.ds(pl.multiple_of(core * (height - 1) * width, width), width)
+    copies = [pltpu.make_async_copy(tile.at[line, :], edge, sems.at[3])]
+    copies += [
         pltpu.make_async_copy(source, places.at[n], sems.at[n])
         for n, source in enumerate((owner, row, col))
     ]
@@ -87,48 +79,55 @@
         notes[r] = note.astype(BF)
 
 
-def pack(cotangent, height, place):
+def pack(cotangent, tile, height, width, place):
     side, regions = cotangent.shape[0], cotangent.shape[2]
     return local_kernel(
-        functools.partial(pack_kernel, side, height),
-        (sds((regions, SLOT, 256), BF), sds((regions, 16, 256), BF)),
+        functools.partial(pack_kernel, side, height, width),
+        (
+            sds((regions, SLOT, 256), BF),
+            sds((regions, 16, 256), BF),
+            sds((width, 256), BF),
+        ),
         cotangent,
         *place,
+        tile,
         scratch=[
             pltpu.VMEM((side * side * regions, 128), F32),
             pltpu.VMEM((side * side * regions, 128), F32),
             pltpu.VMEM((SLOT, 256), F32),
             pltpu.SMEM((3, 1, regions), jnp.int32),
-            pltpu.SemaphoreType.DMA((3,)),
+            pltpu.SemaphoreType.DMA((4,)),
         ],
-        hbm=(1, 2, 3),
-    )
-
-
-def pyramid_part(height, width, own, other, rim_a, rim_b, wf, pyr, xp, fetched):
+        hbm=(1, 2, 3, 4),
+    )
+
+
+def shifted(v, width):
+    col = lax.broadcasted_iota(jnp.int32, (width, 256), 0)
+    left = jnp.where(col == 0, 0.0, pltpu.roll(v, 1, 0)).astype(BF)
+    right = jnp.where(col == width - 1, 0.0, pltpu.roll(v, width - 1, 0)).astype(BF)
+    return left, v.astype(BF), right
+
+
+def pyramid_part(height, width, own, other, wf, pyr, xp, fetched):
     core = lax.rem(lax.axis_index("tile"), 2)
     cells = height * width
-    col = lax.broadcasted_iota(jnp.int32, (width, 256), 0)
-
-    def fill(src, count, where):
+
+    def fill(src, where):
         def step(t, carry):
             v = src[pl.ds(pl.multiple_of(t * width, width), width), :].astype(F32)
             to = pl.ds(pl.multiple_of(where + t * width, width), width)
-            xp[to, 0:256] = jnp.where(col == 0, 0.0, pltpu.roll(v, 1, 0)).astype(BF)
-            xp[to, 256:512] = v.astype(BF)
-            xp[to, 512:768] = jnp.where(
-                col == width - 1, 0.0, pltpu.roll(v, width - 1, 0)
-            ).astype(BF)
+            for b, piece in enumerate(shifted(v, width)):
+                xp[to, b * 256 : b * 256 + 256] = piece
             return carry
 
-        lax.fori_loop(0, count, step, 0)
+        lax.fori_loop(0, height, step, 0)
 
     bottom = width + 2 * cells
-    fill(own, height, width + core * cells)
-    fill(other, height, width + (1 - core) * cells)
-    fill(rim_a, 1, core * bottom)
-    fill(rim_b, 1, (1 - core) * bottom)
-
+    fill(own, width + core * cells)
+    fill(other, width + (1 - core) * cells)
+    xp[0:width, :] = jnp.zeros((width, 768), BF)
+    xp[bottom : bottom + width, :] = jnp.zeros((width, 768), BF)
     fetched.wait()
 
     def conv(t, carry):
@@ -137,11 +136,37 @@
         for a in range(3):
             piece = xp[pl.ds(pl.multiple_of(at + a * width, 64), 256), :]
             total += jnp.dot(piece, wf[a * 768 : a * 768 + 768, :], preferred_element_type=F32)
-        pyr[pl.ds(pl.multiple_of(at, 256), 256), :] = total.astype(BF).astype(F32)
+        cell = at + lax.broadcasted_iota(jnp.int32, (256, 256), 0)
+        open_row = (cell < width) | (cell >= 2 * cells - width)
+        pyr[pl.ds(pl.multiple_of(at, 256), 256), :] = jnp.where(
+            open_row, total, total.astype(BF).astype(F32)
+        )
         return carry
 
     lax.fori_loop(0, 2 * cells // 256, conv, 0)
     pyr[2 * cells : 2 * cells + 16, :] = jnp.zeros((16, 256), F32)
+
+
+def edges_part(height, width, rim_a, rim_b, wf, pyr):
+    core = lax.rem(lax.axis_index("tile"), 2)
+    last = 2 * height * width - width
+
+    def close(rim, at, tap):
+        total = pyr[at : at + width, :]
+        for b, piece in enumerate(shifted(rim[...].astype(F32), width)):
+            k = 3 * tap + b
+            total += jnp.dot(piece, wf[k * 256 : k * 256 + 256, :], preferred_element_type=F32)
+        pyr[at : at + width, :] = total.astype(BF).astype(F32)
+
+    @pl.when(core == 0)
+    def _():
+        close(rim_a, 0, 0)
+        close(rim_b, last, 2)
+
+    @pl.when(core == 1)
+    def _():
+        close(rim_b, 0, 0)
+        close(rim_a, last, 2)
 
 
 def flip_part(w, wb):
@@ -170,7 +195,7 @@
     cells = side * PITCH
     inside = (lax.broadcasted_iota(jnp.int32, (cells, 256), 0) & (PITCH - 1)) < side
     used = pl.ds(16, cells)
-    per = (blocks or early)[0].shape[0]
+    per = blocks[0].shape[0]
     tail = pl.ds(192, 16)
 
     count = jnp.int32(0)
@@ -333,11 +358,11 @@
     gp_other[...] = gp[pl.ds(pl.multiple_of((1 - core) * cells, cells), cells), :].astype(BF)
 
 
-def main_call(side, height, width, dp, chips, first, last, plan, state, weights, blocks, early, stash):
+def main_call(side, height, width, dp, chips, first, last, plan, state, weights, rims, blocks, early, stash):
     n = len(blocks)
     big = 2 * height * width + 16
     cells = side * PITCH
-    kept = (sds((big, 256), F32),) + (sds((2304, 256), BF),) * 4
+    kept = (sds((big, 256), F32),) + (sds((2304, 256), BF),) * 5
     sums = (sds((256, 2304), F32), sds((256, 2304), F32), sds((big, 256), F32))
     ends = (
         sds((2304, 256), BF),
@@ -345,13 +370,13 @@
         sds((height * width, 256), F32),
         sds((height * width, 256), BF),
     )
-    per = blocks[0].shape[0]
+    per = early[0].shape[0] if early else 0
     stashed = (
         sds((per, cells, 256), BF),
         sds((per, cells, 256), F32),
         sds((per, cells, 256), F32),
     )
-    outs = (kept if first else ()) + sums + (ends if last else ()) + (stashed if early else ())
+    outs = (kept if first else kept[:1] if rims else ()) + sums + (ends if last else ()) + (stashed if early else ())
     scratch = [
         pltpu.VMEM((cells + 32, 768), BF),
         pltpu.VMEM((cells + 32, 768), BF),
@@ -365,7 +390,6 @@
     if first:
         extra = [
             pltpu.VMEM(((2 * height + 2) * width, 768), BF),
-            pltpu.VMEM((2304, 256), BF),
             pltpu.VMEM((height * width, 256), BF),
             pltpu.SemaphoreType.DMA((4,)),
         ]
@@ -380,6 +404,7 @@
 
         state_refs = take(len(state))
         weight_refs = take(len(weights))
+        rim_refs = take(len(rims))
         block_refs = take(n)
         early_refs = take(len(early))
         stash_refs = take(len(stash))
@@ -388,9 +413,9 @@
             stash_refs = out_refs[-3:]
         scratch_refs = take(len(scratch))
         if first:
-            pyr, wb1, wb2, w1, w2 = out_refs[:5]
-            acc1, acc2, gp = out_refs[5:8]
-            xp, wf, own, sems = refs
+            pyr, wb1, wb2, w1, w2, wf = out_refs[:6]
+            acc1, acc2, gp = out_refs[6:9]
+            xp, own, sems = refs
             copies = [
                 pltpu.make_async_copy(source, to, sems.at[k])
                 for k, (source, to) in enumerate(zip((state_refs[0], *weight_refs), (own, wf, w1, w2)))
@@ -400,27 +425,34 @@
             for total in (acc1, acc2, gp):
                 total[...] = jnp.zeros(total.shape, F32)
             copies[0].wait()
-            pyramid_part(height, width, own, *state_refs[1:], wf, pyr, xp, copies[1])
+            pyramid_part(height, width, own, state_refs[1], wf, pyr, xp, copies[1])
             copies[2].wait()
             flip_part(w1, wb1)
             copies[3].wait()
             flip_part(w2, wb2)
         else:
-            pyr, wb1, wb2, w1, w2 = state_refs[:5]
-            acc1, acc2, gp = out_refs[:3]
-        regions_part(
-            *(side, height, width, plan, block_refs, early_refs, stash_refs),
-            *((pyr, wb1, wb2, w1, w2), (acc1, acc2, gp), scratch_refs),
-        )
+            pyr, wb1, wb2, w1, w2, wf = state_refs[:6]
+            shared = list(out_refs)
+            if rims:
+                pyr = shared.pop(0)
+                edges_part(height, width, *rim_refs, wf, pyr)
+            acc1, acc2, gp = shared[:3]
+        if n:
+            regions_part(
+                *(side, height, width, plan, block_refs, early_refs, stash_refs),
+                *((pyr, wb1, wb2, w1, w2), (acc1, acc2, gp), scratch_refs),
+            )
         if last:
             keep, *sends, gp_own, gp_other = out_refs[3:]
             finish_part(height, width, dp, chips, acc1, acc2, gp, keep, sends, gp_own, gp_other)
 
-    aliases = {} if first else {5: 0, 6: 1, 7: 2}
+    aliases = {} if first else {6: 0, 7: 1, 8: 2}
+    if rims:
+        aliases = {0: 0, 6: 1, 7: 2, 8: 3}
     return run(
         kernel,
         outs,
-        [*state, *weights, *blocks, *early, *stash],
+        [*state, *weights, *rims, *blocks, *early, *stash],
         scratch=scratch + extra,
         aliases=aliases,
         hbm=(0, *range(len(state), len(state) + len(weights))) if first else (),
@@ -600,13 +632,11 @@
     tile = features.reshape(height * width, channels)
     regions = cotangent.shape[1]
     place = [x.reshape(1, regions) for x in (owner, row_off, col_off)]
-    edge = edge_of(tile, height, width)
+    other = lax.ppermute(tile, "tile", swap)
+    packed, notes, edge = pack(cotangent[0].transpose(1, 2, 0, 3), tile, height, width, place)
     rim_a = lax.ppermute(
         edge, "tile", [(i, i + 1 if i % 2 else i - 1) for i in range(1, tiles - 1)]
     )
-    other = lax.ppermute(tile, "tile", swap)
-    packed, notes = pack(cotangent[0].transpose(1, 2, 0, 3), height, place)
-    packed, rim_a = lax.optimization_barrier((packed, rim_a))
     rim_b = lax.ppermute(rim_a, "tile", swap)
 
     order = [0] + list(range(1, chips, 2)) + list(range(2, chips, 2))[::-1]
@@ -619,28 +649,26 @@
     block = lax.ppermute(packed, "tile", ring)
     notes = lax.ppermute(notes, "tile", [(j, i) for i, j in ring])
     sizes = (side, height, width, dp, chips)
-    held, plan = [packed], [1] + [4] * (chips - 2) if chips > 2 else [None]
-    if chips > 2:
-        plan[-1] = None
-    state, weights, stash = [tile, other, rim_a, rim_b], [wf, w1, w2], []
-    for step in range(chips):
-        first, last = step == 0, step == chips - 1
-        early = [notes] if step == chips - 2 else []
-        if last:
-            got = main_call(*sizes, first, last, [None], state, [], [block], [], stash)
+    plan = [0] + [4] * (chips - 3) + [None]
+    start = main_call(*sizes, True, False, [], [tile, other], [wf, w1, w2], [], [], [], [])
+    kept, sums, held = list(start[:6]), list(start[6:]), [packed]
+    for step in range(1, chips):
+        state = kept + sums
+        if step == chips - 1:
+            got = main_call(*sizes, False, True, [None], state, [], [], [block], [], stash)
             ends = got[3:]
             break
-        got = list(main_call(*sizes, first, last, plan, state, weights, held, early, []))
-        if first:
-            kept, got = got[:5], got[5:]
-        sums, stash, weights = got[:3], got[3:], []
-        if step < chips - 2:
-            block, kept[0], sums[0], notes = lax.optimization_barrier(
-                (block, kept[0], sums[0], notes)
-            )
-            held = held + [block]
-            block = lax.ppermute(block, "tile", ring)
-        state = kept + sums
+        block, state[0], state[-1], notes, rim_a = lax.optimization_barrier(
+            (block, state[0], state[-1], notes, rim_a)
+        )
+        held = held + [block]
+        block = lax.ppermute(block, "tile", ring)
+        early = [notes] if step == chips - 2 else []
+        rims = [rim_a, rim_b] if step == 1 else []
+        got = list(main_call(*sizes, False, False, plan, state, [], rims, held, early, []))
+        if rims:
+            kept[0] = got.pop(0)
+        sums, stash = got[:3], got[3:]
     keep, *sends, gp_own, gp_other = ends
     gp_got = lax.ppermute(gp_other, "tile", swap)
 

time: 90.9 us -> 90.2 us (level)
  Pallas kernels: 21.6 us -> 24.6 us
  waiting for transfers between devices: 41.1 us -> 38.4 us
    ppermute x2, waiting for transfers between devices: 15.6 us -> 8.02 us  [body(): block = lax.ppermute(block, 'tile', ring)]
    ppermute x4, starting transfers between devices: 7.08 us -> 2.89 us  [exchange(): c.received.append(lax.ppermute(c.parts[2 * half + 1], 'dp', pairs))]
    ppermute x1, waiting for transfers between devices: 1.2 us -> 4.2 us  [body(): notes = lax.ppermute(notes, 'tile', [(j, i) for i, j in ring])]
    ppermute x4, waiting for transfers between devices: 9.9 us -> 12.9 us  [exchange(): c.received.append(lax.ppermute(c.parts[2 * half + 1], 'dp', pairs))]
    pallas_call x13 -> x12, Pallas kernels: 21.6 us -> 24.6 us  [run(): pl.pallas_call(kernel, out_shape=tuple((s if i in hbm_out else pltpu.VMEM...]
    ppermute x1, starting transfers between devices: 5.36 us -> 2.64 us  [body(): block = lax.ppermute(packed, 'tile', ring)]
    ppermute x2, starting transfers between devices: 2.09 us -> 4.68 us  [body(): block = lax.ppermute(block, 'tile', ring)]
    ppermute x3, starting transfers between devices: 5.5 us -> 7.71 us  [deal(): lax.ppermute(dealt[k], 'tile', shifts[k])]
  transfers between devices with their start and end apart: 20 -> 20, of which waited for: 15 -> 15; matrix products, arithmetic and copies ran while one was open for 0% -> 0% of each run, Pallas kernels for 21% -> 22%
where the time goes in v8:
time: 90.2 us; the launch traced here: 90.6 us
  waiting for transfers between devices  38.4 us (43%)
  starting transfers between devices  25.9 us (29%)
  Pallas kernels  24.6 us (27%)
  local copies, waits for them, and re-layouts  1 us (1%)
    pallas_call x12, Pallas kernels, run(): pl.pallas_call(kernel, out_shape=tuple((s if i in hbm_out else pltpu.VMEM...  24.6 us
    ppermute x4, waiting for transfers between devices, exchange(): c.received.append(lax.ppermute(c.parts[2 * half + 1], 'dp', pairs))  12.9 us
    ppermute x2, waiting for transfers between devices, body(): block = lax.ppermute(block, 'tile', ring)  8.02 us
    ppermute x3, starting transfers between devices, deal(): lax.ppermute(dealt[k], 'tile', shifts[k])  7.71 us
    ppermute x3, waiting for transfers between devices, gather(): lax.ppermute(c.mine, 'tile', shifts[k])  4.79 us
    ppermute x2, starting transfers between devices, body(): block = lax.ppermute(block, 'tile', ring)  4.68 us
    ppermute x1, waiting for transfers between devices, body(): notes = lax.ppermute(notes, 'tile', [(j, i) for i, j in ring])  4.2 us
    ppermute x3, starting transfers between devices, gather(): lax.ppermute(c.mine, 'tile', shifts[k])  4.2 us
  transfers between devices with their start and end apart: 20, of which 15 were waited for; matrix products, arithmetic and copies ran while one was open for 0% of the time, Pallas kernels for 22%

profile of v8, /device:TPU:0, one launch (start us, length us, event | category | flops | bytes accessed | tf_op | source)
XLA Modules:
  0.0 90.6 jit_solution(16302184153565545833)
XLA Ops:
  3.1 2.6 %collective-permute-start = (bf16[4,208,256]{2,1,0:T(8,128)(2,1)S(1)}, bf16[4,208,256]{2,1,0:T(8,128)(2,1)S(1)}, u32[]{:S(2)}, u32[]{:S(2)}) collective-permute-start(bf16[4,208,256]{2,1,0:T(8,128)(2,1)S(1)} %get-tuple-element.54.refs_11_.refs_9_), channel_id=1, source_target_pairs={{0,2},{1,3},{2,6},{3,7},{6,4},{7,5},{4,0},{5,1},{8,10},{9,11},{10,... | collective-permute-start | bytes 1277960 | tf_op jit(solution)/shard_map/ppermute | solution.py:649
  7.5 6.2 %shard_map.104 = (f32[2064,256]{1,0:T(8,128)S(1)}, bf16[2304,256]{1,0:T(8,128)(2,1)S(1)}, bf16[2304,256]{1,0:T(8,128)(2,1)S(1)}, bf16[2304,256]{1,0:T(8,128)(2,1...) custom-call(bf16[1024,256]{1,0:T(8,128)(2,1)} %bitcast.12, ...), custom_call_target="tpu_custom_call" | custom-call | tf_op jit(solution)/shard_map/pallas_call | solution.py:27
  13.7 4.2 %collective-permute-done.2.refs_12_ = bf16[4,16,256]{2,1,0:T(8,128)(2,1)S(1)} collective-permute-done((bf16[4,16,256]{2,1,0:T(8,128)(2,1)S(1)}, bf16[4,16,256]{2,1,0:T(8,128)(2,1)S(1)}, u32[]{:S(2)}, u32[]{:S(2)}) %collective-permute-start.2) | collective-permute-done | bytes 32800 | tf_op jit(solution)/shard_map/ppermute | solution.py:650
  17.9 1.7 %collective-permute-start.5 = (bf16[4,208,256]{2,1,0:T(8,128)(2,1)S(1)}, bf16[4,208,256]{2,1,0:T(8,128)(2,1)S(1)}, u32[]{:S(2)}, u32[]{:S(2)}) collective-permute-start(bf16[4,208,256]{2,1,0:T(8,128)(2,1)S(1)} %collective-permute-done.refs_12_.refs_10_), channel_id=1, source_target_pairs={{0,2},{1,3},{2,6},{3,7},{6,4},{7,5},{4,0},{5,1},{8,10},{9,11},{10,... | collective-permute-start | bytes 1277960 | tf_op jit(solution)/shard_map/ppermute | solution.py:665
  19.7 1.2 %collective-permute-done.4.refs_10_ = bf16[64,256]{1,0:T(8,128)(2,1)S(1)} collective-permute-done((bf16[64,256]{1,0:T(8,128)(2,1)S(1)}, bf16[64,256]{1,0:T(8,128)(2,1)S(1)}, u32[]{:S(2)}, u32[]{:S(2)}) %collective-permute-start.4) | collective-permute-done | bytes 32800 | tf_op jit(solution)/shard_map/ppermute | solution.py:640
  20.9 9.9 %shard_map.105 = (f32[2064,256]{1,0:T(8,128)S(1)}, f32[256,2304]{1,0:T(8,128)S(1)}, f32[256,2304]{1,0:T(8,128)S(1)}, f32[2064,256]{1,0:T(8,128)S(1)}) custom-call(f32[2064,256]{1,0:T(8,128)S(1)} %get-tuple-element.59.refs_0_, ...), custom_call_target="tpu_custom_call", output_to_operand_aliasing={{0}: (0, {}), {1}: (6, {}), {2}: (7, {}), {3}: (8, {})} | custom-call | tf_op jit(solution)/shard_map/pallas_call | solution.py:27
  30.8 2.9 %collective-permute-start.6 = (bf16[4,208,256]{2,1,0:T(8,128)(2,1)S(1)}, bf16[4,208,256]{2,1,0:T(8,128)(2,1)S(1)}, u32[]{:S(2)}, u32[]{:S(2)}) collective-permute-start(bf16[4,208,256]{2,1,0:T(8,128)(2,1)S(1)} %collective-permute-done.5.refs_11_), channel_id=1, source_target_pairs={{0,2},{1,3},{2,6},{3,7},{6,4},{7,5},{4,0},{5,1},{8,10},{9,11},{10,... | collective-permute-start | bytes 1277960 | tf_op jit(solution)/shard_map/ppermute | solution.py:665
  33.7 1.9 %shard_map.106 = (f32[256,2304]{1,0:T(8,128)S(1)}, f32[256,2304]{1,0:T(8,128)S(1)}, f32[2064,256]{1,0:T(8,128)S(1)}, bf16[4,224,256]{2,1,0:T(8,128)(2,1)S(1)}, f...) custom-call(f32[2064,256]{1,0:T(8,128)S(1)} %get-tuple-element.73.re, ...), custom_call_target="tpu_custom_call", output_to_operand_aliasing={{0}: (6, {}), {1}: (7, {}), {2}: (8, {})} | custom-call | tf_op jit(solution)/shard_map/pallas_call | solution.py:27
  35.6 8.0 %collective-permute-done.6.refs_9_ = bf16[4,208,256]{2,1,0:T(8,128)(2,1)S(1)} collective-permute-done((bf16[4,208,256]{2,1,0:T(8,128)(2,1)S(1)}, bf16[4,208,256]{2,1,0:T(8,128)(2,1)S(1)}, u32[]{:S(2)}, u32[]{:S(2)}) %collective-permute-start.6) | collective-permute-done | bytes 426016 | tf_op jit(solution)/shard_map/ppermute | solution.py:665
  43.6 3.1 %shard_map.107 = (f32[256,2304]{1,0:T(8,128)S(1)}, f32[256,2304]{1,0:T(8,128)S(1)}, f32[2064,256]{1,0:T(8,128)S(1)}, bf16[2304,256]{1,0:T(8,128)(2,1)S(1)}, bf16...) custom-call(f32[2064,256]{1,0:T(8,128)S(1)} %get-tuple-element.73.re, ...), custom_call_target="tpu_custom_call", output_to_operand_aliasing={{0}: (6, {}), {1}: (7, {}), {2}: (8, {})} | custom-call | tf_op jit(solution)/shard_map/pallas_call | solution.py:27
  46.7 1.3 %collective-permute-start.7 = (bf16[2304,256]{1,0:T(8,128)(2,1)S(1)}, bf16[2304,256]{1,0:T(8,128)(2,1)S(1)}, u32[]{:S(2)}, u32[]{:S(2)}) collective-permute-start(bf16[2304,256]{1,0:T(8,128)(2,1)S(1)} %get-tuple-element.86), channel_id=1, source_target_pairs={{0,1},{1,0},{2,3},{3,2},{4,5},{5,4},{6,7},{7,6},{8,9},{9,8},{10,11... | collective-permute-start | bytes 3538952 | tf_op jit(solution)/shard_map/ppermute | solution.py:480
  48.1 2.4 %collective-permute-done.7.got_ref = bf16[2304,256]{1,0:T(8,128)(2,1)S(1)} collective-permute-done((bf16[2304,256]{1,0:T(8,128)(2,1)S(1)}, bf16[2304,256]{1,0:T(8,128)(2,1)S(1)}, u32[]{:S(2)}, u32[]{:S(2)}) %collective-permute-start.7) | collective-permute-done | bytes 1179680 | tf_op jit(solution)/shard_map/ppermute | solution.py:480
  50.8 2.2 %collective-permute-start.8 = (bf16[2,288,256]{2,1,0:T(8,128)(2,1)S(1)}, bf16[2,288,256]{2,1,0:T(8,128)(2,1)S(1)}, u32[]{:S(2)}, u32[]{:S(2)}) collective-permute-start(bf16[2,288,256]{2,1,0:T(8,128)(2,1)S(1)} %get-tuple-element.88), channel_id=1, source_target_pairs={{0,8},{8,0},{16,24},{24,16},{1,9},{9,1},{17,25},{25,17},{2,10},{10... | collective-permute-start | bytes 884744 | tf_op jit(solution)/shard_map/ppermute | solution.py:517
  53.9 6.6 %collective-permute-done.8.pr = bf16[2,288,256]{2,1,0:T(8,128)(2,1)S(1)} collective-permute-done((bf16[2,288,256]{2,1,0:T(8,128)(2,1)S(1)}, bf16[2,288,256]{2,1,0:T(8,128)(2,1)S(1)}, u32[]{:S(2)}, u32[]{:S(2)}) %collective-permute-start.8) | collective-permute-done | bytes 294944 | tf_op jit(solution)/shard_map/ppermute | solution.py:517
  60.5 1.5 %collective-permute-done.10.qr = bf16[2,288,256]{2,1,0:T(8,128)(2,1)S(1)} collective-permute-done((bf16[2,288,256]{2,1,0:T(8,128)(2,1)S(1)}, bf16[2,288,256]{2,1,0:T(8,128)(2,1)S(1)}, u32[]{:S(2)}, u32[]{:S(2)}) %collective-permute-start.10) | collective-permute-done | bytes 294944 | tf_op jit(solution)/shard_map/ppermute | solution.py:517
  62.8 4.5 %collective-permute-done.11.pr = bf16[1,288,256]{2,1,0:T(8,128)(2,1)S(1)} collective-permute-done((bf16[1,288,256]{2,1,0:T(8,128)(2,1)S(1)}, bf16[1,288,256]{2,1,0:T(8,128)(2,1)S(1)}, u32[]{:S(2)}, u32[]{:S(2)}) %collective-permute-start.11) | collective-permute-done | bytes 147488 | tf_op jit(solution)/shard_map/ppermute | solution.py:517
  67.7 5.3 %collective-permute-start.13 = (bf16[144,256]{1,0:T(8,128)(2,1)S(1)}, bf16[144,256]{1,0:T(8,128)(2,1)S(1)}, u32[]{:S(2)}, u32[]{:S(2)}) collective-permute-start(bf16[144,256]{1,0:T(8,128)(2,1)S(1)} %get-tuple-element.99), channel_id=1, source_target_pairs={{0,2},{1,3},{2,4},{3,5},{4,6},{5,7},{6,0},{7,1},{8,10},{9,11},{10,... | collective-permute-start | bytes 221192 | tf_op jit(solution)/shard_map/ppermute | solution.py:561
  73.7 1.8 %collective-permute-start.15 = (bf16[144,256]{1,0:T(8,128)(2,1)S(1)}, bf16[144,256]{1,0:T(8,128)(2,1)S(1)}, u32[]{:S(2)}, u32[]{:S(2)}) collective-permute-start(bf16[144,256]{1,0:T(8,128)(2,1)S(1)} %get-tuple-element.101), channel_id=1, source_target_pairs={{0,6},{1,7},{2,0},{3,1},{4,2},{5,3},{6,4},{7,5},{8,14},{9,15},{10,... | collective-permute-start | bytes 221192 | tf_op jit(solution)/shard_map/ppermute | solution.py:561
  75.8 3.0 %collective-permute-done.14.refs_2_ = bf16[144,256]{1,0:T(8,128)(2,1)S(1)} collective-permute-done((bf16[144,256]{1,0:T(8,128)(2,1)S(1)}, bf16[144,256]{1,0:T(8,128)(2,1)S(1)}, u32[]{:S(2)}, u32[]{:S(2)}) %collective-permute-start.14) | collective-permute-done | bytes 73760 | tf_op jit(solution)/shard_map/ppermute | solution.py:561
  78.9 2.8 %collective-permute-start.18 = (bf16[144,256]{1,0:T(8,128)(2,1)S(1)}, bf16[144,256]{1,0:T(8,128)(2,1)S(1)}, u32[]{:S(2)}, u32[]{:S(2)}) collective-permute-start(bf16[144,256]{1,0:T(8,128)(2,1)S(1)} %shard_map.112.refs_0_), channel_id=1, source_target_pairs={{0,6},{1,7},{2,0},{3,1},{4,2},{5,3},{6,4},{7,5},{8,14},{9,15},{10,... | collective-permute-start | bytes 221192 | tf_op jit(solution)/shard_map/ppermute | solution.py:571
  81.7 1.4 %collective-permute-start.16 = (bf16[144,256]{1,0:T(8,128)(2,1)S(1)}, bf16[144,256]{1,0:T(8,128)(2,1)S(1)}, u32[]{:S(2)}, u32[]{:S(2)}) collective-permute-start(bf16[144,256]{1,0:T(8,128)(2,1)S(1)} %shard_map.112.refs_0_), channel_id=1, source_target_pairs={{0,2},{1,3},{2,4},{3,5},{4,6},{5,7},{6,0},{7,1},{8,10},{9,11},{10,... | collective-permute-start | bytes 221192 | tf_op jit(solution)/shard_map/ppermute | solution.py:571
  83.0 1.2 %collective-permute-done.18.refs_3_ = bf16[144,256]{1,0:T(8,128)(2,1)S(1)} collective-permute-done((bf16[144,256]{1,0:T(8,128)(2,1)S(1)}, bf16[144,256]{1,0:T(8,128)(2,1)S(1)}, u32[]{:S(2)}, u32[]{:S(2)}) %collective-permute-start.18) | collective-permute-done | bytes 73760 | tf_op jit(solution)/shard_map/ppermute | solution.py:571
  84.2 2.7 %collective-permute-done.17.refs_2_ = bf16[144,256]{1,0:T(8,128)(2,1)S(1)} collective-permute-done((bf16[144,256]{1,0:T(8,128)(2,1)S(1)}, bf16[144,256]{1,0:T(8,128)(2,1)S(1)}, u32[]{:S(2)}, u32[]{:S(2)}) %collective-permute-start.17) | collective-permute-done | bytes 73760 | tf_op jit(solution)/shard_map/ppermute | solution.py:571
  88.0 1.6 %collective-permute-done.19.refs_1_ = bf16[576,256]{1,0:T(8,128)(2,1)S(1)} collective-permute-done((bf16[576,256]{1,0:T(8,128)(2,1)S(1)}, bf16[576,256]{1,0:T(8,128)(2,1)S(1)}, u32[]{:S(2)}, u32[]{:S(2)}) %collective-permute-start.19) | collective-permute-done | bytes 294944 | tf_op jit(solution)/shard_map/ppermute | solution.py:581
  (30 shorter events, 9.9 us)
Async XLA Ops:
  0.6 6.8 %collective-permute-start.1 = (bf16[1024,256]{1,0:T(8,128)(2,1)}, bf16[1024,256]{1,0:T(8,128)(2,1)S(1)}, u32[]{:S(2)}, u32[]{:S(2)}) collective-permute-start(bf16[1024,256]{1,0:T(8,128)(2,1)} %bitcast.10), channel_id=1, source_target_pairs={{0,1},{1,0},{2,3},{3,2},{4,5},{5,4},{6,7},{7,6},{8,9},{9,8},{10,11... | collective-permute-start | bytes 1572872 | tf_op jit(solution)/shard_map/ppermute | solution.py:635
  1.1 1.0 %copy-start = (bf16[1,4,14,14,256]{4,1,3,2,0:T(4,128)(2,1)S(1)}, bf16[1,4,14,14,256]{4,1,3,2,0:T(4,128)(2,1)}, u32[]{:S(2)}) copy-start(bf16[1,4,14,14,256]{4,1,3,2,0:T(4,128)(2,1)} %param.15) | copy-start | bytes 1204228
  3.1 14.8 %collective-permute-start = (bf16[4,208,256]{2,1,0:T(8,128)(2,1)S(1)}, bf16[4,208,256]{2,1,0:T(8,128)(2,1)S(1)}, u32[]{:S(2)}, u32[]{:S(2)}) collective-permute-start(bf16[4,208,256]{2,1,0:T(8,128)(2,1)S(1)} %get-tuple-element.54.refs_11_.refs_9_), channel_id=1, source_target_pairs={{0,2},{1,3},{2,6},{3,7},{6,4},{7,5},{4,0},{5,1},{8,10},{9,11},{10,... | collective-permute-start | bytes 1277960 | tf_op jit(solution)/shard_map/ppermute | solution.py:649
  5.7 12.2 %collective-permute-start.2 = (bf16[4,16,256]{2,1,0:T(8,128)(2,1)S(1)}, bf16[4,16,256]{2,1,0:T(8,128)(2,1)S(1)}, u32[]{:S(2)}, u32[]{:S(2)}) collective-permute-start(bf16[4,16,256]{2,1,0:T(8,128)(2,1)S(1)} %get-tuple-element.57), channel_id=1, source_target_pairs={{2,0},{3,1},{6,2},{7,3},{4,6},{5,7},{0,4},{1,5},{10,8},{11,9},{14,... | collective-permute-start | bytes 98312 | tf_op jit(solution)/shard_map/ppermute | solution.py:650
  6.8 11.1 %collective-permute-start.3 = (bf16[64,256]{1,0:T(8,128)(2,1)S(1)}, bf16[64,256]{1,0:T(8,128)(2,1)S(1)}, u32[]{:S(2)}, u32[]{:S(2)}) collective-permute-start(bf16[64,256]{1,0:T(8,128)(2,1)S(1)} %get-tuple-element.58), channel_id=1, source_target_pairs={{1,2},{2,1},{3,4},{4,3},{5,6},{6,5},{9,10},{10,9},{11,12},{12,11},... | collective-permute-start | bytes 98312 | tf_op jit(solution)/shard_map/ppermute | solution.py:637
  17.9 12.8 %collective-permute-start.5 = (bf16[4,208,256]{2,1,0:T(8,128)(2,1)S(1)}, bf16[4,208,256]{2,1,0:T(8,128)(2,1)S(1)}, u32[]{:S(2)}, u32[]{:S(2)}) collective-permute-start(bf16[4,208,256]{2,1,0:T(8,128)(2,1)S(1)} %collective-permute-done.refs_12_.refs_10_), channel_id=1, source_target_pairs={{0,2},{1,3},{2,6},{3,7},{6,4},{7,5},{4,0},{5,1},{8,10},{9,11},{10,... | collective-permute-start | bytes 1277960 | tf_op jit(solution)/shard_map/ppermute | solution.py:665
  19.7 1.2 %collective-permute-start.4 = (bf16[64,256]{1,0:T(8,128)(2,1)S(1)}, bf16[64,256]{1,0:T(8,128)(2,1)S(1)}, u32[]{:S(2)}, u32[]{:S(2)}) collective-permute-start(bf16[64,256]{1,0:T(8,128)(2,1)S(1)} %collective-permute-done.3.refs_9_), channel_id=1, source_target_pairs={{0,1},{1,0},{2,3},{3,2},{4,5},{5,4},{6,7},{7,6},{8,9},{9,8},{10,11... | collective-permute-start | bytes 98312 | tf_op jit(solution)/shard_map/ppermute | solution.py:640
  30.8 12.9 %collective-permute-start.6 = (bf16[4,208,256]{2,1,0:T(8,128)(2,1)S(1)}, bf16[4,208,256]{2,1,0:T(8,128)(2,1)S(1)}, u32[]{:S(2)}, u32[]{:S(2)}) collective-permute-start(bf16[4,208,256]{2,1,0:T(8,128)(2,1)S(1)} %collective-permute-done.5.refs_11_), channel_id=1, source_target_pairs={{0,2},{1,3},{2,6},{3,7},{6,4},{7,5},{4,0},{5,1},{8,10},{9,11},{10,... | collective-permute-start | bytes 1277960 | tf_op jit(solution)/shard_map/ppermute | solution.py:665
  46.7 3.8 %collective-permute-start.7 = (bf16[2304,256]{1,0:T(8,128)(2,1)S(1)}, bf16[2304,256]{1,0:T(8,128)(2,1)S(1)}, u32[]{:S(2)}, u32[]{:S(2)}) collective-permute-start(bf16[2304,256]{1,0:T(8,128)(2,1)S(1)} %get-tuple-element.86), channel_id=1, source_target_pairs={{0,1},{1,0},{2,3},{3,2},{4,5},{5,4},{6,7},{7,6},{8,9},{9,8},{10,11... | collective-permute-start | bytes 3538952 | tf_op jit(solution)/shard_map/ppermute | solution.py:480
  48.0 4.9 %collective-permute-start.9 = (bf16[1024,256]{1,0:T(8,128)(2,1)S(1)}, bf16[1024,256]{1,0:T(8,128)(2,1)S(1)}, u32[]{:S(2)}, u32[]{:S(2)}) collective-permute-start(bf16[1024,256]{1,0:T(8,128)(2,1)S(1)} %get-tuple-element.90), channel_id=1, source_target_pairs={{0,1},{1,0},{2,3},{3,2},{4,5},{5,4},{6,7},{7,6},{8,9},{9,8},{10,11... | collective-permute-start | bytes 1572872 | tf_op jit(solution)/shard_map/ppermute | solution.py:673
  50.8 9.7 %collective-permute-start.8 = (bf16[2,288,256]{2,1,0:T(8,128)(2,1)S(1)}, bf16[2,288,256]{2,1,0:T(8,128)(2,1)S(1)}, u32[]{:S(2)}, u32[]{:S(2)}) collective-permute-start(bf16[2,288,256]{2,1,0:T(8,128)(2,1)S(1)} %get-tuple-element.88), channel_id=1, source_target_pairs={{0,8},{8,0},{16,24},{24,16},{1,9},{9,1},{17,25},{25,17},{2,10},{10... | collective-permute-start | bytes 884744 | tf_op jit(solution)/shard_map/ppermute | solution.py:517
  53.0 9.0 %collective-permute-start.10 = (bf16[2,288,256]{2,1,0:T(8,128)(2,1)S(1)}, bf16[2,288,256]{2,1,0:T(8,128)(2,1)S(1)}, u32[]{:S(2)}, u32[]{:S(2)}) collective-permute-start(bf16[2,288,256]{2,1,0:T(8,128)(2,1)S(1)} %get-tuple-element.93), channel_id=1, source_target_pairs={{0,16},{8,24},{16,0},{24,8},{1,17},{9,25},{17,1},{25,9},{2,18},{10... | collective-permute-start | bytes 884744 | tf_op jit(solution)/shard_map/ppermute | solution.py:517
  62.1 5.2 %collective-permute-start.11 = (bf16[1,288,256]{2,1,0:T(8,128)(2,1)S(1)}, bf16[1,288,256]{2,1,0:T(8,128)(2,1)S(1)}, u32[]{:S(2)}, u32[]{:S(2)}) collective-permute-start(bf16[1,288,256]{2,1,0:T(8,128)(2,1)S(1)} %get-tuple-element.95), channel_id=1, source_target_pairs={{0,16},{8,24},{16,0},{24,8},{1,17},{9,25},{17,1},{25,9},{2,18},{10... | collective-permute-start | bytes 442376 | tf_op jit(solution)/shard_map/ppermute | solution.py:517
  62.5 5.1 %collective-permute-start.12 = (bf16[1,288,256]{2,1,0:T(8,128)(2,1)S(1)}, bf16[1,288,256]{2,1,0:T(8,128)(2,1)S(1)}, u32[]{:S(2)}, u32[]{:S(2)}) collective-permute-start(bf16[1,288,256]{2,1,0:T(8,128)(2,1)S(1)} %get-tuple-element.97), channel_id=1, source_target_pairs={{0,8},{8,0},{16,24},{24,16},{1,9},{9,1},{17,25},{25,17},{2,10},{10... | collective-permute-start | bytes 442376 | tf_op jit(solution)/shard_map/ppermute | solution.py:517
  67.7 8.1 %collective-permute-start.13 = (bf16[144,256]{1,0:T(8,128)(2,1)S(1)}, bf16[144,256]{1,0:T(8,128)(2,1)S(1)}, u32[]{:S(2)}, u32[]{:S(2)}) collective-permute-start(bf16[144,256]{1,0:T(8,128)(2,1)S(1)} %get-tuple-element.99), channel_id=1, source_target_pairs={{0,2},{1,3},{2,4},{3,5},{4,6},{5,7},{6,0},{7,1},{8,10},{9,11},{10,... | collective-permute-start | bytes 221192 | tf_op jit(solution)/shard_map/ppermute | solution.py:561
  73.0 5.8 %collective-permute-start.14 = (bf16[144,256]{1,0:T(8,128)(2,1)S(1)}, bf16[144,256]{1,0:T(8,128)(2,1)S(1)}, u32[]{:S(2)}, u32[]{:S(2)}) collective-permute-start(bf16[144,256]{1,0:T(8,128)(2,1)S(1)} %get-tuple-element.100), channel_id=1, source_target_pairs={{0,4},{1,5},{2,6},{3,7},{4,0},{5,1},{6,2},{7,3},{8,12},{9,13},{10,... | collective-permute-start | bytes 221192 | tf_op jit(solution)/shard_map/ppermute | solution.py:561
  73.7 5.1 %collective-permute-start.15 = (bf16[144,256]{1,0:T(8,128)(2,1)S(1)}, bf16[144,256]{1,0:T(8,128)(2,1)S(1)}, u32[]{:S(2)}, u32[]{:S(2)}) collective-permute-start(bf16[144,256]{1,0:T(8,128)(2,1)S(1)} %get-tuple-element.101), channel_id=1, source_target_pairs={{0,6},{1,7},{2,0},{3,1},{4,2},{5,3},{6,4},{7,5},{8,14},{9,15},{10,... | collective-permute-start | bytes 221192 | tf_op jit(solution)/shard_map/ppermute | solution.py:561
  78.9 5.4 %collective-permute-start.18 = (bf16[144,256]{1,0:T(8,128)(2,1)S(1)}, bf16[144,256]{1,0:T(8,128)(2,1)S(1)}, u32[]{:S(2)}, u32[]{:S(2)}) collective-permute-start(bf16[144,256]{1,0:T(8,128)(2,1)S(1)} %shard_map.112.refs_0_), channel_id=1, source_target_pairs={{0,6},{1,7},{2,0},{3,1},{4,2},{5,3},{6,4},{7,5},{8,14},{9,15},{10,... | collective-permute-start | bytes 221192 | tf_op jit(solution)/shard_map/ppermute | solution.py:571
  81.7 5.3 %collective-permute-start.17 = (bf16[144,256]{1,0:T(8,128)(2,1)S(1)}, bf16[144,256]{1,0:T(8,128)(2,1)S(1)}, u32[]{:S(2)}, u32[]{:S(2)}) collective-permute-start(bf16[144,256]{1,0:T(8,128)(2,1)S(1)} %shard_map.112.refs_0_), channel_id=1, source_target_pairs={{0,4},{1,5},{2,6},{3,7},{4,0},{5,1},{6,2},{7,3},{8,12},{9,13},{10,... | collective-permute-start | bytes 221192 | tf_op jit(solution)/shard_map/ppermute | solution.py:571
  81.7 6.2 %collective-permute-start.16 = (bf16[144,256]{1,0:T(8,128)(2,1)S(1)}, bf16[144,256]{1,0:T(8,128)(2,1)S(1)}, u32[]{:S(2)}, u32[]{:S(2)}) collective-permute-start(bf16[144,256]{1,0:T(8,128)(2,1)S(1)} %shard_map.112.refs_0_), channel_id=1, source_target_pairs={{0,2},{1,3},{2,4},{3,5},{4,6},{5,7},{6,0},{7,1},{8,10},{9,11},{10,... | collective-permute-start | bytes 221192 | tf_op jit(solution)/shard_map/ppermute | solution.py:571
  87.9 1.6 %collective-permute-start.19 = (bf16[576,256]{1,0:T(8,128)(2,1)S(1)}, bf16[576,256]{1,0:T(8,128)(2,1)S(1)}, u32[]{:S(2)}, u32[]{:S(2)}) collective-permute-start(bf16[576,256]{1,0:T(8,128)(2,1)S(1)} %shard_map.113.refs_0_), channel_id=1, source_target_pairs={{0,1},{1,0},{2,3},{3,2},{4,5},{5,4},{6,7},{7,6},{8,9},{9,8},{10,11... | collective-permute-start | bytes 884744 | tf_op jit(solution)/shard_map/ppermute | solution.py:581

commit v9 on v8

--- a/solution.py
+++ b/solution.py
@@ -12,7 +12,6 @@
 F32 = jnp.float32
 VMEM_LIMIT = 24 * 1024 * 1024
 PITCH = 16
-SLOT = 208
 
 
 def roundup(n, m):
@@ -45,7 +44,7 @@
 
 
 def pack_kernel(
-    side, height, width, cot, owner, row, col, tile, packed, notes, edge, low, high, wide, places, sems
+    side, height, width, cot, owner, row, col, tile, packed, notes, edge, low, high, wide, tails, places, sems
 ):
     regions = cot.shape[2]
     core = lax.rem(lax.axis_index("tile"), 2)
@@ -68,15 +67,28 @@
     lanes = lax.broadcasted_iota(jnp.int32, (16, 256), 1)
     rows = lax.broadcasted_iota(jnp.int32, (16, 256), 0)
     cells = side * side
+    main = cells // 16 * 16
+    rest = cells - main
+    note = jnp.zeros((16, 256), F32)
     for r in range(regions):
         wide[0:cells, 0:128] = low[pl.ds(r, cells, stride=regions), :]
         wide[0:cells, 128:256] = high[pl.ds(r, cells, stride=regions), :]
         spot = (places[0, 0, r] * height + places[1, 0, r] + 1).astype(F32)
         column = places[2, 0, r].astype(F32)
-        note = jnp.where(lanes == 0, spot, jnp.where(lanes == 1, column, 0.0))
-        wide[192:208, :] = jnp.where(rows < cells - 192, wide[192:208, :], note)
-        packed[r] = wide[...].astype(BF)
-        notes[r] = note.astype(BF)
+        value = jnp.where(lanes == 0, spot, jnp.where(lanes == 1, column, 0.0))
+        note = jnp.where(rows == r, value, note)
+        packed[r * main : r * main + main, :] = wide[0:main, :].astype(BF)
+        tails[r * rest : r * rest + rest, :] = wide[main:cells, :]
+    at = regions * main
+    packed[at : at + tails.shape[0], :] = tails[...].astype(BF)
+    at += tails.shape[0]
+    packed[at : at + 16, :] = note.astype(BF)
+    notes[...] = note.astype(BF)
+
+
+def packed_rows(side, regions):
+    cells = side * side
+    return regions * (cells // 16 * 16), roundup(regions * (cells % 16), 16)
 
 
 def pack(cotangent, tile, height, width, place):
@@ -84,8 +96,8 @@
     return local_kernel(
         functools.partial(pack_kernel, side, height, width),
         (
-            sds((regions, SLOT, 256), BF),
-            sds((regions, 16, 256), BF),
+            sds((sum(packed_rows(side, regions)) + 16, 256), BF),
+            sds((16, 256), BF),
             sds((width, 256), BF),
         ),
         cotangent,
@@ -94,7 +106,8 @@
         scratch=[
             pltpu.VMEM((side * side * regions, 128), F32),
             pltpu.VMEM((side * side * regions, 128), F32),
-            pltpu.VMEM((SLOT, 256), F32),
+            pltpu.VMEM((side * side, 256), F32),
+            pltpu.VMEM((packed_rows(side, regions)[1], 256), F32),
             pltpu.SMEM((3, 1, regions), jnp.int32),
             pltpu.SemaphoreType.DMA((4,)),
         ],
@@ -184,7 +197,7 @@
     return v * half, slope
 
 
-def regions_part(side, height, width, plan, blocks, early, stash, tables, sums, scratch):
+def regions_part(side, height, width, per, plan, blocks, early, stash, tables, sums, scratch):
     pyr, wb1, wb2, w1, w2 = tables
     acc1, acc2, gp = sums
     xs, hs, gs, wide, vs, slope1, todo = scratch
@@ -195,32 +208,40 @@
     cells = side * PITCH
     inside = (lax.broadcasted_iota(jnp.int32, (cells, 256), 0) & (PITCH - 1)) < side
     used = pl.ds(16, cells)
-    per = blocks[0].shape[0]
-    tail = pl.ds(192, 16)
+    main, tails = packed_rows(side, per)
+    one = main // per
+    rest = side * side - one
 
     count = jnp.int32(0)
     start, end = jnp.int32(0), jnp.int32(0)
 
-    def enlist(s, r, note):
-        note = jnp.where(rows16 == 15, note.astype(F32), 0.0)
+    def enlist(s, r, note, wanted=None):
+        note = jnp.where(rows16 == r, note.astype(F32), 0.0)
         spot = jnp.sum(jnp.where(lanes == 0, note, 0.0)).astype(jnp.int32) - 1
         column = jnp.sum(jnp.where(lanes == 1, note, 0.0)).astype(jnp.int32)
         local = spot - chip * 2 * height
         here = (spot >= 0) & (local >= 0) & (local < 2 * height)
+        if wanted is not None:
+            outer = (local == 0) | (local == 2 * height - side)
+            here = here & (outer == wanted)
         todo[0, count] = jnp.int32(s * per + r)
         todo[1, count] = jnp.where(here, local * width + column // 8 * 8, 0)
         todo[2, count] = jnp.where(here, lax.rem(column, 8), 0)
         return count + here.astype(jnp.int32)
 
     for s, block in enumerate(blocks):
+        note = block[main + tails : main + tails + 16, :]
         for r in range(per):
-            count = enlist(s, r, block[r, tail, :])
+            count = enlist(s, r, note, False if s == 0 and plan[0] is not None else None)
         most = plan[s]
         start, end = end, count if most is None else jnp.minimum(count, end + most)
+        if s == 0 and plan[0] is not None:
+            for r in range(per):
+                count = enlist(s, r, note, True)
     total = count
-    for block in early:
+    for note in early:
         for r in range(per):
-            count = enlist(len(blocks), r, block[r])
+            count = enlist(len(blocks), r, note[...])
 
     for buf in (xs, hs, gs):
         buf[0:16, :] = jnp.zeros((16, 768), BF)
@@ -272,7 +293,11 @@
 
             @pl.when(which // per == s)
             def _(block=block):
-                wide[...] = block[lax.rem(which, per)].astype(F32)
+                r = lax.rem(which, per)
+                cell = pl.ds(pl.multiple_of(r * one, 16), one)
+                wide[0:one, :] = block[cell, :].astype(F32)
+                left = block[main : main + tails, :].astype(F32)
+                wide[one : one + tails, :] = pltpu.roll(left, lax.rem(tails - r * rest, tails), 0)
 
         for i in range(side):
             got = wide[i * side : i * side + 16, :]
@@ -358,7 +383,7 @@
     gp_other[...] = gp[pl.ds(pl.multiple_of((1 - core) * cells, cells), cells), :].astype(BF)
 
 
-def main_call(side, height, width, dp, chips, first, last, plan, state, weights, rims, blocks, early, stash):
+def main_call(side, height, width, per, dp, chips, first, last, plan, state, weights, rims, blocks, early, stash):
     n = len(blocks)
     big = 2 * height * width + 16
     cells = side * PITCH
@@ -370,7 +395,6 @@
         sds((height * width, 256), F32),
         sds((height * width, 256), BF),
     )
-    per = early[0].shape[0] if early else 0
     stashed = (
         sds((per, cells, 256), BF),
         sds((per, cells, 256), F32),
@@ -381,7 +405,7 @@
         pltpu.VMEM((cells + 32, 768), BF),
         pltpu.VMEM((cells + 32, 768), BF),
         pltpu.VMEM((cells + 32, 768), BF),
-        pltpu.VMEM((SLOT, 256), F32),
+        pltpu.VMEM((side * side // 16 * 16 + packed_rows(side, per)[1], 256), F32),
         pltpu.VMEM((cells, 256), F32),
         pltpu.VMEM((cells, 256), F32),
         pltpu.SMEM((3, 256), jnp.int32),
@@ -439,7 +463,7 @@
             acc1, acc2, gp = shared[:3]
         if n:
             regions_part(
-                *(side, height, width, plan, block_refs, early_refs, stash_refs),
+                *(side, height, width, per, plan, block_refs, early_refs, stash_refs),
                 *((pyr, wb1, wb2, w1, w2), (acc1, acc2, gp), scratch_refs),
             )
         if last:
@@ -469,7 +493,7 @@
     return (a.astype(F32) + b.astype(F32)).astype(BF)
 
 
-def reduce_weights(keep, sends, core_swap, dp, chips, beside):
+def reduce_weights(keep, sends, core_swap, dp, chips, beside, gp_other):
     rows = keep.shape[0] // dp
     bits = dp.bit_length() - 1
     orders = (list(range(bits)), list(reversed(range(bits))))
@@ -582,8 +606,11 @@
 
     spans = chunks_of(rows)
     chunks = [begin(lo, hi, got) for (lo, hi), got in zip(spans, arrived)]
+    chunks[0].parts = list(chunks[0].parts)
+    chunks[0].parts[1], gp_other = lax.optimization_barrier((chunks[0].parts[1], gp_other))
     for c in chunks:
         exchange(c, 0)
+    beside = beside(gp_other)
     chunks[0].received[0], beside = lax.optimization_barrier((chunks[0].received[0], beside))
     for stage in range(1, bits):
         for c in chunks:
@@ -648,9 +675,11 @@
     wf, w1, w2 = flat(fpn_weight), flat(mask_w1), flat(mask_w2)
     block = lax.ppermute(packed, "tile", ring)
     notes = lax.ppermute(notes, "tile", [(j, i) for i, j in ring])
-    sizes = (side, height, width, dp, chips)
-    plan = [0] + [4] * (chips - 3) + [None]
-    start = main_call(*sizes, True, False, [], [tile, other], [wf, w1, w2], [], [], [], [])
+    sizes = (side, height, width, regions, dp, chips)
+    plan = [1] + [3] * (chips - 3) + [None]
+    start = main_call(
+        *(*sizes, True, False, plan, [tile, other], [wf, w1, w2], [], [packed], [], [])
+    )
     kept, sums, held = list(start[:6]), list(start[6:]), [packed]
     for step in range(1, chips):
         state = kept + sums
@@ -670,15 +699,19 @@
             kept[0] = got.pop(0)
         sums, stash = got[:3], got[3:]
     keep, *sends, gp_own, gp_other = ends
-    gp_got = lax.ppermute(gp_other, "tile", swap)
 
     def join(a, b, out):
         out[...] = (a[...] + b[...].astype(F32)).astype(BF)
 
-    joined = local_kernel(
-        join, sds((height * width, channels), BF), gp_own, gp_got, hbm_out=(0,)
-    )
-    grad_one, grad_two, grad_pyramid = reduce_weights(keep, sends, swap, dp, chips, joined)
+    def joined(gp_other):
+        gp_got = lax.ppermute(gp_other, "tile", swap)
+        return local_kernel(
+            join, sds((height * width, channels), BF), gp_own, gp_got, hbm_out=(0,)
+        )
+
+    grad_one, grad_two, grad_pyramid = reduce_weights(
+        keep, sends, swap, dp, chips, joined, gp_other
+    )
     return grad_one, grad_two, grad_pyramid.reshape(1, height, width, channels)
 
 

time: 90.2 us -> 90.8 us (level)
  Pallas kernels: 24.6 us -> 37.6 us
  waiting for transfers between devices: 38.4 us -> 28 us
  starting transfers between devices: 25.9 us -> 23.5 us
    pallas_call x12, Pallas kernels: 24.6 us -> 37.6 us  [run(): pl.pallas_call(kernel, out_shape=tuple((s if i in hbm_out else pltpu.VMEM...]
    ppermute x2, waiting for transfers between devices: 8.02 us -> 0.01 us  [body(): block = lax.ppermute(block, 'tile', ring)]
    ppermute x1, waiting for transfers between devices: 4.2 us -> 0.01 us  [body(): notes = lax.ppermute(notes, 'tile', [(j, i) for i, j in ring])]
    ppermute x1, starting transfers between devices: 1.08 us -> 5.17 us  [body(): notes = lax.ppermute(notes, 'tile', [(j, i) for i, j in ring])]
    ppermute x2, starting transfers between devices: 4.68 us -> 0.78 us  [body(): block = lax.ppermute(block, 'tile', ring)]
    ppermute x3, starting transfers between devices: 7.71 us -> 3.86 us  [deal(): lax.ppermute(dealt[k], 'tile', shifts[k])]
    ppermute x4, starting transfers between devices: 2.89 us -> 6.09 us  [exchange(): c.received.append(lax.ppermute(c.parts[2 * half + 1], 'dp', pairs))]
    ppermute x1, starting transfers between devices: 1.34 us -> 0.07 us  [reduce_weights(): arrived = [lax.ppermute(send, 'tile', core_swap) for send in sends]]
  transfers between devices with their start and end apart: 20 -> 20, of which waited for: 15 -> 12; matrix products, arithmetic and copies ran while one was open for 0% -> 0% of each run, Pallas kernels for 22% -> 34%
where the time goes in v9:
time: 90.8 us
  Pallas kernels  37.6 us (41%)
  waiting for transfers between devices  28 us (31%)
  starting transfers between devices  23.5 us (26%)
  local copies, waits for them, and re-layouts  1 us (1%)
    pallas_call x12, Pallas kernels, run(): pl.pallas_call(kernel, out_shape=tuple((s if i in hbm_out else pltpu.VMEM...  37.6 us
    ppermute x4, waiting for transfers between devices, exchange(): c.received.append(lax.ppermute(c.parts[2 * half + 1], 'dp', pairs))  13 us
    ppermute x4, starting transfers between devices, exchange(): c.received.append(lax.ppermute(c.parts[2 * half + 1], 'dp', pairs))  6.09 us
    ppermute x3, waiting for transfers between devices, gather(): lax.ppermute(c.mine, 'tile', shifts[k])  5.9 us
    ppermute x1, starting transfers between devices, body(): notes = lax.ppermute(notes, 'tile', [(j, i) for i, j in ring])  5.17 us
    ppermute x3, starting transfers between devices, deal(): lax.ppermute(dealt[k], 'tile', shifts[k])  3.86 us
    ppermute x3, waiting for transfers between devices, deal(): lax.ppermute(dealt[k], 'tile', shifts[k])  3.73 us
    ppermute x3, starting transfers between devices, gather(): lax.ppermute(c.mine, 'tile', shifts[k])  3.12 us
  transfers between devices with their start and end apart: 20, of which 12 were waited for; matrix products, arithmetic and copies ran while one was open for 0% of the time, Pallas kernels for 34%

profile of v9, /device:TPU:0, one launch (start us, length us, event | category | flops | bytes accessed | tf_op | source)
XLA Modules:
  0.0 90.8 jit_solution(15810088065742909629)
XLA Ops:
  1.2 1.0 %copy-done = bf16[1,4,14,14,256]{4,1,3,2,0:T(4,128)(2,1)S(1)} copy-done((bf16[1,4,14,14,256]{4,1,3,2,0:T(4,128)(2,1)S(1)}, bf16[1,4,14,14,256]{4,1,3,2,0:T(4,128)(2,1)}, u32[]{:S(2)}) %copy-start) | copy-done | bytes 401432
  2.1 0.9 %shard_map.103 = (bf16[800,256]{1,0:T(8,128)(2,1)S(1)}, bf16[16,256]{1,0:T(8,128)(2,1)S(1)}, bf16[64,256]{1,0:T(8,128)(2,1)S(1)}) custom-call(bf16[14,14,4,256]{3,2,1,0:T(4,128)(2,1)S(1)} %bitcast.9, s32[1,4]{1,0:T(1,128)} %bitcast.17, s32[1,4]{1,0:T(1,128)} %row.1, s32[1,4]{1,0:T(1,128)} %col.1, bf16[1024,256]{1,0:T(8,128)(2,1)} %bitcast.11), custom_call_target="tpu_custom_call" | custom-call | tf_op jit(solution)/shard_map/pallas_call | solution.py:26
  3.1 2.6 %collective-permute-start = (bf16[800,256]{1,0:T(8,128)(2,1)S(1)}, bf16[800,256]{1,0:T(8,128)(2,1)S(1)}, u32[]{:S(2)}, u32[]{:S(2)}) collective-permute-start(bf16[800,256]{1,0:T(8,128)(2,1)S(1)} %get-tuple-element.56.refs_5_.refs_11_.refs_9_), channel_id=1, source_target_pairs={{0,2},{1,3},{2,6},{3,7},{6,4},{7,5},{4,0},{5,1},{8,10},{9,11},{10,... | collective-permute-start | bytes 1228808 | tf_op jit(solution)/shard_map/ppermute | solution.py:676
  6.4 5.2 %collective-permute-start.2 = (bf16[16,256]{1,0:T(8,128)(2,1)S(1)}, bf16[16,256]{1,0:T(8,128)(2,1)S(1)}, u32[]{:S(2)}, u32[]{:S(2)}) collective-permute-start(bf16[16,256]{1,0:T(8,128)(2,1)S(1)} %get-tuple-element.59), channel_id=1, source_target_pairs={{2,0},{3,1},{6,2},{7,3},{4,6},{5,7},{0,4},{1,5},{10,8},{11,9},{14,... | collective-permute-start | bytes 24584 | tf_op jit(solution)/shard_map/ppermute | solution.py:677
  11.6 9.4 %shard_map.104 = (f32[2064,256]{1,0:T(8,128)S(1)}, bf16[2304,256]{1,0:T(8,128)(2,1)S(1)}, bf16[2304,256]{1,0:T(8,128)(2,1)S(1)}, bf16[2304,256]{1,0:T(8,128)(2,1...) custom-call(bf16[1024,256]{1,0:T(8,128)(2,1)} %bitcast.12, ...), custom_call_target="tpu_custom_call" | custom-call | tf_op jit(solution)/shard_map/pallas_call | solution.py:26
  21.4 1.0 %collective-permute-done.4.refs_10_ = bf16[64,256]{1,0:T(8,128)(2,1)S(1)} collective-permute-done((bf16[64,256]{1,0:T(8,128)(2,1)S(1)}, bf16[64,256]{1,0:T(8,128)(2,1)S(1)}, u32[]{:S(2)}, u32[]{:S(2)}) %collective-permute-start.4) | collective-permute-done | bytes 32800 | tf_op jit(solution)/shard_map/ppermute | solution.py:667
  22.4 9.9 %shard_map.105 = (f32[2064,256]{1,0:T(8,128)S(1)}, f32[256,2304]{1,0:T(8,128)S(1)}, f32[256,2304]{1,0:T(8,128)S(1)}, f32[2064,256]{1,0:T(8,128)S(1)}) custom-call(f32[2064,256]{1,0:T(8,128)S(1)} %get-tuple-element.61.refs_0_, ...), custom_call_target="tpu_custom_call", output_to_operand_aliasing={{0}: (0, {}), {1}: (6, {}), {2}: (7, {}), {3}: (8, {})} | custom-call | tf_op jit(solution)/shard_map/pallas_call | solution.py:26
  33.0 9.8 %shard_map.106 = (f32[256,2304]{1,0:T(8,128)S(1)}, f32[256,2304]{1,0:T(8,128)S(1)}, f32[2064,256]{1,0:T(8,128)S(1)}, bf16[4,224,256]{2,1,0:T(8,128)(2,1)S(1)}, f...) custom-call(f32[2064,256]{1,0:T(8,128)S(1)} %get-tuple-element.75.re, ...), custom_call_target="tpu_custom_call", output_to_operand_aliasing={{0}: (6, {}), {1}: (7, {}), {2}: (8, {})} | custom-call | tf_op jit(solution)/shard_map/pallas_call | solution.py:26
  42.8 5.0 %shard_map.107 = (f32[256,2304]{1,0:T(8,128)S(1)}, f32[256,2304]{1,0:T(8,128)S(1)}, f32[2064,256]{1,0:T(8,128)S(1)}, bf16[2304,256]{1,0:T(8,128)(2,1)S(1)}, bf16...) custom-call(f32[2064,256]{1,0:T(8,128)S(1)} %get-tuple-element.75.re, ...), custom_call_target="tpu_custom_call", output_to_operand_aliasing={{0}: (6, {}), {1}: (7, {}), {2}: (8, {})} | custom-call | tf_op jit(solution)/shard_map/pallas_call | solution.py:26
  47.9 2.8 %collective-permute-done.7.got_ref = bf16[2304,256]{1,0:T(8,128)(2,1)S(1)} collective-permute-done((bf16[2304,256]{1,0:T(8,128)(2,1)S(1)}, bf16[2304,256]{1,0:T(8,128)(2,1)S(1)}, u32[]{:S(2)}, u32[]{:S(2)}) %collective-permute-start.7) | collective-permute-done | bytes 1179680 | tf_op jit(solution)/shard_map/ppermute | solution.py:504
  51.2 5.5 %collective-permute-start.8 = (bf16[2,288,256]{2,1,0:T(8,128)(2,1)S(1)}, bf16[2,288,256]{2,1,0:T(8,128)(2,1)S(1)}, u32[]{:S(2)}, u32[]{:S(2)}) collective-permute-start(bf16[2,288,256]{2,1,0:T(8,128)(2,1)S(1)} %get-tuple-element.92), channel_id=1, source_target_pairs={{0,8},{8,0},{16,24},{24,16},{1,9},{9,1},{17,25},{25,17},{2,10},{10... | collective-permute-start | bytes 884744 | tf_op jit(solution)/shard_map/ppermute | solution.py:541
  56.6 0.9 shard_map.109
  57.5 6.6 %collective-permute-done.8.pr = bf16[2,288,256]{2,1,0:T(8,128)(2,1)S(1)} collective-permute-done((bf16[2,288,256]{2,1,0:T(8,128)(2,1)S(1)}, bf16[2,288,256]{2,1,0:T(8,128)(2,1)S(1)}, u32[]{:S(2)}, u32[]{:S(2)}) %collective-permute-start.8) | collective-permute-done | bytes 294944 | tf_op jit(solution)/shard_map/ppermute | solution.py:541
  64.2 1.5 %collective-permute-done.10.qr = bf16[2,288,256]{2,1,0:T(8,128)(2,1)S(1)} collective-permute-done((bf16[2,288,256]{2,1,0:T(8,128)(2,1)S(1)}, bf16[2,288,256]{2,1,0:T(8,128)(2,1)S(1)}, u32[]{:S(2)}, u32[]{:S(2)}) %collective-permute-start.10) | collective-permute-done | bytes 294944 | tf_op jit(solution)/shard_map/ppermute | solution.py:541
  66.4 4.6 %collective-permute-done.11.pr = bf16[1,288,256]{2,1,0:T(8,128)(2,1)S(1)} collective-permute-done((bf16[1,288,256]{2,1,0:T(8,128)(2,1)S(1)}, bf16[1,288,256]{2,1,0:T(8,128)(2,1)S(1)}, u32[]{:S(2)}, u32[]{:S(2)}) %collective-permute-start.11) | collective-permute-done | bytes 147488 | tf_op jit(solution)/shard_map/ppermute | solution.py:541
  71.5 3.7 %collective-permute-start.15 = (bf16[144,256]{1,0:T(8,128)(2,1)S(1)}, bf16[144,256]{1,0:T(8,128)(2,1)S(1)}, u32[]{:S(2)}, u32[]{:S(2)}) collective-permute-start(bf16[144,256]{1,0:T(8,128)(2,1)S(1)} %get-tuple-element.105), channel_id=1, source_target_pairs={{0,6},{1,7},{2,0},{3,1},{4,2},{5,3},{6,4},{7,5},{8,14},{9,15},{10,... | collective-permute-start | bytes 221192 | tf_op jit(solution)/shard_map/ppermute | solution.py:585
  75.3 2.5 %collective-permute-done.13.refs_1_ = bf16[144,256]{1,0:T(8,128)(2,1)S(1)} collective-permute-done((bf16[144,256]{1,0:T(8,128)(2,1)S(1)}, bf16[144,256]{1,0:T(8,128)(2,1)S(1)}, u32[]{:S(2)}, u32[]{:S(2)}) %collective-permute-start.13) | collective-permute-done | bytes 73760 | tf_op jit(solution)/shard_map/ppermute | solution.py:585
  77.7 1.3 %collective-permute-done.14.refs_2_ = bf16[144,256]{1,0:T(8,128)(2,1)S(1)} collective-permute-done((bf16[144,256]{1,0:T(8,128)(2,1)S(1)}, bf16[144,256]{1,0:T(8,128)(2,1)S(1)}, u32[]{:S(2)}, u32[]{:S(2)}) %collective-permute-start.14) | collective-permute-done | bytes 73760 | tf_op jit(solution)/shard_map/ppermute | solution.py:585
  79.0 2.5 %collective-permute-start.18 = (bf16[144,256]{1,0:T(8,128)(2,1)S(1)}, bf16[144,256]{1,0:T(8,128)(2,1)S(1)}, u32[]{:S(2)}, u32[]{:S(2)}) collective-permute-start(bf16[144,256]{1,0:T(8,128)(2,1)S(1)} %shard_map.112.refs_0_), channel_id=1, source_target_pairs={{0,6},{1,7},{2,0},{3,1},{4,2},{5,3},{6,4},{7,5},{8,14},{9,15},{10,... | collective-permute-start | bytes 221192 | tf_op jit(solution)/shard_map/ppermute | solution.py:595
  82.2 1.9 %collective-permute-done.18.refs_3_ = bf16[144,256]{1,0:T(8,128)(2,1)S(1)} collective-permute-done((bf16[144,256]{1,0:T(8,128)(2,1)S(1)}, bf16[144,256]{1,0:T(8,128)(2,1)S(1)}, u32[]{:S(2)}, u32[]{:S(2)}) %collective-permute-start.18) | collective-permute-done | bytes 73760 | tf_op jit(solution)/shard_map/ppermute | solution.py:595
  84.1 3.0 %collective-permute-done.17.refs_2_ = bf16[144,256]{1,0:T(8,128)(2,1)S(1)} collective-permute-done((bf16[144,256]{1,0:T(8,128)(2,1)S(1)}, bf16[144,256]{1,0:T(8,128)(2,1)S(1)}, u32[]{:S(2)}, u32[]{:S(2)}) %collective-permute-start.17) | collective-permute-done | bytes 73760 | tf_op jit(solution)/shard_map/ppermute | solution.py:595
  87.1 1.0 %collective-permute-done.16.refs_1_ = bf16[144,256]{1,0:T(8,128)(2,1)S(1)} collective-permute-done((bf16[144,256]{1,0:T(8,128)(2,1)S(1)}, bf16[144,256]{1,0:T(8,128)(2,1)S(1)}, u32[]{:S(2)}, u32[]{:S(2)}) %collective-permute-start.16) | collective-permute-done | bytes 73760 | tf_op jit(solution)/shard_map/ppermute | solution.py:595
  88.2 1.6 %collective-permute-done.19.refs_1_ = bf16[576,256]{1,0:T(8,128)(2,1)S(1)} collective-permute-done((bf16[576,256]{1,0:T(8,128)(2,1)S(1)}, bf16[576,256]{1,0:T(8,128)(2,1)S(1)}, u32[]{:S(2)}, u32[]{:S(2)}) %collective-permute-start.19) | collective-permute-done | bytes 294944 | tf_op jit(solution)/shard_map/ppermute | solution.py:605
  89.8 1.1 %shard_map.114 = (f32[576,256]{1,0:T(8,128)}, f32[576,256]{1,0:T(8,128)}) custom-call(bf16[576,256]{1,0:T(8,128)(2,1)S(1)} %shard_map.113.refs_0_, bf16[576,256]{1,0:T(8,128)(2,1)S(1)} %collective-permute-done.19.refs_1_), custom_call_target="tpu_custom_call" | custom-call | tf_op jit(solution)/shard_map/pallas_call | solution.py:26
  (30 shorter events, 4.9 us)
Async XLA Ops:
  0.6 10.9 %collective-permute-start.1 = (bf16[1024,256]{1,0:T(8,128)(2,1)}, bf16[1024,256]{1,0:T(8,128)(2,1)S(1)}, u32[]{:S(2)}, u32[]{:S(2)}) collective-permute-start(bf16[1024,256]{1,0:T(8,128)(2,1)} %bitcast.10), channel_id=1, source_target_pairs={{0,1},{1,0},{2,3},{3,2},{4,5},{5,4},{6,7},{7,6},{8,9},{9,8},{10,11... | collective-permute-start | bytes 1572872 | tf_op jit(solution)/shard_map/ppermute | solution.py:662
  1.1 1.0 %copy-start = (bf16[1,4,14,14,256]{4,1,3,2,0:T(4,128)(2,1)S(1)}, bf16[1,4,14,14,256]{4,1,3,2,0:T(4,128)(2,1)}, u32[]{:S(2)}) copy-start(bf16[1,4,14,14,256]{4,1,3,2,0:T(4,128)(2,1)} %param.15) | copy-start | bytes 1204228
  3.1 17.9 %collective-permute-start = (bf16[800,256]{1,0:T(8,128)(2,1)S(1)}, bf16[800,256]{1,0:T(8,128)(2,1)S(1)}, u32[]{:S(2)}, u32[]{:S(2)}) collective-permute-start(bf16[800,256]{1,0:T(8,128)(2,1)S(1)} %get-tuple-element.56.refs_5_.refs_11_.refs_9_), channel_id=1, source_target_pairs={{0,2},{1,3},{2,6},{3,7},{6,4},{7,5},{4,0},{5,1},{8,10},{9,11},{10,... | collective-permute-start | bytes 1228808 | tf_op jit(solution)/shard_map/ppermute | solution.py:676
  5.7 15.3 %collective-permute-start.3 = (bf16[64,256]{1,0:T(8,128)(2,1)S(1)}, bf16[64,256]{1,0:T(8,128)(2,1)S(1)}, u32[]{:S(2)}, u32[]{:S(2)}) collective-permute-start(bf16[64,256]{1,0:T(8,128)(2,1)S(1)} %get-tuple-element.60), channel_id=1, source_target_pairs={{1,2},{2,1},{3,4},{4,3},{5,6},{6,5},{9,10},{10,9},{11,12},{12,11},... | collective-permute-start | bytes 98312 | tf_op jit(solution)/shard_map/ppermute | solution.py:664
  6.4 14.6 %collective-permute-start.2 = (bf16[16,256]{1,0:T(8,128)(2,1)S(1)}, bf16[16,256]{1,0:T(8,128)(2,1)S(1)}, u32[]{:S(2)}, u32[]{:S(2)}) collective-permute-start(bf16[16,256]{1,0:T(8,128)(2,1)S(1)} %get-tuple-element.59), channel_id=1, source_target_pairs={{2,0},{3,1},{6,2},{7,3},{4,6},{5,7},{0,4},{1,5},{10,8},{11,9},{14,... | collective-permute-start | bytes 24584 | tf_op jit(solution)/shard_map/ppermute | solution.py:677
  21.0 11.3 %collective-permute-start.5 = (bf16[800,256]{1,0:T(8,128)(2,1)S(1)}, bf16[800,256]{1,0:T(8,128)(2,1)S(1)}, u32[]{:S(2)}, u32[]{:S(2)}) collective-permute-start(bf16[800,256]{1,0:T(8,128)(2,1)S(1)} %collective-permute-done.refs_12_.refs_10_), channel_id=1, source_target_pairs={{0,2},{1,3},{2,6},{3,7},{6,4},{7,5},{4,0},{5,1},{8,10},{9,11},{10,... | collective-permute-start | bytes 1228808 | tf_op jit(solution)/shard_map/ppermute | solution.py:694
  21.1 1.3 %collective-permute-start.4 = (bf16[64,256]{1,0:T(8,128)(2,1)S(1)}, bf16[64,256]{1,0:T(8,128)(2,1)S(1)}, u32[]{:S(2)}, u32[]{:S(2)}) collective-permute-start(bf16[64,256]{1,0:T(8,128)(2,1)S(1)} %collective-permute-done.3.refs_9_), channel_id=1, source_target_pairs={{0,1},{1,0},{2,3},{3,2},{4,5},{5,4},{6,7},{7,6},{8,9},{9,8},{10,11... | collective-permute-start | bytes 98312 | tf_op jit(solution)/shard_map/ppermute | solution.py:667
  32.3 10.5 %collective-permute-start.6 = (bf16[800,256]{1,0:T(8,128)(2,1)S(1)}, bf16[800,256]{1,0:T(8,128)(2,1)S(1)}, u32[]{:S(2)}, u32[]{:S(2)}) collective-permute-start(bf16[800,256]{1,0:T(8,128)(2,1)S(1)} %collective-permute-done.5.refs_11_), channel_id=1, source_target_pairs={{0,2},{1,3},{2,6},{3,7},{6,4},{7,5},{4,0},{5,1},{8,10},{9,11},{10,... | collective-permute-start | bytes 1228808 | tf_op jit(solution)/shard_map/ppermute | solution.py:694
  47.8 2.9 %collective-permute-start.7 = (bf16[2304,256]{1,0:T(8,128)(2,1)S(1)}, bf16[2304,256]{1,0:T(8,128)(2,1)S(1)}, u32[]{:S(2)}, u32[]{:S(2)}) collective-permute-start(bf16[2304,256]{1,0:T(8,128)(2,1)S(1)} %get-tuple-element.88), channel_id=1, source_target_pairs={{0,1},{1,0},{2,3},{3,2},{4,5},{5,4},{6,7},{7,6},{8,9},{9,8},{10,11... | collective-permute-start | bytes 3538952 | tf_op jit(solution)/shard_map/ppermute | solution.py:504
  51.0 5.7 %collective-permute-start.9 = (bf16[1024,256]{1,0:T(8,128)(2,1)S(1)}, bf16[1024,256]{1,0:T(8,128)(2,1)S(1)}, u32[]{:S(2)}, u32[]{:S(2)}) collective-permute-start(bf16[1024,256]{1,0:T(8,128)(2,1)S(1)} %get-tuple-element.94), channel_id=1, source_target_pairs={{0,1},{1,0},{2,3},{3,2},{4,5},{5,4},{6,7},{7,6},{8,9},{9,8},{10,11... | collective-permute-start | bytes 1572872 | tf_op jit(solution)/shard_map/ppermute | solution.py:707
  51.2 13.0 %collective-permute-start.8 = (bf16[2,288,256]{2,1,0:T(8,128)(2,1)S(1)}, bf16[2,288,256]{2,1,0:T(8,128)(2,1)S(1)}, u32[]{:S(2)}, u32[]{:S(2)}) collective-permute-start(bf16[2,288,256]{2,1,0:T(8,128)(2,1)S(1)} %get-tuple-element.92), channel_id=1, source_target_pairs={{0,8},{8,0},{16,24},{24,16},{1,9},{9,1},{17,25},{25,17},{2,10},{10... | collective-permute-start | bytes 884744 | tf_op jit(solution)/shard_map/ppermute | solution.py:541
  56.6 9.0 %collective-permute-start.10 = (bf16[2,288,256]{2,1,0:T(8,128)(2,1)S(1)}, bf16[2,288,256]{2,1,0:T(8,128)(2,1)S(1)}, u32[]{:S(2)}, u32[]{:S(2)}) collective-permute-start(bf16[2,288,256]{2,1,0:T(8,128)(2,1)S(1)} %get-tuple-element.97), channel_id=1, source_target_pairs={{0,16},{8,24},{16,0},{24,8},{1,17},{9,25},{17,1},{25,9},{2,18},{10... | collective-permute-start | bytes 884744 | tf_op jit(solution)/shard_map/ppermute | solution.py:541
  65.8 5.2 %collective-permute-start.11 = (bf16[1,288,256]{2,1,0:T(8,128)(2,1)S(1)}, bf16[1,288,256]{2,1,0:T(8,128)(2,1)S(1)}, u32[]{:S(2)}, u32[]{:S(2)}) collective-permute-start(bf16[1,288,256]{2,1,0:T(8,128)(2,1)S(1)} %get-tuple-element.99), channel_id=1, source_target_pairs={{0,16},{8,24},{16,0},{24,8},{1,17},{9,25},{17,1},{25,9},{2,18},{10... | collective-permute-start | bytes 442376 | tf_op jit(solution)/shard_map/ppermute | solution.py:541
  66.1 5.1 %collective-permute-start.12 = (bf16[1,288,256]{2,1,0:T(8,128)(2,1)S(1)}, bf16[1,288,256]{2,1,0:T(8,128)(2,1)S(1)}, u32[]{:S(2)}, u32[]{:S(2)}) collective-permute-start(bf16[1,288,256]{2,1,0:T(8,128)(2,1)S(1)} %get-tuple-element.101), channel_id=1, source_target_pairs={{0,8},{8,0},{16,24},{24,16},{1,9},{9,1},{17,25},{25,17},{2,10},{10... | collective-permute-start | bytes 442376 | tf_op jit(solution)/shard_map/ppermute | solution.py:541
  71.4 6.3 %collective-permute-start.13 = (bf16[144,256]{1,0:T(8,128)(2,1)S(1)}, bf16[144,256]{1,0:T(8,128)(2,1)S(1)}, u32[]{:S(2)}, u32[]{:S(2)}) collective-permute-start(bf16[144,256]{1,0:T(8,128)(2,1)S(1)} %get-tuple-element.103), channel_id=1, source_target_pairs={{0,2},{1,3},{2,4},{3,5},{4,6},{5,7},{6,0},{7,1},{8,10},{9,11},{10,... | collective-permute-start | bytes 221192 | tf_op jit(solution)/shard_map/ppermute | solution.py:585
  71.5 7.5 %collective-permute-start.14 = (bf16[144,256]{1,0:T(8,128)(2,1)S(1)}, bf16[144,256]{1,0:T(8,128)(2,1)S(1)}, u32[]{:S(2)}, u32[]{:S(2)}) collective-permute-start(bf16[144,256]{1,0:T(8,128)(2,1)S(1)} %get-tuple-element.104), channel_id=1, source_target_pairs={{0,4},{1,5},{2,6},{3,7},{4,0},{5,1},{6,2},{7,3},{8,12},{9,13},{10,... | collective-permute-start | bytes 221192 | tf_op jit(solution)/shard_map/ppermute | solution.py:585
  71.5 7.5 %collective-permute-start.15 = (bf16[144,256]{1,0:T(8,128)(2,1)S(1)}, bf16[144,256]{1,0:T(8,128)(2,1)S(1)}, u32[]{:S(2)}, u32[]{:S(2)}) collective-permute-start(bf16[144,256]{1,0:T(8,128)(2,1)S(1)} %get-tuple-element.105), channel_id=1, source_target_pairs={{0,6},{1,7},{2,0},{3,1},{4,2},{5,3},{6,4},{7,5},{8,14},{9,15},{10,... | collective-permute-start | bytes 221192 | tf_op jit(solution)/shard_map/ppermute | solution.py:585
  79.0 5.0 %collective-permute-start.18 = (bf16[144,256]{1,0:T(8,128)(2,1)S(1)}, bf16[144,256]{1,0:T(8,128)(2,1)S(1)}, u32[]{:S(2)}, u32[]{:S(2)}) collective-permute-start(bf16[144,256]{1,0:T(8,128)(2,1)S(1)} %shard_map.112.refs_0_), channel_id=1, source_target_pairs={{0,6},{1,7},{2,0},{3,1},{4,2},{5,3},{6,4},{7,5},{8,14},{9,15},{10,... | collective-permute-start | bytes 221192 | tf_op jit(solution)/shard_map/ppermute | solution.py:595
  81.5 5.6 %collective-permute-start.17 = (bf16[144,256]{1,0:T(8,128)(2,1)S(1)}, bf16[144,256]{1,0:T(8,128)(2,1)S(1)}, u32[]{:S(2)}, u32[]{:S(2)}) collective-permute-start(bf16[144,256]{1,0:T(8,128)(2,1)S(1)} %shard_map.112.refs_0_), channel_id=1, source_target_pairs={{0,4},{1,5},{2,6},{3,7},{4,0},{5,1},{6,2},{7,3},{8,12},{9,13},{10,... | collective-permute-start | bytes 221192 | tf_op jit(solution)/shard_map/ppermute | solution.py:595
  81.9 6.2 %collective-permute-start.16 = (bf16[144,256]{1,0:T(8,128)(2,1)S(1)}, bf16[144,256]{1,0:T(8,128)(2,1)S(1)}, u32[]{:S(2)}, u32[]{:S(2)}) collective-permute-start(bf16[144,256]{1,0:T(8,128)(2,1)S(1)} %shard_map.112.refs_0_), channel_id=1, source_target_pairs={{0,2},{1,3},{2,4},{3,5},{4,6},{5,7},{6,0},{7,1},{8,10},{9,11},{10,... | collective-permute-start | bytes 221192 | tf_op jit(solution)/shard_map/ppermute | solution.py:595
  88.1 1.6 %collective-permute-start.19 = (bf16[576,256]{1,0:T(8,128)(2,1)S(1)}, bf16[576,256]{1,0:T(8,128)(2,1)S(1)}, u32[]{:S(2)}, u32[]{:S(2)}) collective-permute-start(bf16[576,256]{1,0:T(8,128)(2,1)S(1)} %shard_map.113.refs_0_), channel_id=1, source_target_pairs={{0,1},{1,0},{2,3},{3,2},{4,5},{5,4},{6,7},{7,6},{8,9},{9,8},{10,11... | collective-permute-start | bytes 884744 | tf_op jit(solution)/shard_map/ppermute | solution.py:605

commit v10 on v9

--- a/solution.py
+++ b/solution.py
@@ -144,19 +144,19 @@
     fetched.wait()
 
     def conv(t, carry):
-        at = t * 256
-        total = jnp.zeros((256, 256), F32)
+        at = t * 512
+        total = jnp.zeros((512, 256), F32)
         for a in range(3):
-            piece = xp[pl.ds(pl.multiple_of(at + a * width, 64), 256), :]
+            piece = xp[pl.ds(pl.multiple_of(at + a * width, 64), 512), :]
             total += jnp.dot(piece, wf[a * 768 : a * 768 + 768, :], preferred_element_type=F32)
-        cell = at + lax.broadcasted_iota(jnp.int32, (256, 256), 0)
+        cell = at + lax.broadcasted_iota(jnp.int32, (512, 256), 0)
         open_row = (cell < width) | (cell >= 2 * cells - width)
-        pyr[pl.ds(pl.multiple_of(at, 256), 256), :] = jnp.where(
+        pyr[pl.ds(pl.multiple_of(at, 512), 512), :] = jnp.where(
             open_row, total, total.astype(BF).astype(F32)
         )
         return carry
 
-    lax.fori_loop(0, 2 * cells // 256, conv, 0)
+    lax.fori_loop(0, 2 * cells // 512, conv, 0)
     pyr[2 * cells : 2 * cells + 16, :] = jnp.zeros((16, 256), F32)
 
 
@@ -215,7 +215,7 @@
     count = jnp.int32(0)
     start, end = jnp.int32(0), jnp.int32(0)
 
-    def enlist(s, r, note, wanted=None):
+    def enlist(count, s, r, note, wanted=None):
         note = jnp.where(rows16 == r, note.astype(F32), 0.0)
         spot = jnp.sum(jnp.where(lanes == 0, note, 0.0)).astype(jnp.int32) - 1
         column = jnp.sum(jnp.where(lanes == 1, note, 0.0)).astype(jnp.int32)
@@ -229,19 +229,23 @@
         todo[2, count] = jnp.where(here, lax.rem(column, 8), 0)
         return count + here.astype(jnp.int32)
 
-    for s, block in enumerate(blocks):
-        note = block[main + tails : main + tails + 16, :]
+    def scan(s, wanted):
+        note = blocks[s][main + tails : main + tails + 16, :]
+        found = count
         for r in range(per):
-            count = enlist(s, r, note, False if s == 0 and plan[0] is not None else None)
-        most = plan[s]
+            found = enlist(found, s, r, note, wanted)
+        return found
+
+    for s, most in enumerate(plan[: len(blocks)]):
+        if s == 2:
+            count = scan(0, True)
+            count = scan(1, True)
+        count = scan(s, False if s < 2 and len(plan) > 1 else None)
         start, end = end, count if most is None else jnp.minimum(count, end + most)
-        if s == 0 and plan[0] is not None:
-            for r in range(per):
-                count = enlist(s, r, note, True)
     total = count
     for note in early:
         for r in range(per):
-            count = enlist(len(blocks), r, note[...])
+            count = enlist(count, len(blocks), r, note[...])
 
     for buf in (xs, hs, gs):
         buf[0:16, :] = jnp.zeros((16, 768), BF)
@@ -661,10 +665,6 @@
     place = [x.reshape(1, regions) for x in (owner, row_off, col_off)]
     other = lax.ppermute(tile, "tile", swap)
     packed, notes, edge = pack(cotangent[0].transpose(1, 2, 0, 3), tile, height, width, place)
-    rim_a = lax.ppermute(
-        edge, "tile", [(i, i + 1 if i % 2 else i - 1) for i in range(1, tiles - 1)]
-    )
-    rim_b = lax.ppermute(rim_a, "tile", swap)
 
     order = [0] + list(range(1, chips, 2)) + list(range(2, chips, 2))[::-1]
     ring = [
@@ -674,26 +674,34 @@
     flat = lambda w: w.reshape(9 * channels, channels)
     wf, w1, w2 = flat(fpn_weight), flat(mask_w1), flat(mask_w2)
     block = lax.ppermute(packed, "tile", ring)
-    notes = lax.ppermute(notes, "tile", [(j, i) for i, j in ring])
     sizes = (side, height, width, regions, dp, chips)
     plan = [1] + [3] * (chips - 3) + [None]
     start = main_call(
         *(*sizes, True, False, plan, [tile, other], [wf, w1, w2], [], [packed], [], [])
     )
     kept, sums, held = list(start[:6]), list(start[6:]), [packed]
+    edge, notes, kept[0] = lax.optimization_barrier((edge, notes, kept[0]))
+    rim_a = lax.ppermute(
+        edge, "tile", [(i, i + 1 if i % 2 else i - 1) for i in range(1, tiles - 1)]
+    )
+    notes = lax.ppermute(notes, "tile", [(j, i) for i, j in ring])
     for step in range(1, chips):
         state = kept + sums
         if step == chips - 1:
             got = main_call(*sizes, False, True, [None], state, [], [], [block], [], stash)
             ends = got[3:]
             break
-        block, state[0], state[-1], notes, rim_a = lax.optimization_barrier(
-            (block, state[0], state[-1], notes, rim_a)
-        )
+        block, state[0], state[-1] = lax.optimization_barrier((block, state[0], state[-1]))
+        if step == 1:
+            block, rim_a = lax.optimization_barrier((block, rim_a))
+        if step == 2:
+            block, notes, rim_b = lax.optimization_barrier((block, notes, rim_b))
         held = held + [block]
         block = lax.ppermute(block, "tile", ring)
+        if step == 1:
+            rim_b = lax.ppermute(rim_a, "tile", swap)
         early = [notes] if step == chips - 2 else []
-        rims = [rim_a, rim_b] if step == 1 else []
+        rims = [rim_a, rim_b] if step == 2 else []
         got = list(main_call(*sizes, False, False, plan, state, [], rims, held, early, []))
         if rims:
             kept[0] = got.pop(0)

time: 90.8 us -> 94.2 us (1.037)
  Pallas kernels: 37.6 us -> 17.9 us
  waiting for transfers between devices: 28 us -> 42.4 us
  starting transfers between devices: 23.5 us -> 32.2 us
    pallas_call x12, Pallas kernels: 37.6 us -> 17.9 us  [run(): pl.pallas_call(kernel, out_shape=tuple((s if i in hbm_out else pltpu.VMEM...]
    ppermute x2, waiting for transfers between devices: 0.01 us -> 14.4 us  [body(): block = lax.ppermute(block, 'tile', ring)]
    ppermute x3, starting transfers between devices: 3.86 us -> 10.6 us  [deal(): lax.ppermute(dealt[k], 'tile', shifts[k])]
    ppermute x1, waiting for transfers between devices: 0.01 us -> 4.85 us  [body(): block = lax.ppermute(packed, 'tile', ring)]
    ppermute x1, starting transfers between devices: 5.17 us -> 1.75 us  [body(): notes = lax.ppermute(notes, 'tile', [(j, i) for i, j in ring])]
    ppermute x2, starting transfers between devices: 0.78 us -> 4.06 us  [body(): block = lax.ppermute(block, 'tile', ring)]
    ppermute x4, waiting for transfers between devices: 13 us -> 11.1 us  [exchange(): c.received.append(lax.ppermute(c.parts[2 * half + 1], 'dp', pairs))]
    ppermute x3, starting transfers between devices: 3.12 us -> 4.86 us  [gather(): lax.ppermute(c.mine, 'tile', shifts[k])]
  transfers between devices with their start and end apart: 20 -> 20, of which waited for: 12 -> 15; matrix products, arithmetic and copies ran while one was open for 0% -> 0% of each run, Pallas kernels for 34% -> 14%
where the time goes in v10:
time: 94.2 us
  waiting for transfers between devices  42.4 us (45%)
  starting transfers between devices  32.2 us (34%)
  Pallas kernels  17.9 us (19%)
  local copies, waits for them, and re-layouts  1 us (1%)
    pallas_call x12, Pallas kernels, run(): pl.pallas_call(kernel, out_shape=tuple((s if i in hbm_out else pltpu.VMEM...  17.9 us
    ppermute x2, waiting for transfers between devices, body(): block = lax.ppermute(block, 'tile', ring)  14.4 us
    ppermute x4, waiting for transfers between devices, exchange(): c.received.append(lax.ppermute(c.parts[2 * half + 1], 'dp', pairs))  11.1 us
    ppermute x3, starting transfers between devices, deal(): lax.ppermute(dealt[k], 'tile', shifts[k])  10.6 us
    ppermute x4, starting transfers between devices, exchange(): c.received.append(lax.ppermute(c.parts[2 * half + 1], 'dp', pairs))  6.46 us
    ppermute x3, waiting for transfers between devices, gather(): lax.ppermute(c.mine, 'tile', shifts[k])  5.51 us
    ppermute x3, starting transfers between devices, gather(): lax.ppermute(c.mine, 'tile', shifts[k])  4.86 us
    ppermute x1, waiting for transfers between devices, body(): block = lax.ppermute(packed, 'tile', ring)  4.85 us
  transfers between devices with their start and end apart: 20, of which 15 were waited for; matrix products, arithmetic and copies ran while one was open for 0% of the time, Pallas kernels for 14%

profile of v10, /device:TPU:0, one launch (start us, length us, event | category | flops | bytes accessed | tf_op | source)
XLA Modules:
  0.0 94.2 jit_solution(4544490357751573887)
XLA Ops:
  3.1 2.6 %collective-permute-start = (bf16[800,256]{1,0:T(8,128)(2,1)S(1)}, bf16[800,256]{1,0:T(8,128)(2,1)S(1)}, u32[]{:S(2)}, u32[]{:S(2)}) collective-permute-start(bf16[800,256]{1,0:T(8,128)(2,1)S(1)} %get-tuple-element.61.refs_5_.refs_9_.refs_11_), channel_id=1, source_target_pairs={{0,2},{1,3},{2,6},{3,7},{6,4},{7,5},{4,0},{5,1},{8,10},{9,11},{10,... | collective-permute-start | bytes 1228808 | tf_op jit(solution)/shard_map/ppermute | solution.py:676
  5.7 5.6 %shard_map.104 = (f32[2064,256]{1,0:T(8,128)S(1)}, bf16[2304,256]{1,0:T(8,128)(2,1)S(1)}, bf16[2304,256]{1,0:T(8,128)(2,1)S(1)}, bf16[2304,256]{1,0:T(8,128)(2,1...) custom-call(bf16[1024,256]{1,0:T(8,128)(2,1)} %bitcast.12, ...), custom_call_target="tpu_custom_call" | custom-call | tf_op jit(solution)/shard_map/pallas_call | solution.py:26
  12.0 4.9 %collective-permute-done.refs_10_.refs_12_ = bf16[800,256]{1,0:T(8,128)(2,1)S(1)} collective-permute-done((bf16[800,256]{1,0:T(8,128)(2,1)S(1)}, bf16[800,256]{1,0:T(8,128)(2,1)S(1)}, u32[]{:S(2)}, u32[]{:S(2)}) %collective-permute-start) | collective-permute-done | bytes 409632 | tf_op jit(solution)/shard_map/ppermute | solution.py:676
  16.9 2.3 %collective-permute-start.3 = (bf16[800,256]{1,0:T(8,128)(2,1)S(1)}, bf16[800,256]{1,0:T(8,128)(2,1)S(1)}, u32[]{:S(2)}, u32[]{:S(2)}) collective-permute-start(bf16[800,256]{1,0:T(8,128)(2,1)S(1)} %collective-permute-done.refs_10_.refs_12_), channel_id=1, source_target_pairs={{0,2},{1,3},{2,6},{3,7},{6,4},{7,5},{4,0},{5,1},{8,10},{9,11},{10,... | collective-permute-start | bytes 1228808 | tf_op jit(solution)/shard_map/ppermute | solution.py:700
  19.5 1.7 %collective-permute-start.4 = (bf16[16,256]{1,0:T(8,128)(2,1)S(1)}, bf16[16,256]{1,0:T(8,128)(2,1)S(1)}, u32[]{:S(2)}, u32[]{:S(2)}) collective-permute-start(bf16[16,256]{1,0:T(8,128)(2,1)S(1)} %get-tuple-element.86), channel_id=1, source_target_pairs={{2,0},{3,1},{6,2},{7,3},{4,6},{5,7},{0,4},{1,5},{10,8},{11,9},{14,... | collective-permute-start | bytes 24584 | tf_op jit(solution)/shard_map/ppermute | solution.py:687
  21.5 9.5 %collective-permute-done.3.refs_13_ = bf16[800,256]{1,0:T(8,128)(2,1)S(1)} collective-permute-done((bf16[800,256]{1,0:T(8,128)(2,1)S(1)}, bf16[800,256]{1,0:T(8,128)(2,1)S(1)}, u32[]{:S(2)}, u32[]{:S(2)}) %collective-permute-start.3) | collective-permute-done | bytes 409632 | tf_op jit(solution)/shard_map/ppermute | solution.py:700
  31.1 1.8 %collective-permute-start.6 = (bf16[800,256]{1,0:T(8,128)(2,1)S(1)}, bf16[800,256]{1,0:T(8,128)(2,1)S(1)}, u32[]{:S(2)}, u32[]{:S(2)}) collective-permute-start(bf16[800,256]{1,0:T(8,128)(2,1)S(1)} %collective-permute-done.3.refs_13_), channel_id=1, source_target_pairs={{0,2},{1,3},{2,6},{3,7},{6,4},{7,5},{4,0},{5,1},{8,10},{9,11},{10,... | collective-permute-start | bytes 1228808 | tf_op jit(solution)/shard_map/ppermute | solution.py:700
  32.8 5.6 %shard_map.106 = (f32[2064,256]{1,0:T(8,128)S(1)}, f32[256,2304]{1,0:T(8,128)S(1)}, f32[256,2304]{1,0:T(8,128)S(1)}, f32[2064,256]{1,0:T(8,128)S(1)}, bf16[4,224...) custom-call(f32[2064,256]{1,0:T(8,128)S(1)} %get-tuple-element.80.re, ...), custom_call_target="tpu_custom_call", output_to_operand_aliasing={{0}: (0, {}), {1}: (6, {}), {2}: (7, {}), {3}: (8, {})} | custom-call | tf_op jit(solution)/shard_map/pallas_call | solution.py:26
  38.5 5.0 %collective-permute-done.6.refs_9_ = bf16[800,256]{1,0:T(8,128)(2,1)S(1)} collective-permute-done((bf16[800,256]{1,0:T(8,128)(2,1)S(1)}, bf16[800,256]{1,0:T(8,128)(2,1)S(1)}, u32[]{:S(2)}, u32[]{:S(2)}) %collective-permute-start.6) | collective-permute-done | bytes 409632 | tf_op jit(solution)/shard_map/ppermute | solution.py:700
  43.4 2.9 %shard_map.107 = (f32[256,2304]{1,0:T(8,128)S(1)}, f32[256,2304]{1,0:T(8,128)S(1)}, f32[2064,256]{1,0:T(8,128)S(1)}, bf16[2304,256]{1,0:T(8,128)(2,1)S(1)}, bf16...) custom-call(f32[2064,256]{1,0:T(8,128)S(1)} %get-tuple-element.90.re, ...), custom_call_target="tpu_custom_call", output_to_operand_aliasing={{0}: (6, {}), {1}: (7, {}), {2}: (8, {})} | custom-call | tf_op jit(solution)/shard_map/pallas_call | solution.py:26
  46.4 2.8 %collective-permute-done.7.got_ref = bf16[2304,256]{1,0:T(8,128)(2,1)S(1)} collective-permute-done((bf16[2304,256]{1,0:T(8,128)(2,1)S(1)}, bf16[2304,256]{1,0:T(8,128)(2,1)S(1)}, u32[]{:S(2)}, u32[]{:S(2)}) %collective-permute-start.7) | collective-permute-done | bytes 1179680 | tf_op jit(solution)/shard_map/ppermute | solution.py:508
  49.7 2.8 %collective-permute-start.8 = (bf16[2,288,256]{2,1,0:T(8,128)(2,1)S(1)}, bf16[2,288,256]{2,1,0:T(8,128)(2,1)S(1)}, u32[]{:S(2)}, u32[]{:S(2)}) collective-permute-start(bf16[2,288,256]{2,1,0:T(8,128)(2,1)S(1)} %get-tuple-element.102), channel_id=1, source_target_pairs={{0,8},{8,0},{16,24},{24,16},{1,9},{9,1},{17,25},{25,17},{2,10},{10... | collective-permute-start | bytes 884744 | tf_op jit(solution)/shard_map/ppermute | solution.py:545
  52.5 1.5 %collective-permute-start.10 = (bf16[2,288,256]{2,1,0:T(8,128)(2,1)S(1)}, bf16[2,288,256]{2,1,0:T(8,128)(2,1)S(1)}, u32[]{:S(2)}, u32[]{:S(2)}) collective-permute-start(bf16[2,288,256]{2,1,0:T(8,128)(2,1)S(1)} %get-tuple-element.107), channel_id=1, source_target_pairs={{0,16},{8,24},{16,0},{24,8},{1,17},{9,25},{17,1},{25,9},{2,18},{10... | collective-permute-start | bytes 884744 | tf_op jit(solution)/shard_map/ppermute | solution.py:545
  54.8 5.2 %collective-permute-done.8.pr = bf16[2,288,256]{2,1,0:T(8,128)(2,1)S(1)} collective-permute-done((bf16[2,288,256]{2,1,0:T(8,128)(2,1)S(1)}, bf16[2,288,256]{2,1,0:T(8,128)(2,1)S(1)}, u32[]{:S(2)}, u32[]{:S(2)}) %collective-permute-start.8) | collective-permute-done | bytes 294944 | tf_op jit(solution)/shard_map/ppermute | solution.py:545
  60.0 1.5 %collective-permute-done.10.qr = bf16[2,288,256]{2,1,0:T(8,128)(2,1)S(1)} collective-permute-done((bf16[2,288,256]{2,1,0:T(8,128)(2,1)S(1)}, bf16[2,288,256]{2,1,0:T(8,128)(2,1)S(1)}, u32[]{:S(2)}, u32[]{:S(2)}) %collective-permute-start.10) | collective-permute-done | bytes 294944 | tf_op jit(solution)/shard_map/ppermute | solution.py:545
  61.6 1.6 %collective-permute-start.11 = (bf16[1,288,256]{2,1,0:T(8,128)(2,1)S(1)}, bf16[1,288,256]{2,1,0:T(8,128)(2,1)S(1)}, u32[]{:S(2)}, u32[]{:S(2)}) collective-permute-start(bf16[1,288,256]{2,1,0:T(8,128)(2,1)S(1)} %get-tuple-element.109), channel_id=1, source_target_pairs={{0,16},{8,24},{16,0},{24,8},{1,17},{9,25},{17,1},{25,9},{2,18},{10... | collective-permute-start | bytes 442376 | tf_op jit(solution)/shard_map/ppermute | solution.py:545
  63.8 3.0 %collective-permute-done.11.pr = bf16[1,288,256]{2,1,0:T(8,128)(2,1)S(1)} collective-permute-done((bf16[1,288,256]{2,1,0:T(8,128)(2,1)S(1)}, bf16[1,288,256]{2,1,0:T(8,128)(2,1)S(1)}, u32[]{:S(2)}, u32[]{:S(2)}) %collective-permute-start.11) | collective-permute-done | bytes 147488 | tf_op jit(solution)/shard_map/ppermute | solution.py:545
  66.8 1.5 %collective-permute-done.12.qr = bf16[1,288,256]{2,1,0:T(8,128)(2,1)S(1)} collective-permute-done((bf16[1,288,256]{2,1,0:T(8,128)(2,1)S(1)}, bf16[1,288,256]{2,1,0:T(8,128)(2,1)S(1)}, u32[]{:S(2)}, u32[]{:S(2)}) %collective-permute-start.12) | collective-permute-done | bytes 147488 | tf_op jit(solution)/shard_map/ppermute | solution.py:545
  69.8 6.4 %collective-permute-start.14 = (bf16[144,256]{1,0:T(8,128)(2,1)S(1)}, bf16[144,256]{1,0:T(8,128)(2,1)S(1)}, u32[]{:S(2)}, u32[]{:S(2)}) collective-permute-start(bf16[144,256]{1,0:T(8,128)(2,1)S(1)} %get-tuple-element.114), channel_id=1, source_target_pairs={{0,4},{1,5},{2,6},{3,7},{4,0},{5,1},{6,2},{7,3},{8,12},{9,13},{10,... | collective-permute-start | bytes 221192 | tf_op jit(solution)/shard_map/ppermute | solution.py:589
  76.2 2.8 %collective-permute-start.15 = (bf16[144,256]{1,0:T(8,128)(2,1)S(1)}, bf16[144,256]{1,0:T(8,128)(2,1)S(1)}, u32[]{:S(2)}, u32[]{:S(2)}) collective-permute-start(bf16[144,256]{1,0:T(8,128)(2,1)S(1)} %get-tuple-element.115), channel_id=1, source_target_pairs={{0,6},{1,7},{2,0},{3,1},{4,2},{5,3},{6,4},{7,5},{8,14},{9,15},{10,... | collective-permute-start | bytes 221192 | tf_op jit(solution)/shard_map/ppermute | solution.py:589
  79.3 1.7 %collective-permute-done.15.refs_3_ = bf16[144,256]{1,0:T(8,128)(2,1)S(1)} collective-permute-done((bf16[144,256]{1,0:T(8,128)(2,1)S(1)}, bf16[144,256]{1,0:T(8,128)(2,1)S(1)}, u32[]{:S(2)}, u32[]{:S(2)}) %collective-permute-start.15) | collective-permute-done | bytes 73760 | tf_op jit(solution)/shard_map/ppermute | solution.py:589
  81.1 4.2 %collective-permute-start.18 = (bf16[144,256]{1,0:T(8,128)(2,1)S(1)}, bf16[144,256]{1,0:T(8,128)(2,1)S(1)}, u32[]{:S(2)}, u32[]{:S(2)}) collective-permute-start(bf16[144,256]{1,0:T(8,128)(2,1)S(1)} %shard_map.112.refs_0_), channel_id=1, source_target_pairs={{0,6},{1,7},{2,0},{3,1},{4,2},{5,3},{6,4},{7,5},{8,14},{9,15},{10,... | collective-permute-start | bytes 221192 | tf_op jit(solution)/shard_map/ppermute | solution.py:599
  87.3 3.3 %collective-permute-done.17.refs_2_ = bf16[144,256]{1,0:T(8,128)(2,1)S(1)} collective-permute-done((bf16[144,256]{1,0:T(8,128)(2,1)S(1)}, bf16[144,256]{1,0:T(8,128)(2,1)S(1)}, u32[]{:S(2)}, u32[]{:S(2)}) %collective-permute-start.17) | collective-permute-done | bytes 73760 | tf_op jit(solution)/shard_map/ppermute | solution.py:599
  91.6 1.6 %collective-permute-done.19.refs_1_ = bf16[576,256]{1,0:T(8,128)(2,1)S(1)} collective-permute-done((bf16[576,256]{1,0:T(8,128)(2,1)S(1)}, bf16[576,256]{1,0:T(8,128)(2,1)S(1)}, u32[]{:S(2)}, u32[]{:S(2)}) %collective-permute-start.19) | collective-permute-done | bytes 294944 | tf_op jit(solution)/shard_map/ppermute | solution.py:609
  (30 shorter events, 11.8 us)
Async XLA Ops:
  0.6 5.1 %collective-permute-start.1 = (bf16[1024,256]{1,0:T(8,128)(2,1)}, bf16[1024,256]{1,0:T(8,128)(2,1)S(1)}, u32[]{:S(2)}, u32[]{:S(2)}) collective-permute-start(bf16[1024,256]{1,0:T(8,128)(2,1)} %bitcast.10), channel_id=1, source_target_pairs={{0,1},{1,0},{2,3},{3,2},{4,5},{5,4},{6,7},{7,6},{8,9},{9,8},{10,11... | collective-permute-start | bytes 1572872 | tf_op jit(solution)/shard_map/ppermute | solution.py:666
  1.1 1.0 %copy-start = (bf16[1,4,14,14,256]{4,1,3,2,0:T(4,128)(2,1)S(1)}, bf16[1,4,14,14,256]{4,1,3,2,0:T(4,128)(2,1)}, u32[]{:S(2)}) copy-start(bf16[1,4,14,14,256]{4,1,3,2,0:T(4,128)(2,1)} %param.15) | copy-start | bytes 1204228
  3.1 13.8 %collective-permute-start = (bf16[800,256]{1,0:T(8,128)(2,1)S(1)}, bf16[800,256]{1,0:T(8,128)(2,1)S(1)}, u32[]{:S(2)}, u32[]{:S(2)}) collective-permute-start(bf16[800,256]{1,0:T(8,128)(2,1)S(1)} %get-tuple-element.61.refs_5_.refs_9_.refs_11_), channel_id=1, source_target_pairs={{0,2},{1,3},{2,6},{3,7},{6,4},{7,5},{4,0},{5,1},{8,10},{9,11},{10,... | collective-permute-start | bytes 1228808 | tf_op jit(solution)/shard_map/ppermute | solution.py:676
  11.4 5.5 %collective-permute-start.2 = (bf16[64,256]{1,0:T(8,128)(2,1)S(1)}, bf16[64,256]{1,0:T(8,128)(2,1)S(1)}, u32[]{:S(2)}, u32[]{:S(2)}) collective-permute-start(bf16[64,256]{1,0:T(8,128)(2,1)S(1)} %get-tuple-element.68), channel_id=1, source_target_pairs={{1,2},{2,1},{3,4},{4,3},{5,6},{6,5},{9,10},{10,9},{11,12},{12,11},... | collective-permute-start | bytes 98312 | tf_op jit(solution)/shard_map/ppermute | solution.py:684
  16.9 14.1 %collective-permute-start.3 = (bf16[800,256]{1,0:T(8,128)(2,1)S(1)}, bf16[800,256]{1,0:T(8,128)(2,1)S(1)}, u32[]{:S(2)}, u32[]{:S(2)}) collective-permute-start(bf16[800,256]{1,0:T(8,128)(2,1)S(1)} %collective-permute-done.refs_10_.refs_12_), channel_id=1, source_target_pairs={{0,2},{1,3},{2,6},{3,7},{6,4},{7,5},{4,0},{5,1},{8,10},{9,11},{10,... | collective-permute-start | bytes 1228808 | tf_op jit(solution)/shard_map/ppermute | solution.py:700
  19.2 11.9 %collective-permute-start.5 = (bf16[64,256]{1,0:T(8,128)(2,1)S(1)}, bf16[64,256]{1,0:T(8,128)(2,1)S(1)}, u32[]{:S(2)}, u32[]{:S(2)}) collective-permute-start(bf16[64,256]{1,0:T(8,128)(2,1)S(1)} %collective-permute-done.2.refs_9_), channel_id=1, source_target_pairs={{0,1},{1,0},{2,3},{3,2},{4,5},{5,4},{6,7},{7,6},{8,9},{9,8},{10,11... | collective-permute-start | bytes 98312 | tf_op jit(solution)/shard_map/ppermute | solution.py:702
  19.5 11.5 %collective-permute-start.4 = (bf16[16,256]{1,0:T(8,128)(2,1)S(1)}, bf16[16,256]{1,0:T(8,128)(2,1)S(1)}, u32[]{:S(2)}, u32[]{:S(2)}) collective-permute-start(bf16[16,256]{1,0:T(8,128)(2,1)S(1)} %get-tuple-element.86), channel_id=1, source_target_pairs={{2,0},{3,1},{6,2},{7,3},{4,6},{5,7},{0,4},{1,5},{10,8},{11,9},{14,... | collective-permute-start | bytes 24584 | tf_op jit(solution)/shard_map/ppermute | solution.py:687
  31.1 12.4 %collective-permute-start.6 = (bf16[800,256]{1,0:T(8,128)(2,1)S(1)}, bf16[800,256]{1,0:T(8,128)(2,1)S(1)}, u32[]{:S(2)}, u32[]{:S(2)}) collective-permute-start(bf16[800,256]{1,0:T(8,128)(2,1)S(1)} %collective-permute-done.3.refs_13_), channel_id=1, source_target_pairs={{0,2},{1,3},{2,6},{3,7},{6,4},{7,5},{4,0},{5,1},{8,10},{9,11},{10,... | collective-permute-start | bytes 1228808 | tf_op jit(solution)/shard_map/ppermute | solution.py:700
  46.3 2.9 %collective-permute-start.7 = (bf16[2304,256]{1,0:T(8,128)(2,1)S(1)}, bf16[2304,256]{1,0:T(8,128)(2,1)S(1)}, u32[]{:S(2)}, u32[]{:S(2)}) collective-permute-start(bf16[2304,256]{1,0:T(8,128)(2,1)S(1)} %get-tuple-element.98), channel_id=1, source_target_pairs={{0,1},{1,0},{2,3},{3,2},{4,5},{5,4},{6,7},{7,6},{8,9},{9,8},{10,11... | collective-permute-start | bytes 3538952 | tf_op jit(solution)/shard_map/ppermute | solution.py:508
  49.5 4.5 %collective-permute-start.9 = (bf16[1024,256]{1,0:T(8,128)(2,1)S(1)}, bf16[1024,256]{1,0:T(8,128)(2,1)S(1)}, u32[]{:S(2)}, u32[]{:S(2)}) collective-permute-start(bf16[1024,256]{1,0:T(8,128)(2,1)S(1)} %get-tuple-element.104), channel_id=1, source_target_pairs={{0,1},{1,0},{2,3},{3,2},{4,5},{5,4},{6,7},{7,6},{8,9},{9,8},{10,11... | collective-permute-start | bytes 1572872 | tf_op jit(solution)/shard_map/ppermute | solution.py:715
  49.7 10.3 %collective-permute-start.8 = (bf16[2,288,256]{2,1,0:T(8,128)(2,1)S(1)}, bf16[2,288,256]{2,1,0:T(8,128)(2,1)S(1)}, u32[]{:S(2)}, u32[]{:S(2)}) collective-permute-start(bf16[2,288,256]{2,1,0:T(8,128)(2,1)S(1)} %get-tuple-element.102), channel_id=1, source_target_pairs={{0,8},{8,0},{16,24},{24,16},{1,9},{9,1},{17,25},{25,17},{2,10},{10... | collective-permute-start | bytes 884744 | tf_op jit(solution)/shard_map/ppermute | solution.py:545
  52.5 9.0 %collective-permute-start.10 = (bf16[2,288,256]{2,1,0:T(8,128)(2,1)S(1)}, bf16[2,288,256]{2,1,0:T(8,128)(2,1)S(1)}, u32[]{:S(2)}, u32[]{:S(2)}) collective-permute-start(bf16[2,288,256]{2,1,0:T(8,128)(2,1)S(1)} %get-tuple-element.107), channel_id=1, source_target_pairs={{0,16},{8,24},{16,0},{24,8},{1,17},{9,25},{17,1},{25,9},{2,18},{10... | collective-permute-start | bytes 884744 | tf_op jit(solution)/shard_map/ppermute | solution.py:545
  61.6 5.2 %collective-permute-start.11 = (bf16[1,288,256]{2,1,0:T(8,128)(2,1)S(1)}, bf16[1,288,256]{2,1,0:T(8,128)(2,1)S(1)}, u32[]{:S(2)}, u32[]{:S(2)}) collective-permute-start(bf16[1,288,256]{2,1,0:T(8,128)(2,1)S(1)} %get-tuple-element.109), channel_id=1, source_target_pairs={{0,16},{8,24},{16,0},{24,8},{1,17},{9,25},{17,1},{25,9},{2,18},{10... | collective-permute-start | bytes 442376 | tf_op jit(solution)/shard_map/ppermute | solution.py:545
  63.2 5.1 %collective-permute-start.12 = (bf16[1,288,256]{2,1,0:T(8,128)(2,1)S(1)}, bf16[1,288,256]{2,1,0:T(8,128)(2,1)S(1)}, u32[]{:S(2)}, u32[]{:S(2)}) collective-permute-start(bf16[1,288,256]{2,1,0:T(8,128)(2,1)S(1)} %get-tuple-element.111), channel_id=1, source_target_pairs={{0,8},{8,0},{16,24},{24,16},{1,9},{9,1},{17,25},{25,17},{2,10},{10... | collective-permute-start | bytes 442376 | tf_op jit(solution)/shard_map/ppermute | solution.py:545
  68.4 10.6 %collective-permute-start.13 = (bf16[144,256]{1,0:T(8,128)(2,1)S(1)}, bf16[144,256]{1,0:T(8,128)(2,1)S(1)}, u32[]{:S(2)}, u32[]{:S(2)}) collective-permute-start(bf16[144,256]{1,0:T(8,128)(2,1)S(1)} %get-tuple-element.113), channel_id=1, source_target_pairs={{0,2},{1,3},{2,4},{3,5},{4,6},{5,7},{6,0},{7,1},{8,10},{9,11},{10,... | collective-permute-start | bytes 221192 | tf_op jit(solution)/shard_map/ppermute | solution.py:589
  69.8 9.6 %collective-permute-start.14 = (bf16[144,256]{1,0:T(8,128)(2,1)S(1)}, bf16[144,256]{1,0:T(8,128)(2,1)S(1)}, u32[]{:S(2)}, u32[]{:S(2)}) collective-permute-start(bf16[144,256]{1,0:T(8,128)(2,1)S(1)} %get-tuple-element.114), channel_id=1, source_target_pairs={{0,4},{1,5},{2,6},{3,7},{4,0},{5,1},{6,2},{7,3},{8,12},{9,13},{10,... | collective-permute-start | bytes 221192 | tf_op jit(solution)/shard_map/ppermute | solution.py:589
  76.2 4.8 %collective-permute-start.15 = (bf16[144,256]{1,0:T(8,128)(2,1)S(1)}, bf16[144,256]{1,0:T(8,128)(2,1)S(1)}, u32[]{:S(2)}, u32[]{:S(2)}) collective-permute-start(bf16[144,256]{1,0:T(8,128)(2,1)S(1)} %get-tuple-element.115), channel_id=1, source_target_pairs={{0,6},{1,7},{2,0},{3,1},{4,2},{5,3},{6,4},{7,5},{8,14},{9,15},{10,... | collective-permute-start | bytes 221192 | tf_op jit(solution)/shard_map/ppermute | solution.py:589
  81.1 6.2 %collective-permute-start.18 = (bf16[144,256]{1,0:T(8,128)(2,1)S(1)}, bf16[144,256]{1,0:T(8,128)(2,1)S(1)}, u32[]{:S(2)}, u32[]{:S(2)}) collective-permute-start(bf16[144,256]{1,0:T(8,128)(2,1)S(1)} %shard_map.112.refs_0_), channel_id=1, source_target_pairs={{0,6},{1,7},{2,0},{3,1},{4,2},{5,3},{6,4},{7,5},{8,14},{9,15},{10,... | collective-permute-start | bytes 221192 | tf_op jit(solution)/shard_map/ppermute | solution.py:599
  85.3 5.3 %collective-permute-start.17 = (bf16[144,256]{1,0:T(8,128)(2,1)S(1)}, bf16[144,256]{1,0:T(8,128)(2,1)S(1)}, u32[]{:S(2)}, u32[]{:S(2)}) collective-permute-start(bf16[144,256]{1,0:T(8,128)(2,1)S(1)} %shard_map.112.refs_0_), channel_id=1, source_target_pairs={{0,4},{1,5},{2,6},{3,7},{4,0},{5,1},{6,2},{7,3},{8,12},{9,13},{10,... | collective-permute-start | bytes 221192 | tf_op jit(solution)/shard_map/ppermute | solution.py:599
  85.3 6.2 %collective-permute-start.16 = (bf16[144,256]{1,0:T(8,128)(2,1)S(1)}, bf16[144,256]{1,0:T(8,128)(2,1)S(1)}, u32[]{:S(2)}, u32[]{:S(2)}) collective-permute-start(bf16[144,256]{1,0:T(8,128)(2,1)S(1)} %shard_map.112.refs_0_), channel_id=1, source_target_pairs={{0,2},{1,3},{2,4},{3,5},{4,6},{5,7},{6,0},{7,1},{8,10},{9,11},{10,... | collective-permute-start | bytes 221192 | tf_op jit(solution)/shard_map/ppermute | solution.py:599
  91.5 1.6 %collective-permute-start.19 = (bf16[576,256]{1,0:T(8,128)(2,1)S(1)}, bf16[576,256]{1,0:T(8,128)(2,1)S(1)}, u32[]{:S(2)}, u32[]{:S(2)}) collective-permute-start(bf16[576,256]{1,0:T(8,128)(2,1)S(1)} %shard_map.113.refs_0_), channel_id=1, source_target_pairs={{0,1},{1,0},{2,3},{3,2},{4,5},{5,4},{6,7},{7,6},{8,9},{9,8},{10,11... | collective-permute-start | bytes 884744 | tf_op jit(solution)/shard_map/ppermute | solution.py:609

commit v11 on v10

--- a/solution.py
+++ b/solution.py
@@ -237,10 +237,9 @@
         return found
 
     for s, most in enumerate(plan[: len(blocks)]):
-        if s == 2:
+        if s == 1:
             count = scan(0, True)
-            count = scan(1, True)
-        count = scan(s, False if s < 2 and len(plan) > 1 else None)
+        count = scan(s, False if s == 0 and len(plan) > 1 else None)
         start, end = end, count if most is None else jnp.minimum(count, end + most)
     total = count
     for note in early:
@@ -694,14 +693,14 @@
         block, state[0], state[-1] = lax.optimization_barrier((block, state[0], state[-1]))
         if step == 1:
             block, rim_a = lax.optimization_barrier((block, rim_a))
-        if step == 2:
-            block, notes, rim_b = lax.optimization_barrier((block, notes, rim_b))
+        if step == chips - 2:
+            block, notes = lax.optimization_barrier((block, notes))
         held = held + [block]
         block = lax.ppermute(block, "tile", ring)
         if step == 1:
             rim_b = lax.ppermute(rim_a, "tile", swap)
         early = [notes] if step == chips - 2 else []
-        rims = [rim_a, rim_b] if step == 2 else []
+        rims = [rim_a, rim_b] if step == 1 else []
         got = list(main_call(*sizes, False, False, plan, state, [], rims, held, early, []))
         if rims:
             kept[0] = got.pop(0)

time: 94.2 us -> 89.5 us (0.950)
  waiting for transfers between devices: 42.4 us -> 39 us
  starting transfers between devices: 32.2 us -> 31 us
    ppermute x2, waiting for transfers between devices: 14.4 us -> 9.17 us  [body(): block = lax.ppermute(block, 'tile', ring)]
    ppermute x3, starting transfers between devices: 10.6 us -> 6.05 us  [deal(): lax.ppermute(dealt[k], 'tile', shifts[k])]
    ppermute x2, starting transfers between devices: 4.06 us -> 7.67 us  [body(): block = lax.ppermute(block, 'tile', ring)]
    ppermute x1, starting transfers between devices: 0.07 us -> 3.13 us  [reduce_weights(): arrived = [lax.ppermute(send, 'tile', core_swap) for send in sends]]
    ppermute x3, waiting for transfers between devices: 1.98 us -> 4.71 us  [deal(): lax.ppermute(dealt[k], 'tile', shifts[k])]
    ppermute x3, starting transfers between devices: 4.86 us -> 2.92 us  [gather(): lax.ppermute(c.mine, 'tile', shifts[k])]
    ppermute x4, waiting for transfers between devices: 11.1 us -> 10 us  [exchange(): c.received.append(lax.ppermute(c.parts[2 * half + 1], 'dp', pairs))]
  transfers between devices with their start and end apart: 20 -> 20, of which waited for: 15 -> 17; matrix products, arithmetic and copies ran while one was open for 0% -> 0% of each run, Pallas kernels for 14% -> 17%
where the time goes in v11:
time: 89.5 us; the launch traced here: 89.3 us
  waiting for transfers between devices  39 us (44%)
  starting transfers between devices  31 us (35%)
  Pallas kernels  17.5 us (20%)
  local copies, waits for them, and re-layouts  1 us (1%)
    pallas_call x12, Pallas kernels, run(): pl.pallas_call(kernel, out_shape=tuple((s if i in hbm_out else pltpu.VMEM...  17.5 us
    ppermute x4, waiting for transfers between devices, exchange(): c.received.append(lax.ppermute(c.parts[2 * half + 1], 'dp', pairs))  10 us
    ppermute x2, waiting for transfers between devices, body(): block = lax.ppermute(block, 'tile', ring)  9.17 us
    ppermute x2, starting transfers between devices, body(): block = lax.ppermute(block, 'tile', ring)  7.67 us
    ppermute x3, starting transfers between devices, deal(): lax.ppermute(dealt[k], 'tile', shifts[k])  6.05 us
    ppermute x4, starting transfers between devices, exchange(): c.received.append(lax.ppermute(c.parts[2 * half + 1], 'dp', pairs))  5.87 us
    ppermute x3, waiting for transfers between devices, gather(): lax.ppermute(c.mine, 'tile', shifts[k])  5.51 us
    ppermute x1, waiting for transfers between devices, body(): block = lax.ppermute(packed, 'tile', ring)  4.85 us
  transfers between devices with their start and end apart: 20, of which 17 were waited for; matrix products, arithmetic and copies ran while one was open for 0% of the time, Pallas kernels for 17%

profile of v11, /device:TPU:0, one launch (start us, length us, event | category | flops | bytes accessed | tf_op | source)
XLA Modules:
  0.0 89.3 jit_solution(10120884498902924036)
XLA Ops:
  3.1 2.6 %collective-permute-start = (bf16[800,256]{1,0:T(8,128)(2,1)S(1)}, bf16[800,256]{1,0:T(8,128)(2,1)S(1)}, u32[]{:S(2)}, u32[]{:S(2)}) collective-permute-start(bf16[800,256]{1,0:T(8,128)(2,1)S(1)} %get-tuple-element.60.refs_5_.refs_11_.refs_9_), channel_id=1, source_target_pairs={{0,2},{1,3},{2,6},{3,7},{6,4},{7,5},{4,0},{5,1},{8,10},{9,11},{10,... | collective-permute-start | bytes 1228808 | tf_op jit(solution)/shard_map/ppermute | solution.py:675
  5.7 5.6 %shard_map.104 = (f32[2064,256]{1,0:T(8,128)S(1)}, bf16[2304,256]{1,0:T(8,128)(2,1)S(1)}, bf16[2304,256]{1,0:T(8,128)(2,1)S(1)}, bf16[2304,256]{1,0:T(8,128)(2,1...) custom-call(bf16[1024,256]{1,0:T(8,128)(2,1)} %bitcast.12, ...), custom_call_target="tpu_custom_call" | custom-call | tf_op jit(solution)/shard_map/pallas_call | solution.py:26
  12.0 4.9 %collective-permute-done.refs_12_.refs_10_ = bf16[800,256]{1,0:T(8,128)(2,1)S(1)} collective-permute-done((bf16[800,256]{1,0:T(8,128)(2,1)S(1)}, bf16[800,256]{1,0:T(8,128)(2,1)S(1)}, u32[]{:S(2)}, u32[]{:S(2)}) %collective-permute-start) | collective-permute-done | bytes 409632 | tf_op jit(solution)/shard_map/ppermute | solution.py:675
  16.9 5.4 %collective-permute-start.4 = (bf16[800,256]{1,0:T(8,128)(2,1)S(1)}, bf16[800,256]{1,0:T(8,128)(2,1)S(1)}, u32[]{:S(2)}, u32[]{:S(2)}) collective-permute-start(bf16[800,256]{1,0:T(8,128)(2,1)S(1)} %collective-permute-done.refs_12_.refs_10_), channel_id=1, source_target_pairs={{0,2},{1,3},{2,6},{3,7},{6,4},{7,5},{4,0},{5,1},{8,10},{9,11},{10,... | collective-permute-start | bytes 1228808 | tf_op jit(solution)/shard_map/ppermute | solution.py:699
  23.5 3.7 %shard_map.105 = (f32[2064,256]{1,0:T(8,128)S(1)}, f32[256,2304]{1,0:T(8,128)S(1)}, f32[256,2304]{1,0:T(8,128)S(1)}, f32[2064,256]{1,0:T(8,128)S(1)}) custom-call(f32[2064,256]{1,0:T(8,128)S(1)} %get-tuple-element.66.refs_0_, ...), custom_call_target="tpu_custom_call", output_to_operand_aliasing={{0}: (0, {}), {1}: (6, {}), {2}: (7, {}), {3}: (8, {})} | custom-call | tf_op jit(solution)/shard_map/pallas_call | solution.py:26
  27.2 2.7 %collective-permute-done.4.refs_11_ = bf16[800,256]{1,0:T(8,128)(2,1)S(1)} collective-permute-done((bf16[800,256]{1,0:T(8,128)(2,1)S(1)}, bf16[800,256]{1,0:T(8,128)(2,1)S(1)}, u32[]{:S(2)}, u32[]{:S(2)}) %collective-permute-start.4) | collective-permute-done | bytes 409632 | tf_op jit(solution)/shard_map/ppermute | solution.py:699
  30.4 2.3 %collective-permute-start.6 = (bf16[800,256]{1,0:T(8,128)(2,1)S(1)}, bf16[800,256]{1,0:T(8,128)(2,1)S(1)}, u32[]{:S(2)}, u32[]{:S(2)}) collective-permute-start(bf16[800,256]{1,0:T(8,128)(2,1)S(1)} %collective-permute-done.4.refs_11_), channel_id=1, source_target_pairs={{0,2},{1,3},{2,6},{3,7},{6,4},{7,5},{4,0},{5,1},{8,10},{9,11},{10,... | collective-permute-start | bytes 1228808 | tf_op jit(solution)/shard_map/ppermute | solution.py:699
  32.7 3.7 %shard_map.106 = (f32[256,2304]{1,0:T(8,128)S(1)}, f32[256,2304]{1,0:T(8,128)S(1)}, f32[2064,256]{1,0:T(8,128)S(1)}, bf16[4,224,256]{2,1,0:T(8,128)(2,1)S(1)}, f...) custom-call(f32[2064,256]{1,0:T(8,128)S(1)} %get-tuple-element.81.re, ...), custom_call_target="tpu_custom_call", output_to_operand_aliasing={{0}: (6, {}), {1}: (7, {}), {2}: (8, {})} | custom-call | tf_op jit(solution)/shard_map/pallas_call | solution.py:26
  36.4 6.4 %collective-permute-done.6.refs_9_ = bf16[800,256]{1,0:T(8,128)(2,1)S(1)} collective-permute-done((bf16[800,256]{1,0:T(8,128)(2,1)S(1)}, bf16[800,256]{1,0:T(8,128)(2,1)S(1)}, u32[]{:S(2)}, u32[]{:S(2)}) %collective-permute-start.6) | collective-permute-done | bytes 409632 | tf_op jit(solution)/shard_map/ppermute | solution.py:699
  43.9 3.1 %collective-permute-start.7 = (bf16[2304,256]{1,0:T(8,128)(2,1)S(1)}, bf16[2304,256]{1,0:T(8,128)(2,1)S(1)}, u32[]{:S(2)}, u32[]{:S(2)}) collective-permute-start(bf16[2304,256]{1,0:T(8,128)(2,1)S(1)} %get-tuple-element.96), channel_id=1, source_target_pairs={{0,1},{1,0},{2,3},{3,2},{4,5},{5,4},{6,7},{7,6},{8,9},{9,8},{10,11... | collective-permute-start | bytes 3538952 | tf_op jit(solution)/shard_map/ppermute | solution.py:507
  47.0 2.5 %collective-permute-done.7.got_ref = bf16[2304,256]{1,0:T(8,128)(2,1)S(1)} collective-permute-done((bf16[2304,256]{1,0:T(8,128)(2,1)S(1)}, bf16[2304,256]{1,0:T(8,128)(2,1)S(1)}, u32[]{:S(2)}, u32[]{:S(2)}) %collective-permute-start.7) | collective-permute-done | bytes 1179680 | tf_op jit(solution)/shard_map/ppermute | solution.py:507
  50.2 2.3 %collective-permute-start.10 = (bf16[2,288,256]{2,1,0:T(8,128)(2,1)S(1)}, bf16[2,288,256]{2,1,0:T(8,128)(2,1)S(1)}, u32[]{:S(2)}, u32[]{:S(2)}) collective-permute-start(bf16[2,288,256]{2,1,0:T(8,128)(2,1)S(1)} %get-tuple-element.105), channel_id=1, source_target_pairs={{0,16},{8,24},{16,0},{24,8},{1,17},{9,25},{17,1},{25,9},{2,18},{10... | collective-permute-start | bytes 884744 | tf_op jit(solution)/shard_map/ppermute | solution.py:544
  53.4 5.8 %collective-permute-done.8.pr = bf16[2,288,256]{2,1,0:T(8,128)(2,1)S(1)} collective-permute-done((bf16[2,288,256]{2,1,0:T(8,128)(2,1)S(1)}, bf16[2,288,256]{2,1,0:T(8,128)(2,1)S(1)}, u32[]{:S(2)}, u32[]{:S(2)}) %collective-permute-start.8) | collective-permute-done | bytes 294944 | tf_op jit(solution)/shard_map/ppermute | solution.py:544
  60.2 1.8 %collective-permute-start.11 = (bf16[1,288,256]{2,1,0:T(8,128)(2,1)S(1)}, bf16[1,288,256]{2,1,0:T(8,128)(2,1)S(1)}, u32[]{:S(2)}, u32[]{:S(2)}) collective-permute-start(bf16[1,288,256]{2,1,0:T(8,128)(2,1)S(1)} %get-tuple-element.107), channel_id=1, source_target_pairs={{0,16},{8,24},{16,0},{24,8},{1,17},{9,25},{17,1},{25,9},{2,18},{10... | collective-permute-start | bytes 442376 | tf_op jit(solution)/shard_map/ppermute | solution.py:544
  62.0 1.7 %collective-permute-start.12 = (bf16[1,288,256]{2,1,0:T(8,128)(2,1)S(1)}, bf16[1,288,256]{2,1,0:T(8,128)(2,1)S(1)}, u32[]{:S(2)}, u32[]{:S(2)}) collective-permute-start(bf16[1,288,256]{2,1,0:T(8,128)(2,1)S(1)} %get-tuple-element.109), channel_id=1, source_target_pairs={{0,8},{8,0},{16,24},{24,16},{1,9},{9,1},{17,25},{25,17},{2,10},{10... | collective-permute-start | bytes 442376 | tf_op jit(solution)/shard_map/ppermute | solution.py:544
  63.7 2.0 %collective-permute-done.11.pr = bf16[1,288,256]{2,1,0:T(8,128)(2,1)S(1)} collective-permute-done((bf16[1,288,256]{2,1,0:T(8,128)(2,1)S(1)}, bf16[1,288,256]{2,1,0:T(8,128)(2,1)S(1)}, u32[]{:S(2)}, u32[]{:S(2)}) %collective-permute-start.11) | collective-permute-done | bytes 147488 | tf_op jit(solution)/shard_map/ppermute | solution.py:544
  65.8 1.4 %collective-permute-done.12.qr = bf16[1,288,256]{2,1,0:T(8,128)(2,1)S(1)} collective-permute-done((bf16[1,288,256]{2,1,0:T(8,128)(2,1)S(1)}, bf16[1,288,256]{2,1,0:T(8,128)(2,1)S(1)}, u32[]{:S(2)}, u32[]{:S(2)}) %collective-permute-start.12) | collective-permute-done | bytes 147488 | tf_op jit(solution)/shard_map/ppermute | solution.py:544
  68.5 4.8 %collective-permute-start.14 = (bf16[144,256]{1,0:T(8,128)(2,1)S(1)}, bf16[144,256]{1,0:T(8,128)(2,1)S(1)}, u32[]{:S(2)}, u32[]{:S(2)}) collective-permute-start(bf16[144,256]{1,0:T(8,128)(2,1)S(1)} %get-tuple-element.112), channel_id=1, source_target_pairs={{0,4},{1,5},{2,6},{3,7},{4,0},{5,1},{6,2},{7,3},{8,12},{9,13},{10,... | collective-permute-start | bytes 221192 | tf_op jit(solution)/shard_map/ppermute | solution.py:588
  73.3 1.9 %collective-permute-done.13.refs_1_ = bf16[144,256]{1,0:T(8,128)(2,1)S(1)} collective-permute-done((bf16[144,256]{1,0:T(8,128)(2,1)S(1)}, bf16[144,256]{1,0:T(8,128)(2,1)S(1)}, u32[]{:S(2)}, u32[]{:S(2)}) %collective-permute-start.13) | collective-permute-done | bytes 73760 | tf_op jit(solution)/shard_map/ppermute | solution.py:588
  75.2 2.0 %collective-permute-done.14.refs_2_ = bf16[144,256]{1,0:T(8,128)(2,1)S(1)} collective-permute-done((bf16[144,256]{1,0:T(8,128)(2,1)S(1)}, bf16[144,256]{1,0:T(8,128)(2,1)S(1)}, u32[]{:S(2)}, u32[]{:S(2)}) %collective-permute-start.14) | collective-permute-done | bytes 73760 | tf_op jit(solution)/shard_map/ppermute | solution.py:588
  78.1 2.3 %collective-permute-start.18 = (bf16[144,256]{1,0:T(8,128)(2,1)S(1)}, bf16[144,256]{1,0:T(8,128)(2,1)S(1)}, u32[]{:S(2)}, u32[]{:S(2)}) collective-permute-start(bf16[144,256]{1,0:T(8,128)(2,1)S(1)} %shard_map.112.refs_0_), channel_id=1, source_target_pairs={{0,6},{1,7},{2,0},{3,1},{4,2},{5,3},{6,4},{7,5},{8,14},{9,15},{10,... | collective-permute-start | bytes 221192 | tf_op jit(solution)/shard_map/ppermute | solution.py:598
  81.0 1.7 %collective-permute-done.18.refs_3_ = bf16[144,256]{1,0:T(8,128)(2,1)S(1)} collective-permute-done((bf16[144,256]{1,0:T(8,128)(2,1)S(1)}, bf16[144,256]{1,0:T(8,128)(2,1)S(1)}, u32[]{:S(2)}, u32[]{:S(2)}) %collective-permute-start.18) | collective-permute-done | bytes 73760 | tf_op jit(solution)/shard_map/ppermute | solution.py:598
  82.7 2.9 %collective-permute-done.17.refs_2_ = bf16[144,256]{1,0:T(8,128)(2,1)S(1)} collective-permute-done((bf16[144,256]{1,0:T(8,128)(2,1)S(1)}, bf16[144,256]{1,0:T(8,128)(2,1)S(1)}, u32[]{:S(2)}, u32[]{:S(2)}) %collective-permute-start.17) | collective-permute-done | bytes 73760 | tf_op jit(solution)/shard_map/ppermute | solution.py:598
  86.6 1.6 %collective-permute-done.19.refs_1_ = bf16[576,256]{1,0:T(8,128)(2,1)S(1)} collective-permute-done((bf16[576,256]{1,0:T(8,128)(2,1)S(1)}, bf16[576,256]{1,0:T(8,128)(2,1)S(1)}, u32[]{:S(2)}, u32[]{:S(2)}) %collective-permute-start.19) | collective-permute-done | bytes 294944 | tf_op jit(solution)/shard_map/ppermute | solution.py:608
  (30 shorter events, 13.2 us)
Async XLA Ops:
  0.6 5.1 %collective-permute-start.1 = (bf16[1024,256]{1,0:T(8,128)(2,1)}, bf16[1024,256]{1,0:T(8,128)(2,1)S(1)}, u32[]{:S(2)}, u32[]{:S(2)}) collective-permute-start(bf16[1024,256]{1,0:T(8,128)(2,1)} %bitcast.10), channel_id=1, source_target_pairs={{0,1},{1,0},{2,3},{3,2},{4,5},{5,4},{6,7},{7,6},{8,9},{9,8},{10,11... | collective-permute-start | bytes 1572872 | tf_op jit(solution)/shard_map/ppermute | solution.py:665
  1.1 1.0 %copy-start = (bf16[1,4,14,14,256]{4,1,3,2,0:T(4,128)(2,1)S(1)}, bf16[1,4,14,14,256]{4,1,3,2,0:T(4,128)(2,1)}, u32[]{:S(2)}) copy-start(bf16[1,4,14,14,256]{4,1,3,2,0:T(4,128)(2,1)} %param.15) | copy-start | bytes 1204228
  3.1 13.8 %collective-permute-start = (bf16[800,256]{1,0:T(8,128)(2,1)S(1)}, bf16[800,256]{1,0:T(8,128)(2,1)S(1)}, u32[]{:S(2)}, u32[]{:S(2)}) collective-permute-start(bf16[800,256]{1,0:T(8,128)(2,1)S(1)} %get-tuple-element.60.refs_5_.refs_11_.refs_9_), channel_id=1, source_target_pairs={{0,2},{1,3},{2,6},{3,7},{6,4},{7,5},{4,0},{5,1},{8,10},{9,11},{10,... | collective-permute-start | bytes 1228808 | tf_op jit(solution)/shard_map/ppermute | solution.py:675
  11.4 5.5 %collective-permute-start.2 = (bf16[64,256]{1,0:T(8,128)(2,1)S(1)}, bf16[64,256]{1,0:T(8,128)(2,1)S(1)}, u32[]{:S(2)}, u32[]{:S(2)}) collective-permute-start(bf16[64,256]{1,0:T(8,128)(2,1)S(1)} %get-tuple-element.76), channel_id=1, source_target_pairs={{1,2},{2,1},{3,4},{4,3},{5,6},{6,5},{9,10},{10,9},{11,12},{12,11},... | collective-permute-start | bytes 98312 | tf_op jit(solution)/shard_map/ppermute | solution.py:683
  16.9 13.1 %collective-permute-start.4 = (bf16[800,256]{1,0:T(8,128)(2,1)S(1)}, bf16[800,256]{1,0:T(8,128)(2,1)S(1)}, u32[]{:S(2)}, u32[]{:S(2)}) collective-permute-start(bf16[800,256]{1,0:T(8,128)(2,1)S(1)} %collective-permute-done.refs_12_.refs_10_), channel_id=1, source_target_pairs={{0,2},{1,3},{2,6},{3,7},{6,4},{7,5},{4,0},{5,1},{8,10},{9,11},{10,... | collective-permute-start | bytes 1228808 | tf_op jit(solution)/shard_map/ppermute | solution.py:699
  22.3 1.2 %collective-permute-start.3 = (bf16[64,256]{1,0:T(8,128)(2,1)S(1)}, bf16[64,256]{1,0:T(8,128)(2,1)S(1)}, u32[]{:S(2)}, u32[]{:S(2)}) collective-permute-start(bf16[64,256]{1,0:T(8,128)(2,1)S(1)} %collective-permute-done.2.refs_9_), channel_id=1, source_target_pairs={{0,1},{1,0},{2,3},{3,2},{4,5},{5,4},{6,7},{7,6},{8,9},{9,8},{10,11... | collective-permute-start | bytes 98312 | tf_op jit(solution)/shard_map/ppermute | solution.py:701
  22.3 8.1 %collective-permute-start.5 = (bf16[16,256]{1,0:T(8,128)(2,1)S(1)}, bf16[16,256]{1,0:T(8,128)(2,1)S(1)}, u32[]{:S(2)}, u32[]{:S(2)}) collective-permute-start(bf16[16,256]{1,0:T(8,128)(2,1)S(1)} %get-tuple-element.86), channel_id=1, source_target_pairs={{2,0},{3,1},{6,2},{7,3},{4,6},{5,7},{0,4},{1,5},{10,8},{11,9},{14,... | collective-permute-start | bytes 24584 | tf_op jit(solution)/shard_map/ppermute | solution.py:686
  30.4 12.4 %collective-permute-start.6 = (bf16[800,256]{1,0:T(8,128)(2,1)S(1)}, bf16[800,256]{1,0:T(8,128)(2,1)S(1)}, u32[]{:S(2)}, u32[]{:S(2)}) collective-permute-start(bf16[800,256]{1,0:T(8,128)(2,1)S(1)} %collective-permute-done.4.refs_11_), channel_id=1, source_target_pairs={{0,2},{1,3},{2,6},{3,7},{6,4},{7,5},{4,0},{5,1},{8,10},{9,11},{10,... | collective-permute-start | bytes 1228808 | tf_op jit(solution)/shard_map/ppermute | solution.py:699
  43.9 5.6 %collective-permute-start.7 = (bf16[2304,256]{1,0:T(8,128)(2,1)S(1)}, bf16[2304,256]{1,0:T(8,128)(2,1)S(1)}, u32[]{:S(2)}, u32[]{:S(2)}) collective-permute-start(bf16[2304,256]{1,0:T(8,128)(2,1)S(1)} %get-tuple-element.96), channel_id=1, source_target_pairs={{0,1},{1,0},{2,3},{3,2},{4,5},{5,4},{6,7},{7,6},{8,9},{9,8},{10,11... | collective-permute-start | bytes 3538952 | tf_op jit(solution)/shard_map/ppermute | solution.py:507
  49.7 2.8 %collective-permute-start.9 = (bf16[1024,256]{1,0:T(8,128)(2,1)S(1)}, bf16[1024,256]{1,0:T(8,128)(2,1)S(1)}, u32[]{:S(2)}, u32[]{:S(2)}) collective-permute-start(bf16[1024,256]{1,0:T(8,128)(2,1)S(1)} %get-tuple-element.102), channel_id=1, source_target_pairs={{0,1},{1,0},{2,3},{3,2},{4,5},{5,4},{6,7},{7,6},{8,9},{9,8},{10,11... | collective-permute-start | bytes 1572872 | tf_op jit(solution)/shard_map/ppermute | solution.py:714
  50.2 9.0 %collective-permute-start.8 = (bf16[2,288,256]{2,1,0:T(8,128)(2,1)S(1)}, bf16[2,288,256]{2,1,0:T(8,128)(2,1)S(1)}, u32[]{:S(2)}, u32[]{:S(2)}) collective-permute-start(bf16[2,288,256]{2,1,0:T(8,128)(2,1)S(1)} %get-tuple-element.100), channel_id=1, source_target_pairs={{0,8},{8,0},{16,24},{24,16},{1,9},{9,1},{17,25},{25,17},{2,10},{10... | collective-permute-start | bytes 884744 | tf_op jit(solution)/shard_map/ppermute | solution.py:544
  50.2 9.8 %collective-permute-start.10 = (bf16[2,288,256]{2,1,0:T(8,128)(2,1)S(1)}, bf16[2,288,256]{2,1,0:T(8,128)(2,1)S(1)}, u32[]{:S(2)}, u32[]{:S(2)}) collective-permute-start(bf16[2,288,256]{2,1,0:T(8,128)(2,1)S(1)} %get-tuple-element.105), channel_id=1, source_target_pairs={{0,16},{8,24},{16,0},{24,8},{1,17},{9,25},{17,1},{25,9},{2,18},{10... | collective-permute-start | bytes 884744 | tf_op jit(solution)/shard_map/ppermute | solution.py:544
  60.2 5.6 %collective-permute-start.11 = (bf16[1,288,256]{2,1,0:T(8,128)(2,1)S(1)}, bf16[1,288,256]{2,1,0:T(8,128)(2,1)S(1)}, u32[]{:S(2)}, u32[]{:S(2)}) collective-permute-start(bf16[1,288,256]{2,1,0:T(8,128)(2,1)S(1)} %get-tuple-element.107), channel_id=1, source_target_pairs={{0,16},{8,24},{16,0},{24,8},{1,17},{9,25},{17,1},{25,9},{2,18},{10... | collective-permute-start | bytes 442376 | tf_op jit(solution)/shard_map/ppermute | solution.py:544
  62.0 5.1 %collective-permute-start.12 = (bf16[1,288,256]{2,1,0:T(8,128)(2,1)S(1)}, bf16[1,288,256]{2,1,0:T(8,128)(2,1)S(1)}, u32[]{:S(2)}, u32[]{:S(2)}) collective-permute-start(bf16[1,288,256]{2,1,0:T(8,128)(2,1)S(1)} %get-tuple-element.109), channel_id=1, source_target_pairs={{0,8},{8,0},{16,24},{24,16},{1,9},{9,1},{17,25},{25,17},{2,10},{10... | collective-permute-start | bytes 442376 | tf_op jit(solution)/shard_map/ppermute | solution.py:544
  67.3 8.0 %collective-permute-start.13 = (bf16[144,256]{1,0:T(8,128)(2,1)S(1)}, bf16[144,256]{1,0:T(8,128)(2,1)S(1)}, u32[]{:S(2)}, u32[]{:S(2)}) collective-permute-start(bf16[144,256]{1,0:T(8,128)(2,1)S(1)} %get-tuple-element.111), channel_id=1, source_target_pairs={{0,2},{1,3},{2,4},{3,5},{4,6},{5,7},{6,0},{7,1},{8,10},{9,11},{10,... | collective-permute-start | bytes 221192 | tf_op jit(solution)/shard_map/ppermute | solution.py:588
  68.5 8.8 %collective-permute-start.14 = (bf16[144,256]{1,0:T(8,128)(2,1)S(1)}, bf16[144,256]{1,0:T(8,128)(2,1)S(1)}, u32[]{:S(2)}, u32[]{:S(2)}) collective-permute-start(bf16[144,256]{1,0:T(8,128)(2,1)S(1)} %get-tuple-element.112), channel_id=1, source_target_pairs={{0,4},{1,5},{2,6},{3,7},{4,0},{5,1},{6,2},{7,3},{8,12},{9,13},{10,... | collective-permute-start | bytes 221192 | tf_op jit(solution)/shard_map/ppermute | solution.py:588
  73.3 4.7 %collective-permute-start.15 = (bf16[144,256]{1,0:T(8,128)(2,1)S(1)}, bf16[144,256]{1,0:T(8,128)(2,1)S(1)}, u32[]{:S(2)}, u32[]{:S(2)}) collective-permute-start(bf16[144,256]{1,0:T(8,128)(2,1)S(1)} %get-tuple-element.113), channel_id=1, source_target_pairs={{0,6},{1,7},{2,0},{3,1},{4,2},{5,3},{6,4},{7,5},{8,14},{9,15},{10,... | collective-permute-start | bytes 221192 | tf_op jit(solution)/shard_map/ppermute | solution.py:588
  78.1 4.7 %collective-permute-start.18 = (bf16[144,256]{1,0:T(8,128)(2,1)S(1)}, bf16[144,256]{1,0:T(8,128)(2,1)S(1)}, u32[]{:S(2)}, u32[]{:S(2)}) collective-permute-start(bf16[144,256]{1,0:T(8,128)(2,1)S(1)} %shard_map.112.refs_0_), channel_id=1, source_target_pairs={{0,6},{1,7},{2,0},{3,1},{4,2},{5,3},{6,4},{7,5},{8,14},{9,15},{10,... | collective-permute-start | bytes 221192 | tf_op jit(solution)/shard_map/ppermute | solution.py:598
  80.3 5.3 %collective-permute-start.17 = (bf16[144,256]{1,0:T(8,128)(2,1)S(1)}, bf16[144,256]{1,0:T(8,128)(2,1)S(1)}, u32[]{:S(2)}, u32[]{:S(2)}) collective-permute-start(bf16[144,256]{1,0:T(8,128)(2,1)S(1)} %shard_map.112.refs_0_), channel_id=1, source_target_pairs={{0,4},{1,5},{2,6},{3,7},{4,0},{5,1},{6,2},{7,3},{8,12},{9,13},{10,... | collective-permute-start | bytes 221192 | tf_op jit(solution)/shard_map/ppermute | solution.py:598
  80.3 6.2 %collective-permute-start.16 = (bf16[144,256]{1,0:T(8,128)(2,1)S(1)}, bf16[144,256]{1,0:T(8,128)(2,1)S(1)}, u32[]{:S(2)}, u32[]{:S(2)}) collective-permute-start(bf16[144,256]{1,0:T(8,128)(2,1)S(1)} %shard_map.112.refs_0_), channel_id=1, source_target_pairs={{0,2},{1,3},{2,4},{3,5},{4,6},{5,7},{6,0},{7,1},{8,10},{9,11},{10,... | collective-permute-start | bytes 221192 | tf_op jit(solution)/shard_map/ppermute | solution.py:598
  86.5 1.6 %collective-permute-start.19 = (bf16[576,256]{1,0:T(8,128)(2,1)S(1)}, bf16[576,256]{1,0:T(8,128)(2,1)S(1)}, u32[]{:S(2)}, u32[]{:S(2)}) collective-permute-start(bf16[576,256]{1,0:T(8,128)(2,1)S(1)} %shard_map.113.refs_0_), channel_id=1, source_target_pairs={{0,1},{1,0},{2,3},{3,2},{4,5},{5,4},{6,7},{7,6},{8,9},{9,8},{10,11... | collective-permute-start | bytes 884744 | tf_op jit(solution)/shard_map/ppermute | solution.py:608
